TPU v7x, 32 devices: a whole 2x2x4 slice. The times are simulated.
32 devices in a mesh: groups: 2 (over x), sect: 8 (over z, y), tp: 2 (over core).
Axes of the slice: x: 2, y: 2, z: 4, core: 2. Of those that a mesh axis runs over, the one named last changes fastest.
Arguments:
- hidden_in: bfloat16 [512, 4096], P(('groups', 'sect')), parts along dimension 0, may hold values from -6 to 6
- expert_ids: int32 [512, 8], P(('groups', 'sect')), parts along dimension 0, may hold values from 0 to 31, as said below
- route_scores: float32 [512, 8], P(('groups', 'sect')), parts along dimension 0, may hold values from 0.1 to 1
- expert_slot: int32 [32], replicated, may hold values from 0 to 31, each once
- gate_matrix: bfloat16 [32, 4096, 1024], P('sect', None, 'tp'), may hold values from -0.09375 to 0.09375
- up_matrix: bfloat16 [32, 4096, 1024], P('sect', None, 'tp'), may hold values from -0.09375 to 0.09375
- down_matrix: bfloat16 [32, 1024, 4096], P('sect', 'tp'), may hold values from -0.1875 to 0.1875
Outputs:
- mixed: bfloat16 [512, 4096], P(('groups', 'sect'), 'tp'), parts along dimension 0
There are 2 independent parts, one for each index of `groups`. A program takes and returns all parts, laid end to end along the dimension named above; an argument that names none is the same for every part. Nothing has to cross between parts.
Inputs may be any that keep to these rules, and one draw needn't show every extreme that they name: `expert_ids`: each row names 8 different experts; the 32 rows of one device name any expert at most 16 times, and on every device one or more experts exactly 16 times.
All inputs are finite; a program needn't handle non-finite values.
Results may differ from a plain program's by a relative error of at most 0.0031.
Values may be sent and summed in bfloat16 or wider, within the bound.
No kernel may reach another device: no remote copies, remote signals or barrier semaphores. Data moves between devices by JAX's collectives and lax.ppermute only.
A program may use at most 128 MiB of HBM per device.

v0:
```python
import jax
import jax.numpy as jnp
from jax import lax
from jax.sharding import PartitionSpec as P


def on_device(
    hidden_in, expert_ids, route_scores, expert_slot, gate_matrix, up_matrix, down_matrix
):
    token_count, feature_count = hidden_in.shape
    top_count = expert_ids.shape[1]
    experts = expert_slot.shape[0]
    devices = lax.axis_size("sect")
    local_count = experts // devices
    capacity = 2 * token_count * top_count // experts
    half_width = feature_count // lax.axis_size("tp")
    half_index = lax.axis_index("tp")
    resid = hidden_in.astype(jnp.float32)
    normed = (resid * lax.rsqrt(jnp.mean(resid * resid, axis=-1, keepdims=True) + 1e-06)).astype(
        jnp.bfloat16
    )
    mixing = route_scores / jnp.sum(route_scores, axis=-1, keepdims=True)
    chosen = expert_ids.reshape(-1)
    expert_range = jnp.arange(experts, dtype=jnp.int32)
    expert_hot = (chosen[:, None] == expert_range[None, :]).astype(jnp.int32)
    slot_index = jnp.sum(expert_hot * expert_slot[None, :], axis=1)
    slot_hot = (slot_index[:, None] == expert_range[None, :]).astype(jnp.int32)
    within = jnp.sum((jnp.cumsum(slot_hot, axis=0) - slot_hot) * slot_hot, axis=1)
    position = slot_index * capacity + within
    entries = chosen.shape[0]
    source_row = (
        jnp.zeros((experts * capacity,), jnp.int32)
        .at[position]
        .set(jnp.arange(entries, dtype=jnp.int32) // top_count + 1)
    )
    filled = source_row > 0
    taken_rows = normed[jnp.maximum(source_row - 1, 0)]
    packed = jnp.where(filled[:, None], taken_rows, jnp.zeros_like(taken_rows))
    received = lax.all_to_all(
        packed.reshape(experts, capacity, normed.shape[1]),
        "sect",
        split_axis=0,
        concat_axis=0,
        tiled=True,
    )
    row_count = received.shape[1]
    arrived = received.reshape(devices, local_count, row_count, feature_count)
    gate_act = jnp.einsum(
        "sekd,edf->sekf", arrived, gate_matrix, preferred_element_type=jnp.float32
    )
    up_act = jnp.einsum("sekd,edf->sekf", arrived, up_matrix, preferred_element_type=jnp.float32)
    hidden = (jax.nn.silu(gate_act) * up_act).astype(jnp.bfloat16)
    partial_value = jnp.einsum(
        "sekf,efd->sekd", hidden, down_matrix, preferred_element_type=jnp.float32
    )
    partial_value = partial_value.reshape(experts, row_count, feature_count)
    arrived_back = lax.all_to_all(partial_value, "sect", split_axis=0, concat_axis=0, tiled=True)
    expert_out = lax.psum_scatter(
        arrived_back.reshape(experts * capacity, feature_count),
        "tp",
        scatter_dimension=1,
        tiled=True,
    ).astype(jnp.bfloat16)
    picked = expert_out[position].astype(jnp.float32).reshape(token_count, top_count, half_width)
    combined = jnp.sum(picked * mixing[:, :, None], axis=1)
    own_half = lax.dynamic_slice_in_dim(resid, half_index * half_width, half_width, 1)
    return (own_half + combined).astype(jnp.bfloat16)


def solution(mesh):
    placed = (
        P(("groups", "sect"), None),
        P(("groups", "sect"), None),
        P(("groups", "sect"), None),
        P(),
        P("sect", None, "tp"),
        P("sect", None, "tp"),
        P("sect", "tp", None),
    )
    return jax.shard_map(
        on_device,
        mesh=mesh,
        in_specs=placed,
        out_specs=P(("groups", "sect"), "tp"),
        check_vma=False,
    )
```

profile of v0, /device:TPU:0, one launch (start us, length us, event | category | flops | bytes accessed | tf_op | source)
XLA Modules:
  0.0 361.0 jit_solution(469833072910844849)
XLA Ops:
  6.5 0.0 reduce-scatter.2.cloned.1.call-start
  6.5 0.8 copy.9
  7.3 0.1 eq.38
  7.4 0.7 select_reduce_fusion
  8.2 0.6 reduce-window.6
  8.7 0.2 slice_reduce_fusion
  9.0 0.1 fusion.34
  9.1 1.4 scatter_custom_fusion
  10.5 1.1 multiply_reduce_fusion
  11.7 1.1 multiply_convert_fusion
  12.7 0.1 broadcast_in_dim.11
  12.8 4.3 %gather_fusion = bf16[512,4096]{1,0:T(8,128)(2,1)} fusion(bf16[32,4096]{1,0:T(8,128)(2,1)S(1)} %multiply_convert_fusion, s32[1024]{0:T(1024)S(1)} %pad_clamp_fusion.1), kind=kCustom, calls=%fused_computation | custom fusion | bytes 8390656 | tf_op jit(solution)/shard_map/gather | solution.py:37
  17.2 2.5 broadcast_select_fusion
  19.7 100.3 %all_to_all.10 = bf16[32,16,4096]{2,1,0:T(8,128)(2,1)S(1)} all-to-all(bf16[32,16,4096]{2,1,0:T(8,128)(2,1)S(1)} %broadcast_select_fusion), channel_id=1, replica_groups=mesh['groups'=2,'sect'=8,'tp'=2] {'sect'}, dimensions={0} | all-to-all | bytes 8388608 | tf_op jit(solution)/shard_map/all_to_all | solution.py:39
  120.0 8.1 %fusion.12 = f32[8,4,16,512]{3,2,0,1:T(8,128)S(1)} fusion(bf16[4,4096,512]{2,1,0:T(8,128)(2,1)} %param.11, bf16[8,4,16,4096]{3,2,1,0:T(8,128)(2,1)S(1)} %bitcast.68), kind=kOutput, calls=%fused_computation.15 | convolution fusion | flops 2147483648 | bytes 22020096 | tf_op jit(solution)/shard_map/sekd,edf->sekf/dot_general | solution.py:48
  128.1 8.2 %fusion.27 = bf16[8,4,16,512]{3,2,0,1:T(8,128)(2,1)S(1)} fusion(bf16[4,4096,512]{2,1,0:T(8,128)(2,1)} %param.12, bf16[8,4,16,4096]{3,2,1,0:T(8,128)(2,1)S(1)} %bitcast.69, f32[8,4,16,512]{3,2,0,1:T(8,128)S(1)} %fusion.12), kind=kOutput, calls=%fused_computation.18 | convolution fusion | flops 2149056512 | bytes 22544384 | tf_op jit(solution)/shard_map/sekd,edf->sekf/dot_general | solution.py:51
  136.3 8.1 %fusion.6 = f32[8,4,16,4096]{3,2,0,1:T(8,128)S(1)} fusion(bf16[8,4,16,512]{3,2,0,1:T(8,128)(2,1)S(1)} %fusion.27, bf16[4,512,4096]{2,1,0:T(8,128)(2,1)} %param.13), kind=kOutput, calls=%fused_computation.9 | convolution fusion | flops 2147483648 | bytes 25690112 | tf_op jit(solution)/shard_map/sekf,efd->sekd/dot_general | solution.py:53
  144.4 1.0 copy.12
  145.4 186.6 %all_to_all.11 = f32[32,16,4096]{2,1,0:T(8,128)} all-to-all(f32[32,16,4096]{2,1,0:T(8,128)S(1)} %bitcast.66), channel_id=1, replica_groups=mesh['groups'=2,'sect'=8,'tp'=2] {'sect'}, dimensions={0} | all-to-all | bytes 16777216 | tf_op jit(solution)/shard_map/all_to_all | solution.py:57
  332.1 0.0 copy-start
  332.1 0.0 copy-start.1
  332.1 0.0 reduce-scatter.2.cloned.1.call-update
  332.1 0.9 copy-done
  333.0 0.9 convert_element_type.30
  333.9 0.0 copy-done.1
  333.9 0.1 copy.13
  334.0 13.6 %reduce-scatter.2.cloned.1.call-done = f32[512,2048]{1,0:T(8,128)} async-done(((f32[512,4096]{1,0:T(8,128)}), f32[512,2048]{1,0:T(8,128)}) %reduce-scatter.2.cloned.1.call-update) | async-done | bytes 4194320 | tf_op jit(solution)/shard_map/reduce_scatter | solution.py:58
  347.6 2.5 convert_element_type.35
  350.1 1.4 gather_fusion.1
  351.5 1.0 fusion.11
  352.5 1.6 add_convert_fusion
  (13 shorter events, 0.1 us)
Async XLA Ops:
  6.5 341.1 %reduce-scatter.2.cloned.1.call-start = ((), (), s32[]{:S(2)}) async-start(), calls=%async_computation.3 | async-start | bytes 12582912 | tf_op jit(solution)/shard_map/reduce_scatter | solution.py:58
  332.1 1.0 copy-start
  332.1 1.8 copy-start.1
Sparse Core Ops, SparseCore 0:
  332.2 15.3 reduce-scatter.1
where the time goes:
time: 362 us; the launch traced here: 361 us
  blocking collectives  287 us (79%)
  matrix products  24.4 us (7%)
  waiting for transfers between devices  13.7 us (4%)
  between operations  13.5 us (4%)
  other arithmetic  12.2 us (3%)
  local copies, waits for them, and re-layouts  10.2 us (3%)
    all_to_all x1, blocking collectives, on_device(): lax.all_to_all(partial_value, 'sect', split_axis=0, concat_axis=0, tiled=...  187 us
    all_to_all x1, blocking collectives, on_device(): lax.all_to_all(packed.reshape(experts, capacity, normed.shape[1]), 'sect'...  100 us
    reduce_scatter x1, waiting for transfers between devices, on_device(): lax.psum_scatter(arrived_back.reshape(experts * capacity, feature_count),...  13.6 us
    dot_general x1, matrix products, on_device(): jnp.einsum('sekd,edf->sekf', arrived, up_matrix, preferred_element_type=j...  8.23 us
    dot_general x1, matrix products, on_device(): jnp.einsum('sekf,efd->sekd', hidden, down_matrix, preferred_element_type=...  8.12 us
    dot_general x1, matrix products, on_device(): jnp.einsum('sekd,edf->sekf', arrived, gate_matrix, preferred_element_type...  8.1 us
  transfers between devices with their start and end apart: 1, of which 1 were waited for; matrix products, arithmetic and copies ran while one was open for 0% of the time, Pallas kernels for 0%

commit v1 on v0

v1 whole, which is shorter than its diff:
```python
import functools

import jax
import jax.numpy as jnp
from jax import lax
from jax.experimental import pallas as pl
from jax.experimental.pallas import tpu as pltpu
from jax.sharding import PartitionSpec as P

LANES = 128


def prepare_kernel(half, experts, slot_ref, hidden_ref, own_ref, ids_ref, scores_ref, out_ref):
    resid = hidden_ref[...].astype(jnp.float32)
    scale = lax.rsqrt(jnp.mean(resid * resid, axis=-1, keepdims=True) + 1e-06)
    out_ref[:, :half] = (own_ref[...].astype(jnp.float32) * scale).astype(jnp.bfloat16)
    scores = scores_ref[...]
    mixing = scores / jnp.sum(scores, axis=-1, keepdims=True)
    ids = ids_ref[...]
    width = out_ref.shape[1] - half
    lane = lax.broadcasted_iota(jnp.int32, (1, width), 1)
    slot_of_lane = lax.rem(lane, experts)
    expert_of_lane = jnp.zeros((1, width), jnp.int32)
    for e in range(experts):
        expert_of_lane = jnp.where(slot_of_lane == slot_ref[e], e, expert_of_lane)
    weight = jnp.zeros((ids.shape[0], width), jnp.float32)
    for k in range(ids.shape[1]):
        weight = weight + jnp.where(ids[:, k : k + 1] == expert_of_lane, mixing[:, k : k + 1], 0.0)
    high = weight.astype(jnp.bfloat16)
    rest = weight - high.astype(jnp.float32)
    middle = rest.astype(jnp.bfloat16)
    low = (rest - middle.astype(jnp.float32)).astype(jnp.bfloat16)
    coded = jnp.where(
        lane < experts,
        high.astype(jnp.float32),
        jnp.where(
            lane < 2 * experts,
            middle.astype(jnp.float32),
            jnp.where(lane < 3 * experts, low.astype(jnp.float32), 0.0),
        ),
    )
    out_ref[:, half:] = coded.astype(jnp.bfloat16)


def prepare(hidden_in, own_half, expert_ids, route_scores, expert_slot):
    rows = hidden_in.shape[0]
    half = own_half.shape[1]
    experts = expert_slot.shape[0]
    width = -(-3 * experts // LANES) * LANES
    vmem = pl.BlockSpec(memory_space=pltpu.VMEM)
    return pl.pallas_call(
        functools.partial(prepare_kernel, half, experts),
        out_shape=jax.ShapeDtypeStruct((rows, half + width), jnp.bfloat16),
        in_specs=[pl.BlockSpec(memory_space=pltpu.SMEM), vmem, vmem, vmem, vmem],
        out_specs=vmem,
        compiler_params=pltpu.CompilerParams(vmem_limit_bytes=8 << 20),
        name="prepare",
    )(expert_slot, hidden_in, own_half, expert_ids, route_scores)


def experts_kernel(
    half, experts, place_ref, own_ref, other_ref, gate_ref, up_ref, down_ref, keep_ref, send_ref, acc
):
    e, f = pl.program_id(0), pl.program_id(1)
    last = (e == pl.num_programs(0) - 1) & (f == pl.num_programs(1) - 1)
    first_slot = place_ref[0] * pl.num_programs(0)
    core = place_ref[1]
    own_at = pl.ds(pl.multiple_of(core * half, half), half)
    other_at = pl.ds(pl.multiple_of((1 - core) * half, half), half)
    own, other = own_ref[:, :half], other_ref[...]

    def project(ref):
        return jnp.dot(
            own, ref[0, own_at, :], preferred_element_type=jnp.float32
        ) + jnp.dot(other, ref[0, other_at, :], preferred_element_type=jnp.float32)

    coded = own_ref[:, half:].astype(jnp.float32)
    lane = lax.broadcasted_iota(jnp.int32, coded.shape, 1)
    weight = jnp.sum(
        jnp.where(lax.rem(lane, experts) == first_slot + e, coded, 0.0), axis=1, keepdims=True
    )
    gate_act = project(gate_ref)
    up_act = project(up_ref)
    hidden = gate_act / (1.0 + jnp.exp(-gate_act)) * up_act
    hidden = jnp.where(weight > 0.0, hidden * weight, 0.0).astype(jnp.bfloat16)
    product = jnp.dot(hidden, down_ref[0], preferred_element_type=jnp.float32)

    @pl.when((e == 0) & (f == 0))
    def _():
        acc[...] = product

    @pl.when((e > 0) | (f > 0))
    def _():
        acc[...] += product

    @pl.when(last)
    def _():
        keep_ref[...] = acc[:, own_at]
        send_ref[...] = acc[:, other_at].astype(jnp.bfloat16)


def run_experts(place, own, other, gate_matrix, up_matrix, down_matrix, experts):
    rows, half = other.shape
    local, features, hidden_units = gate_matrix.shape
    cut = 2
    block = hidden_units // cut
    whole = lambda e, f, place: (0, 0)
    return pl.pallas_call(
        functools.partial(experts_kernel, half, experts),
        out_shape=(
            jax.ShapeDtypeStruct((rows, half), jnp.float32),
            jax.ShapeDtypeStruct((rows, half), jnp.bfloat16),
        ),
        grid_spec=pltpu.PrefetchScalarGridSpec(
            num_scalar_prefetch=1,
            grid=(local, cut),
            in_specs=[
                pl.BlockSpec(own.shape, whole),
                pl.BlockSpec(other.shape, whole),
                pl.BlockSpec((1, features, block), lambda e, f, place: (e, 0, f)),
                pl.BlockSpec((1, features, block), lambda e, f, place: (e, 0, f)),
                pl.BlockSpec((1, block, features), lambda e, f, place: (e, f, 0)),
            ],
            out_specs=[pl.BlockSpec((rows, half), whole), pl.BlockSpec((rows, half), whole)],
            scratch_shapes=[pltpu.VMEM((rows, features), jnp.float32)],
        ),
        compiler_params=pltpu.CompilerParams(vmem_limit_bytes=48 << 20),
        name="experts",
    )(place, own, other, gate_matrix, up_matrix, down_matrix)


def on_device(
    hidden_in, expert_ids, route_scores, expert_slot, gate_matrix, up_matrix, down_matrix
):
    token_count, feature_count = hidden_in.shape
    experts = expert_slot.shape[0]
    devices = lax.axis_size("sect")
    half = feature_count // 2
    core = lax.axis_index("tp")
    sect = lax.axis_index("sect")
    inner = 2
    outer = devices // inner

    def along(shift):
        return [
            (o * inner + i, (o + shift) % outer * inner + i)
            for o in range(outer)
            for i in range(inner)
        ]

    across = [(d, d ^ 1) for d in range(devices)]
    cores = [(0, 1), (1, 0)]

    own_half = lax.dynamic_slice_in_dim(hidden_in, core * half, half, 1)
    packed = prepare(hidden_in, own_half, expert_ids, route_scores, expert_slot)
    same = [packed] + [lax.ppermute(packed, "sect", along(k)) for k in range(1, outer)]
    opposite = [lax.ppermute(block, "sect", across) for block in same]
    blocks = same + opposite
    halves = [lax.ppermute(block[:, :half], "tp", cores) for block in blocks]
    own = jnp.concatenate(blocks, 0)
    other = jnp.concatenate(halves, 0)

    place = jnp.stack([sect, core]).astype(jnp.int32)
    total = own.shape[0]
    step = min(total, 256)
    keeps, sends = [], []
    for at in range(0, total, step):
        keep, send = run_experts(
            place, own[at : at + step], other[at : at + step], gate_matrix, up_matrix, down_matrix, experts
        )
        keeps.append(keep)
        sends.append(send)
    keep, send = jnp.concatenate(keeps, 0), jnp.concatenate(sends, 0)
    partial = keep + lax.ppermute(send, "tp", cores).astype(jnp.float32)
    partial = partial.reshape(inner, outer, token_count, half)
    result = own_half.astype(jnp.float32)
    for k in list(range(1, outer)) + [0]:
        crossed = lax.ppermute(partial[1, k].astype(jnp.bfloat16), "sect", across)
        block = partial[0, k] + crossed.astype(jnp.float32)
        if k:
            block = lax.ppermute(block.astype(jnp.bfloat16), "sect", along(-k)).astype(jnp.float32)
        result = result + block
    return result.astype(jnp.bfloat16)


def solution(mesh):
    placed = (
        P(("groups", "sect"), None),
        P(("groups", "sect"), None),
        P(("groups", "sect"), None),
        P(),
        P("sect", None, "tp"),
        P("sect", None, "tp"),
        P("sect", "tp", None),
    )
    return jax.shard_map(
        on_device,
        mesh=mesh,
        in_specs=placed,
        out_specs=P(("groups", "sect"), "tp"),
        check_vma=False,
    )
```

time: 362 us -> 90.5 us (0.25)
  blocking collectives: 287 us -> 0 us
  waiting for transfers between devices: 13.7 us -> 38.9 us
  Pallas kernels: 0 us -> 24.8 us
  matrix products: 24.4 us -> 0 us
  starting transfers between devices: 0.01 us -> 20.5 us
  between operations: 13.5 us -> 0.31 us
  other arithmetic: 12.2 us -> 1.37 us
  local copies, waits for them, and re-layouts: 10.2 us -> 4.38 us
    all_to_all x2 -> x0, blocking collectives: 287 us -> none  [the longest x1 187 us: on_device(): lax.all_to_all(partial_value, 'sect', split_axis=0, concat_axis=0, tiled=...]
    ppermute x0 -> x23, waiting for transfers between devices: none -> 38.9 us  [the longest x3 8.71 us: on_device(): lax.ppermute(packed, 'sect', along(k))]
    pallas_call x0 -> x2, Pallas kernels: none -> 24.8 us  [the longest x1 24 us: run_experts(): pl.pallas_call(functools.partial(experts_kernel, half, experts), out_shap...]
    dot_general x3 -> x0, matrix products: 24.4 us -> none  [the longest x1 8.23 us: on_device(): jnp.einsum('sekd,edf->sekf', arrived, up_matrix, preferred_element_type=j...]
    ppermute x0 -> x23, starting transfers between devices: none -> 20.5 us  [the longest x4 5.64 us: on_device(): opposite = [lax.ppermute(block, 'sect', across) for block in same]]
    reduce_scatter x1 -> x0, waiting for transfers between devices: 13.6 us -> none  [on_device(): lax.psum_scatter(arrived_back.reshape(experts * capacity, feature_count),...]
    gather x2 -> x0, local copies, waits for them, and re-layouts: 5.71 us -> none  [the longest x1 4.35 us: on_device(): taken_rows = normed[jnp.maximum(source_row - 1, 0)]]
    convert_element_type x5 -> x2, other arithmetic: 6.08 us -> 0.86 us  [the longest x1 0.76 us: on_device(): return result.astype(jnp.bfloat16)]
  transfers between devices with their start and end apart: 1 -> 23, of which waited for: 1 -> 15; matrix products, arithmetic and copies ran while one was open for 0% -> 1% of each run, Pallas kernels for 0% -> 0%
where the time goes in v1:
time: 90.5 us; the launch traced here: 90.2 us
  waiting for transfers between devices  38.9 us (43%)
  Pallas kernels  24.8 us (27%)
  starting transfers between devices  20.5 us (23%)
  local copies, waits for them, and re-layouts  4.38 us (5%)
  other arithmetic  1.37 us (2%)
    pallas_call x1, Pallas kernels, run_experts(): pl.pallas_call(functools.partial(experts_kernel, half, experts), out_shap...  24 us
    ppermute x3, waiting for transfers between devices, on_device(): lax.ppermute(packed, 'sect', along(k))  8.71 us
    ppermute x3, waiting for transfers between devices, on_device(): lax.ppermute(block.astype(jnp.bfloat16), 'sect', along(-k))  8.65 us
    ppermute x4, waiting for transfers between devices, on_device(): opposite = [lax.ppermute(block, 'sect', across) for block in same]  8.25 us
    ppermute x4, waiting for transfers between devices, on_device(): crossed = lax.ppermute(partial[1, k].astype(jnp.bfloat16), 'sect', across)  7.91 us
    ppermute x4, starting transfers between devices, on_device(): opposite = [lax.ppermute(block, 'sect', across) for block in same]  5.64 us
    ppermute x3, starting transfers between devices, on_device(): lax.ppermute(block.astype(jnp.bfloat16), 'sect', along(-k))  4.69 us
    ppermute x3, starting transfers between devices, on_device(): lax.ppermute(packed, 'sect', along(k))  4.61 us
  transfers between devices with their start and end apart: 23, of which 15 were waited for; matrix products, arithmetic and copies ran while one was open for 1% of the time, Pallas kernels for 0%

profile of v1, /device:TPU:0, one launch (start us, length us, event | category | flops | bytes accessed | tf_op | source)
XLA Modules:
  0.0 90.2 jit_solution(13699319710235194003)
XLA Ops:
  0.0 0.8 copy.8.ids_ref
  0.8 0.8 copy.9.scores_ref
  1.5 0.9 %constant_dynamic-slice_fusion.own_ref = bf16[32,2048]{1,0:T(8,128)(2,1)S(1)} fusion(bf16[32,4096]{1,0:T(8,128)(2,1)} %hidden_ref.1, s32[]{:T(128)S(6)} %select_n.3), kind=kLoop, calls=%fused_computation.35 | loop fusion | bytes 262148 | tf_op jit(solution)/shard_map/dynamic_slice | solution.py:154
  2.4 0.0 copy-start
  2.5 0.9 %copy-done = bf16[32,4096]{1,0:T(8,128)(2,1)S(1)} copy-done((bf16[32,4096]{1,0:T(8,128)(2,1)S(1)}, bf16[32,4096]{1,0:T(8,128)(2,1)}, u32[]{:S(2)}) %copy-start) | copy-done | bytes 262168
  3.4 0.0 copy-start.2
  3.4 0.7 copy-done.2
  4.0 0.8 prepare.1
  4.8 3.0 %collective-permute-start.3 = (bf16[32,2176]{1,0:T(8,128)(2,1)S(1)}, bf16[32,2176]{1,0:T(8,128)(2,1)S(1)}, u32[]{:S(2)}, u32[]{:S(2)}) collective-permute-start(bf16[32,2176]{1,0:T(8,128)(2,1)S(1)} %prepare.1), channel_id=1, source_target_pairs={{0,2},{2,0},{4,6},{6,4},{8,10},{10,8},{12,14},{14,12},{1,3},{3,1},... | collective-permute-start | bytes 417800 | tf_op jit(solution)/shard_map/ppermute | solution.py:157
  7.9 3.6 %collective-permute-start.2 = (bf16[32,2176]{1,0:T(8,128)(2,1)S(1)}, bf16[32,2176]{1,0:T(8,128)(2,1)S(1)}, u32[]{:S(2)}, u32[]{:S(2)}) collective-permute-start(bf16[32,2176]{1,0:T(8,128)(2,1)S(1)} %prepare.1), channel_id=1, source_target_pairs={{0,12},{2,14},{4,0},{6,2},{8,4},{10,6},{12,8},{14,10},{1,13},{3,15... | collective-permute-start | bytes 417800 | tf_op jit(solution)/shard_map/ppermute | solution.py:156
  11.5 0.0 collective-permute-start.1
  11.5 1.0 %collective-permute-start = (bf16[32,2176]{1,0:T(8,128)(2,1)S(1)}, bf16[32,2176]{1,0:T(8,128)(2,1)S(1)}, u32[]{:S(2)}, u32[]{:S(2)}) collective-permute-start(bf16[32,2176]{1,0:T(8,128)(2,1)S(1)} %prepare.1), channel_id=1, source_target_pairs={{0,4},{2,6},{4,8},{6,10},{8,12},{10,14},{12,0},{14,2},{1,5},{3,7},... | collective-permute-start | bytes 417800 | tf_op jit(solution)/shard_map/ppermute | solution.py:156
  12.5 0.1 collective-permute-start.7
  12.6 0.1 pad_add_fusion.place_ref
  12.7 1.2 %collective-permute-done.7 = bf16[32,2048]{1,0:T(8,128)(2,1)S(1)} collective-permute-done((bf16[32,2048]{1,0:T(8,128)(2,1)S(1)}, bf16[32,2048]{1,0:T(8,128)(2,1)S(1)}, u32[]{:S(2)}, u32[]{:S(2)}) %collective-permute-start.7) | collective-permute-done | bytes 131104 | tf_op jit(solution)/shard_map/ppermute | solution.py:159
  13.9 0.0 collective-permute-done.3
  13.9 0.2 collective-permute-start.11
  14.2 1.4 %collective-permute-done.2 = bf16[32,2176]{1,0:T(8,128)(2,1)S(1)} collective-permute-done((bf16[32,2176]{1,0:T(8,128)(2,1)S(1)}, bf16[32,2176]{1,0:T(8,128)(2,1)S(1)}, u32[]{:S(2)}, u32[]{:S(2)}) %collective-permute-start.2) | collective-permute-done | bytes 139296 | tf_op jit(solution)/shard_map/ppermute | solution.py:156
  15.6 0.1 collective-permute-start.10
  15.7 7.3 %collective-permute-done.1 = bf16[32,2176]{1,0:T(8,128)(2,1)S(1)} collective-permute-done((bf16[32,2176]{1,0:T(8,128)(2,1)S(1)}, bf16[32,2176]{1,0:T(8,128)(2,1)S(1)}, u32[]{:S(2)}, u32[]{:S(2)}) %collective-permute-start.1) | collective-permute-done | bytes 139296 | tf_op jit(solution)/shard_map/ppermute | solution.py:156
  23.0 0.1 collective-permute-start.9
  23.1 0.0 collective-permute-done
  23.1 0.6 collective-permute-start.8
  23.6 0.5 collective-permute-start.6
  24.2 0.4 collective-permute-done.8
  24.6 1.2 %collective-permute-start.5 = (bf16[32,2176]{1,0:T(8,128)(2,1)S(1)}, bf16[32,2176]{1,0:T(8,128)(2,1)S(1)}, u32[]{:S(2)}, u32[]{:S(2)}) collective-permute-start(bf16[32,2176]{1,0:T(8,128)(2,1)S(1)} %collective-permute-done.1), channel_id=1, source_target_pairs={{0,2},{2,0},{4,6},{6,4},{8,10},{10,8},{12,14},{14,12},{1,3},{3,1},... | collective-permute-start | bytes 417800 | tf_op jit(solution)/shard_map/ppermute | solution.py:157
  25.8 0.0 collective-permute-done.9
  25.8 0.9 %collective-permute-start.4 = (bf16[32,2176]{1,0:T(8,128)(2,1)S(1)}, bf16[32,2176]{1,0:T(8,128)(2,1)S(1)}, u32[]{:S(2)}, u32[]{:S(2)}) collective-permute-start(bf16[32,2176]{1,0:T(8,128)(2,1)S(1)} %collective-permute-done), channel_id=1, source_target_pairs={{0,2},{2,0},{4,6},{6,4},{8,10},{10,8},{12,14},{14,12},{1,3},{3,1},... | collective-permute-start | bytes 417800 | tf_op jit(solution)/shard_map/ppermute | solution.py:157
  26.8 0.0 collective-permute-done.10
  26.8 0.0 collective-permute-done.11
  26.8 3.3 %collective-permute-done.6 = bf16[32,2176]{1,0:T(8,128)(2,1)S(1)} collective-permute-done((bf16[32,2176]{1,0:T(8,128)(2,1)S(1)}, bf16[32,2176]{1,0:T(8,128)(2,1)S(1)}, u32[]{:S(2)}, u32[]{:S(2)}) %collective-permute-start.6) | collective-permute-done | bytes 139296 | tf_op jit(solution)/shard_map/ppermute | solution.py:157
  30.2 0.1 collective-permute-start.14
  30.3 2.9 %collective-permute-done.5 = bf16[32,2176]{1,0:T(8,128)(2,1)S(1)} collective-permute-done((bf16[32,2176]{1,0:T(8,128)(2,1)S(1)}, bf16[32,2176]{1,0:T(8,128)(2,1)S(1)}, u32[]{:S(2)}, u32[]{:S(2)}) %collective-permute-start.5) | collective-permute-done | bytes 139296 | tf_op jit(solution)/shard_map/ppermute | solution.py:157
  33.2 0.1 collective-permute-start.13
  33.2 2.0 %collective-permute-done.4 = bf16[32,2176]{1,0:T(8,128)(2,1)S(1)} collective-permute-done((bf16[32,2176]{1,0:T(8,128)(2,1)S(1)}, bf16[32,2176]{1,0:T(8,128)(2,1)S(1)}, u32[]{:S(2)}, u32[]{:S(2)}) %collective-permute-start.4) | collective-permute-done | bytes 139296 | tf_op jit(solution)/shard_map/ppermute | solution.py:157
  35.3 0.1 collective-permute-start.12
  35.4 1.3 %collective-permute-done.12 = bf16[32,2048]{1,0:T(8,128)(2,1)S(1)} collective-permute-done((bf16[32,2048]{1,0:T(8,128)(2,1)S(1)}, bf16[32,2048]{1,0:T(8,128)(2,1)S(1)}, u32[]{:S(2)}, u32[]{:S(2)}) %collective-permute-start.12) | collective-permute-done | bytes 131104 | tf_op jit(solution)/shard_map/ppermute | solution.py:159
  36.7 0.0 collective-permute-done.13
  36.7 0.0 collective-permute-done.14
  36.8 24.0 %experts.1 = (f32[256,2048]{1,0:T(8,128)S(1)}, bf16[256,2048]{1,0:T(8,128)(2,1)S(1)}) custom-call(s32[2]{0:T(128)S(1)} %pad_add_fusion.place_ref, bf16[256,2176]{1,0:T(8,128)(2,1)S(1)} %constant_dynamic-update-slice_fusion.own_ref, bf16[256,2048]{1,0:T(8,128)(2,1)S(1)} %constant_dynamic-update-slice_fusion.8.other_ref, bf16[4,4096,512]{2,1,0:T(8,128)(2,1)} %gate_ref.1, ...), custom_call_target="tpu_custom_call" | custom-call | tf_op jit(solution)/shard_map/experts/pallas_call | solution.py:108
  60.8 0.2 collective-permute-start.15
  61.0 2.5 %collective-permute-done.15 = bf16[256,2048]{1,0:T(8,128)(2,1)S(1)} collective-permute-done((bf16[256,2048]{1,0:T(8,128)(2,1)S(1)}, bf16[256,2048]{1,0:T(8,128)(2,1)S(1)}, u32[]{:S(2)}, u32[]{:S(2)}) %collective-permute-start.15) | collective-permute-done | bytes 1048608 | tf_op jit(solution)/shard_map/ppermute | solution.py:174
  63.5 0.3 convert_add_fusion
  63.8 0.1 convert.6
  63.9 0.0 copy-start.1
  64.0 0.6 collective-permute-start.16
  64.6 1.5 %collective-permute-start.20 = (bf16[32,2048]{1,0:T(8,128)(2,1)S(1)}, bf16[32,2048]{1,0:T(8,128)(2,1)S(1)}, u32[]{:S(2)}, u32[]{:S(2)}) collective-permute-start(bf16[32,2048]{1,0:T(8,128)(2,1)S(1)} %get-tuple-element.14), channel_id=1, source_target_pairs={{0,2},{2,0},{4,6},{6,4},{8,10},{10,8},{12,14},{14,12},{1,3},{3,1},... | collective-permute-start | bytes 393224 | tf_op jit(solution)/shard_map/ppermute | solution.py:178
  66.1 0.5 collective-permute-start.18
  66.6 1.5 %collective-permute-start.22 = (bf16[32,2048]{1,0:T(8,128)(2,1)S(1)}, bf16[32,2048]{1,0:T(8,128)(2,1)S(1)}, u32[]{:S(2)}, u32[]{:S(2)}) collective-permute-start(bf16[32,2048]{1,0:T(8,128)(2,1)S(1)} %get-tuple-element.13), channel_id=1, source_target_pairs={{0,2},{2,0},{4,6},{6,4},{8,10},{10,8},{12,14},{14,12},{1,3},{3,1},... | collective-permute-start | bytes 393224 | tf_op jit(solution)/shard_map/ppermute | solution.py:178
  68.1 2.3 %collective-permute-done.16 = bf16[32,2048]{1,0:T(8,128)(2,1)S(1)} collective-permute-done((bf16[32,2048]{1,0:T(8,128)(2,1)S(1)}, bf16[32,2048]{1,0:T(8,128)(2,1)S(1)}, u32[]{:S(2)}, u32[]{:S(2)}) %collective-permute-start.16) | collective-permute-done | bytes 131104 | tf_op jit(solution)/shard_map/ppermute | solution.py:178
  70.4 2.8 %collective-permute-done.20 = bf16[32,2048]{1,0:T(8,128)(2,1)S(1)} collective-permute-done((bf16[32,2048]{1,0:T(8,128)(2,1)S(1)}, bf16[32,2048]{1,0:T(8,128)(2,1)S(1)}, u32[]{:S(2)}, u32[]{:S(2)}) %collective-permute-start.20) | collective-permute-done | bytes 131104 | tf_op jit(solution)/shard_map/ppermute | solution.py:178
  73.2 2.8 %collective-permute-done.18 = bf16[32,2048]{1,0:T(8,128)(2,1)S(1)} collective-permute-done((bf16[32,2048]{1,0:T(8,128)(2,1)S(1)}, bf16[32,2048]{1,0:T(8,128)(2,1)S(1)}, u32[]{:S(2)}, u32[]{:S(2)}) %collective-permute-start.18) | collective-permute-done | bytes 131104 | tf_op jit(solution)/shard_map/ppermute | solution.py:178
  76.0 0.1 fusion.8
  76.1 1.6 %collective-permute-start.17 = (bf16[32,2048]{1,0:T(8,128)(2,1)S(1)}, bf16[32,2048]{1,0:T(8,128)(2,1)S(1)}, u32[]{:S(2)}, u32[]{:S(2)}) collective-permute-start(bf16[32,2048]{1,0:T(8,128)(2,1)S(1)} %get-tuple-element.9), channel_id=1, source_target_pairs={{0,12},{2,14},{4,0},{6,2},{8,4},{10,6},{12,8},{14,10},{1,13},{3,15... | collective-permute-start | bytes 393224 | tf_op jit(solution)/shard_map/ppermute | solution.py:181
  77.8 0.5 collective-permute-start.21
  78.2 2.6 %collective-permute-start.19 = (bf16[32,2048]{1,0:T(8,128)(2,1)S(1)}, bf16[32,2048]{1,0:T(8,128)(2,1)S(1)}, u32[]{:S(2)}, u32[]{:S(2)}) collective-permute-start(bf16[32,2048]{1,0:T(8,128)(2,1)S(1)} %get-tuple-element.11), channel_id=1, source_target_pairs={{0,8},{2,10},{4,12},{6,14},{8,0},{10,2},{12,4},{14,6},{1,9},{3,11}... | collective-permute-start | bytes 393224 | tf_op jit(solution)/shard_map/ppermute | solution.py:181
  80.8 0.0 collective-permute-done.22
  80.8 3.0 %collective-permute-done.17 = bf16[32,2048]{1,0:T(8,128)(2,1)S(1)} collective-permute-done((bf16[32,2048]{1,0:T(8,128)(2,1)S(1)}, bf16[32,2048]{1,0:T(8,128)(2,1)S(1)}, u32[]{:S(2)}, u32[]{:S(2)}) %collective-permute-start.17) | collective-permute-done | bytes 131104 | tf_op jit(solution)/shard_map/ppermute | solution.py:181
  83.8 2.6 %collective-permute-done.21 = bf16[32,2048]{1,0:T(8,128)(2,1)S(1)} collective-permute-done((bf16[32,2048]{1,0:T(8,128)(2,1)S(1)}, bf16[32,2048]{1,0:T(8,128)(2,1)S(1)}, u32[]{:S(2)}, u32[]{:S(2)}) %collective-permute-start.21) | collective-permute-done | bytes 131104 | tf_op jit(solution)/shard_map/ppermute | solution.py:181
  86.4 3.0 %collective-permute-done.19 = bf16[32,2048]{1,0:T(8,128)(2,1)S(1)} collective-permute-done((bf16[32,2048]{1,0:T(8,128)(2,1)S(1)}, bf16[32,2048]{1,0:T(8,128)(2,1)S(1)}, u32[]{:S(2)}, u32[]{:S(2)}) %collective-permute-start.19) | collective-permute-done | bytes 131104 | tf_op jit(solution)/shard_map/ppermute | solution.py:181
  89.5 0.0 copy-done.1
  89.5 0.8 fusion.2
  (25 shorter events, 0.3 us)
Async XLA Ops:
  2.4 1.0 %copy-start = (bf16[32,4096]{1,0:T(8,128)(2,1)S(1)}, bf16[32,4096]{1,0:T(8,128)(2,1)}, u32[]{:S(2)}) copy-start(bf16[32,4096]{1,0:T(8,128)(2,1)} %hidden_ref.1) | copy-start | bytes 786436
  3.4 0.7 copy-start.2
  4.8 9.1 %collective-permute-start.3 = (bf16[32,2176]{1,0:T(8,128)(2,1)S(1)}, bf16[32,2176]{1,0:T(8,128)(2,1)S(1)}, u32[]{:S(2)}, u32[]{:S(2)}) collective-permute-start(bf16[32,2176]{1,0:T(8,128)(2,1)S(1)} %prepare.1), channel_id=1, source_target_pairs={{0,2},{2,0},{4,6},{6,4},{8,10},{10,8},{12,14},{14,12},{1,3},{3,1},... | collective-permute-start | bytes 417800 | tf_op jit(solution)/shard_map/ppermute | solution.py:157
  7.9 7.7 %collective-permute-start.2 = (bf16[32,2176]{1,0:T(8,128)(2,1)S(1)}, bf16[32,2176]{1,0:T(8,128)(2,1)S(1)}, u32[]{:S(2)}, u32[]{:S(2)}) collective-permute-start(bf16[32,2176]{1,0:T(8,128)(2,1)S(1)} %prepare.1), channel_id=1, source_target_pairs={{0,12},{2,14},{4,0},{6,2},{8,4},{10,6},{12,8},{14,10},{1,13},{3,15... | collective-permute-start | bytes 417800 | tf_op jit(solution)/shard_map/ppermute | solution.py:156
  11.5 11.5 %collective-permute-start.1 = (bf16[32,2176]{1,0:T(8,128)(2,1)S(1)}, bf16[32,2176]{1,0:T(8,128)(2,1)S(1)}, u32[]{:S(2)}, u32[]{:S(2)}) collective-permute-start(bf16[32,2176]{1,0:T(8,128)(2,1)S(1)} %prepare.1), channel_id=1, source_target_pairs={{0,8},{2,10},{4,12},{6,14},{8,0},{10,2},{12,4},{14,6},{1,9},{3,11}... | collective-permute-start | bytes 417800 | tf_op jit(solution)/shard_map/ppermute | solution.py:156
  11.5 11.6 %collective-permute-start = (bf16[32,2176]{1,0:T(8,128)(2,1)S(1)}, bf16[32,2176]{1,0:T(8,128)(2,1)S(1)}, u32[]{:S(2)}, u32[]{:S(2)}) collective-permute-start(bf16[32,2176]{1,0:T(8,128)(2,1)S(1)} %prepare.1), channel_id=1, source_target_pairs={{0,4},{2,6},{4,8},{6,10},{8,12},{10,14},{12,0},{14,2},{1,5},{3,7},... | collective-permute-start | bytes 417800 | tf_op jit(solution)/shard_map/ppermute | solution.py:156
  12.5 1.4 %collective-permute-start.7 = (bf16[32,2048]{1,0:T(8,128)(2,1)S(1)}, bf16[32,2048]{1,0:T(8,128)(2,1)S(1)}, u32[]{:S(2)}, u32[]{:S(2)}) collective-permute-start(bf16[32,2048]{1,0:T(8,128)(2,1)S(1)} %slice.68), channel_id=1, source_target_pairs={{0,1},{1,0},{2,3},{3,2},{4,5},{5,4},{6,7},{7,6},{8,9},{9,8},{10,11... | collective-permute-start | bytes 393224 | tf_op jit(solution)/shard_map/ppermute | solution.py:159
  13.9 12.8 %collective-permute-start.11 = (bf16[32,2048]{1,0:T(8,128)(2,1)S(1)}, bf16[32,2048]{1,0:T(8,128)(2,1)S(1)}, u32[]{:S(2)}, u32[]{:S(2)}) collective-permute-start(bf16[32,2048]{1,0:T(8,128)(2,1)S(1)} %slice.72), channel_id=1, source_target_pairs={{0,1},{1,0},{2,3},{3,2},{4,5},{5,4},{6,7},{7,6},{8,9},{9,8},{10,11... | collective-permute-start | bytes 393224 | tf_op jit(solution)/shard_map/ppermute | solution.py:159
  15.6 11.2 %collective-permute-start.10 = (bf16[32,2048]{1,0:T(8,128)(2,1)S(1)}, bf16[32,2048]{1,0:T(8,128)(2,1)S(1)}, u32[]{:S(2)}, u32[]{:S(2)}) collective-permute-start(bf16[32,2048]{1,0:T(8,128)(2,1)S(1)} %slice.71), channel_id=1, source_target_pairs={{0,1},{1,0},{2,3},{3,2},{4,5},{5,4},{6,7},{7,6},{8,9},{9,8},{10,11... | collective-permute-start | bytes 393224 | tf_op jit(solution)/shard_map/ppermute | solution.py:159
  23.0 2.9 %collective-permute-start.9 = (bf16[32,2048]{1,0:T(8,128)(2,1)S(1)}, bf16[32,2048]{1,0:T(8,128)(2,1)S(1)}, u32[]{:S(2)}, u32[]{:S(2)}) collective-permute-start(bf16[32,2048]{1,0:T(8,128)(2,1)S(1)} %slice.70), channel_id=1, source_target_pairs={{0,1},{1,0},{2,3},{3,2},{4,5},{5,4},{6,7},{7,6},{8,9},{9,8},{10,11... | collective-permute-start | bytes 393224 | tf_op jit(solution)/shard_map/ppermute | solution.py:159
  23.1 1.5 %collective-permute-start.8 = (bf16[32,2048]{1,0:T(8,128)(2,1)S(1)}, bf16[32,2048]{1,0:T(8,128)(2,1)S(1)}, u32[]{:S(2)}, u32[]{:S(2)}) collective-permute-start(bf16[32,2048]{1,0:T(8,128)(2,1)S(1)} %slice.69), channel_id=1, source_target_pairs={{0,1},{1,0},{2,3},{3,2},{4,5},{5,4},{6,7},{7,6},{8,9},{9,8},{10,11... | collective-permute-start | bytes 393224 | tf_op jit(solution)/shard_map/ppermute | solution.py:159
  23.6 6.5 %collective-permute-start.6 = (bf16[32,2176]{1,0:T(8,128)(2,1)S(1)}, bf16[32,2176]{1,0:T(8,128)(2,1)S(1)}, u32[]{:S(2)}, u32[]{:S(2)}) collective-permute-start(bf16[32,2176]{1,0:T(8,128)(2,1)S(1)} %collective-permute-done.2), channel_id=1, source_target_pairs={{0,2},{2,0},{4,6},{6,4},{8,10},{10,8},{12,14},{14,12},{1,3},{3,1},... | collective-permute-start | bytes 417800 | tf_op jit(solution)/shard_map/ppermute | solution.py:157
  24.6 8.5 %collective-permute-start.5 = (bf16[32,2176]{1,0:T(8,128)(2,1)S(1)}, bf16[32,2176]{1,0:T(8,128)(2,1)S(1)}, u32[]{:S(2)}, u32[]{:S(2)}) collective-permute-start(bf16[32,2176]{1,0:T(8,128)(2,1)S(1)} %collective-permute-done.1), channel_id=1, source_target_pairs={{0,2},{2,0},{4,6},{6,4},{8,10},{10,8},{12,14},{14,12},{1,3},{3,1},... | collective-permute-start | bytes 417800 | tf_op jit(solution)/shard_map/ppermute | solution.py:157
  25.8 9.4 %collective-permute-start.4 = (bf16[32,2176]{1,0:T(8,128)(2,1)S(1)}, bf16[32,2176]{1,0:T(8,128)(2,1)S(1)}, u32[]{:S(2)}, u32[]{:S(2)}) collective-permute-start(bf16[32,2176]{1,0:T(8,128)(2,1)S(1)} %collective-permute-done), channel_id=1, source_target_pairs={{0,2},{2,0},{4,6},{6,4},{8,10},{10,8},{12,14},{14,12},{1,3},{3,1},... | collective-permute-start | bytes 417800 | tf_op jit(solution)/shard_map/ppermute | solution.py:157
  30.2 6.6 %collective-permute-start.14 = (bf16[32,2048]{1,0:T(8,128)(2,1)S(1)}, bf16[32,2048]{1,0:T(8,128)(2,1)S(1)}, u32[]{:S(2)}, u32[]{:S(2)}) collective-permute-start(bf16[32,2048]{1,0:T(8,128)(2,1)S(1)} %slice.75), channel_id=1, source_target_pairs={{0,1},{1,0},{2,3},{3,2},{4,5},{5,4},{6,7},{7,6},{8,9},{9,8},{10,11... | collective-permute-start | bytes 393224 | tf_op jit(solution)/shard_map/ppermute | solution.py:159
  33.2 3.5 %collective-permute-start.13 = (bf16[32,2048]{1,0:T(8,128)(2,1)S(1)}, bf16[32,2048]{1,0:T(8,128)(2,1)S(1)}, u32[]{:S(2)}, u32[]{:S(2)}) collective-permute-start(bf16[32,2048]{1,0:T(8,128)(2,1)S(1)} %slice.74), channel_id=1, source_target_pairs={{0,1},{1,0},{2,3},{3,2},{4,5},{5,4},{6,7},{7,6},{8,9},{9,8},{10,11... | collective-permute-start | bytes 393224 | tf_op jit(solution)/shard_map/ppermute | solution.py:159
  35.3 1.4 %collective-permute-start.12 = (bf16[32,2048]{1,0:T(8,128)(2,1)S(1)}, bf16[32,2048]{1,0:T(8,128)(2,1)S(1)}, u32[]{:S(2)}, u32[]{:S(2)}) collective-permute-start(bf16[32,2048]{1,0:T(8,128)(2,1)S(1)} %slice.73), channel_id=1, source_target_pairs={{0,1},{1,0},{2,3},{3,2},{4,5},{5,4},{6,7},{7,6},{8,9},{9,8},{10,11... | collective-permute-start | bytes 393224 | tf_op jit(solution)/shard_map/ppermute | solution.py:159
  60.8 2.7 %collective-permute-start.15 = (bf16[256,2048]{1,0:T(8,128)(2,1)S(1)}, bf16[256,2048]{1,0:T(8,128)(2,1)S(1)}, u32[]{:S(2)}, u32[]{:S(2)}) collective-permute-start(bf16[256,2048]{1,0:T(8,128)(2,1)S(1)} %get-tuple-element.8), channel_id=1, source_target_pairs={{0,1},{1,0},{2,3},{3,2},{4,5},{5,4},{6,7},{7,6},{8,9},{9,8},{10,11... | collective-permute-start | bytes 3145736 | tf_op jit(solution)/shard_map/ppermute | solution.py:174
  63.9 25.5 %copy-start.1 = (bf16[32,4096]{1,0:T(8,128)(2,1)S(1)}, bf16[32,4096]{1,0:T(8,128)(2,1)}, u32[]{:S(2)}) copy-start(bf16[32,4096]{1,0:T(8,128)(2,1)} %hidden_ref.1) | copy-start | bytes 786436
  64.0 6.4 %collective-permute-start.16 = (bf16[32,2048]{1,0:T(8,128)(2,1)S(1)}, bf16[32,2048]{1,0:T(8,128)(2,1)S(1)}, u32[]{:S(2)}, u32[]{:S(2)}) collective-permute-start(bf16[32,2048]{1,0:T(8,128)(2,1)S(1)} %get-tuple-element.12), channel_id=1, source_target_pairs={{0,2},{2,0},{4,6},{6,4},{8,10},{10,8},{12,14},{14,12},{1,3},{3,1},... | collective-permute-start | bytes 393224 | tf_op jit(solution)/shard_map/ppermute | solution.py:178
  64.6 8.7 %collective-permute-start.20 = (bf16[32,2048]{1,0:T(8,128)(2,1)S(1)}, bf16[32,2048]{1,0:T(8,128)(2,1)S(1)}, u32[]{:S(2)}, u32[]{:S(2)}) collective-permute-start(bf16[32,2048]{1,0:T(8,128)(2,1)S(1)} %get-tuple-element.14), channel_id=1, source_target_pairs={{0,2},{2,0},{4,6},{6,4},{8,10},{10,8},{12,14},{14,12},{1,3},{3,1},... | collective-permute-start | bytes 393224 | tf_op jit(solution)/shard_map/ppermute | solution.py:178
  66.1 9.9 %collective-permute-start.18 = (bf16[32,2048]{1,0:T(8,128)(2,1)S(1)}, bf16[32,2048]{1,0:T(8,128)(2,1)S(1)}, u32[]{:S(2)}, u32[]{:S(2)}) collective-permute-start(bf16[32,2048]{1,0:T(8,128)(2,1)S(1)} %get-tuple-element.15), channel_id=1, source_target_pairs={{0,2},{2,0},{4,6},{6,4},{8,10},{10,8},{12,14},{14,12},{1,3},{3,1},... | collective-permute-start | bytes 393224 | tf_op jit(solution)/shard_map/ppermute | solution.py:178
  66.6 14.2 %collective-permute-start.22 = (bf16[32,2048]{1,0:T(8,128)(2,1)S(1)}, bf16[32,2048]{1,0:T(8,128)(2,1)S(1)}, u32[]{:S(2)}, u32[]{:S(2)}) collective-permute-start(bf16[32,2048]{1,0:T(8,128)(2,1)S(1)} %get-tuple-element.13), channel_id=1, source_target_pairs={{0,2},{2,0},{4,6},{6,4},{8,10},{10,8},{12,14},{14,12},{1,3},{3,1},... | collective-permute-start | bytes 393224 | tf_op jit(solution)/shard_map/ppermute | solution.py:178
  76.1 7.7 %collective-permute-start.17 = (bf16[32,2048]{1,0:T(8,128)(2,1)S(1)}, bf16[32,2048]{1,0:T(8,128)(2,1)S(1)}, u32[]{:S(2)}, u32[]{:S(2)}) collective-permute-start(bf16[32,2048]{1,0:T(8,128)(2,1)S(1)} %get-tuple-element.9), channel_id=1, source_target_pairs={{0,12},{2,14},{4,0},{6,2},{8,4},{10,6},{12,8},{14,10},{1,13},{3,15... | collective-permute-start | bytes 393224 | tf_op jit(solution)/shard_map/ppermute | solution.py:181
  77.8 8.7 %collective-permute-start.21 = (bf16[32,2048]{1,0:T(8,128)(2,1)S(1)}, bf16[32,2048]{1,0:T(8,128)(2,1)S(1)}, u32[]{:S(2)}, u32[]{:S(2)}) collective-permute-start(bf16[32,2048]{1,0:T(8,128)(2,1)S(1)} %get-tuple-element.10), channel_id=1, source_target_pairs={{0,4},{2,6},{4,8},{6,10},{8,12},{10,14},{12,0},{14,2},{1,5},{3,7},... | collective-permute-start | bytes 393224 | tf_op jit(solution)/shard_map/ppermute | solution.py:181
  78.2 11.3 %collective-permute-start.19 = (bf16[32,2048]{1,0:T(8,128)(2,1)S(1)}, bf16[32,2048]{1,0:T(8,128)(2,1)S(1)}, u32[]{:S(2)}, u32[]{:S(2)}) collective-permute-start(bf16[32,2048]{1,0:T(8,128)(2,1)S(1)} %get-tuple-element.11), channel_id=1, source_target_pairs={{0,8},{2,10},{4,12},{6,14},{8,0},{10,2},{12,4},{14,6},{1,9},{3,11}... | collective-permute-start | bytes 393224 | tf_op jit(solution)/shard_map/ppermute | solution.py:181

commit v2 on v0

v2 whole, which is shorter than its diff:
```python
import functools

import jax
import jax.numpy as jnp
from jax import lax
from jax.experimental import pallas as pl
from jax.experimental.pallas import tpu as pltpu
from jax.sharding import PartitionSpec as P

LANES = 128


def prepare_kernel(half, experts, place_ref, slot_ref, hidden_ref, ids_ref, scores_ref, out_ref):
    resid = hidden_ref[...].astype(jnp.float32)
    scale = lax.rsqrt(jnp.mean(resid * resid, axis=-1, keepdims=True) + 1e-06)
    own = hidden_ref[:, pl.ds(pl.multiple_of(place_ref[1] * half, half), half)]
    out_ref[:, :half] = (own.astype(jnp.float32) * scale).astype(jnp.bfloat16)
    scores = scores_ref[...]
    mixing = scores / jnp.sum(scores, axis=0, keepdims=True)
    ids = ids_ref[...]
    width = out_ref.shape[1] - half
    row = lax.broadcasted_iota(jnp.int32, (width, 1), 0)
    slot_of_row = lax.rem(row, experts)
    expert_of_row = jnp.zeros((width, 1), jnp.int32)
    for e in range(experts):
        expert_of_row = jnp.where(slot_of_row == slot_ref[e], e, expert_of_row)
    weight = jnp.zeros((width, ids.shape[1]), jnp.float32)
    for k in range(ids.shape[0]):
        weight = weight + jnp.where(ids[k : k + 1, :] == expert_of_row, mixing[k : k + 1, :], 0.0)
    high = weight.astype(jnp.bfloat16).astype(jnp.float32)
    middle = (weight - high).astype(jnp.bfloat16).astype(jnp.float32)
    low = weight - high - middle
    coded = jnp.where(
        row < experts,
        high,
        jnp.where(row < 2 * experts, middle, jnp.where(row < 3 * experts, low, 0.0)),
    )
    out_ref[:, half:] = coded.T.astype(jnp.bfloat16)


def prepare(place, hidden_in, expert_ids, route_scores, expert_slot):
    rows, features = hidden_in.shape
    half = features // 2
    experts = expert_slot.shape[0]
    width = -(-3 * experts // LANES) * LANES
    vmem = pl.BlockSpec(memory_space=pltpu.VMEM)
    smem = pl.BlockSpec(memory_space=pltpu.SMEM)
    return pl.pallas_call(
        functools.partial(prepare_kernel, half, experts),
        out_shape=jax.ShapeDtypeStruct((rows, half + width), jnp.bfloat16),
        in_specs=[smem, smem, vmem, vmem, vmem],
        out_specs=vmem,
        compiler_params=pltpu.CompilerParams(vmem_limit_bytes=8 << 20),
        name="prepare",
    )(place, expert_slot, hidden_in, expert_ids.T, route_scores.T)


def load_kernel(matrix_ref, *refs):
    out_refs, sem = refs[:-1], refs[-1]
    copies = [
        pltpu.make_async_copy(matrix_ref.at[i], out_ref, sem.at[i])
        for i, out_ref in enumerate(out_refs)
    ]
    for copy in copies:
        copy.start()
    for copy in copies:
        copy.wait()


def load(matrix):
    local = matrix.shape[0]
    return pl.pallas_call(
        load_kernel,
        out_shape=[pltpu.VMEM(matrix.shape[1:], matrix.dtype)] * local,
        in_specs=[pl.BlockSpec(memory_space=pltpu.HBM)],
        out_specs=[pl.BlockSpec(memory_space=pltpu.VMEM)] * local,
        scratch_shapes=[pltpu.SemaphoreType.DMA((local,))],
        compiler_params=pltpu.CompilerParams(vmem_limit_bytes=1 << 20),
        cost_estimate=pl.CostEstimate(flops=0, bytes_accessed=matrix.size // 8, transcendentals=0),
        name="load",
    )(pltpu.with_memory_space_constraint(matrix, pltpu.HBM))


def after(value, *others):
    return lax.optimization_barrier((value, *others))[0]


def hidden_kernel(half, experts, blocks, place_ref, *refs):
    own_refs, other_refs = refs[:blocks], refs[blocks : 2 * blocks]
    out_ref, own, other, coded = refs[-4:]
    weights = refs[2 * blocks : -4]
    local = len(weights) // 2
    gate_refs, up_refs = weights[:local], weights[local:]
    units = gate_refs[0].shape[1]
    first_slot = place_ref[0] * local
    own_at = pl.ds(pl.multiple_of(place_ref[1] * half, half), half)
    other_at = pl.ds(pl.multiple_of((1 - place_ref[1]) * half, half), half)
    tokens = own_refs[0].shape[0]
    for i in range(blocks):
        rows = slice(i * tokens, (i + 1) * tokens)
        own[rows, :] = own_refs[i][:, :half]
        other[rows, :] = other_refs[i][:, :half]
        coded[rows, :] = own_refs[i][:, half:].astype(jnp.float32)
    slot = lax.rem(lax.broadcasted_iota(jnp.int32, coded.shape, 1), experts)
    block = min(units, 256)
    for e in range(local):
        weight = jnp.sum(jnp.where(slot == first_slot + e, coded[...], 0.0), axis=1, keepdims=True)
        for at in range(0, units, block):
            cut = slice(at, at + block)

            def project(ref):
                return jnp.dot(
                    own[...], ref[own_at, cut], preferred_element_type=jnp.float32
                ) + jnp.dot(other[...], ref[other_at, cut], preferred_element_type=jnp.float32)

            gate_act = project(gate_refs[e])
            up_act = project(up_refs[e])
            hidden = gate_act / (1.0 + jnp.exp(-gate_act)) * up_act
            hidden = jnp.where(weight > 0.0, hidden * weight, 0.0)
            out_ref[:, e * units + at : e * units + at + block] = hidden.astype(jnp.bfloat16)


def run_hidden(place, own, other, gate, up, experts):
    blocks = len(own)
    rows, half = blocks * own[0].shape[0], gate[0].shape[0] // 2
    units = len(gate) * gate[0].shape[1]
    vmem = pl.BlockSpec(memory_space=pltpu.VMEM)
    return pl.pallas_call(
        functools.partial(hidden_kernel, half, experts, blocks),
        out_shape=jax.ShapeDtypeStruct((rows, units), jnp.bfloat16),
        in_specs=[pl.BlockSpec(memory_space=pltpu.SMEM)] + [vmem] * (2 * blocks + 2 * len(gate)),
        out_specs=vmem,
        scratch_shapes=[
            pltpu.VMEM((rows, half), jnp.bfloat16),
            pltpu.VMEM((rows, half), jnp.bfloat16),
            pltpu.VMEM((rows, own[0].shape[1] - half), jnp.float32),
        ],
        compiler_params=pltpu.CompilerParams(vmem_limit_bytes=6 << 20),
        cost_estimate=pl.CostEstimate(
            flops=4 * rows * units * 2 * half, bytes_accessed=rows * half * 4, transcendentals=rows * units
        ),
        name="hidden",
    )(place, *own, *other, *gate, *up)


def down_kernel(mine, place_ref, hidden_ref, *refs):
    out_ref = refs[-1]
    down_refs = refs[: -2 if mine else -1]
    local, (units, features) = len(down_refs), down_refs[0].shape
    half = features // 2
    core = place_ref[1] if mine else 1 - place_ref[1]
    block = 512
    for at in range(0, half, block):
        cut = pl.ds(pl.multiple_of(core * half + at, block), block)
        total = jnp.zeros((hidden_ref.shape[0], block), jnp.float32)
        for e in range(local):
            total = total + jnp.dot(
                hidden_ref[:, e * units : (e + 1) * units],
                down_refs[e][:, cut],
                preferred_element_type=jnp.float32,
            )
        if mine:
            total = total + refs[-2][:, at : at + block].astype(jnp.float32)
        out_ref[:, at : at + block] = total.astype(out_ref.dtype)


def run_down(place, hidden, down, received, kind):
    rows, half = hidden.shape[0], down[0].shape[1] // 2
    vmem = pl.BlockSpec(memory_space=pltpu.VMEM)
    extra = [] if received is None else [received]
    return pl.pallas_call(
        functools.partial(down_kernel, received is not None),
        out_shape=jax.ShapeDtypeStruct((rows, half), kind),
        in_specs=[pl.BlockSpec(memory_space=pltpu.SMEM), vmem] + [vmem] * len((*down, *extra)),
        out_specs=vmem,
        compiler_params=pltpu.CompilerParams(vmem_limit_bytes=6 << 20),
        cost_estimate=pl.CostEstimate(
            flops=2 * rows * half * hidden.shape[1], bytes_accessed=rows * half * 4, transcendentals=0
        ),
        name="down_mine" if extra else "down_other",
    )(place, hidden, *down, *extra)


def on_device(
    hidden_in, expert_ids, route_scores, expert_slot, gate_matrix, up_matrix, down_matrix
):
    token_count, feature_count = hidden_in.shape
    experts = expert_slot.shape[0]
    devices = lax.axis_size("sect")
    half = feature_count // 2
    core = lax.axis_index("tp")
    sect = lax.axis_index("sect")
    inner = 2
    outer = devices // inner

    def along(shift):
        return [
            (o * inner + i, (o + shift) % outer * inner + i)
            for o in range(outer)
            for i in range(inner)
        ]

    across = [(d, d ^ 1) for d in range(devices)]
    cores = [(0, 1), (1, 0)]
    place = jnp.stack([sect, core]).astype(jnp.int32)
    bf16, f32 = jnp.bfloat16, jnp.float32

    packed = prepare(place, hidden_in, expert_ids, route_scores, expert_slot)
    shifts = sorted(range(1, outer), key=lambda k: min(k, outer - k))
    early, late = shifts[: len(shifts) * 2 // 3], shifts[len(shifts) * 2 // 3 :]
    same, opposite = {0: packed}, {0: lax.ppermute(packed, "sect", across)}
    for k in shifts:
        same[k] = lax.ppermute(packed, "sect", along(k))
    gate_here = load(after(gate_matrix, packed))
    for k in early:
        opposite[k] = lax.ppermute(after(same[k], *gate_here), "sect", across)
    up_here = load(after(up_matrix, *gate_here, *[same[k] for k in early]))
    for k in late:
        opposite[k] = lax.ppermute(after(same[k], *up_here), "sect", across)
    down_here = load(after(down_matrix, *up_here, *[same[k] for k in late]))
    hidden = []
    for blocks in (same, opposite):
        blocks = [blocks[k] for k in range(outer)]
        halves = [lax.ppermute(block, "tp", cores) for block in blocks]
        if hidden:
            blocks[0] = after(blocks[0], hidden[0])
        hidden.append(run_hidden(place, blocks, halves, gate_here, up_here, experts))
    near, far = hidden
    far_send = lax.ppermute(run_down(place, far, down_here, None, bf16), "tp", cores)
    near_send = lax.ppermute(run_down(place, near, down_here, None, bf16), "tp", cores)
    far_sum = run_down(place, far, down_here, far_send, bf16)
    near_sum = run_down(place, near, down_here, near_send, f32)
    far_sum = far_sum.reshape(outer, token_count, half)
    near_sum = near_sum.reshape(outer, token_count, half)
    result = lax.dynamic_slice_in_dim(hidden_in, core * half, half, 1).astype(f32)
    order = sorted(range(1, outer), key=lambda k: -min(k, outer - k)) + [0]
    for k in order:
        block = near_sum[k] + lax.ppermute(far_sum[k], "sect", across).astype(f32)
        if k:
            block = lax.ppermute(block.astype(bf16), "sect", along(-k)).astype(f32)
        result = result + block
    return result.astype(bf16)


def solution(mesh):
    placed = (
        P(("groups", "sect"), None),
        P(("groups", "sect"), None),
        P(("groups", "sect"), None),
        P(),
        P("sect", None, "tp"),
        P("sect", None, "tp"),
        P("sect", "tp", None),
    )
    return jax.shard_map(
        on_device,
        mesh=mesh,
        in_specs=placed,
        out_specs=P(("groups", "sect"), "tp"),
        check_vma=False,
    )
```

time: 362 us -> 81.3 us (0.22)
  blocking collectives: 287 us -> 0 us
  Pallas kernels: 0 us -> 36.5 us
  matrix products: 24.4 us -> 0 us
  starting transfers between devices: 0.01 us -> 21 us
  between operations: 13.5 us -> 0.18 us
  other arithmetic: 12.2 us -> 0.91 us
  local copies, waits for them, and re-layouts: 10.2 us -> 4.98 us
  waiting for transfers between devices: 13.7 us -> 17.6 us
    all_to_all x2 -> x0, blocking collectives: 287 us -> none  [the longest x1 187 us: on_device(): lax.all_to_all(partial_value, 'sect', split_axis=0, concat_axis=0, tiled=...]
    pallas_call x0 -> x10, Pallas kernels: none -> 36.5 us  [the longest x3 17.7 us: load(): pl.pallas_call(load_kernel, out_shape=[pltpu.VMEM(matrix.shape[1:], matri...]
    dot_general x3 -> x0, matrix products: 24.4 us -> none  [the longest x1 8.23 us: on_device(): jnp.einsum('sekd,edf->sekf', arrived, up_matrix, preferred_element_type=j...]
    ppermute x0 -> x24, starting transfers between devices: none -> 21 us  [the longest x3 6.1 us: on_device(): same[k] = lax.ppermute(packed, 'sect', along(k))]
    ppermute x0 -> x24, waiting for transfers between devices: none -> 17.6 us  [the longest x3 8.14 us: on_device(): block = lax.ppermute(block.astype(bf16), 'sect', along(-k)).astype(f32)]
    reduce_scatter x1 -> x0, waiting for transfers between devices: 13.6 us -> none  [on_device(): lax.psum_scatter(arrived_back.reshape(experts * capacity, feature_count),...]
    gather x2 -> x0, local copies, waits for them, and re-layouts: 5.71 us -> none  [the longest x1 4.35 us: on_device(): taken_rows = normed[jnp.maximum(source_row - 1, 0)]]
    convert_element_type x5 -> x2, other arithmetic: 6.08 us -> 0.83 us  [the longest x1 0.76 us: on_device(): return result.astype(bf16)]
  transfers between devices with their start and end apart: 1 -> 24, of which waited for: 1 -> 5; matrix products, arithmetic and copies ran while one was open for 0% -> 0% of each run, Pallas kernels for 0% -> 35%
where the time goes in v2:
time: 81.3 us; the launch traced here: 81.1 us
  Pallas kernels  36.5 us (45%)
  starting transfers between devices  21 us (26%)
  waiting for transfers between devices  17.6 us (22%)
  local copies, waits for them, and re-layouts  4.98 us (6%)
  other arithmetic  0.91 us (1%)
    pallas_call x3, Pallas kernels, load(): pl.pallas_call(load_kernel, out_shape=[pltpu.VMEM(matrix.shape[1:], matri...  17.7 us
    pallas_call x2, Pallas kernels, run_hidden(): pl.pallas_call(functools.partial(hidden_kernel, half, experts, blocks), o...  10.5 us
    ppermute x3, waiting for transfers between devices, on_device(): block = lax.ppermute(block.astype(bf16), 'sect', along(-k)).astype(f32)  8.14 us
    pallas_call x4, Pallas kernels, run_down(): pl.pallas_call(functools.partial(down_kernel, received is not None), out_...  7.51 us
    ppermute x3, starting transfers between devices, on_device(): same[k] = lax.ppermute(packed, 'sect', along(k))  6.1 us
    ppermute x4, waiting for transfers between devices, on_device(): block = near_sum[k] + lax.ppermute(far_sum[k], 'sect', across).astype(f32)  5.94 us
    unnamed x14, local copies, waits for them, and re-layouts  4.94 us
    ppermute x3, starting transfers between devices, on_device(): block = lax.ppermute(block.astype(bf16), 'sect', along(-k)).astype(f32)  4.22 us
  transfers between devices with their start and end apart: 24, of which 5 were waited for; matrix products, arithmetic and copies ran while one was open for 0% of the time, Pallas kernels for 35%

profile of v2, /device:TPU:0, one launch (start us, length us, event | category | flops | bytes accessed | tf_op | source)
XLA Modules:
  0.0 81.1 jit_solution(1608604090121068571)
XLA Ops:
  0.0 0.1 pad_add_fusion.place_ref
  0.1 0.9 %copy-done.2 = bf16[32,4096]{1,0:T(8,128)(2,1)S(1)} copy-done((bf16[32,4096]{1,0:T(8,128)(2,1)S(1)}, bf16[32,4096]{1,0:T(8,128)(2,1)}, u32[]{:S(2)}) %copy-start.2) | copy-done | bytes 262168
  1.0 0.7 copy-done.4
  1.7 0.7 copy-done.5
  2.4 0.7 copy-done.6
  3.1 0.8 prepare.1.refs_0_
  3.9 3.1 %collective-permute-start = (bf16[32,2176]{1,0:T(8,128)(2,1)S(1)}, bf16[32,2176]{1,0:T(8,128)(2,1)S(1)}, u32[]{:S(2)}, u32[]{:S(2)}) collective-permute-start(bf16[32,2176]{1,0:T(8,128)(2,1)S(1)} %prepare.1.refs_0_), channel_id=1, source_target_pairs={{0,4},{2,6},{4,8},{6,10},{8,12},{10,14},{12,0},{14,2},{1,5},{3,7},... | collective-permute-start | bytes 417800 | tf_op jit(solution)/shard_map/ppermute | solution.py:213
  6.9 2.1 %collective-permute-start.2 = (bf16[32,2176]{1,0:T(8,128)(2,1)S(1)}, bf16[32,2176]{1,0:T(8,128)(2,1)S(1)}, u32[]{:S(2)}, u32[]{:S(2)}) collective-permute-start(bf16[32,2176]{1,0:T(8,128)(2,1)S(1)} %prepare.1.refs_0_), channel_id=1, source_target_pairs={{0,12},{2,14},{4,0},{6,2},{8,4},{10,6},{12,8},{14,10},{1,13},{3,15... | collective-permute-start | bytes 417800 | tf_op jit(solution)/shard_map/ppermute | solution.py:213
  9.0 0.9 %collective-permute-start.1 = (bf16[32,2176]{1,0:T(8,128)(2,1)S(1)}, bf16[32,2176]{1,0:T(8,128)(2,1)S(1)}, u32[]{:S(2)}, u32[]{:S(2)}) collective-permute-start(bf16[32,2176]{1,0:T(8,128)(2,1)S(1)} %prepare.1.refs_0_), channel_id=1, source_target_pairs={{0,8},{2,10},{4,12},{6,14},{8,0},{10,2},{12,4},{14,6},{1,9},{3,11}... | collective-permute-start | bytes 417800 | tf_op jit(solution)/shard_map/ppermute | solution.py:213
  10.0 0.0 collective-permute-start.3
  10.0 1.5 %collective-permute-start.8 = (bf16[32,2176]{1,0:T(8,128)(2,1)S(1)}, bf16[32,2176]{1,0:T(8,128)(2,1)S(1)}, u32[]{:S(2)}, u32[]{:S(2)}) collective-permute-start(bf16[32,2176]{1,0:T(8,128)(2,1)S(1)} %prepare.1.refs_0_), channel_id=1, source_target_pairs={{0,2},{2,0},{4,6},{6,4},{8,10},{10,8},{12,14},{14,12},{1,3},{3,1},... | collective-permute-start | bytes 417800 | tf_op jit(solution)/shard_map/ppermute | solution.py:211
  11.5 5.9 %load.3 = (bf16[4096,512]{1,0:T(8,128)(2,1)S(1)}, bf16[4096,512]{1,0:T(8,128)(2,1)S(1)}, bf16[4096,512]{1,0:T(8,128)(2,1)S(1)}, bf16[4096,512]{1,0:T(8,128)(2,1)S(1)}) custom-call(bf16[4,4096,512]{2,1,0:T(8,128)(2,1)} %matrix_ref), custom_call_target="tpu_custom_call" | custom-call | bytes 1048576 | tf_op jit(solution)/shard_map/load/pallas_call | solution.py:72
  17.4 2.0 %copy-done = bf16[4096,512]{1,0:T(8,128)(2,1)} copy-done((bf16[4096,512]{1,0:T(8,128)(2,1)}, bf16[4096,512]{1,0:T(8,128)(2,1)S(1)}, u32[]{:S(2)}) %copy-start) | copy-done | bytes 4194328
  19.3 0.0 collective-permute-done.refs_1_
  19.3 0.0 collective-permute-done.2.refs_3_
  19.4 5.9 %load.4 = (bf16[4096,512]{1,0:T(8,128)(2,1)S(1)}, bf16[4096,512]{1,0:T(8,128)(2,1)S(1)}, bf16[4096,512]{1,0:T(8,128)(2,1)S(1)}, bf16[4096,512]{1,0:T(8,128)(2,1)S(1)}) custom-call(bf16[4,4096,512]{2,1,0:T(8,128)(2,1)} %matrix_ref.1), custom_call_target="tpu_custom_call" | custom-call | bytes 1048576 | tf_op jit(solution)/shard_map/load/pallas_call | solution.py:72
  25.2 0.0 collective-permute-done.1.refs_2_
  25.3 0.6 collective-permute-start.10
  25.8 0.0 collective-permute-start.4
  25.8 0.5 collective-permute-start.5
  26.4 0.0 collective-permute-done.3.refs_4_
  26.4 1.5 %collective-permute-start.11 = (bf16[32,2176]{1,0:T(8,128)(2,1)S(1)}, bf16[32,2176]{1,0:T(8,128)(2,1)S(1)}, u32[]{:S(2)}, u32[]{:S(2)}) collective-permute-start(bf16[32,2176]{1,0:T(8,128)(2,1)S(1)} %collective-permute-done.2.refs_3_), channel_id=1, source_target_pairs={{0,2},{2,0},{4,6},{6,4},{8,10},{10,8},{12,14},{14,12},{1,3},{3,1},... | collective-permute-start | bytes 417800 | tf_op jit(solution)/shard_map/ppermute | solution.py:216
  27.9 0.0 collective-permute-done.8.refs_0_
  27.9 0.5 collective-permute-start.9
  28.4 3.5 %collective-permute-done.10.refs_2_ = bf16[32,2176]{1,0:T(8,128)(2,1)S(1)} collective-permute-done((bf16[32,2176]{1,0:T(8,128)(2,1)S(1)}, bf16[32,2176]{1,0:T(8,128)(2,1)S(1)}, u32[]{:S(2)}, u32[]{:S(2)}) %collective-permute-start.10) | collective-permute-done | bytes 139296 | tf_op jit(solution)/shard_map/ppermute | solution.py:219
  31.8 0.0 collective-permute-start.6
  31.8 5.9 %load.5 = (bf16[512,4096]{1,0:T(8,128)(2,1)S(1)}, bf16[512,4096]{1,0:T(8,128)(2,1)S(1)}, bf16[512,4096]{1,0:T(8,128)(2,1)S(1)}, bf16[512,4096]{1,0:T(8,128)(2,1)S(1)}) custom-call(bf16[4,512,4096]{2,1,0:T(8,128)(2,1)} %matrix_ref.2), custom_call_target="tpu_custom_call" | custom-call | bytes 1048576 | tf_op jit(solution)/shard_map/load/pallas_call | solution.py:72
  37.7 0.0 collective-permute-done.4.refs_5_
  37.8 0.6 collective-permute-start.12
  38.3 0.0 collective-permute-done.5.refs_6_
  38.3 0.1 collective-permute-start.14
  38.4 0.0 collective-permute-done.11.refs_3_
  38.4 0.4 collective-permute-start.15
  38.8 0.0 collective-permute-done.9.refs_1_
  38.8 0.1 collective-permute-start.13
  38.9 0.0 collective-permute-done.6.refs_7_
  38.9 5.2 %hidden.2.hidden_ref = bf16[128,2048]{1,0:T(8,128)(2,1)S(1)} custom-call(s32[2]{0:T(128)S(1)} %pad_add_fusion.place_ref, bf16[32,2176]{1,0:T(8,128)(2,1)S(1)} %prepare.1.refs_0_, bf16[32,2176]{1,0:T(8,128)(2,1)S(1)} %collective-permute-done.refs_1_, bf16[32,2176]{1,0:T(8,128)(2,1)S(1)} %collective-permute-done.1.refs_2_, ...), custom_call_target="tpu_custom_call" | custom-call | flops 4294967296 | bytes 1048576 | tf_op jit(solution)/shard_map/hidden/pallas_call | solution.py:128
  44.2 0.0 collective-permute-done.12.refs_4_
  44.2 0.0 collective-permute-done.14.refs_6_
  44.2 0.0 collective-permute-done.15.refs_7_
  44.2 0.0 collective-permute-done.13.refs_5_
  44.2 5.2 %hidden.3.hidden_ref = bf16[128,2048]{1,0:T(8,128)(2,1)S(1)} custom-call(s32[2]{0:T(128)S(1)} %pad_add_fusion.place_ref, bf16[32,2176]{1,0:T(8,128)(2,1)S(1)} %collective-permute-done.8.refs_0_, bf16[32,2176]{1,0:T(8,128)(2,1)S(1)} %collective-permute-done.9.refs_1_, bf16[32,2176]{1,0:T(8,128)(2,1)S(1)} %collective-permute-done.10.refs_2_, ...), custom_call_target="tpu_custom_call" | custom-call | flops 4294967296 | bytes 1048576 | tf_op jit(solution)/shard_map/hidden/pallas_call | solution.py:128
  49.5 1.8 %down_other.3 = bf16[128,2048]{1,0:T(8,128)(2,1)S(1)} custom-call(s32[2]{0:T(128)S(1)} %pad_add_fusion.place_ref, bf16[128,2048]{1,0:T(8,128)(2,1)S(1)} %hidden.3.hidden_ref, bf16[512,4096]{1,0:T(8,128)(2,1)S(1)} %get-tuple-element.35.refs_0_, bf16[512,4096]{1,0:T(8,128)(2,1)S(1)} %get-tuple-element.36.refs_1_, ...), custom_call_target="tpu_custom_call" | custom-call | flops 1073741824 | bytes 1048576 | tf_op jit(solution)/shard_map/down_other/pallas_call | solution.py:171
  51.3 0.5 collective-permute-start.16
  51.8 2.0 %down_other.2 = bf16[128,2048]{1,0:T(8,128)(2,1)S(1)} custom-call(s32[2]{0:T(128)S(1)} %pad_add_fusion.place_ref, bf16[128,2048]{1,0:T(8,128)(2,1)S(1)} %hidden.2.hidden_ref, bf16[512,4096]{1,0:T(8,128)(2,1)S(1)} %get-tuple-element.35.refs_0_, bf16[512,4096]{1,0:T(8,128)(2,1)S(1)} %get-tuple-element.36.refs_1_, ...), custom_call_target="tpu_custom_call" | custom-call | flops 1073741824 | bytes 1048576 | tf_op jit(solution)/shard_map/down_other/pallas_call | solution.py:171
  53.8 0.2 collective-permute-start.7
  54.0 0.0 collective-permute-done.16.refs_4_
  54.0 1.8 %down_mine.3 = bf16[128,2048]{1,0:T(8,128)(2,1)S(1)} custom-call(s32[2]{0:T(128)S(1)} %pad_add_fusion.place_ref, bf16[128,2048]{1,0:T(8,128)(2,1)S(1)} %hidden.3.hidden_ref, bf16[512,4096]{1,0:T(8,128)(2,1)S(1)} %get-tuple-element.35.refs_0_, bf16[512,4096]{1,0:T(8,128)(2,1)S(1)} %get-tuple-element.36.refs_1_, ...), custom_call_target="tpu_custom_call" | custom-call | flops 1073741824 | bytes 1048576 | tf_op jit(solution)/shard_map/down_mine/pallas_call | solution.py:171
  55.9 0.6 collective-permute-start.17
  56.4 1.5 %collective-permute-start.19 = (bf16[32,2048]{1,0:T(8,128)(2,1)S(1)}, bf16[32,2048]{1,0:T(8,128)(2,1)S(1)}, u32[]{:S(2)}, u32[]{:S(2)}) collective-permute-start(bf16[32,2048]{1,0:T(8,128)(2,1)S(1)} %get-tuple-element.49), channel_id=1, source_target_pairs={{0,2},{2,0},{4,6},{6,4},{8,10},{10,8},{12,14},{14,12},{1,3},{3,1},... | collective-permute-start | bytes 393224 | tf_op jit(solution)/shard_map/ppermute | solution.py:238
  58.0 0.5 collective-permute-start.21
  58.5 0.0 collective-permute-done.7.refs_4_
  58.5 1.8 %down_mine.2 = f32[128,2048]{1,0:T(8,128)S(1)} custom-call(s32[2]{0:T(128)S(1)} %pad_add_fusion.place_ref, bf16[128,2048]{1,0:T(8,128)(2,1)S(1)} %hidden.2.hidden_ref, bf16[512,4096]{1,0:T(8,128)(2,1)S(1)} %get-tuple-element.35.refs_0_, bf16[512,4096]{1,0:T(8,128)(2,1)S(1)} %get-tuple-element.36.refs_1_, bf16[512,4096]{1,0:T(8,128)(2,1)S(1)} %get-tuple-element.37.refs_2_, ...), custom_call_target="tpu_custom_call" | custom-call | flops 1073741824 | bytes 1048576 | tf_op jit(solution)/shard_map/down_mine/pallas_call | solution.py:171
  60.3 1.6 %collective-permute-start.23 = (bf16[32,2048]{1,0:T(8,128)(2,1)S(1)}, bf16[32,2048]{1,0:T(8,128)(2,1)S(1)}, u32[]{:S(2)}, u32[]{:S(2)}) collective-permute-start(bf16[32,2048]{1,0:T(8,128)(2,1)S(1)} %get-tuple-element.47), channel_id=1, source_target_pairs={{0,2},{2,0},{4,6},{6,4},{8,10},{10,8},{12,14},{14,12},{1,3},{3,1},... | collective-permute-start | bytes 393224 | tf_op jit(solution)/shard_map/ppermute | solution.py:238
  61.9 0.3 collective-permute-done.17
  62.2 2.8 %collective-permute-done.19 = bf16[32,2048]{1,0:T(8,128)(2,1)S(1)} collective-permute-done((bf16[32,2048]{1,0:T(8,128)(2,1)S(1)}, bf16[32,2048]{1,0:T(8,128)(2,1)S(1)}, u32[]{:S(2)}, u32[]{:S(2)}) %collective-permute-start.19) | collective-permute-done | bytes 131104 | tf_op jit(solution)/shard_map/ppermute | solution.py:238
  65.0 2.8 %collective-permute-done.21 = bf16[32,2048]{1,0:T(8,128)(2,1)S(1)} collective-permute-done((bf16[32,2048]{1,0:T(8,128)(2,1)S(1)}, bf16[32,2048]{1,0:T(8,128)(2,1)S(1)}, u32[]{:S(2)}, u32[]{:S(2)}) %collective-permute-start.21) | collective-permute-done | bytes 131104 | tf_op jit(solution)/shard_map/ppermute | solution.py:238
  67.8 0.1 fusion.4
  67.9 2.2 %collective-permute-start.18 = (bf16[32,2048]{1,0:T(8,128)(2,1)S(1)}, bf16[32,2048]{1,0:T(8,128)(2,1)S(1)}, u32[]{:S(2)}, u32[]{:S(2)}) collective-permute-start(bf16[32,2048]{1,0:T(8,128)(2,1)S(1)} %get-tuple-element.43), channel_id=1, source_target_pairs={{0,8},{2,10},{4,12},{6,14},{8,0},{10,2},{12,4},{14,6},{1,9},{3,11}... | collective-permute-start | bytes 393224 | tf_op jit(solution)/shard_map/ppermute | solution.py:240
  70.1 1.8 %collective-permute-start.20 = (bf16[32,2048]{1,0:T(8,128)(2,1)S(1)}, bf16[32,2048]{1,0:T(8,128)(2,1)S(1)}, u32[]{:S(2)}, u32[]{:S(2)}) collective-permute-start(bf16[32,2048]{1,0:T(8,128)(2,1)S(1)} %get-tuple-element.45), channel_id=1, source_target_pairs={{0,12},{2,14},{4,0},{6,2},{8,4},{10,6},{12,8},{14,10},{1,13},{3,15... | collective-permute-start | bytes 393224 | tf_op jit(solution)/shard_map/ppermute | solution.py:240
  71.9 0.2 collective-permute-start.22
  72.1 0.0 collective-permute-done.23
  72.2 8.1 %collective-permute-done.18 = bf16[32,2048]{1,0:T(8,128)(2,1)S(1)} collective-permute-done((bf16[32,2048]{1,0:T(8,128)(2,1)S(1)}, bf16[32,2048]{1,0:T(8,128)(2,1)S(1)}, u32[]{:S(2)}, u32[]{:S(2)}) %collective-permute-start.18) | collective-permute-done | bytes 131104 | tf_op jit(solution)/shard_map/ppermute | solution.py:240
  80.3 0.8 fusion.1
  (12 shorter events, 0.1 us)
Async XLA Ops:
  0.1 0.9 %copy-start.2 = (bf16[32,4096]{1,0:T(8,128)(2,1)S(1)}, bf16[32,4096]{1,0:T(8,128)(2,1)}, u32[]{:S(2)}) copy-start(bf16[32,4096]{1,0:T(8,128)(2,1)} %hidden_ref.1) | copy-start | bytes 786436
  1.0 0.7 copy-start.4
  1.7 0.7 copy-start.5
  2.4 0.7 copy-start.6
  3.9 15.5 %collective-permute-start = (bf16[32,2176]{1,0:T(8,128)(2,1)S(1)}, bf16[32,2176]{1,0:T(8,128)(2,1)S(1)}, u32[]{:S(2)}, u32[]{:S(2)}) collective-permute-start(bf16[32,2176]{1,0:T(8,128)(2,1)S(1)} %prepare.1.refs_0_), channel_id=1, source_target_pairs={{0,4},{2,6},{4,8},{6,10},{8,12},{10,14},{12,0},{14,2},{1,5},{3,7},... | collective-permute-start | bytes 417800 | tf_op jit(solution)/shard_map/ppermute | solution.py:213
  6.9 12.4 %collective-permute-start.2 = (bf16[32,2176]{1,0:T(8,128)(2,1)S(1)}, bf16[32,2176]{1,0:T(8,128)(2,1)S(1)}, u32[]{:S(2)}, u32[]{:S(2)}) collective-permute-start(bf16[32,2176]{1,0:T(8,128)(2,1)S(1)} %prepare.1.refs_0_), channel_id=1, source_target_pairs={{0,12},{2,14},{4,0},{6,2},{8,4},{10,6},{12,8},{14,10},{1,13},{3,15... | collective-permute-start | bytes 417800 | tf_op jit(solution)/shard_map/ppermute | solution.py:213
  9.0 16.2 %collective-permute-start.1 = (bf16[32,2176]{1,0:T(8,128)(2,1)S(1)}, bf16[32,2176]{1,0:T(8,128)(2,1)S(1)}, u32[]{:S(2)}, u32[]{:S(2)}) collective-permute-start(bf16[32,2176]{1,0:T(8,128)(2,1)S(1)} %prepare.1.refs_0_), channel_id=1, source_target_pairs={{0,8},{2,10},{4,12},{6,14},{8,0},{10,2},{12,4},{14,6},{1,9},{3,11}... | collective-permute-start | bytes 417800 | tf_op jit(solution)/shard_map/ppermute | solution.py:213
  10.0 16.4 %collective-permute-start.3 = (bf16[32,2176]{1,0:T(8,128)(2,1)S(1)}, bf16[32,2176]{1,0:T(8,128)(2,1)S(1)}, u32[]{:S(2)}, u32[]{:S(2)}) collective-permute-start(bf16[32,2176]{1,0:T(8,128)(2,1)S(1)} %prepare.1.refs_0_), channel_id=1, source_target_pairs={{0,1},{1,0},{2,3},{3,2},{4,5},{5,4},{6,7},{7,6},{8,9},{9,8},{10,11... | collective-permute-start | bytes 417800 | tf_op jit(solution)/shard_map/ppermute | solution.py:224
  10.0 17.9 %collective-permute-start.8 = (bf16[32,2176]{1,0:T(8,128)(2,1)S(1)}, bf16[32,2176]{1,0:T(8,128)(2,1)S(1)}, u32[]{:S(2)}, u32[]{:S(2)}) collective-permute-start(bf16[32,2176]{1,0:T(8,128)(2,1)S(1)} %prepare.1.refs_0_), channel_id=1, source_target_pairs={{0,2},{2,0},{4,6},{6,4},{8,10},{10,8},{12,14},{14,12},{1,3},{3,1},... | collective-permute-start | bytes 417800 | tf_op jit(solution)/shard_map/ppermute | solution.py:211
  17.4 2.0 %copy-start = (bf16[4096,512]{1,0:T(8,128)(2,1)}, bf16[4096,512]{1,0:T(8,128)(2,1)S(1)}, u32[]{:S(2)}) copy-start(bf16[4096,512]{1,0:T(8,128)(2,1)S(1)} %get-tuple-element.27.refs_10_) | copy-start | bytes 12582916
  25.3 13.7 %copy-start.1 = (bf16[4096,512]{1,0:T(8,128)(2,1)S(1)}, bf16[4096,512]{1,0:T(8,128)(2,1)}, u32[]{:S(2)}) copy-start(bf16[4096,512]{1,0:T(8,128)(2,1)} %copy-done) | copy-start | bytes 12582916
  25.3 6.6 %collective-permute-start.10 = (bf16[32,2176]{1,0:T(8,128)(2,1)S(1)}, bf16[32,2176]{1,0:T(8,128)(2,1)S(1)}, u32[]{:S(2)}, u32[]{:S(2)}) collective-permute-start(bf16[32,2176]{1,0:T(8,128)(2,1)S(1)} %collective-permute-done.1.refs_2_), channel_id=1, source_target_pairs={{0,2},{2,0},{4,6},{6,4},{8,10},{10,8},{12,14},{14,12},{1,3},{3,1},... | collective-permute-start | bytes 417800 | tf_op jit(solution)/shard_map/ppermute | solution.py:219
  25.8 11.9 %collective-permute-start.4 = (bf16[32,2176]{1,0:T(8,128)(2,1)S(1)}, bf16[32,2176]{1,0:T(8,128)(2,1)S(1)}, u32[]{:S(2)}, u32[]{:S(2)}) collective-permute-start(bf16[32,2176]{1,0:T(8,128)(2,1)S(1)} %collective-permute-done.refs_1_), channel_id=1, source_target_pairs={{0,1},{1,0},{2,3},{3,2},{4,5},{5,4},{6,7},{7,6},{8,9},{9,8},{10,11... | collective-permute-start | bytes 417800 | tf_op jit(solution)/shard_map/ppermute | solution.py:224
  25.8 12.5 %collective-permute-start.5 = (bf16[32,2176]{1,0:T(8,128)(2,1)S(1)}, bf16[32,2176]{1,0:T(8,128)(2,1)S(1)}, u32[]{:S(2)}, u32[]{:S(2)}) collective-permute-start(bf16[32,2176]{1,0:T(8,128)(2,1)S(1)} %collective-permute-done.1.refs_2_), channel_id=1, source_target_pairs={{0,1},{1,0},{2,3},{3,2},{4,5},{5,4},{6,7},{7,6},{8,9},{9,8},{10,11... | collective-permute-start | bytes 417800 | tf_op jit(solution)/shard_map/ppermute | solution.py:224
  26.4 12.1 %collective-permute-start.11 = (bf16[32,2176]{1,0:T(8,128)(2,1)S(1)}, bf16[32,2176]{1,0:T(8,128)(2,1)S(1)}, u32[]{:S(2)}, u32[]{:S(2)}) collective-permute-start(bf16[32,2176]{1,0:T(8,128)(2,1)S(1)} %collective-permute-done.2.refs_3_), channel_id=1, source_target_pairs={{0,2},{2,0},{4,6},{6,4},{8,10},{10,8},{12,14},{14,12},{1,3},{3,1},... | collective-permute-start | bytes 417800 | tf_op jit(solution)/shard_map/ppermute | solution.py:216
  27.9 11.0 %collective-permute-start.9 = (bf16[32,2176]{1,0:T(8,128)(2,1)S(1)}, bf16[32,2176]{1,0:T(8,128)(2,1)S(1)}, u32[]{:S(2)}, u32[]{:S(2)}) collective-permute-start(bf16[32,2176]{1,0:T(8,128)(2,1)S(1)} %collective-permute-done.refs_1_), channel_id=1, source_target_pairs={{0,2},{2,0},{4,6},{6,4},{8,10},{10,8},{12,14},{14,12},{1,3},{3,1},... | collective-permute-start | bytes 417800 | tf_op jit(solution)/shard_map/ppermute | solution.py:216
  31.8 7.1 %collective-permute-start.6 = (bf16[32,2176]{1,0:T(8,128)(2,1)S(1)}, bf16[32,2176]{1,0:T(8,128)(2,1)S(1)}, u32[]{:S(2)}, u32[]{:S(2)}) collective-permute-start(bf16[32,2176]{1,0:T(8,128)(2,1)S(1)} %collective-permute-done.2.refs_3_), channel_id=1, source_target_pairs={{0,1},{1,0},{2,3},{3,2},{4,5},{5,4},{6,7},{7,6},{8,9},{9,8},{10,11... | collective-permute-start | bytes 417800 | tf_op jit(solution)/shard_map/ppermute | solution.py:224
  37.8 6.4 %collective-permute-start.12 = (bf16[32,2176]{1,0:T(8,128)(2,1)S(1)}, bf16[32,2176]{1,0:T(8,128)(2,1)S(1)}, u32[]{:S(2)}, u32[]{:S(2)}) collective-permute-start(bf16[32,2176]{1,0:T(8,128)(2,1)S(1)} %collective-permute-done.8.refs_0_), channel_id=1, source_target_pairs={{0,1},{1,0},{2,3},{3,2},{4,5},{5,4},{6,7},{7,6},{8,9},{9,8},{10,11... | collective-permute-start | bytes 417800 | tf_op jit(solution)/shard_map/ppermute | solution.py:224
  38.3 5.9 %collective-permute-start.14 = (bf16[32,2176]{1,0:T(8,128)(2,1)S(1)}, bf16[32,2176]{1,0:T(8,128)(2,1)S(1)}, u32[]{:S(2)}, u32[]{:S(2)}) collective-permute-start(bf16[32,2176]{1,0:T(8,128)(2,1)S(1)} %collective-permute-done.10.refs_2_), channel_id=1, source_target_pairs={{0,1},{1,0},{2,3},{3,2},{4,5},{5,4},{6,7},{7,6},{8,9},{9,8},{10,11... | collective-permute-start | bytes 417800 | tf_op jit(solution)/shard_map/ppermute | solution.py:224
  38.4 5.8 %collective-permute-start.15 = (bf16[32,2176]{1,0:T(8,128)(2,1)S(1)}, bf16[32,2176]{1,0:T(8,128)(2,1)S(1)}, u32[]{:S(2)}, u32[]{:S(2)}) collective-permute-start(bf16[32,2176]{1,0:T(8,128)(2,1)S(1)} %collective-permute-done.11.refs_3_), channel_id=1, source_target_pairs={{0,1},{1,0},{2,3},{3,2},{4,5},{5,4},{6,7},{7,6},{8,9},{9,8},{10,11... | collective-permute-start | bytes 417800 | tf_op jit(solution)/shard_map/ppermute | solution.py:224
  38.8 5.4 %collective-permute-start.13 = (bf16[32,2176]{1,0:T(8,128)(2,1)S(1)}, bf16[32,2176]{1,0:T(8,128)(2,1)S(1)}, u32[]{:S(2)}, u32[]{:S(2)}) collective-permute-start(bf16[32,2176]{1,0:T(8,128)(2,1)S(1)} %collective-permute-done.9.refs_1_), channel_id=1, source_target_pairs={{0,1},{1,0},{2,3},{3,2},{4,5},{5,4},{6,7},{7,6},{8,9},{9,8},{10,11... | collective-permute-start | bytes 417800 | tf_op jit(solution)/shard_map/ppermute | solution.py:224
  51.3 2.7 %collective-permute-start.16 = (bf16[128,2048]{1,0:T(8,128)(2,1)S(1)}, bf16[128,2048]{1,0:T(8,128)(2,1)S(1)}, u32[]{:S(2)}, u32[]{:S(2)}) collective-permute-start(bf16[128,2048]{1,0:T(8,128)(2,1)S(1)} %down_other.3), channel_id=1, source_target_pairs={{0,1},{1,0},{2,3},{3,2},{4,5},{5,4},{6,7},{7,6},{8,9},{9,8},{10,11... | collective-permute-start | bytes 1572872 | tf_op jit(solution)/shard_map/ppermute | solution.py:229
  53.8 4.6 %collective-permute-start.7 = (bf16[128,2048]{1,0:T(8,128)(2,1)S(1)}, bf16[128,2048]{1,0:T(8,128)(2,1)S(1)}, u32[]{:S(2)}, u32[]{:S(2)}) collective-permute-start(bf16[128,2048]{1,0:T(8,128)(2,1)S(1)} %down_other.2), channel_id=1, source_target_pairs={{0,1},{1,0},{2,3},{3,2},{4,5},{5,4},{6,7},{7,6},{8,9},{9,8},{10,11... | collective-permute-start | bytes 1572872 | tf_op jit(solution)/shard_map/ppermute | solution.py:230
  55.9 6.4 %collective-permute-start.17 = (bf16[32,2048]{1,0:T(8,128)(2,1)S(1)}, bf16[32,2048]{1,0:T(8,128)(2,1)S(1)}, u32[]{:S(2)}, u32[]{:S(2)}) collective-permute-start(bf16[32,2048]{1,0:T(8,128)(2,1)S(1)} %get-tuple-element.46), channel_id=1, source_target_pairs={{0,2},{2,0},{4,6},{6,4},{8,10},{10,8},{12,14},{14,12},{1,3},{3,1},... | collective-permute-start | bytes 393224 | tf_op jit(solution)/shard_map/ppermute | solution.py:238
  56.4 8.6 %collective-permute-start.19 = (bf16[32,2048]{1,0:T(8,128)(2,1)S(1)}, bf16[32,2048]{1,0:T(8,128)(2,1)S(1)}, u32[]{:S(2)}, u32[]{:S(2)}) collective-permute-start(bf16[32,2048]{1,0:T(8,128)(2,1)S(1)} %get-tuple-element.49), channel_id=1, source_target_pairs={{0,2},{2,0},{4,6},{6,4},{8,10},{10,8},{12,14},{14,12},{1,3},{3,1},... | collective-permute-start | bytes 393224 | tf_op jit(solution)/shard_map/ppermute | solution.py:238
  58.0 22.3 %copy-start.3 = (bf16[32,4096]{1,0:T(8,128)(2,1)S(1)}, bf16[32,4096]{1,0:T(8,128)(2,1)}, u32[]{:S(2)}) copy-start(bf16[32,4096]{1,0:T(8,128)(2,1)} %hidden_ref.1) | copy-start | bytes 786436
  58.0 9.9 %collective-permute-start.21 = (bf16[32,2048]{1,0:T(8,128)(2,1)S(1)}, bf16[32,2048]{1,0:T(8,128)(2,1)S(1)}, u32[]{:S(2)}, u32[]{:S(2)}) collective-permute-start(bf16[32,2048]{1,0:T(8,128)(2,1)S(1)} %get-tuple-element.48), channel_id=1, source_target_pairs={{0,2},{2,0},{4,6},{6,4},{8,10},{10,8},{12,14},{14,12},{1,3},{3,1},... | collective-permute-start | bytes 393224 | tf_op jit(solution)/shard_map/ppermute | solution.py:238
  60.3 11.9 %collective-permute-start.23 = (bf16[32,2048]{1,0:T(8,128)(2,1)S(1)}, bf16[32,2048]{1,0:T(8,128)(2,1)S(1)}, u32[]{:S(2)}, u32[]{:S(2)}) collective-permute-start(bf16[32,2048]{1,0:T(8,128)(2,1)S(1)} %get-tuple-element.47), channel_id=1, source_target_pairs={{0,2},{2,0},{4,6},{6,4},{8,10},{10,8},{12,14},{14,12},{1,3},{3,1},... | collective-permute-start | bytes 393224 | tf_op jit(solution)/shard_map/ppermute | solution.py:238
  67.9 12.4 %collective-permute-start.18 = (bf16[32,2048]{1,0:T(8,128)(2,1)S(1)}, bf16[32,2048]{1,0:T(8,128)(2,1)S(1)}, u32[]{:S(2)}, u32[]{:S(2)}) collective-permute-start(bf16[32,2048]{1,0:T(8,128)(2,1)S(1)} %get-tuple-element.43), channel_id=1, source_target_pairs={{0,8},{2,10},{4,12},{6,14},{8,0},{10,2},{12,4},{14,6},{1,9},{3,11}... | collective-permute-start | bytes 393224 | tf_op jit(solution)/shard_map/ppermute | solution.py:240
  70.1 10.2 %collective-permute-start.20 = (bf16[32,2048]{1,0:T(8,128)(2,1)S(1)}, bf16[32,2048]{1,0:T(8,128)(2,1)S(1)}, u32[]{:S(2)}, u32[]{:S(2)}) collective-permute-start(bf16[32,2048]{1,0:T(8,128)(2,1)S(1)} %get-tuple-element.45), channel_id=1, source_target_pairs={{0,12},{2,14},{4,0},{6,2},{8,4},{10,6},{12,8},{14,10},{1,13},{3,15... | collective-permute-start | bytes 393224 | tf_op jit(solution)/shard_map/ppermute | solution.py:240
  71.9 8.4 %collective-permute-start.22 = (bf16[32,2048]{1,0:T(8,128)(2,1)S(1)}, bf16[32,2048]{1,0:T(8,128)(2,1)S(1)}, u32[]{:S(2)}, u32[]{:S(2)}) collective-permute-start(bf16[32,2048]{1,0:T(8,128)(2,1)S(1)} %get-tuple-element.44), channel_id=1, source_target_pairs={{0,4},{2,6},{4,8},{6,10},{8,12},{10,14},{12,0},{14,2},{1,5},{3,7},... | collective-permute-start | bytes 393224 | tf_op jit(solution)/shard_map/ppermute | solution.py:240

commit v3 on v2

v3 whole, which is shorter than its diff:
```python
import functools

import jax
import jax.numpy as jnp
from jax import lax
from jax.experimental import pallas as pl
from jax.experimental.pallas import tpu as pltpu
from jax.sharding import PartitionSpec as P

LANES = 128
WIDTH = 512
LEAD_FLOPS = 40_000_000_000


def prepare_kernel(half, experts, place_ref, *refs):
    out_ref, slot_ref, hidden_ref, ids_ref, scores_ref, sem = refs[4:]
    copies = [
        pltpu.make_async_copy(refs[i], refs[5 + i], sem.at[i]) for i in range(4)
    ]
    for copy in copies:
        copy.start()
    for copy in copies:
        copy.wait()
    resid = hidden_ref[...].astype(jnp.float32)
    scale = lax.rsqrt(jnp.mean(resid * resid, axis=-1, keepdims=True) + 1e-06)
    own = hidden_ref[:, pl.ds(pl.multiple_of(place_ref[1] * half, half), half)]
    out_ref[:, :half] = (own.astype(jnp.float32) * scale).astype(jnp.bfloat16)
    scores = scores_ref[...]
    mixing = scores / jnp.sum(scores, axis=0, keepdims=True)
    ids = ids_ref[...]
    width = out_ref.shape[1] - half
    row = lax.broadcasted_iota(jnp.int32, (width, 1), 0)
    slot_of_row = lax.rem(row, experts)
    expert_of_row = jnp.zeros((width, 1), jnp.int32)
    for e in range(experts):
        expert_of_row = jnp.where(slot_of_row == slot_ref[e], e, expert_of_row)
    weight = jnp.zeros((width, ids.shape[1]), jnp.float32)
    for k in range(ids.shape[0]):
        weight = weight + jnp.where(ids[k : k + 1, :] == expert_of_row, mixing[k : k + 1, :], 0.0)
    high = weight.astype(jnp.bfloat16).astype(jnp.float32)
    middle = (weight - high).astype(jnp.bfloat16).astype(jnp.float32)
    low = weight - high - middle
    coded = jnp.where(
        row < experts,
        high,
        jnp.where(row < 2 * experts, middle, jnp.where(row < 3 * experts, low, 0.0)),
    )
    out_ref[:, half:] = coded.T.astype(jnp.bfloat16)


def prepare(place, hidden_in, expert_ids, route_scores, expert_slot):
    rows, features = hidden_in.shape
    half = features // 2
    experts = expert_slot.shape[0]
    width = -(-3 * experts // LANES) * LANES
    vmem = pl.BlockSpec(memory_space=pltpu.VMEM)
    smem, hbm = pl.BlockSpec(memory_space=pltpu.SMEM), pl.BlockSpec(memory_space=pltpu.HBM)
    far = [expert_slot, hidden_in, expert_ids.T, route_scores.T]
    far = [pltpu.with_memory_space_constraint(a, pltpu.HBM) for a in far]
    return pl.pallas_call(
        functools.partial(prepare_kernel, half, experts),
        out_shape=jax.ShapeDtypeStruct((rows, half + width), jnp.bfloat16),
        in_specs=[smem, hbm, hbm, hbm, hbm],
        out_specs=vmem,
        scratch_shapes=[
            pltpu.SMEM(expert_slot.shape, jnp.int32),
            pltpu.VMEM(hidden_in.shape, hidden_in.dtype),
            pltpu.VMEM(expert_ids.shape[::-1], jnp.int32),
            pltpu.VMEM(route_scores.shape[::-1], jnp.float32),
            pltpu.SemaphoreType.DMA((4,)),
        ],
        compiler_params=pltpu.CompilerParams(vmem_limit_bytes=16 << 20),
        cost_estimate=pl.CostEstimate(
            flops=LEAD_FLOPS, bytes_accessed=2 * rows * features, transcendentals=0
        ),
        name="prepare",
    )(place, *far)


def fill_rows(half, blocks, refs, own, other, coded):
    tokens = refs[0].shape[0]
    for i in range(blocks):
        rows = slice(i * tokens, (i + 1) * tokens)
        own[rows, :] = refs[i][:, :half]
        other[rows, :] = refs[blocks + i][:, :half]
        coded[rows, :] = refs[i][:, half:].astype(jnp.float32)


def hidden_units(half, experts, place_ref, gate_ref, up_ref, own, other, coded, out_ref):
    local, _, units = gate_ref.shape
    first_slot = place_ref[0] * local
    own_at = pl.ds(pl.multiple_of(place_ref[1] * half, half), half)
    other_at = pl.ds(pl.multiple_of((1 - place_ref[1]) * half, half), half)
    slot = lax.rem(lax.broadcasted_iota(jnp.int32, coded.shape, 1), experts)
    block = min(units, 256)
    for e in range(local):
        weight = jnp.sum(jnp.where(slot == first_slot + e, coded[...], 0.0), axis=1, keepdims=True)
        for at in range(0, units, block):
            cut = slice(at, at + block)

            def project(ref):
                return jnp.dot(
                    own[...], ref[e, own_at, cut], preferred_element_type=jnp.float32
                ) + jnp.dot(other[...], ref[e, other_at, cut], preferred_element_type=jnp.float32)

            gate_act = project(gate_ref)
            up_act = project(up_ref)
            hidden = gate_act / (1.0 + jnp.exp(-gate_act)) * up_act
            hidden = jnp.where(weight > 0.0, hidden * weight, 0.0)
            out_ref[:, e * units + at : e * units + at + block] = hidden.astype(jnp.bfloat16)


def down_copies(down_ref, buffer, sem, at):
    width = buffer.shape[3]
    return [
        pltpu.make_async_copy(
            down_ref.at[:, :, pl.ds(pl.multiple_of(at + j * width, width), width)],
            buffer.at[j],
            sem.at[j],
        )
        for j in range(buffer.shape[0])
    ]


def other_kernel(half, experts, blocks, place_ref, *refs):
    gate_ref, up_ref, down_ref, hidden_ref, send_ref = refs[2 * blocks : 2 * blocks + 5]
    own, other, coded, buffer, sem = refs[2 * blocks + 5 :]
    copies = down_copies(down_ref, buffer, sem, (1 - place_ref[1]) * half)
    for copy in copies:
        copy.start()
    fill_rows(half, blocks, refs, own, other, coded)
    hidden_units(half, experts, place_ref, gate_ref, up_ref, own, other, coded, hidden_ref)
    width = buffer.shape[3]
    for j, copy in enumerate(copies):
        copy.wait()
        total = jnp.dot(
            hidden_ref[...], buffer[j].reshape(-1, width), preferred_element_type=jnp.float32
        )
        send_ref[:, j * width : (j + 1) * width] = total.astype(send_ref.dtype)


def mine_kernel(half, place_ref, hidden_ref, down_ref, *refs):
    out_refs, buffer, sem = refs[:-2], refs[-2], refs[-1]
    copies = down_copies(down_ref, buffer, sem, place_ref[1] * half)
    for copy in copies:
        copy.start()
    width = buffer.shape[3]
    tokens = out_refs[0].shape[0]
    for j, copy in enumerate(copies):
        copy.wait()
        total = jnp.dot(
            hidden_ref[...], buffer[j].reshape(-1, width), preferred_element_type=jnp.float32
        )
        for i, out_ref in enumerate(out_refs):
            out_ref[:, j * width : (j + 1) * width] = total[i * tokens : (i + 1) * tokens]


def run_other(place, own, other, gate, up, down, experts):
    blocks = len(own)
    local, features, width = gate.shape
    rows, half, units = blocks * own[0].shape[0], features // 2, local * width
    vmem, hbm = pl.BlockSpec(memory_space=pltpu.VMEM), pl.BlockSpec(memory_space=pltpu.HBM)
    return pl.pallas_call(
        functools.partial(other_kernel, half, experts, blocks),
        out_shape=[
            jax.ShapeDtypeStruct((rows, units), jnp.bfloat16),
            jax.ShapeDtypeStruct((rows, half), jnp.bfloat16),
        ],
        in_specs=[pl.BlockSpec(memory_space=pltpu.SMEM)] + [vmem] * (2 * blocks + 2) + [hbm],
        out_specs=[vmem] * 2,
        scratch_shapes=[
            pltpu.VMEM((rows, half), jnp.bfloat16),
            pltpu.VMEM((rows, half), jnp.bfloat16),
            pltpu.VMEM((rows, own[0].shape[1] - half), jnp.float32),
            pltpu.VMEM((half // WIDTH, local, width, WIDTH), jnp.bfloat16),
            pltpu.SemaphoreType.DMA((half // WIDTH,)),
        ],
        compiler_params=pltpu.CompilerParams(vmem_limit_bytes=16 << 20),
        cost_estimate=pl.CostEstimate(
            flops=2 * rows * units * (2 * features + half),
            bytes_accessed=4 * rows * half,
            transcendentals=rows * units,
        ),
        name="other",
    )(place, *own, *other, gate, up, down)


def run_mine(place, hidden, down, blocks):
    rows = hidden.shape[0]
    local, width, features = down.shape
    half = features // 2
    vmem, hbm = pl.BlockSpec(memory_space=pltpu.VMEM), pl.BlockSpec(memory_space=pltpu.HBM)
    return pl.pallas_call(
        functools.partial(mine_kernel, half),
        out_shape=[jax.ShapeDtypeStruct((rows // blocks, half), jnp.float32)] * blocks,
        in_specs=[pl.BlockSpec(memory_space=pltpu.SMEM), vmem, hbm],
        out_specs=[vmem] * blocks,
        scratch_shapes=[
            pltpu.VMEM((half // WIDTH, local, width, WIDTH), jnp.bfloat16),
            pltpu.SemaphoreType.DMA((half // WIDTH,)),
        ],
        compiler_params=pltpu.CompilerParams(vmem_limit_bytes=16 << 20),
        cost_estimate=pl.CostEstimate(
            flops=2 * rows * half * hidden.shape[1], bytes_accessed=4 * rows * half, transcendentals=0
        ),
        name="mine",
    )(place, hidden, down)


def on_device(
    hidden_in, expert_ids, route_scores, expert_slot, gate_matrix, up_matrix, down_matrix
):
    token_count, feature_count = hidden_in.shape
    experts = expert_slot.shape[0]
    devices = lax.axis_size("sect")
    half = feature_count // 2
    core = lax.axis_index("tp")
    sect = lax.axis_index("sect")
    inner = 2
    outer = devices // inner

    def along(shift):
        return [
            (o * inner + i, (o + shift) % outer * inner + i)
            for o in range(outer)
            for i in range(inner)
        ]

    across = [(d, d ^ 1) for d in range(devices)]
    cores = [(0, 1), (1, 0)]
    place = jnp.stack([sect, core]).astype(jnp.int32)
    bf16, f32 = jnp.bfloat16, jnp.float32

    packed = prepare(place, hidden_in, expert_ids, route_scores, expert_slot)
    shifts = sorted(range(1, outer), key=lambda k: min(k, outer - k))
    same, opposite = {0: packed}, {}
    for k in shifts:
        same[k] = lax.ppermute(packed, "sect", along(k))
    for k in [0] + shifts:
        opposite[k] = lax.ppermute(same[k], "sect", across)
    down_matrix = pltpu.with_memory_space_constraint(down_matrix, pltpu.HBM)
    near = [same[k] for k in range(outer)]
    far = [opposite[k] for k in range(outer)]
    near_other = [lax.ppermute(block, "tp", cores) for block in near]
    far_other = [lax.ppermute(block, "tp", cores) for block in far]
    hidden, send = run_other(
        place, near + far, near_other + far_other, gate_matrix, up_matrix, down_matrix, experts
    )
    received = lax.ppermute(send, "tp", cores).reshape(inner, outer, token_count, half)
    mine = run_mine(place, hidden, down_matrix, inner * outer)
    near_sum = [mine[k] + received[0, k].astype(f32) for k in range(outer)]
    far_sum = [(mine[outer + k] + received[1, k].astype(f32)).astype(bf16) for k in range(outer)]
    near_sum, far_sum = lax.optimization_barrier((near_sum, far_sum))
    result = lax.dynamic_slice_in_dim(hidden_in, core * half, half, 1).astype(f32)
    order = sorted(range(1, outer), key=lambda k: -min(k, outer - k)) + [0]
    for k in order:
        block = near_sum[k] + lax.ppermute(far_sum[k], "sect", across).astype(f32)
        if k:
            block = lax.ppermute(block.astype(bf16), "sect", along(-k)).astype(f32)
        result = result + block
    return result.astype(bf16)


def solution(mesh):
    placed = (
        P(("groups", "sect"), None),
        P(("groups", "sect"), None),
        P(("groups", "sect"), None),
        P(),
        P("sect", None, "tp"),
        P("sect", None, "tp"),
        P("sect", "tp", None),
    )
    return jax.shard_map(
        on_device,
        mesh=mesh,
        in_specs=placed,
        out_specs=P(("groups", "sect"), "tp"),
        check_vma=False,
    )
```

time: 81.3 us -> 69.7 us (0.86)
  Pallas kernels: 36.5 us -> 20.8 us
  waiting for transfers between devices: 17.6 us -> 30.8 us
  local copies, waits for them, and re-layouts: 4.98 us -> 0.01 us
  starting transfers between devices: 21 us -> 16.6 us
    pallas_call x9 -> x2, Pallas kernels: 35.7 us -> 18.8 us  [the longest x1 13.8 us: run_other(): pl.pallas_call(functools.partial(other_kernel, half, experts, blocks), ou...]
    ppermute x3, waiting for transfers between devices: 0.01 us -> 10.5 us  [on_device(): same[k] = lax.ppermute(packed, 'sect', along(k))]
    unnamed x14 -> x6, local copies, waits for them, and re-layouts: 4.94 us -> 0.01 us
    ppermute x14 -> x13, waiting for transfers between devices: 3.49 us -> 7.17 us  [the longest x4 5.83 us: on_device(): opposite[k] = lax.ppermute(same[k], 'sect', across)]
    ppermute x3, waiting for transfers between devices: 8.14 us -> 4.6 us  [on_device(): block = lax.ppermute(block.astype(bf16), 'sect', along(-k)).astype(f32)]
    ppermute x3, starting transfers between devices: 4.22 us -> 1.45 us  [on_device(): block = lax.ppermute(block.astype(bf16), 'sect', along(-k)).astype(f32)]
    ppermute x4, waiting for transfers between devices: 5.94 us -> 8.57 us  [on_device(): block = near_sum[k] + lax.ppermute(far_sum[k], 'sect', across).astype(f32)]
    ppermute x3, starting transfers between devices: 6.1 us -> 4.61 us  [on_device(): same[k] = lax.ppermute(packed, 'sect', along(k))]
  transfers between devices with their start and end apart: 24 -> 23, of which waited for: 5 -> 11; matrix products, arithmetic and copies ran while one was open for 0% -> 0% of each run, Pallas kernels for 35% -> 7%
where the time goes in v3:
time: 69.7 us; the launch traced here: 69.5 us
  waiting for transfers between devices  30.8 us (44%)
  Pallas kernels  20.8 us (30%)
  starting transfers between devices  16.6 us (24%)
  other arithmetic  1.17 us (2%)
    pallas_call x1, Pallas kernels, run_other(): pl.pallas_call(functools.partial(other_kernel, half, experts, blocks), ou...  13.8 us
    ppermute x3, waiting for transfers between devices, on_device(): same[k] = lax.ppermute(packed, 'sect', along(k))  10.5 us
    ppermute x4, waiting for transfers between devices, on_device(): block = near_sum[k] + lax.ppermute(far_sum[k], 'sect', across).astype(f32)  8.57 us
    ppermute x4, waiting for transfers between devices, on_device(): opposite[k] = lax.ppermute(same[k], 'sect', across)  5.83 us
    ppermute x4, starting transfers between devices, on_device(): opposite[k] = lax.ppermute(same[k], 'sect', across)  5.57 us
    pallas_call x1, Pallas kernels, run_mine(): pl.pallas_call(functools.partial(mine_kernel, half), out_shape=[jax.Shape...  5.06 us
    ppermute x3, starting transfers between devices, on_device(): same[k] = lax.ppermute(packed, 'sect', along(k))  4.61 us
    ppermute x3, waiting for transfers between devices, on_device(): block = lax.ppermute(block.astype(bf16), 'sect', along(-k)).astype(f32)  4.6 us
  transfers between devices with their start and end apart: 23, of which 11 were waited for; matrix products, arithmetic and copies ran while one was open for 0% of the time, Pallas kernels for 7%

profile of v3, /device:TPU:0, one launch (start us, length us, event | category | flops | bytes accessed | tf_op | source)
XLA Modules:
  0.0 69.5 jit_solution(475022856247311052)
XLA Ops:
  0.0 0.1 pad_add_fusion.place_ref
  0.1 0.0 copy-start
  0.1 0.0 copy-start.1
  0.1 2.0 %prepare.1.refs_0_ = bf16[32,2176]{1,0:T(8,128)(2,1)S(1)} custom-call(s32[2]{0:T(128)S(1)} %pad_add_fusion.place_ref, s32[32]{0:T(128)} %refs_0_.1, bf16[32,4096]{1,0:T(8,128)(2,1)} %refs_1_.1, s32[8,32]{1,0:T(8,128)} %bitcast.46, f32[8,32]{1,0:T(8,128)} %bitcast.47), custom_call_target="tpu_custom_call" | custom-call | flops 40000000000 | bytes 262144 | tf_op jit(solution)/shard_map/prepare/pallas_call | solution.py:60
  2.1 3.0 %collective-permute-start.3 = (bf16[32,2176]{1,0:T(8,128)(2,1)S(1)}, bf16[32,2176]{1,0:T(8,128)(2,1)S(1)}, u32[]{:S(2)}, u32[]{:S(2)}) collective-permute-start(bf16[32,2176]{1,0:T(8,128)(2,1)S(1)} %prepare.1.refs_0_), channel_id=1, source_target_pairs={{0,2},{2,0},{4,6},{6,4},{8,10},{10,8},{12,14},{14,12},{1,3},{3,1},... | collective-permute-start | bytes 417800 | tf_op jit(solution)/shard_map/ppermute | solution.py:240
  5.1 3.6 %collective-permute-start.2 = (bf16[32,2176]{1,0:T(8,128)(2,1)S(1)}, bf16[32,2176]{1,0:T(8,128)(2,1)S(1)}, u32[]{:S(2)}, u32[]{:S(2)}) collective-permute-start(bf16[32,2176]{1,0:T(8,128)(2,1)S(1)} %prepare.1.refs_0_), channel_id=1, source_target_pairs={{0,12},{2,14},{4,0},{6,2},{8,4},{10,6},{12,8},{14,10},{1,13},{3,15... | collective-permute-start | bytes 417800 | tf_op jit(solution)/shard_map/ppermute | solution.py:238
  8.7 0.0 collective-permute-start.7
  8.7 0.0 collective-permute-start.1
  8.7 1.0 %collective-permute-start = (bf16[32,2176]{1,0:T(8,128)(2,1)S(1)}, bf16[32,2176]{1,0:T(8,128)(2,1)S(1)}, u32[]{:S(2)}, u32[]{:S(2)}) collective-permute-start(bf16[32,2176]{1,0:T(8,128)(2,1)S(1)} %prepare.1.refs_0_), channel_id=1, source_target_pairs={{0,4},{2,6},{4,8},{6,10},{8,12},{10,14},{12,0},{14,2},{1,5},{3,7},... | collective-permute-start | bytes 417800 | tf_op jit(solution)/shard_map/ppermute | solution.py:238
  9.8 0.0 collective-permute-done.3.refs_4_
  9.8 0.0 collective-permute-start.11
  9.8 3.1 %collective-permute-done.2.refs_3_ = bf16[32,2176]{1,0:T(8,128)(2,1)S(1)} collective-permute-done((bf16[32,2176]{1,0:T(8,128)(2,1)S(1)}, bf16[32,2176]{1,0:T(8,128)(2,1)S(1)}, u32[]{:S(2)}, u32[]{:S(2)}) %collective-permute-start.2) | collective-permute-done | bytes 139296 | tf_op jit(solution)/shard_map/ppermute | solution.py:238
  12.9 0.0 collective-permute-start.10
  12.9 0.0 collective-permute-done.7.refs_8_
  12.9 0.5 collective-permute-start.6
  13.4 7.3 %collective-permute-done.1.refs_2_ = bf16[32,2176]{1,0:T(8,128)(2,1)S(1)} collective-permute-done((bf16[32,2176]{1,0:T(8,128)(2,1)S(1)}, bf16[32,2176]{1,0:T(8,128)(2,1)S(1)}, u32[]{:S(2)}, u32[]{:S(2)}) %collective-permute-start.1) | collective-permute-done | bytes 139296 | tf_op jit(solution)/shard_map/ppermute | solution.py:238
  20.7 0.5 collective-permute-start.5
  21.2 0.0 collective-permute-done.refs_1_
  21.2 1.5 %collective-permute-start.4 = (bf16[32,2176]{1,0:T(8,128)(2,1)S(1)}, bf16[32,2176]{1,0:T(8,128)(2,1)S(1)}, u32[]{:S(2)}, u32[]{:S(2)}) collective-permute-start(bf16[32,2176]{1,0:T(8,128)(2,1)S(1)} %collective-permute-done.refs_1_), channel_id=1, source_target_pairs={{0,2},{2,0},{4,6},{6,4},{8,10},{10,8},{12,14},{14,12},{1,3},{3,1},... | collective-permute-start | bytes 417800 | tf_op jit(solution)/shard_map/ppermute | solution.py:240
  22.8 0.0 collective-permute-done.11.refs_12_
  22.8 0.0 collective-permute-start.9
  22.8 0.0 collective-permute-done.10.refs_11_
  22.8 0.5 collective-permute-start.8
  23.3 0.0 collective-permute-done.6.refs_7_
  23.3 0.1 collective-permute-start.14
  23.4 3.9 %collective-permute-done.5.refs_6_ = bf16[32,2176]{1,0:T(8,128)(2,1)S(1)} collective-permute-done((bf16[32,2176]{1,0:T(8,128)(2,1)S(1)}, bf16[32,2176]{1,0:T(8,128)(2,1)S(1)}, u32[]{:S(2)}, u32[]{:S(2)}) %collective-permute-start.5) | collective-permute-done | bytes 139296 | tf_op jit(solution)/shard_map/ppermute | solution.py:240
  27.3 0.0 collective-permute-start.13
  27.3 1.9 %collective-permute-done.4.refs_5_ = bf16[32,2176]{1,0:T(8,128)(2,1)S(1)} collective-permute-done((bf16[32,2176]{1,0:T(8,128)(2,1)S(1)}, bf16[32,2176]{1,0:T(8,128)(2,1)S(1)}, u32[]{:S(2)}, u32[]{:S(2)}) %collective-permute-start.4) | collective-permute-done | bytes 139296 | tf_op jit(solution)/shard_map/ppermute | solution.py:240
  29.2 0.0 collective-permute-start.12
  29.2 0.0 collective-permute-done.9.refs_10_
  29.2 0.0 collective-permute-done.8.refs_9_
  29.2 0.0 collective-permute-done.14.refs_15_
  29.2 0.0 collective-permute-done.13.refs_14_
  29.2 1.3 %collective-permute-done.12.refs_13_ = bf16[32,2176]{1,0:T(8,128)(2,1)S(1)} collective-permute-done((bf16[32,2176]{1,0:T(8,128)(2,1)S(1)}, bf16[32,2176]{1,0:T(8,128)(2,1)S(1)}, u32[]{:S(2)}, u32[]{:S(2)}) %collective-permute-start.12) | collective-permute-done | bytes 139296 | tf_op jit(solution)/shard_map/ppermute | solution.py:245
  30.5 0.0 copy-done
  30.5 0.0 copy-done.1
  30.5 13.8 %other.1 = (bf16[256,2048]{1,0:T(8,128)(2,1)S(1)}, bf16[256,2048]{1,0:T(8,128)(2,1)S(1)}) custom-call(s32[2]{0:T(128)S(1)} %pad_add_fusion.place_ref, bf16[32,2176]{1,0:T(8,128)(2,1)S(1)} %prepare.1.refs_0_, bf16[32,2176]{1,0:T(8,128)(2,1)S(1)} %collective-permute-done.refs_1_, bf16[32,2176]{1,0:T(8,128)(2,1)S(1)} %collective-permute-done.1.refs_2_, ...), custom_call_target="tpu_custom_call" | custom-call | flops 10737418240 | bytes 2097152 | tf_op jit(solution)/shard_map/other/pallas_call | solution.py:163
  44.3 0.0 copy-start.2
  44.3 0.2 collective-permute-start.15
  44.5 5.1 %mine.1 = (f32[32,2048]{1,0:T(8,128)S(1)}, f32[32,2048]{1,0:T(8,128)S(1)}, f32[32,2048]{1,0:T(8,128)S(1)}, f32[32,2048]{1,0:T(8,128)S(1)}, f32[32,2048]{1,0:T(8,...) custom-call(s32[2]{0:T(128)S(1)} %pad_add_fusion.place_ref, ...), custom_call_target="tpu_custom_call" | custom-call | flops 2147483648 | bytes 2097152 | tf_op jit(solution)/shard_map/mine/pallas_call | solution.py:193
  49.6 0.0 collective-permute-done.15
  49.6 0.3 fusion
  49.9 0.6 collective-permute-start.16
  50.5 1.5 %collective-permute-start.18 = (bf16[32,2048]{1,0:T(8,128)(2,1)S(1)}, bf16[32,2048]{1,0:T(8,128)(2,1)S(1)}, u32[]{:S(2)}, u32[]{:S(2)}) collective-permute-start(bf16[32,2048]{1,0:T(8,128)(2,1)S(1)} %get-tuple-element.36), channel_id=1, source_target_pairs={{0,2},{2,0},{4,6},{6,4},{8,10},{10,8},{12,14},{14,12},{1,3},{3,1},... | collective-permute-start | bytes 393224 | tf_op jit(solution)/shard_map/ppermute | solution.py:257
  52.0 0.5 collective-permute-start.20
  52.5 1.5 %collective-permute-start.22 = (bf16[32,2048]{1,0:T(8,128)(2,1)S(1)}, bf16[32,2048]{1,0:T(8,128)(2,1)S(1)}, u32[]{:S(2)}, u32[]{:S(2)}) collective-permute-start(bf16[32,2048]{1,0:T(8,128)(2,1)S(1)} %get-tuple-element.40), channel_id=1, source_target_pairs={{0,2},{2,0},{4,6},{6,4},{8,10},{10,8},{12,14},{14,12},{1,3},{3,1},... | collective-permute-start | bytes 393224 | tf_op jit(solution)/shard_map/ppermute | solution.py:257
  54.0 2.3 %collective-permute-done.16 = bf16[32,2048]{1,0:T(8,128)(2,1)S(1)} collective-permute-done((bf16[32,2048]{1,0:T(8,128)(2,1)S(1)}, bf16[32,2048]{1,0:T(8,128)(2,1)S(1)}, u32[]{:S(2)}, u32[]{:S(2)}) %collective-permute-start.16) | collective-permute-done | bytes 131104 | tf_op jit(solution)/shard_map/ppermute | solution.py:257
  56.3 0.3 collective-permute-start.17
  56.6 2.5 %collective-permute-done.18 = bf16[32,2048]{1,0:T(8,128)(2,1)S(1)} collective-permute-done((bf16[32,2048]{1,0:T(8,128)(2,1)S(1)}, bf16[32,2048]{1,0:T(8,128)(2,1)S(1)}, u32[]{:S(2)}, u32[]{:S(2)}) %collective-permute-start.18) | collective-permute-done | bytes 131104 | tf_op jit(solution)/shard_map/ppermute | solution.py:257
  59.1 1.1 %collective-permute-start.19 = (bf16[32,2048]{1,0:T(8,128)(2,1)S(1)}, bf16[32,2048]{1,0:T(8,128)(2,1)S(1)}, u32[]{:S(2)}, u32[]{:S(2)}) collective-permute-start(bf16[32,2048]{1,0:T(8,128)(2,1)S(1)} %add_convert_fusion.2), channel_id=1, source_target_pairs={{0,12},{2,14},{4,0},{6,2},{8,4},{10,6},{12,8},{14,10},{1,13},{3,15... | collective-permute-start | bytes 393224 | tf_op jit(solution)/shard_map/ppermute | solution.py:259
  60.3 1.6 %collective-permute-done.20 = bf16[32,2048]{1,0:T(8,128)(2,1)S(1)} collective-permute-done((bf16[32,2048]{1,0:T(8,128)(2,1)S(1)}, bf16[32,2048]{1,0:T(8,128)(2,1)S(1)}, u32[]{:S(2)}, u32[]{:S(2)}) %collective-permute-start.20) | collective-permute-done | bytes 131104 | tf_op jit(solution)/shard_map/ppermute | solution.py:257
  61.9 0.1 collective-permute-start.21
  62.0 2.1 %collective-permute-done.22 = bf16[32,2048]{1,0:T(8,128)(2,1)S(1)} collective-permute-done((bf16[32,2048]{1,0:T(8,128)(2,1)S(1)}, bf16[32,2048]{1,0:T(8,128)(2,1)S(1)}, u32[]{:S(2)}, u32[]{:S(2)}) %collective-permute-start.22) | collective-permute-done | bytes 131104 | tf_op jit(solution)/shard_map/ppermute | solution.py:257
  64.2 0.0 collective-permute-done.17
  64.2 3.1 %collective-permute-done.19 = bf16[32,2048]{1,0:T(8,128)(2,1)S(1)} collective-permute-done((bf16[32,2048]{1,0:T(8,128)(2,1)S(1)}, bf16[32,2048]{1,0:T(8,128)(2,1)S(1)}, u32[]{:S(2)}, u32[]{:S(2)}) %collective-permute-start.19) | collective-permute-done | bytes 131104 | tf_op jit(solution)/shard_map/ppermute | solution.py:259
  67.3 1.5 %collective-permute-done.21 = bf16[32,2048]{1,0:T(8,128)(2,1)S(1)} collective-permute-done((bf16[32,2048]{1,0:T(8,128)(2,1)S(1)}, bf16[32,2048]{1,0:T(8,128)(2,1)S(1)}, u32[]{:S(2)}, u32[]{:S(2)}) %collective-permute-start.21) | collective-permute-done | bytes 131104 | tf_op jit(solution)/shard_map/ppermute | solution.py:259
  68.8 0.0 copy-done.2
  68.8 0.8 %add_convert_fusion = bf16[32,2048]{1,0:T(8,128)(2,1)} fusion(f32[32,2048]{1,0:T(8,128)S(1)} %get-tuple-element.39, bf16[32,2048]{1,0:T(8,128)(2,1)S(1)} %collective-permute-done.22, bf16[32,2048]{1,0:T(8,128)(2,1)S(1)} %collective-permute-done.21, bf16[32,2048]{1,0:T(8,128)(2,1)S(1)} %collective-permute-done.19, ...), kind=kLoop, calls=%fused_computation.12 | loop fusion | flops 720896 | bytes 1048580 | tf_op jit(solution)/shard_map/convert_element_type | solution.py:261
  (3 shorter events, 0.1 us)
Async XLA Ops:
  0.1 30.5 %copy-start = (bf16[4,4096,512]{2,1,0:T(8,128)(2,1)S(1)}, bf16[4,4096,512]{2,1,0:T(8,128)(2,1)}, u32[]{:S(2)}) copy-start(bf16[4,4096,512]{2,1,0:T(8,128)(2,1)} %refs_16_.1) | copy-start | bytes 50331652
  0.1 30.5 %copy-start.1 = (bf16[4,4096,512]{2,1,0:T(8,128)(2,1)S(1)}, bf16[4,4096,512]{2,1,0:T(8,128)(2,1)}, u32[]{:S(2)}) copy-start(bf16[4,4096,512]{2,1,0:T(8,128)(2,1)} %refs_17_.1) | copy-start | bytes 50331652
  2.1 7.7 %collective-permute-start.3 = (bf16[32,2176]{1,0:T(8,128)(2,1)S(1)}, bf16[32,2176]{1,0:T(8,128)(2,1)S(1)}, u32[]{:S(2)}, u32[]{:S(2)}) collective-permute-start(bf16[32,2176]{1,0:T(8,128)(2,1)S(1)} %prepare.1.refs_0_), channel_id=1, source_target_pairs={{0,2},{2,0},{4,6},{6,4},{8,10},{10,8},{12,14},{14,12},{1,3},{3,1},... | collective-permute-start | bytes 417800 | tf_op jit(solution)/shard_map/ppermute | solution.py:240
  5.1 7.8 %collective-permute-start.2 = (bf16[32,2176]{1,0:T(8,128)(2,1)S(1)}, bf16[32,2176]{1,0:T(8,128)(2,1)S(1)}, u32[]{:S(2)}, u32[]{:S(2)}) collective-permute-start(bf16[32,2176]{1,0:T(8,128)(2,1)S(1)} %prepare.1.refs_0_), channel_id=1, source_target_pairs={{0,12},{2,14},{4,0},{6,2},{8,4},{10,6},{12,8},{14,10},{1,13},{3,15... | collective-permute-start | bytes 417800 | tf_op jit(solution)/shard_map/ppermute | solution.py:238
  8.7 4.2 %collective-permute-start.7 = (bf16[32,2176]{1,0:T(8,128)(2,1)S(1)}, bf16[32,2176]{1,0:T(8,128)(2,1)S(1)}, u32[]{:S(2)}, u32[]{:S(2)}) collective-permute-start(bf16[32,2176]{1,0:T(8,128)(2,1)S(1)} %prepare.1.refs_0_), channel_id=1, source_target_pairs={{0,1},{1,0},{2,3},{3,2},{4,5},{5,4},{6,7},{7,6},{8,9},{9,8},{10,11... | collective-permute-start | bytes 417800 | tf_op jit(solution)/shard_map/ppermute | solution.py:244
  8.7 12.0 %collective-permute-start.1 = (bf16[32,2176]{1,0:T(8,128)(2,1)S(1)}, bf16[32,2176]{1,0:T(8,128)(2,1)S(1)}, u32[]{:S(2)}, u32[]{:S(2)}) collective-permute-start(bf16[32,2176]{1,0:T(8,128)(2,1)S(1)} %prepare.1.refs_0_), channel_id=1, source_target_pairs={{0,8},{2,10},{4,12},{6,14},{8,0},{10,2},{12,4},{14,6},{1,9},{3,11}... | collective-permute-start | bytes 417800 | tf_op jit(solution)/shard_map/ppermute | solution.py:238
  8.7 12.5 %collective-permute-start = (bf16[32,2176]{1,0:T(8,128)(2,1)S(1)}, bf16[32,2176]{1,0:T(8,128)(2,1)S(1)}, u32[]{:S(2)}, u32[]{:S(2)}) collective-permute-start(bf16[32,2176]{1,0:T(8,128)(2,1)S(1)} %prepare.1.refs_0_), channel_id=1, source_target_pairs={{0,4},{2,6},{4,8},{6,10},{8,12},{10,14},{12,0},{14,2},{1,5},{3,7},... | collective-permute-start | bytes 417800 | tf_op jit(solution)/shard_map/ppermute | solution.py:238
  9.8 13.0 %collective-permute-start.11 = (bf16[32,2176]{1,0:T(8,128)(2,1)S(1)}, bf16[32,2176]{1,0:T(8,128)(2,1)S(1)}, u32[]{:S(2)}, u32[]{:S(2)}) collective-permute-start(bf16[32,2176]{1,0:T(8,128)(2,1)S(1)} %collective-permute-done.3.refs_4_), channel_id=1, source_target_pairs={{0,1},{1,0},{2,3},{3,2},{4,5},{5,4},{6,7},{7,6},{8,9},{9,8},{10,11... | collective-permute-start | bytes 417800 | tf_op jit(solution)/shard_map/ppermute | solution.py:245
  12.9 9.9 %collective-permute-start.10 = (bf16[32,2176]{1,0:T(8,128)(2,1)S(1)}, bf16[32,2176]{1,0:T(8,128)(2,1)S(1)}, u32[]{:S(2)}, u32[]{:S(2)}) collective-permute-start(bf16[32,2176]{1,0:T(8,128)(2,1)S(1)} %collective-permute-done.2.refs_3_), channel_id=1, source_target_pairs={{0,1},{1,0},{2,3},{3,2},{4,5},{5,4},{6,7},{7,6},{8,9},{9,8},{10,11... | collective-permute-start | bytes 417800 | tf_op jit(solution)/shard_map/ppermute | solution.py:244
  12.9 10.4 %collective-permute-start.6 = (bf16[32,2176]{1,0:T(8,128)(2,1)S(1)}, bf16[32,2176]{1,0:T(8,128)(2,1)S(1)}, u32[]{:S(2)}, u32[]{:S(2)}) collective-permute-start(bf16[32,2176]{1,0:T(8,128)(2,1)S(1)} %collective-permute-done.2.refs_3_), channel_id=1, source_target_pairs={{0,2},{2,0},{4,6},{6,4},{8,10},{10,8},{12,14},{14,12},{1,3},{3,1},... | collective-permute-start | bytes 417800 | tf_op jit(solution)/shard_map/ppermute | solution.py:240
  20.7 6.6 %collective-permute-start.5 = (bf16[32,2176]{1,0:T(8,128)(2,1)S(1)}, bf16[32,2176]{1,0:T(8,128)(2,1)S(1)}, u32[]{:S(2)}, u32[]{:S(2)}) collective-permute-start(bf16[32,2176]{1,0:T(8,128)(2,1)S(1)} %collective-permute-done.1.refs_2_), channel_id=1, source_target_pairs={{0,2},{2,0},{4,6},{6,4},{8,10},{10,8},{12,14},{14,12},{1,3},{3,1},... | collective-permute-start | bytes 417800 | tf_op jit(solution)/shard_map/ppermute | solution.py:240
  21.2 7.9 %collective-permute-start.4 = (bf16[32,2176]{1,0:T(8,128)(2,1)S(1)}, bf16[32,2176]{1,0:T(8,128)(2,1)S(1)}, u32[]{:S(2)}, u32[]{:S(2)}) collective-permute-start(bf16[32,2176]{1,0:T(8,128)(2,1)S(1)} %collective-permute-done.refs_1_), channel_id=1, source_target_pairs={{0,2},{2,0},{4,6},{6,4},{8,10},{10,8},{12,14},{14,12},{1,3},{3,1},... | collective-permute-start | bytes 417800 | tf_op jit(solution)/shard_map/ppermute | solution.py:240
  22.8 6.4 %collective-permute-start.9 = (bf16[32,2176]{1,0:T(8,128)(2,1)S(1)}, bf16[32,2176]{1,0:T(8,128)(2,1)S(1)}, u32[]{:S(2)}, u32[]{:S(2)}) collective-permute-start(bf16[32,2176]{1,0:T(8,128)(2,1)S(1)} %collective-permute-done.1.refs_2_), channel_id=1, source_target_pairs={{0,1},{1,0},{2,3},{3,2},{4,5},{5,4},{6,7},{7,6},{8,9},{9,8},{10,11... | collective-permute-start | bytes 417800 | tf_op jit(solution)/shard_map/ppermute | solution.py:244
  22.8 6.4 %collective-permute-start.8 = (bf16[32,2176]{1,0:T(8,128)(2,1)S(1)}, bf16[32,2176]{1,0:T(8,128)(2,1)S(1)}, u32[]{:S(2)}, u32[]{:S(2)}) collective-permute-start(bf16[32,2176]{1,0:T(8,128)(2,1)S(1)} %collective-permute-done.refs_1_), channel_id=1, source_target_pairs={{0,1},{1,0},{2,3},{3,2},{4,5},{5,4},{6,7},{7,6},{8,9},{9,8},{10,11... | collective-permute-start | bytes 417800 | tf_op jit(solution)/shard_map/ppermute | solution.py:244
  23.3 5.9 %collective-permute-start.14 = (bf16[32,2176]{1,0:T(8,128)(2,1)S(1)}, bf16[32,2176]{1,0:T(8,128)(2,1)S(1)}, u32[]{:S(2)}, u32[]{:S(2)}) collective-permute-start(bf16[32,2176]{1,0:T(8,128)(2,1)S(1)} %collective-permute-done.6.refs_7_), channel_id=1, source_target_pairs={{0,1},{1,0},{2,3},{3,2},{4,5},{5,4},{6,7},{7,6},{8,9},{9,8},{10,11... | collective-permute-start | bytes 417800 | tf_op jit(solution)/shard_map/ppermute | solution.py:245
  27.3 1.9 %collective-permute-start.13 = (bf16[32,2176]{1,0:T(8,128)(2,1)S(1)}, bf16[32,2176]{1,0:T(8,128)(2,1)S(1)}, u32[]{:S(2)}, u32[]{:S(2)}) collective-permute-start(bf16[32,2176]{1,0:T(8,128)(2,1)S(1)} %collective-permute-done.5.refs_6_), channel_id=1, source_target_pairs={{0,1},{1,0},{2,3},{3,2},{4,5},{5,4},{6,7},{7,6},{8,9},{9,8},{10,11... | collective-permute-start | bytes 417800 | tf_op jit(solution)/shard_map/ppermute | solution.py:245
  29.2 1.4 %collective-permute-start.12 = (bf16[32,2176]{1,0:T(8,128)(2,1)S(1)}, bf16[32,2176]{1,0:T(8,128)(2,1)S(1)}, u32[]{:S(2)}, u32[]{:S(2)}) collective-permute-start(bf16[32,2176]{1,0:T(8,128)(2,1)S(1)} %collective-permute-done.4.refs_5_), channel_id=1, source_target_pairs={{0,1},{1,0},{2,3},{3,2},{4,5},{5,4},{6,7},{7,6},{8,9},{9,8},{10,11... | collective-permute-start | bytes 417800 | tf_op jit(solution)/shard_map/ppermute | solution.py:245
  44.3 24.4 %copy-start.2 = (bf16[32,4096]{1,0:T(8,128)(2,1)S(1)}, bf16[32,4096]{1,0:T(8,128)(2,1)}, u32[]{:S(2)}) copy-start(bf16[32,4096]{1,0:T(8,128)(2,1)} %refs_1_.1) | copy-start | bytes 786436
  44.3 5.3 %collective-permute-start.15 = (bf16[256,2048]{1,0:T(8,128)(2,1)S(1)}, bf16[256,2048]{1,0:T(8,128)(2,1)S(1)}, u32[]{:S(2)}, u32[]{:S(2)}) collective-permute-start(bf16[256,2048]{1,0:T(8,128)(2,1)S(1)} %get-tuple-element.25), channel_id=1, source_target_pairs={{0,1},{1,0},{2,3},{3,2},{4,5},{5,4},{6,7},{7,6},{8,9},{9,8},{10,11... | collective-permute-start | bytes 3145736 | tf_op jit(solution)/shard_map/ppermute | solution.py:249
  49.9 6.4 %collective-permute-start.16 = (bf16[32,2048]{1,0:T(8,128)(2,1)S(1)}, bf16[32,2048]{1,0:T(8,128)(2,1)S(1)}, u32[]{:S(2)}, u32[]{:S(2)}) collective-permute-start(bf16[32,2048]{1,0:T(8,128)(2,1)S(1)} %get-tuple-element.34), channel_id=1, source_target_pairs={{0,2},{2,0},{4,6},{6,4},{8,10},{10,8},{12,14},{14,12},{1,3},{3,1},... | collective-permute-start | bytes 393224 | tf_op jit(solution)/shard_map/ppermute | solution.py:257
  50.5 8.6 %collective-permute-start.18 = (bf16[32,2048]{1,0:T(8,128)(2,1)S(1)}, bf16[32,2048]{1,0:T(8,128)(2,1)S(1)}, u32[]{:S(2)}, u32[]{:S(2)}) collective-permute-start(bf16[32,2048]{1,0:T(8,128)(2,1)S(1)} %get-tuple-element.36), channel_id=1, source_target_pairs={{0,2},{2,0},{4,6},{6,4},{8,10},{10,8},{12,14},{14,12},{1,3},{3,1},... | collective-permute-start | bytes 393224 | tf_op jit(solution)/shard_map/ppermute | solution.py:257
  52.0 9.9 %collective-permute-start.20 = (bf16[32,2048]{1,0:T(8,128)(2,1)S(1)}, bf16[32,2048]{1,0:T(8,128)(2,1)S(1)}, u32[]{:S(2)}, u32[]{:S(2)}) collective-permute-start(bf16[32,2048]{1,0:T(8,128)(2,1)S(1)} %get-tuple-element.38), channel_id=1, source_target_pairs={{0,2},{2,0},{4,6},{6,4},{8,10},{10,8},{12,14},{14,12},{1,3},{3,1},... | collective-permute-start | bytes 393224 | tf_op jit(solution)/shard_map/ppermute | solution.py:257
  52.5 11.6 %collective-permute-start.22 = (bf16[32,2048]{1,0:T(8,128)(2,1)S(1)}, bf16[32,2048]{1,0:T(8,128)(2,1)S(1)}, u32[]{:S(2)}, u32[]{:S(2)}) collective-permute-start(bf16[32,2048]{1,0:T(8,128)(2,1)S(1)} %get-tuple-element.40), channel_id=1, source_target_pairs={{0,2},{2,0},{4,6},{6,4},{8,10},{10,8},{12,14},{14,12},{1,3},{3,1},... | collective-permute-start | bytes 393224 | tf_op jit(solution)/shard_map/ppermute | solution.py:257
  56.3 7.8 %collective-permute-start.17 = (bf16[32,2048]{1,0:T(8,128)(2,1)S(1)}, bf16[32,2048]{1,0:T(8,128)(2,1)S(1)}, u32[]{:S(2)}, u32[]{:S(2)}) collective-permute-start(bf16[32,2048]{1,0:T(8,128)(2,1)S(1)} %add_convert_fusion.3), channel_id=1, source_target_pairs={{0,8},{2,10},{4,12},{6,14},{8,0},{10,2},{12,4},{14,6},{1,9},{3,11}... | collective-permute-start | bytes 393224 | tf_op jit(solution)/shard_map/ppermute | solution.py:259
  59.1 8.2 %collective-permute-start.19 = (bf16[32,2048]{1,0:T(8,128)(2,1)S(1)}, bf16[32,2048]{1,0:T(8,128)(2,1)S(1)}, u32[]{:S(2)}, u32[]{:S(2)}) collective-permute-start(bf16[32,2048]{1,0:T(8,128)(2,1)S(1)} %add_convert_fusion.2), channel_id=1, source_target_pairs={{0,12},{2,14},{4,0},{6,2},{8,4},{10,6},{12,8},{14,10},{1,13},{3,15... | collective-permute-start | bytes 393224 | tf_op jit(solution)/shard_map/ppermute | solution.py:259
  61.9 6.8 %collective-permute-start.21 = (bf16[32,2048]{1,0:T(8,128)(2,1)S(1)}, bf16[32,2048]{1,0:T(8,128)(2,1)S(1)}, u32[]{:S(2)}, u32[]{:S(2)}) collective-permute-start(bf16[32,2048]{1,0:T(8,128)(2,1)S(1)} %add_convert_fusion.1), channel_id=1, source_target_pairs={{0,4},{2,6},{4,8},{6,10},{8,12},{10,14},{12,0},{14,2},{1,5},{3,7},... | collective-permute-start | bytes 393224 | tf_op jit(solution)/shard_map/ppermute | solution.py:259

commit v4 on v3

--- a/solution.py
+++ b/solution.py
@@ -9,6 +9,7 @@
 
 LANES = 128
 WIDTH = 512
+LIMIT = 6 << 20
 LEAD_FLOPS = 40_000_000_000
 
 
@@ -69,7 +70,7 @@
             pltpu.VMEM(route_scores.shape[::-1], jnp.float32),
             pltpu.SemaphoreType.DMA((4,)),
         ],
-        compiler_params=pltpu.CompilerParams(vmem_limit_bytes=16 << 20),
+        compiler_params=pltpu.CompilerParams(vmem_limit_bytes=LIMIT),
         cost_estimate=pl.CostEstimate(
             flops=LEAD_FLOPS, bytes_accessed=2 * rows * features, transcendentals=0
         ),
@@ -110,101 +111,71 @@
             out_ref[:, e * units + at : e * units + at + block] = hidden.astype(jnp.bfloat16)
 
 
-def down_copies(down_ref, buffer, sem, at):
-    width = buffer.shape[3]
-    return [
-        pltpu.make_async_copy(
-            down_ref.at[:, :, pl.ds(pl.multiple_of(at + j * width, width), width)],
-            buffer.at[j],
-            sem.at[j],
-        )
-        for j in range(buffer.shape[0])
-    ]
-
-
-def other_kernel(half, experts, blocks, place_ref, *refs):
-    gate_ref, up_ref, down_ref, hidden_ref, send_ref = refs[2 * blocks : 2 * blocks + 5]
-    own, other, coded, buffer, sem = refs[2 * blocks + 5 :]
-    copies = down_copies(down_ref, buffer, sem, (1 - place_ref[1]) * half)
-    for copy in copies:
-        copy.start()
+def hidden_kernel(half, experts, blocks, place_ref, *refs):
+    gate_ref, up_ref, out_ref, own, other, coded = refs[2 * blocks :]
     fill_rows(half, blocks, refs, own, other, coded)
-    hidden_units(half, experts, place_ref, gate_ref, up_ref, own, other, coded, hidden_ref)
-    width = buffer.shape[3]
-    for j, copy in enumerate(copies):
-        copy.wait()
-        total = jnp.dot(
-            hidden_ref[...], buffer[j].reshape(-1, width), preferred_element_type=jnp.float32
-        )
-        send_ref[:, j * width : (j + 1) * width] = total.astype(send_ref.dtype)
-
-
-def mine_kernel(half, place_ref, hidden_ref, down_ref, *refs):
-    out_refs, buffer, sem = refs[:-2], refs[-2], refs[-1]
-    copies = down_copies(down_ref, buffer, sem, place_ref[1] * half)
-    for copy in copies:
-        copy.start()
-    width = buffer.shape[3]
-    tokens = out_refs[0].shape[0]
-    for j, copy in enumerate(copies):
-        copy.wait()
-        total = jnp.dot(
-            hidden_ref[...], buffer[j].reshape(-1, width), preferred_element_type=jnp.float32
-        )
-        for i, out_ref in enumerate(out_refs):
-            out_ref[:, j * width : (j + 1) * width] = total[i * tokens : (i + 1) * tokens]
-
-
-def run_other(place, own, other, gate, up, down, experts):
+    hidden_units(half, experts, place_ref, gate_ref, up_ref, own, other, coded, out_ref)
+
+
+def run_hidden(place, own, other, gate, up, experts):
     blocks = len(own)
     local, features, width = gate.shape
     rows, half, units = blocks * own[0].shape[0], features // 2, local * width
-    vmem, hbm = pl.BlockSpec(memory_space=pltpu.VMEM), pl.BlockSpec(memory_space=pltpu.HBM)
+    vmem = pl.BlockSpec(memory_space=pltpu.VMEM)
     return pl.pallas_call(
-        functools.partial(other_kernel, half, experts, blocks),
-        out_shape=[
-            jax.ShapeDtypeStruct((rows, units), jnp.bfloat16),
-            jax.ShapeDtypeStruct((rows, half), jnp.bfloat16),
-        ],
-        in_specs=[pl.BlockSpec(memory_space=pltpu.SMEM)] + [vmem] * (2 * blocks + 2) + [hbm],
-        out_specs=[vmem] * 2,
+        functools.partial(hidden_kernel, half, experts, blocks),
+        out_shape=jax.ShapeDtypeStruct((rows, units), jnp.bfloat16),
+        in_specs=[pl.BlockSpec(memory_space=pltpu.SMEM)] + [vmem] * (2 * blocks + 2),
+        out_specs=vmem,
         scratch_shapes=[
             pltpu.VMEM((rows, half), jnp.bfloat16),
             pltpu.VMEM((rows, half), jnp.bfloat16),
             pltpu.VMEM((rows, own[0].shape[1] - half), jnp.float32),
-            pltpu.VMEM((half // WIDTH, local, width, WIDTH), jnp.bfloat16),
-            pltpu.SemaphoreType.DMA((half // WIDTH,)),
         ],
-        compiler_params=pltpu.CompilerParams(vmem_limit_bytes=16 << 20),
+        compiler_params=pltpu.CompilerParams(vmem_limit_bytes=LIMIT),
         cost_estimate=pl.CostEstimate(
-            flops=2 * rows * units * (2 * features + half),
-            bytes_accessed=4 * rows * half,
-            transcendentals=rows * units,
+            flops=4 * rows * units * features, bytes_accessed=4 * rows * half, transcendentals=rows * units
         ),
-        name="other",
-    )(place, *own, *other, gate, up, down)
-
-
-def run_mine(place, hidden, down, blocks):
-    rows = hidden.shape[0]
-    local, width, features = down.shape
+        name="hidden",
+    )(place, *own, *other, gate, up)
+
+
+def down_kernel(mine, far, place_ref, hidden_ref, down_ref, *refs):
+    out_refs = refs[mine:]
+    local, units, features = down_ref.shape
     half = features // 2
-    vmem, hbm = pl.BlockSpec(memory_space=pltpu.VMEM), pl.BlockSpec(memory_space=pltpu.HBM)
+    core = place_ref[1] if mine else 1 - place_ref[1]
+    rows = hidden_ref.shape[0] // 2
+    tokens = out_refs[0].shape[0]
+    hidden = hidden_ref[far * rows : (far + 1) * rows, :]
+    for at in range(0, half, WIDTH):
+        cut = pl.ds(pl.multiple_of(core * half + at, WIDTH), WIDTH)
+        total = jnp.dot(
+            hidden,
+            down_ref[:, :, cut].reshape(local * units, WIDTH),
+            preferred_element_type=jnp.float32,
+        )
+        if mine:
+            total = total + refs[0][:, at : at + WIDTH].astype(jnp.float32)
+        for i, out_ref in enumerate(out_refs):
+            out_ref[:, at : at + WIDTH] = total[i * tokens : (i + 1) * tokens].astype(out_ref.dtype)
+
+
+def run_down(place, hidden, down, far, received, kind, blocks):
+    rows, half = hidden.shape[0] // 2, down.shape[2] // 2
+    vmem = pl.BlockSpec(memory_space=pltpu.VMEM)
+    extra = [] if received is None else [received]
     return pl.pallas_call(
-        functools.partial(mine_kernel, half),
-        out_shape=[jax.ShapeDtypeStruct((rows // blocks, half), jnp.float32)] * blocks,
-        in_specs=[pl.BlockSpec(memory_space=pltpu.SMEM), vmem, hbm],
+        functools.partial(down_kernel, len(extra), far),
+        out_shape=[jax.ShapeDtypeStruct((rows // blocks, half), kind)] * blocks,
+        in_specs=[pl.BlockSpec(memory_space=pltpu.SMEM)] + [vmem] * (2 + len(extra)),
         out_specs=[vmem] * blocks,
-        scratch_shapes=[
-            pltpu.VMEM((half // WIDTH, local, width, WIDTH), jnp.bfloat16),
-            pltpu.SemaphoreType.DMA((half // WIDTH,)),
-        ],
-        compiler_params=pltpu.CompilerParams(vmem_limit_bytes=16 << 20),
+        compiler_params=pltpu.CompilerParams(vmem_limit_bytes=LIMIT),
         cost_estimate=pl.CostEstimate(
             flops=2 * rows * half * hidden.shape[1], bytes_accessed=4 * rows * half, transcendentals=0
         ),
-        name="mine",
-    )(place, hidden, down)
+        name="mine" if extra else "other",
+    )(place, hidden, down, *extra)
 
 
 def on_device(
@@ -238,19 +209,15 @@
         same[k] = lax.ppermute(packed, "sect", along(k))
     for k in [0] + shifts:
         opposite[k] = lax.ppermute(same[k], "sect", across)
-    down_matrix = pltpu.with_memory_space_constraint(down_matrix, pltpu.HBM)
     near = [same[k] for k in range(outer)]
     far = [opposite[k] for k in range(outer)]
     near_other = [lax.ppermute(block, "tp", cores) for block in near]
     far_other = [lax.ppermute(block, "tp", cores) for block in far]
-    hidden, send = run_other(
-        place, near + far, near_other + far_other, gate_matrix, up_matrix, down_matrix, experts
-    )
-    received = lax.ppermute(send, "tp", cores).reshape(inner, outer, token_count, half)
-    mine = run_mine(place, hidden, down_matrix, inner * outer)
-    near_sum = [mine[k] + received[0, k].astype(f32) for k in range(outer)]
-    far_sum = [(mine[outer + k] + received[1, k].astype(f32)).astype(bf16) for k in range(outer)]
-    near_sum, far_sum = lax.optimization_barrier((near_sum, far_sum))
+    hidden = run_hidden(place, near + far, near_other + far_other, gate_matrix, up_matrix, experts)
+    far_send = lax.ppermute(run_down(place, hidden, down_matrix, 1, None, bf16, 1)[0], "tp", cores)
+    near_send = lax.ppermute(run_down(place, hidden, down_matrix, 0, None, bf16, 1)[0], "tp", cores)
+    far_sum = run_down(place, hidden, down_matrix, 1, far_send, bf16, outer)
+    near_sum = run_down(place, hidden, down_matrix, 0, near_send, f32, outer)
     result = lax.dynamic_slice_in_dim(hidden_in, core * half, half, 1).astype(f32)
     order = sorted(range(1, outer), key=lambda k: -min(k, outer - k)) + [0]
     for k in order:

time: 69.7 us -> 66.2 us (0.950)
  Pallas kernels: 20.8 us -> 18.9 us
  waiting for transfers between devices: 30.8 us -> 29 us
    ppermute x4, waiting for transfers between devices: 8.57 us -> 6.49 us  [on_device(): block = near_sum[k] + lax.ppermute(far_sum[k], 'sect', across).astype(f32)]
    pallas_call x2 -> x5, Pallas kernels: 18.8 us -> 16.9 us  [the longest x1 9.48 us: run_hidden(): pl.pallas_call(functools.partial(hidden_kernel, half, experts, blocks), o...]
  transfers between devices with their start and end apart: 23 -> 24, of which waited for: 11 -> 11; matrix products, arithmetic and copies ran while one was open for 0% -> 0% of each run, Pallas kernels for 7% -> 8%
where the time goes in v4:
time: 66.2 us; the launch traced here: 66.1 us
  waiting for transfers between devices  29 us (44%)
  Pallas kernels  18.9 us (29%)
  starting transfers between devices  17 us (26%)
  other arithmetic  0.93 us (1%)
    ppermute x3, waiting for transfers between devices, on_device(): same[k] = lax.ppermute(packed, 'sect', along(k))  10.5 us
    pallas_call x1, Pallas kernels, run_hidden(): pl.pallas_call(functools.partial(hidden_kernel, half, experts, blocks), o...  9.48 us
    pallas_call x4, Pallas kernels, run_down(): pl.pallas_call(functools.partial(down_kernel, len(extra), far), out_shape...  7.41 us
    ppermute x4, waiting for transfers between devices, on_device(): block = near_sum[k] + lax.ppermute(far_sum[k], 'sect', across).astype(f32)  6.49 us
    ppermute x4, waiting for transfers between devices, on_device(): opposite[k] = lax.ppermute(same[k], 'sect', across)  5.83 us
    ppermute x4, starting transfers between devices, on_device(): opposite[k] = lax.ppermute(same[k], 'sect', across)  5.57 us
    ppermute x3, waiting for transfers between devices, on_device(): block = lax.ppermute(block.astype(bf16), 'sect', along(-k)).astype(f32)  4.86 us
    ppermute x3, starting transfers between devices, on_device(): same[k] = lax.ppermute(packed, 'sect', along(k))  4.61 us
  transfers between devices with their start and end apart: 24, of which 11 were waited for; matrix products, arithmetic and copies ran while one was open for 0% of the time, Pallas kernels for 8%

profile of v4, /device:TPU:0, one launch (start us, length us, event | category | flops | bytes accessed | tf_op | source)
XLA Modules:
  0.0 66.1 jit_solution(2438547661425987776)
XLA Ops:
  0.0 0.1 pad_add_fusion.place_ref
  0.1 0.0 slice-start.2
  0.1 0.0 slice-start.3
  0.1 2.0 %prepare.1.refs_0_ = bf16[32,2176]{1,0:T(8,128)(2,1)S(1)} custom-call(s32[2]{0:T(128)S(1)} %pad_add_fusion.place_ref, s32[32]{0:T(128)} %refs_0_.1, bf16[32,4096]{1,0:T(8,128)(2,1)} %refs_1_.1, s32[8,32]{1,0:T(8,128)} %bitcast.6, f32[8,32]{1,0:T(8,128)} %bitcast.7), custom_call_target="tpu_custom_call" | custom-call | flops 40000000000 | bytes 262144 | tf_op jit(solution)/shard_map/prepare/pallas_call | solution.py:61
  2.2 3.0 %collective-permute-start.3 = (bf16[32,2176]{1,0:T(8,128)(2,1)S(1)}, bf16[32,2176]{1,0:T(8,128)(2,1)S(1)}, u32[]{:S(2)}, u32[]{:S(2)}) collective-permute-start(bf16[32,2176]{1,0:T(8,128)(2,1)S(1)} %prepare.1.refs_0_), channel_id=1, source_target_pairs={{0,2},{2,0},{4,6},{6,4},{8,10},{10,8},{12,14},{14,12},{1,3},{3,1},... | collective-permute-start | bytes 417800 | tf_op jit(solution)/shard_map/ppermute | solution.py:211
  5.2 3.6 %collective-permute-start.2 = (bf16[32,2176]{1,0:T(8,128)(2,1)S(1)}, bf16[32,2176]{1,0:T(8,128)(2,1)S(1)}, u32[]{:S(2)}, u32[]{:S(2)}) collective-permute-start(bf16[32,2176]{1,0:T(8,128)(2,1)S(1)} %prepare.1.refs_0_), channel_id=1, source_target_pairs={{0,12},{2,14},{4,0},{6,2},{8,4},{10,6},{12,8},{14,10},{1,13},{3,15... | collective-permute-start | bytes 417800 | tf_op jit(solution)/shard_map/ppermute | solution.py:209
  8.8 0.0 collective-permute-start.7
  8.8 0.0 collective-permute-start.1
  8.8 1.0 %collective-permute-start = (bf16[32,2176]{1,0:T(8,128)(2,1)S(1)}, bf16[32,2176]{1,0:T(8,128)(2,1)S(1)}, u32[]{:S(2)}, u32[]{:S(2)}) collective-permute-start(bf16[32,2176]{1,0:T(8,128)(2,1)S(1)} %prepare.1.refs_0_), channel_id=1, source_target_pairs={{0,4},{2,6},{4,8},{6,10},{8,12},{10,14},{12,0},{14,2},{1,5},{3,7},... | collective-permute-start | bytes 417800 | tf_op jit(solution)/shard_map/ppermute | solution.py:209
  9.8 0.0 collective-permute-done.3.refs_4_
  9.8 0.0 collective-permute-start.11
  9.8 3.1 %collective-permute-done.2.refs_3_ = bf16[32,2176]{1,0:T(8,128)(2,1)S(1)} collective-permute-done((bf16[32,2176]{1,0:T(8,128)(2,1)S(1)}, bf16[32,2176]{1,0:T(8,128)(2,1)S(1)}, u32[]{:S(2)}, u32[]{:S(2)}) %collective-permute-start.2) | collective-permute-done | bytes 139296 | tf_op jit(solution)/shard_map/ppermute | solution.py:209
  12.9 0.0 collective-permute-start.10
  13.0 0.0 collective-permute-done.7.refs_8_
  13.0 0.5 collective-permute-start.6
  13.5 7.3 %collective-permute-done.1.refs_2_ = bf16[32,2176]{1,0:T(8,128)(2,1)S(1)} collective-permute-done((bf16[32,2176]{1,0:T(8,128)(2,1)S(1)}, bf16[32,2176]{1,0:T(8,128)(2,1)S(1)}, u32[]{:S(2)}, u32[]{:S(2)}) %collective-permute-start.1) | collective-permute-done | bytes 139296 | tf_op jit(solution)/shard_map/ppermute | solution.py:209
  20.8 0.5 collective-permute-start.5
  21.3 0.0 collective-permute-done.refs_1_
  21.3 1.5 %collective-permute-start.4 = (bf16[32,2176]{1,0:T(8,128)(2,1)S(1)}, bf16[32,2176]{1,0:T(8,128)(2,1)S(1)}, u32[]{:S(2)}, u32[]{:S(2)}) collective-permute-start(bf16[32,2176]{1,0:T(8,128)(2,1)S(1)} %collective-permute-done.refs_1_), channel_id=1, source_target_pairs={{0,2},{2,0},{4,6},{6,4},{8,10},{10,8},{12,14},{14,12},{1,3},{3,1},... | collective-permute-start | bytes 417800 | tf_op jit(solution)/shard_map/ppermute | solution.py:211
  22.8 0.0 collective-permute-done.11.refs_12_
  22.8 0.0 collective-permute-start.9
  22.8 0.0 collective-permute-done.10.refs_11_
  22.8 0.5 collective-permute-start.8
  23.3 0.0 collective-permute-done.6.refs_7_
  23.3 0.1 collective-permute-start.14
  23.4 3.9 %collective-permute-done.5.refs_6_ = bf16[32,2176]{1,0:T(8,128)(2,1)S(1)} collective-permute-done((bf16[32,2176]{1,0:T(8,128)(2,1)S(1)}, bf16[32,2176]{1,0:T(8,128)(2,1)S(1)}, u32[]{:S(2)}, u32[]{:S(2)}) %collective-permute-start.5) | collective-permute-done | bytes 139296 | tf_op jit(solution)/shard_map/ppermute | solution.py:211
  27.3 0.0 collective-permute-start.13
  27.3 1.9 %collective-permute-done.4.refs_5_ = bf16[32,2176]{1,0:T(8,128)(2,1)S(1)} collective-permute-done((bf16[32,2176]{1,0:T(8,128)(2,1)S(1)}, bf16[32,2176]{1,0:T(8,128)(2,1)S(1)}, u32[]{:S(2)}, u32[]{:S(2)}) %collective-permute-start.4) | collective-permute-done | bytes 139296 | tf_op jit(solution)/shard_map/ppermute | solution.py:211
  29.2 0.0 collective-permute-start.12
  29.2 0.0 collective-permute-done.9.refs_10_
  29.2 0.0 collective-permute-done.8.refs_9_
  29.2 0.0 collective-permute-done.14.refs_15_
  29.3 0.0 collective-permute-done.13.refs_14_
  29.3 1.3 %collective-permute-done.12.refs_13_ = bf16[32,2176]{1,0:T(8,128)(2,1)S(1)} collective-permute-done((bf16[32,2176]{1,0:T(8,128)(2,1)S(1)}, bf16[32,2176]{1,0:T(8,128)(2,1)S(1)}, u32[]{:S(2)}, u32[]{:S(2)}) %collective-permute-start.12) | collective-permute-done | bytes 139296 | tf_op jit(solution)/shard_map/ppermute | solution.py:215
  30.6 0.0 copy-done
  30.6 9.5 %hidden.1.hidden_ref = bf16[256,2048]{1,0:T(8,128)(2,1)S(1)} custom-call(s32[2]{0:T(128)S(1)} %pad_add_fusion.place_ref, bf16[32,2176]{1,0:T(8,128)(2,1)S(1)} %prepare.1.refs_0_, bf16[32,2176]{1,0:T(8,128)(2,1)S(1)} %collective-permute-done.refs_1_, bf16[32,2176]{1,0:T(8,128)(2,1)S(1)} %collective-permute-done.1.refs_2_, ...), custom_call_target="tpu_custom_call" | custom-call | flops 8589934592 | bytes 2097152 | tf_op jit(solution)/shard_map/hidden/pallas_call | solution.py:125
  40.1 0.0 slice-done
  40.1 0.0 slice-done.1
  40.1 0.0 slice-done.2
  40.1 0.0 slice-done.3
  40.1 1.9 %other.3 = bf16[128,2048]{1,0:T(8,128)(2,1)S(1)} custom-call(s32[2]{0:T(128)S(1)} %pad_add_fusion.place_ref, bf16[256,2048]{1,0:T(8,128)(2,1)S(1)} %hidden.1.hidden_ref, bf16[4,512,4096]{2,1,0:T(8,128)(2,1)S(1)} %bitcast.5), custom_call_target="tpu_custom_call" | custom-call | flops 1073741824 | bytes 1048576 | tf_op jit(solution)/shard_map/other/pallas_call | solution.py:168
  42.0 0.2 collective-permute-start.16
  42.2 1.9 %other.2 = bf16[128,2048]{1,0:T(8,128)(2,1)S(1)} custom-call(s32[2]{0:T(128)S(1)} %pad_add_fusion.place_ref, bf16[256,2048]{1,0:T(8,128)(2,1)S(1)} %hidden.1.hidden_ref, bf16[4,512,4096]{2,1,0:T(8,128)(2,1)S(1)} %bitcast.5), custom_call_target="tpu_custom_call" | custom-call | flops 1073741824 | bytes 1048576 | tf_op jit(solution)/shard_map/other/pallas_call | solution.py:168
  44.1 0.0 copy-start.2
  44.1 0.4 collective-permute-start.15
  44.5 0.0 collective-permute-done.16.refs_0_
  44.5 1.9 %mine.3 = (bf16[32,2048]{1,0:T(8,128)(2,1)S(1)}, bf16[32,2048]{1,0:T(8,128)(2,1)S(1)}, bf16[32,2048]{1,0:T(8,128)(2,1)S(1)}, bf16[32,2048]{1,0:T(8,128)(2,1)S(1)}) custom-call(s32[2]{0:T(128)S(1)} %pad_add_fusion.place_ref, bf16[256,2048]{1,0:T(8,128)(2,1)S(1)} %hidden.1.hidden_ref, bf16[4,512,4096]{2,1,0:T(8,128)(2,1)S(1)} %bitcast.5, ...), custom_call_target="tpu_custom_call" | custom-call | flops 1073741824 | bytes 1048576 | tf_op jit(solution)/shard_map/mine/pallas_call | solution.py:168
  46.4 0.6 collective-permute-start.17
  47.0 1.5 %collective-permute-start.19 = (bf16[32,2048]{1,0:T(8,128)(2,1)S(1)}, bf16[32,2048]{1,0:T(8,128)(2,1)S(1)}, u32[]{:S(2)}, u32[]{:S(2)}) collective-permute-start(bf16[32,2048]{1,0:T(8,128)(2,1)S(1)} %get-tuple-element.16), channel_id=1, source_target_pairs={{0,2},{2,0},{4,6},{6,4},{8,10},{10,8},{12,14},{14,12},{1,3},{3,1},... | collective-permute-start | bytes 393224 | tf_op jit(solution)/shard_map/ppermute | solution.py:224
  48.5 0.5 collective-permute-start.21
  49.0 1.5 %collective-permute-start.23 = (bf16[32,2048]{1,0:T(8,128)(2,1)S(1)}, bf16[32,2048]{1,0:T(8,128)(2,1)S(1)}, u32[]{:S(2)}, u32[]{:S(2)}) collective-permute-start(bf16[32,2048]{1,0:T(8,128)(2,1)S(1)} %get-tuple-element.20), channel_id=1, source_target_pairs={{0,2},{2,0},{4,6},{6,4},{8,10},{10,8},{12,14},{14,12},{1,3},{3,1},... | collective-permute-start | bytes 393224 | tf_op jit(solution)/shard_map/ppermute | solution.py:224
  50.5 0.0 collective-permute-done.15.refs_0_
  50.5 1.8 %mine.2 = (f32[32,2048]{1,0:T(8,128)S(1)}, f32[32,2048]{1,0:T(8,128)S(1)}, f32[32,2048]{1,0:T(8,128)S(1)}, f32[32,2048]{1,0:T(8,128)S(1)}) custom-call(s32[2]{0:T(128)S(1)} %pad_add_fusion.place_ref, bf16[256,2048]{1,0:T(8,128)(2,1)S(1)} %hidden.1.hidden_ref, bf16[4,512,4096]{2,1,0:T(8,128)(2,1)S(1)} %bitcast.5, ...), custom_call_target="tpu_custom_call" | custom-call | flops 1073741824 | bytes 1048576 | tf_op jit(solution)/shard_map/mine/pallas_call | solution.py:168
  52.4 0.4 collective-permute-done.17
  52.9 0.2 collective-permute-start.18
  53.1 2.5 %collective-permute-done.19 = bf16[32,2048]{1,0:T(8,128)(2,1)S(1)} collective-permute-done((bf16[32,2048]{1,0:T(8,128)(2,1)S(1)}, bf16[32,2048]{1,0:T(8,128)(2,1)S(1)}, u32[]{:S(2)}, u32[]{:S(2)}) %collective-permute-start.19) | collective-permute-done | bytes 131104 | tf_op jit(solution)/shard_map/ppermute | solution.py:224
  55.7 1.1 %collective-permute-start.20 = (bf16[32,2048]{1,0:T(8,128)(2,1)S(1)}, bf16[32,2048]{1,0:T(8,128)(2,1)S(1)}, u32[]{:S(2)}, u32[]{:S(2)}) collective-permute-start(bf16[32,2048]{1,0:T(8,128)(2,1)S(1)} %add_convert_fusion.2), channel_id=1, source_target_pairs={{0,12},{2,14},{4,0},{6,2},{8,4},{10,6},{12,8},{14,10},{1,13},{3,15... | collective-permute-start | bytes 393224 | tf_op jit(solution)/shard_map/ppermute | solution.py:226
  56.8 1.6 %collective-permute-done.21 = bf16[32,2048]{1,0:T(8,128)(2,1)S(1)} collective-permute-done((bf16[32,2048]{1,0:T(8,128)(2,1)S(1)}, bf16[32,2048]{1,0:T(8,128)(2,1)S(1)}, u32[]{:S(2)}, u32[]{:S(2)}) %collective-permute-start.21) | collective-permute-done | bytes 131104 | tf_op jit(solution)/shard_map/ppermute | solution.py:224
  58.5 0.1 collective-permute-start.22
  58.5 1.9 %collective-permute-done.23 = bf16[32,2048]{1,0:T(8,128)(2,1)S(1)} collective-permute-done((bf16[32,2048]{1,0:T(8,128)(2,1)S(1)}, bf16[32,2048]{1,0:T(8,128)(2,1)S(1)}, u32[]{:S(2)}, u32[]{:S(2)}) %collective-permute-start.23) | collective-permute-done | bytes 131104 | tf_op jit(solution)/shard_map/ppermute | solution.py:224
  60.4 0.0 collective-permute-done.18
  60.4 2.6 %collective-permute-done.20 = bf16[32,2048]{1,0:T(8,128)(2,1)S(1)} collective-permute-done((bf16[32,2048]{1,0:T(8,128)(2,1)S(1)}, bf16[32,2048]{1,0:T(8,128)(2,1)S(1)}, u32[]{:S(2)}, u32[]{:S(2)}) %collective-permute-start.20) | collective-permute-done | bytes 131104 | tf_op jit(solution)/shard_map/ppermute | solution.py:226
  63.1 2.2 %collective-permute-done.22 = bf16[32,2048]{1,0:T(8,128)(2,1)S(1)} collective-permute-done((bf16[32,2048]{1,0:T(8,128)(2,1)S(1)}, bf16[32,2048]{1,0:T(8,128)(2,1)S(1)}, u32[]{:S(2)}, u32[]{:S(2)}) %collective-permute-start.22) | collective-permute-done | bytes 131104 | tf_op jit(solution)/shard_map/ppermute | solution.py:226
  65.3 0.8 %add_convert_fusion = bf16[32,2048]{1,0:T(8,128)(2,1)} fusion(f32[32,2048]{1,0:T(8,128)S(1)} %get-tuple-element.19, bf16[32,2048]{1,0:T(8,128)(2,1)S(1)} %collective-permute-done.23, bf16[32,2048]{1,0:T(8,128)(2,1)S(1)} %collective-permute-done.22, bf16[32,2048]{1,0:T(8,128)(2,1)S(1)} %collective-permute-done.20, ...), kind=kLoop, calls=%fused_computation | loop fusion | flops 720896 | bytes 1048580 | tf_op jit(solution)/shard_map/convert_element_type | solution.py:228
  (10 shorter events, 0.1 us)
Async XLA Ops:
  0.1 40.0 %slice-start = ((s8[16777216]{0:T(1024)(128)(4,1)}), s8[4194304]{0:T(1024)(128)(4,1)S(1)}, s32[]{:S(2)}) async-start(s8[16777216]{0:T(1024)(128)(4,1)} %bitcast.4), calls=%async_computation | async-start | bytes 8388608
  0.1 30.5 %copy-start = (bf16[4,4096,512]{2,1,0:T(8,128)(2,1)S(1)}, bf16[4,4096,512]{2,1,0:T(8,128)(2,1)}, u32[]{:S(2)}) copy-start(bf16[4,4096,512]{2,1,0:T(8,128)(2,1)} %refs_16_.1) | copy-start | bytes 50331652
  0.1 30.5 %copy-start.1 = (bf16[4,4096,512]{2,1,0:T(8,128)(2,1)S(1)}, bf16[4,4096,512]{2,1,0:T(8,128)(2,1)}, u32[]{:S(2)}) copy-start(bf16[4,4096,512]{2,1,0:T(8,128)(2,1)} %refs_17_.1) | copy-start | bytes 50331652
  0.1 40.0 %slice-start.1 = ((s8[16777216]{0:T(1024)(128)(4,1)}), s8[4194304]{0:T(1024)(128)(4,1)S(1)}, s32[]{:S(2)}) async-start(s8[16777216]{0:T(1024)(128)(4,1)} %bitcast.4), calls=%async_computation.1 | async-start | bytes 8388608
  0.1 40.0 %slice-start.2 = ((s8[16777216]{0:T(1024)(128)(4,1)}), s8[4194304]{0:T(1024)(128)(4,1)S(1)}, s32[]{:S(2)}) async-start(s8[16777216]{0:T(1024)(128)(4,1)} %bitcast.4), calls=%async_computation.2 | async-start | bytes 8388608
  0.1 40.0 %slice-start.3 = ((s8[16777216]{0:T(1024)(128)(4,1)}), s8[4194304]{0:T(1024)(128)(4,1)S(1)}, s32[]{:S(2)}) async-start(s8[16777216]{0:T(1024)(128)(4,1)} %bitcast.4), calls=%async_computation.3 | async-start | bytes 8388608
  2.2 7.7 %collective-permute-start.3 = (bf16[32,2176]{1,0:T(8,128)(2,1)S(1)}, bf16[32,2176]{1,0:T(8,128)(2,1)S(1)}, u32[]{:S(2)}, u32[]{:S(2)}) collective-permute-start(bf16[32,2176]{1,0:T(8,128)(2,1)S(1)} %prepare.1.refs_0_), channel_id=1, source_target_pairs={{0,2},{2,0},{4,6},{6,4},{8,10},{10,8},{12,14},{14,12},{1,3},{3,1},... | collective-permute-start | bytes 417800 | tf_op jit(solution)/shard_map/ppermute | solution.py:211
  5.2 7.8 %collective-permute-start.2 = (bf16[32,2176]{1,0:T(8,128)(2,1)S(1)}, bf16[32,2176]{1,0:T(8,128)(2,1)S(1)}, u32[]{:S(2)}, u32[]{:S(2)}) collective-permute-start(bf16[32,2176]{1,0:T(8,128)(2,1)S(1)} %prepare.1.refs_0_), channel_id=1, source_target_pairs={{0,12},{2,14},{4,0},{6,2},{8,4},{10,6},{12,8},{14,10},{1,13},{3,15... | collective-permute-start | bytes 417800 | tf_op jit(solution)/shard_map/ppermute | solution.py:209
  8.8 4.2 %collective-permute-start.7 = (bf16[32,2176]{1,0:T(8,128)(2,1)S(1)}, bf16[32,2176]{1,0:T(8,128)(2,1)S(1)}, u32[]{:S(2)}, u32[]{:S(2)}) collective-permute-start(bf16[32,2176]{1,0:T(8,128)(2,1)S(1)} %prepare.1.refs_0_), channel_id=1, source_target_pairs={{0,1},{1,0},{2,3},{3,2},{4,5},{5,4},{6,7},{7,6},{8,9},{9,8},{10,11... | collective-permute-start | bytes 417800 | tf_op jit(solution)/shard_map/ppermute | solution.py:214
  8.8 12.0 %collective-permute-start.1 = (bf16[32,2176]{1,0:T(8,128)(2,1)S(1)}, bf16[32,2176]{1,0:T(8,128)(2,1)S(1)}, u32[]{:S(2)}, u32[]{:S(2)}) collective-permute-start(bf16[32,2176]{1,0:T(8,128)(2,1)S(1)} %prepare.1.refs_0_), channel_id=1, source_target_pairs={{0,8},{2,10},{4,12},{6,14},{8,0},{10,2},{12,4},{14,6},{1,9},{3,11}... | collective-permute-start | bytes 417800 | tf_op jit(solution)/shard_map/ppermute | solution.py:209
  8.8 12.5 %collective-permute-start = (bf16[32,2176]{1,0:T(8,128)(2,1)S(1)}, bf16[32,2176]{1,0:T(8,128)(2,1)S(1)}, u32[]{:S(2)}, u32[]{:S(2)}) collective-permute-start(bf16[32,2176]{1,0:T(8,128)(2,1)S(1)} %prepare.1.refs_0_), channel_id=1, source_target_pairs={{0,4},{2,6},{4,8},{6,10},{8,12},{10,14},{12,0},{14,2},{1,5},{3,7},... | collective-permute-start | bytes 417800 | tf_op jit(solution)/shard_map/ppermute | solution.py:209
  9.8 13.0 %collective-permute-start.11 = (bf16[32,2176]{1,0:T(8,128)(2,1)S(1)}, bf16[32,2176]{1,0:T(8,128)(2,1)S(1)}, u32[]{:S(2)}, u32[]{:S(2)}) collective-permute-start(bf16[32,2176]{1,0:T(8,128)(2,1)S(1)} %collective-permute-done.3.refs_4_), channel_id=1, source_target_pairs={{0,1},{1,0},{2,3},{3,2},{4,5},{5,4},{6,7},{7,6},{8,9},{9,8},{10,11... | collective-permute-start | bytes 417800 | tf_op jit(solution)/shard_map/ppermute | solution.py:215
  12.9 9.9 %collective-permute-start.10 = (bf16[32,2176]{1,0:T(8,128)(2,1)S(1)}, bf16[32,2176]{1,0:T(8,128)(2,1)S(1)}, u32[]{:S(2)}, u32[]{:S(2)}) collective-permute-start(bf16[32,2176]{1,0:T(8,128)(2,1)S(1)} %collective-permute-done.2.refs_3_), channel_id=1, source_target_pairs={{0,1},{1,0},{2,3},{3,2},{4,5},{5,4},{6,7},{7,6},{8,9},{9,8},{10,11... | collective-permute-start | bytes 417800 | tf_op jit(solution)/shard_map/ppermute | solution.py:214
  13.0 10.4 %collective-permute-start.6 = (bf16[32,2176]{1,0:T(8,128)(2,1)S(1)}, bf16[32,2176]{1,0:T(8,128)(2,1)S(1)}, u32[]{:S(2)}, u32[]{:S(2)}) collective-permute-start(bf16[32,2176]{1,0:T(8,128)(2,1)S(1)} %collective-permute-done.2.refs_3_), channel_id=1, source_target_pairs={{0,2},{2,0},{4,6},{6,4},{8,10},{10,8},{12,14},{14,12},{1,3},{3,1},... | collective-permute-start | bytes 417800 | tf_op jit(solution)/shard_map/ppermute | solution.py:211
  20.8 6.6 %collective-permute-start.5 = (bf16[32,2176]{1,0:T(8,128)(2,1)S(1)}, bf16[32,2176]{1,0:T(8,128)(2,1)S(1)}, u32[]{:S(2)}, u32[]{:S(2)}) collective-permute-start(bf16[32,2176]{1,0:T(8,128)(2,1)S(1)} %collective-permute-done.1.refs_2_), channel_id=1, source_target_pairs={{0,2},{2,0},{4,6},{6,4},{8,10},{10,8},{12,14},{14,12},{1,3},{3,1},... | collective-permute-start | bytes 417800 | tf_op jit(solution)/shard_map/ppermute | solution.py:211
  21.3 7.9 %collective-permute-start.4 = (bf16[32,2176]{1,0:T(8,128)(2,1)S(1)}, bf16[32,2176]{1,0:T(8,128)(2,1)S(1)}, u32[]{:S(2)}, u32[]{:S(2)}) collective-permute-start(bf16[32,2176]{1,0:T(8,128)(2,1)S(1)} %collective-permute-done.refs_1_), channel_id=1, source_target_pairs={{0,2},{2,0},{4,6},{6,4},{8,10},{10,8},{12,14},{14,12},{1,3},{3,1},... | collective-permute-start | bytes 417800 | tf_op jit(solution)/shard_map/ppermute | solution.py:211
  22.8 6.4 %collective-permute-start.9 = (bf16[32,2176]{1,0:T(8,128)(2,1)S(1)}, bf16[32,2176]{1,0:T(8,128)(2,1)S(1)}, u32[]{:S(2)}, u32[]{:S(2)}) collective-permute-start(bf16[32,2176]{1,0:T(8,128)(2,1)S(1)} %collective-permute-done.1.refs_2_), channel_id=1, source_target_pairs={{0,1},{1,0},{2,3},{3,2},{4,5},{5,4},{6,7},{7,6},{8,9},{9,8},{10,11... | collective-permute-start | bytes 417800 | tf_op jit(solution)/shard_map/ppermute | solution.py:214
  22.8 6.4 %collective-permute-start.8 = (bf16[32,2176]{1,0:T(8,128)(2,1)S(1)}, bf16[32,2176]{1,0:T(8,128)(2,1)S(1)}, u32[]{:S(2)}, u32[]{:S(2)}) collective-permute-start(bf16[32,2176]{1,0:T(8,128)(2,1)S(1)} %collective-permute-done.refs_1_), channel_id=1, source_target_pairs={{0,1},{1,0},{2,3},{3,2},{4,5},{5,4},{6,7},{7,6},{8,9},{9,8},{10,11... | collective-permute-start | bytes 417800 | tf_op jit(solution)/shard_map/ppermute | solution.py:214
  23.3 5.9 %collective-permute-start.14 = (bf16[32,2176]{1,0:T(8,128)(2,1)S(1)}, bf16[32,2176]{1,0:T(8,128)(2,1)S(1)}, u32[]{:S(2)}, u32[]{:S(2)}) collective-permute-start(bf16[32,2176]{1,0:T(8,128)(2,1)S(1)} %collective-permute-done.6.refs_7_), channel_id=1, source_target_pairs={{0,1},{1,0},{2,3},{3,2},{4,5},{5,4},{6,7},{7,6},{8,9},{9,8},{10,11... | collective-permute-start | bytes 417800 | tf_op jit(solution)/shard_map/ppermute | solution.py:215
  27.3 1.9 %collective-permute-start.13 = (bf16[32,2176]{1,0:T(8,128)(2,1)S(1)}, bf16[32,2176]{1,0:T(8,128)(2,1)S(1)}, u32[]{:S(2)}, u32[]{:S(2)}) collective-permute-start(bf16[32,2176]{1,0:T(8,128)(2,1)S(1)} %collective-permute-done.5.refs_6_), channel_id=1, source_target_pairs={{0,1},{1,0},{2,3},{3,2},{4,5},{5,4},{6,7},{7,6},{8,9},{9,8},{10,11... | collective-permute-start | bytes 417800 | tf_op jit(solution)/shard_map/ppermute | solution.py:215
  29.2 1.4 %collective-permute-start.12 = (bf16[32,2176]{1,0:T(8,128)(2,1)S(1)}, bf16[32,2176]{1,0:T(8,128)(2,1)S(1)}, u32[]{:S(2)}, u32[]{:S(2)}) collective-permute-start(bf16[32,2176]{1,0:T(8,128)(2,1)S(1)} %collective-permute-done.4.refs_5_), channel_id=1, source_target_pairs={{0,1},{1,0},{2,3},{3,2},{4,5},{5,4},{6,7},{7,6},{8,9},{9,8},{10,11... | collective-permute-start | bytes 417800 | tf_op jit(solution)/shard_map/ppermute | solution.py:215
  42.0 2.5 %collective-permute-start.16 = (bf16[128,2048]{1,0:T(8,128)(2,1)S(1)}, bf16[128,2048]{1,0:T(8,128)(2,1)S(1)}, u32[]{:S(2)}, u32[]{:S(2)}) collective-permute-start(bf16[128,2048]{1,0:T(8,128)(2,1)S(1)} %other.3), channel_id=1, source_target_pairs={{0,1},{1,0},{2,3},{3,2},{4,5},{5,4},{6,7},{7,6},{8,9},{9,8},{10,11... | collective-permute-start | bytes 1572872 | tf_op jit(solution)/shard_map/ppermute | solution.py:217
  44.1 21.2 %copy-start.2 = (bf16[32,4096]{1,0:T(8,128)(2,1)S(1)}, bf16[32,4096]{1,0:T(8,128)(2,1)}, u32[]{:S(2)}) copy-start(bf16[32,4096]{1,0:T(8,128)(2,1)} %refs_1_.1) | copy-start | bytes 786436
  44.1 6.4 %collective-permute-start.15 = (bf16[128,2048]{1,0:T(8,128)(2,1)S(1)}, bf16[128,2048]{1,0:T(8,128)(2,1)S(1)}, u32[]{:S(2)}, u32[]{:S(2)}) collective-permute-start(bf16[128,2048]{1,0:T(8,128)(2,1)S(1)} %other.2), channel_id=1, source_target_pairs={{0,1},{1,0},{2,3},{3,2},{4,5},{5,4},{6,7},{7,6},{8,9},{9,8},{10,11... | collective-permute-start | bytes 1572872 | tf_op jit(solution)/shard_map/ppermute | solution.py:218
  46.4 6.4 %collective-permute-start.17 = (bf16[32,2048]{1,0:T(8,128)(2,1)S(1)}, bf16[32,2048]{1,0:T(8,128)(2,1)S(1)}, u32[]{:S(2)}, u32[]{:S(2)}) collective-permute-start(bf16[32,2048]{1,0:T(8,128)(2,1)S(1)} %get-tuple-element.14), channel_id=1, source_target_pairs={{0,2},{2,0},{4,6},{6,4},{8,10},{10,8},{12,14},{14,12},{1,3},{3,1},... | collective-permute-start | bytes 393224 | tf_op jit(solution)/shard_map/ppermute | solution.py:224
  47.0 8.7 %collective-permute-start.19 = (bf16[32,2048]{1,0:T(8,128)(2,1)S(1)}, bf16[32,2048]{1,0:T(8,128)(2,1)S(1)}, u32[]{:S(2)}, u32[]{:S(2)}) collective-permute-start(bf16[32,2048]{1,0:T(8,128)(2,1)S(1)} %get-tuple-element.16), channel_id=1, source_target_pairs={{0,2},{2,0},{4,6},{6,4},{8,10},{10,8},{12,14},{14,12},{1,3},{3,1},... | collective-permute-start | bytes 393224 | tf_op jit(solution)/shard_map/ppermute | solution.py:224
  48.5 9.9 %collective-permute-start.21 = (bf16[32,2048]{1,0:T(8,128)(2,1)S(1)}, bf16[32,2048]{1,0:T(8,128)(2,1)S(1)}, u32[]{:S(2)}, u32[]{:S(2)}) collective-permute-start(bf16[32,2048]{1,0:T(8,128)(2,1)S(1)} %get-tuple-element.18), channel_id=1, source_target_pairs={{0,2},{2,0},{4,6},{6,4},{8,10},{10,8},{12,14},{14,12},{1,3},{3,1},... | collective-permute-start | bytes 393224 | tf_op jit(solution)/shard_map/ppermute | solution.py:224
  49.0 11.4 %collective-permute-start.23 = (bf16[32,2048]{1,0:T(8,128)(2,1)S(1)}, bf16[32,2048]{1,0:T(8,128)(2,1)S(1)}, u32[]{:S(2)}, u32[]{:S(2)}) collective-permute-start(bf16[32,2048]{1,0:T(8,128)(2,1)S(1)} %get-tuple-element.20), channel_id=1, source_target_pairs={{0,2},{2,0},{4,6},{6,4},{8,10},{10,8},{12,14},{14,12},{1,3},{3,1},... | collective-permute-start | bytes 393224 | tf_op jit(solution)/shard_map/ppermute | solution.py:224
  52.9 7.6 %collective-permute-start.18 = (bf16[32,2048]{1,0:T(8,128)(2,1)S(1)}, bf16[32,2048]{1,0:T(8,128)(2,1)S(1)}, u32[]{:S(2)}, u32[]{:S(2)}) collective-permute-start(bf16[32,2048]{1,0:T(8,128)(2,1)S(1)} %add_convert_fusion.3), channel_id=1, source_target_pairs={{0,8},{2,10},{4,12},{6,14},{8,0},{10,2},{12,4},{14,6},{1,9},{3,11}... | collective-permute-start | bytes 393224 | tf_op jit(solution)/shard_map/ppermute | solution.py:226
  55.7 7.4 %collective-permute-start.20 = (bf16[32,2048]{1,0:T(8,128)(2,1)S(1)}, bf16[32,2048]{1,0:T(8,128)(2,1)S(1)}, u32[]{:S(2)}, u32[]{:S(2)}) collective-permute-start(bf16[32,2048]{1,0:T(8,128)(2,1)S(1)} %add_convert_fusion.2), channel_id=1, source_target_pairs={{0,12},{2,14},{4,0},{6,2},{8,4},{10,6},{12,8},{14,10},{1,13},{3,15... | collective-permute-start | bytes 393224 | tf_op jit(solution)/shard_map/ppermute | solution.py:226
  58.5 6.8 %collective-permute-start.22 = (bf16[32,2048]{1,0:T(8,128)(2,1)S(1)}, bf16[32,2048]{1,0:T(8,128)(2,1)S(1)}, u32[]{:S(2)}, u32[]{:S(2)}) collective-permute-start(bf16[32,2048]{1,0:T(8,128)(2,1)S(1)} %add_convert_fusion.1), channel_id=1, source_target_pairs={{0,4},{2,6},{4,8},{6,10},{8,12},{10,14},{12,0},{14,2},{1,5},{3,7},... | collective-permute-start | bytes 393224 | tf_op jit(solution)/shard_map/ppermute | solution.py:226

commit v5 on v4

--- a/solution.py
+++ b/solution.py
@@ -87,7 +87,7 @@
         coded[rows, :] = refs[i][:, half:].astype(jnp.float32)
 
 
-def hidden_units(half, experts, place_ref, gate_ref, up_ref, own, other, coded, out_ref):
+def hidden_units(half, experts, place_ref, gate_ref, up_ref, own, other, coded, out_refs):
     local, _, units = gate_ref.shape
     first_slot = place_ref[0] * local
     own_at = pl.ds(pl.multiple_of(place_ref[1] * half, half), half)
@@ -108,13 +108,17 @@
             up_act = project(up_ref)
             hidden = gate_act / (1.0 + jnp.exp(-gate_act)) * up_act
             hidden = jnp.where(weight > 0.0, hidden * weight, 0.0)
-            out_ref[:, e * units + at : e * units + at + block] = hidden.astype(jnp.bfloat16)
+            columns = slice(e * units + at, e * units + at + block)
+            for i, out_ref in enumerate(out_refs):
+                rows = out_ref.shape[0]
+                out_ref[:, columns] = hidden[i * rows : (i + 1) * rows].astype(jnp.bfloat16)
 
 
 def hidden_kernel(half, experts, blocks, place_ref, *refs):
-    gate_ref, up_ref, out_ref, own, other, coded = refs[2 * blocks :]
+    gate_ref, up_ref, *out_refs = refs[2 * blocks : 2 * blocks + 4]
+    own, other, coded = refs[2 * blocks + 4 :]
     fill_rows(half, blocks, refs, own, other, coded)
-    hidden_units(half, experts, place_ref, gate_ref, up_ref, own, other, coded, out_ref)
+    hidden_units(half, experts, place_ref, gate_ref, up_ref, own, other, coded, out_refs)
 
 
 def run_hidden(place, own, other, gate, up, experts):
@@ -124,9 +128,9 @@
     vmem = pl.BlockSpec(memory_space=pltpu.VMEM)
     return pl.pallas_call(
         functools.partial(hidden_kernel, half, experts, blocks),
-        out_shape=jax.ShapeDtypeStruct((rows, units), jnp.bfloat16),
+        out_shape=[jax.ShapeDtypeStruct((rows // 2, units), jnp.bfloat16)] * 2,
         in_specs=[pl.BlockSpec(memory_space=pltpu.SMEM)] + [vmem] * (2 * blocks + 2),
-        out_specs=vmem,
+        out_specs=[vmem] * 2,
         scratch_shapes=[
             pltpu.VMEM((rows, half), jnp.bfloat16),
             pltpu.VMEM((rows, half), jnp.bfloat16),
@@ -140,18 +144,16 @@
     )(place, *own, *other, gate, up)
 
 
-def down_kernel(mine, far, place_ref, hidden_ref, down_ref, *refs):
+def down_kernel(mine, place_ref, hidden_ref, down_ref, *refs):
     out_refs = refs[mine:]
     local, units, features = down_ref.shape
     half = features // 2
     core = place_ref[1] if mine else 1 - place_ref[1]
-    rows = hidden_ref.shape[0] // 2
     tokens = out_refs[0].shape[0]
-    hidden = hidden_ref[far * rows : (far + 1) * rows, :]
     for at in range(0, half, WIDTH):
         cut = pl.ds(pl.multiple_of(core * half + at, WIDTH), WIDTH)
         total = jnp.dot(
-            hidden,
+            hidden_ref[...],
             down_ref[:, :, cut].reshape(local * units, WIDTH),
             preferred_element_type=jnp.float32,
         )
@@ -161,21 +163,25 @@
             out_ref[:, at : at + WIDTH] = total[i * tokens : (i + 1) * tokens].astype(out_ref.dtype)
 
 
-def run_down(place, hidden, down, far, received, kind, blocks):
-    rows, half = hidden.shape[0] // 2, down.shape[2] // 2
+def run_down(place, hidden, down, received, kinds):
+    rows, half = hidden.shape[0], down.shape[2] // 2
     vmem = pl.BlockSpec(memory_space=pltpu.VMEM)
     extra = [] if received is None else [received]
     return pl.pallas_call(
-        functools.partial(down_kernel, len(extra), far),
-        out_shape=[jax.ShapeDtypeStruct((rows // blocks, half), kind)] * blocks,
+        functools.partial(down_kernel, len(extra)),
+        out_shape=[jax.ShapeDtypeStruct((rows // len(kinds), half), kind) for kind in kinds],
         in_specs=[pl.BlockSpec(memory_space=pltpu.SMEM)] + [vmem] * (2 + len(extra)),
-        out_specs=[vmem] * blocks,
+        out_specs=[vmem] * len(kinds),
         compiler_params=pltpu.CompilerParams(vmem_limit_bytes=LIMIT),
         cost_estimate=pl.CostEstimate(
             flops=2 * rows * half * hidden.shape[1], bytes_accessed=4 * rows * half, transcendentals=0
         ),
         name="mine" if extra else "other",
     )(place, hidden, down, *extra)
+
+
+def after(value, *others):
+    return lax.optimization_barrier((value, *others))[0]
 
 
 def on_device(
@@ -203,25 +209,42 @@
     bf16, f32 = jnp.bfloat16, jnp.float32
 
     packed = prepare(place, hidden_in, expert_ids, route_scores, expert_slot)
-    shifts = sorted(range(1, outer), key=lambda k: min(k, outer - k))
-    same, opposite = {0: packed}, {}
-    for k in shifts:
-        same[k] = lax.ppermute(packed, "sect", along(k))
-    for k in [0] + shifts:
-        opposite[k] = lax.ppermute(same[k], "sect", across)
+    turned = 1
+    order = sorted(range(1, outer), key=lambda k: -min(k, outer - k))
+    same, opposite = {0: packed}, {0: lax.ppermute(packed, "sect", across)}
+    for k in order:
+        if k != turned:
+            same[k] = lax.ppermute(packed, "sect", along(k))
+    if turned < outer:
+        same[turned] = lax.ppermute(after(packed, opposite[0]), "sect", along(turned))
+        opposite[turned] = lax.ppermute(opposite[0], "sect", along(turned))
+    for k in order[::-1]:
+        if k != turned:
+            block = same[k]
+            if k == order[0]:
+                block = after(block, same[turned], opposite[turned])
+            opposite[k] = lax.ppermute(block, "sect", across)
     near = [same[k] for k in range(outer)]
     far = [opposite[k] for k in range(outer)]
     near_other = [lax.ppermute(block, "tp", cores) for block in near]
     far_other = [lax.ppermute(block, "tp", cores) for block in far]
-    hidden = run_hidden(place, near + far, near_other + far_other, gate_matrix, up_matrix, experts)
-    far_send = lax.ppermute(run_down(place, hidden, down_matrix, 1, None, bf16, 1)[0], "tp", cores)
-    near_send = lax.ppermute(run_down(place, hidden, down_matrix, 0, None, bf16, 1)[0], "tp", cores)
-    far_sum = run_down(place, hidden, down_matrix, 1, far_send, bf16, outer)
-    near_sum = run_down(place, hidden, down_matrix, 0, near_send, f32, outer)
+    near, far = run_hidden(
+        place, near + far, near_other + far_other, gate_matrix, up_matrix, experts
+    )
+    far_send = lax.ppermute(run_down(place, far, down_matrix, None, [bf16])[0], "tp", cores)
+    near_send = lax.ppermute(run_down(place, near, down_matrix, None, [bf16])[0], "tp", cores)
+    kinds = [f32] + [bf16] * (outer - 1)
+    far_sum = list(run_down(place, far, down_matrix, far_send, kinds))
+    kinds = [bf16 if k == turned else f32 for k in range(outer)]
+    near_sum = run_down(place, near, down_matrix, near_send, kinds)
     result = lax.dynamic_slice_in_dim(hidden_in, core * half, half, 1).astype(f32)
-    order = sorted(range(1, outer), key=lambda k: -min(k, outer - k)) + [0]
-    for k in order:
-        block = near_sum[k] + lax.ppermute(far_sum[k], "sect", across).astype(f32)
+    if turned < outer:
+        gone = lax.ppermute(far_sum[turned], "sect", along(-turned)).astype(f32)
+        far_sum[0] = (far_sum[0] + gone).astype(bf16)
+        result = result + lax.ppermute(near_sum[turned], "sect", along(-turned)).astype(f32)
+    for k in [k for k in order if k != turned] + [0]:
+        crossed = lax.ppermute(far_sum[k].astype(bf16), "sect", across).astype(f32)
+        block = near_sum[k] + crossed
         if k:
             block = lax.ppermute(block.astype(bf16), "sect", along(-k)).astype(f32)
         result = result + block

time: 66.2 us -> 68 us (1.027)
  starting transfers between devices: 17 us -> 21.4 us
  waiting for transfers between devices: 29 us -> 26.4 us
    ppermute x10 -> x12, waiting for transfers between devices: 12.3 us -> 6.8 us  [the longest x2 4.9 us: on_device(): opposite[k] = lax.ppermute(block, 'sect', across)]
    ppermute x10 -> x12, starting transfers between devices: 10.3 us -> 13.1 us  [the longest x1 3.03 us: on_device(): same, opposite = ({0: packed}, {0: lax.ppermute(packed, 'sect', across)})]
    ppermute x3 -> x2, waiting for transfers between devices: 4.86 us -> 7.31 us  [on_device(): block = lax.ppermute(block.astype(bf16), 'sect', along(-k)).astype(f32)]
    ppermute x3 -> x2, starting transfers between devices: 1.43 us -> 3.66 us  [on_device(): block = lax.ppermute(block.astype(bf16), 'sect', along(-k)).astype(f32)]
    ppermute x3 -> x2, starting transfers between devices: 4.61 us -> 3.6 us  [on_device(): same[k] = lax.ppermute(packed, 'sect', along(k))]
    ppermute x3 -> x2, waiting for transfers between devices: 10.5 us -> 11 us  [on_device(): same[k] = lax.ppermute(packed, 'sect', along(k))]
  transfers between devices with their start and end apart: 24 -> 24, of which waited for: 11 -> 10; matrix products, arithmetic and copies ran while one was open for 0% -> 0% of each run, Pallas kernels for 8% -> 8%
where the time goes in v5:
time: 68 us; the launch traced here: 67.8 us
  waiting for transfers between devices  26.4 us (39%)
  starting transfers between devices  21.4 us (31%)
  Pallas kernels  18.9 us (28%)
  other arithmetic  0.91 us (1%)
    ppermute x2, waiting for transfers between devices, on_device(): same[k] = lax.ppermute(packed, 'sect', along(k))  11 us
    pallas_call x1, Pallas kernels, run_hidden(): pl.pallas_call(functools.partial(hidden_kernel, half, experts, blocks), o...  9.48 us
    pallas_call x4, Pallas kernels, run_down(): pl.pallas_call(functools.partial(down_kernel, len(extra)), out_shape=[jax...  7.33 us
    ppermute x2, waiting for transfers between devices, on_device(): block = lax.ppermute(block.astype(bf16), 'sect', along(-k)).astype(f32)  7.31 us
    ppermute x2, waiting for transfers between devices, on_device(): opposite[k] = lax.ppermute(block, 'sect', across)  4.9 us
    ppermute x2, starting transfers between devices, on_device(): block = lax.ppermute(block.astype(bf16), 'sect', along(-k)).astype(f32)  3.66 us
    ppermute x2, starting transfers between devices, on_device(): same[k] = lax.ppermute(packed, 'sect', along(k))  3.6 us
    ppermute x1, starting transfers between devices, on_device(): same, opposite = ({0: packed}, {0: lax.ppermute(packed, 'sect', across)})  3.03 us
  transfers between devices with their start and end apart: 24, of which 10 were waited for; matrix products, arithmetic and copies ran while one was open for 0% of the time, Pallas kernels for 8%

profile of v5, /device:TPU:0, one launch (start us, length us, event | category | flops | bytes accessed | tf_op | source)
XLA Modules:
  0.0 67.8 jit_solution(16004328507478867863)
XLA Ops:
  0.0 0.1 pad_add_fusion.place_ref
  0.1 0.0 slice-start.2
  0.1 0.0 slice-start.3
  0.1 2.0 %prepare.1.refs_0_ = bf16[32,2176]{1,0:T(8,128)(2,1)S(1)} custom-call(s32[2]{0:T(128)S(1)} %pad_add_fusion.place_ref, s32[32]{0:T(128)} %refs_0_.1, bf16[32,4096]{1,0:T(8,128)(2,1)} %refs_1_.1, s32[8,32]{1,0:T(8,128)} %bitcast.6, f32[8,32]{1,0:T(8,128)} %bitcast.7), custom_call_target="tpu_custom_call" | custom-call | flops 40000000000 | bytes 262144 | tf_op jit(solution)/shard_map/prepare/pallas_call | solution.py:61
  2.2 3.0 %collective-permute-start = (bf16[32,2176]{1,0:T(8,128)(2,1)S(1)}, bf16[32,2176]{1,0:T(8,128)(2,1)S(1)}, u32[]{:S(2)}, u32[]{:S(2)}) collective-permute-start(bf16[32,2176]{1,0:T(8,128)(2,1)S(1)} %prepare.1.refs_0_), channel_id=1, source_target_pairs={{0,2},{2,0},{4,6},{6,4},{8,10},{10,8},{12,14},{14,12},{1,3},{3,1},... | collective-permute-start | bytes 417800 | tf_op jit(solution)/shard_map/ppermute | solution.py:214
  5.2 3.6 %collective-permute-start.3 = (bf16[32,2176]{1,0:T(8,128)(2,1)S(1)}, bf16[32,2176]{1,0:T(8,128)(2,1)S(1)}, u32[]{:S(2)}, u32[]{:S(2)}) collective-permute-start(bf16[32,2176]{1,0:T(8,128)(2,1)S(1)} %prepare.1.refs_0_), channel_id=1, source_target_pairs={{0,12},{2,14},{4,0},{6,2},{8,4},{10,6},{12,8},{14,10},{1,13},{3,15... | collective-permute-start | bytes 417800 | tf_op jit(solution)/shard_map/ppermute | solution.py:217
  8.8 0.0 collective-permute-start.2
  8.8 0.1 collective-permute-done.refs_4_
  8.9 1.8 %collective-permute-start.1 = (bf16[32,2176]{1,0:T(8,128)(2,1)S(1)}, bf16[32,2176]{1,0:T(8,128)(2,1)S(1)}, u32[]{:S(2)}, u32[]{:S(2)}) collective-permute-start(bf16[32,2176]{1,0:T(8,128)(2,1)S(1)} %prepare.1.refs_0_), channel_id=1, source_target_pairs={{0,4},{2,6},{4,8},{6,10},{8,12},{10,14},{12,0},{14,2},{1,5},{3,7},... | collective-permute-start | bytes 417800 | tf_op jit(solution)/shard_map/ppermute | solution.py:219
  10.7 1.6 %collective-permute-start.4 = (bf16[32,2176]{1,0:T(8,128)(2,1)S(1)}, bf16[32,2176]{1,0:T(8,128)(2,1)S(1)}, u32[]{:S(2)}, u32[]{:S(2)}) collective-permute-start(bf16[32,2176]{1,0:T(8,128)(2,1)S(1)} %collective-permute-done.refs_4_), channel_id=1, source_target_pairs={{0,4},{2,6},{4,8},{6,10},{8,12},{10,14},{12,0},{14,2},{1,5},{3,7},... | collective-permute-start | bytes 417800 | tf_op jit(solution)/shard_map/ppermute | solution.py:220
  12.3 0.0 collective-permute-start.7
  12.3 0.6 collective-permute-done.3.refs_3_
  12.9 0.0 collective-permute-start.10
  12.9 10.4 %collective-permute-done.2.refs_2_ = bf16[32,2176]{1,0:T(8,128)(2,1)S(1)} collective-permute-done((bf16[32,2176]{1,0:T(8,128)(2,1)S(1)}, bf16[32,2176]{1,0:T(8,128)(2,1)S(1)}, u32[]{:S(2)}, u32[]{:S(2)}) %collective-permute-start.2) | collective-permute-done | bytes 139296 | tf_op jit(solution)/shard_map/ppermute | solution.py:217
  23.3 0.5 collective-permute-start.6
  23.8 0.0 collective-permute-done.1.refs_1_
  23.8 0.0 collective-permute-start.9
  23.8 0.0 collective-permute-done.4.refs_5_
  23.8 1.6 %collective-permute-start.5 = (bf16[32,2176]{1,0:T(8,128)(2,1)S(1)}, bf16[32,2176]{1,0:T(8,128)(2,1)S(1)}, u32[]{:S(2)}, u32[]{:S(2)}) collective-permute-start(bf16[32,2176]{1,0:T(8,128)(2,1)S(1)} %collective-permute-done.2.refs_2_), channel_id=1, source_target_pairs={{0,2},{2,0},{4,6},{6,4},{8,10},{10,8},{12,14},{14,12},{1,3},{3,1},... | collective-permute-start | bytes 417800 | tf_op jit(solution)/shard_map/ppermute | solution.py:226
  25.4 0.0 collective-permute-done.7.refs_8_
  25.4 0.2 collective-permute-start.11
  25.5 0.0 collective-permute-done.10.refs_11_
  25.5 0.3 collective-permute-start.8
  25.9 3.9 %collective-permute-done.6.refs_7_ = bf16[32,2176]{1,0:T(8,128)(2,1)S(1)} collective-permute-done((bf16[32,2176]{1,0:T(8,128)(2,1)S(1)}, bf16[32,2176]{1,0:T(8,128)(2,1)S(1)}, u32[]{:S(2)}, u32[]{:S(2)}) %collective-permute-start.6) | collective-permute-done | bytes 139296 | tf_op jit(solution)/shard_map/ppermute | solution.py:226
  29.8 0.0 collective-permute-start.14
  29.8 0.0 collective-permute-done.9.refs_10_
  29.8 0.5 collective-permute-start.12
  30.3 1.0 %collective-permute-done.5.refs_6_ = bf16[32,2176]{1,0:T(8,128)(2,1)S(1)} collective-permute-done((bf16[32,2176]{1,0:T(8,128)(2,1)S(1)}, bf16[32,2176]{1,0:T(8,128)(2,1)S(1)}, u32[]{:S(2)}, u32[]{:S(2)}) %collective-permute-start.5) | collective-permute-done | bytes 139296 | tf_op jit(solution)/shard_map/ppermute | solution.py:226
  31.3 0.0 collective-permute-start.13
  31.3 0.0 collective-permute-done.11.refs_12_
  31.3 0.0 collective-permute-done.14.refs_15_
  31.3 0.0 collective-permute-done.8.refs_9_
  31.3 0.0 collective-permute-done.12.refs_13_
  31.3 1.3 %collective-permute-done.13.refs_14_ = bf16[32,2176]{1,0:T(8,128)(2,1)S(1)} collective-permute-done((bf16[32,2176]{1,0:T(8,128)(2,1)S(1)}, bf16[32,2176]{1,0:T(8,128)(2,1)S(1)}, u32[]{:S(2)}, u32[]{:S(2)}) %collective-permute-start.13) | collective-permute-done | bytes 139296 | tf_op jit(solution)/shard_map/ppermute | solution.py:230
  32.7 0.0 copy-done
  32.7 0.0 copy-done.1
  32.7 9.5 %hidden.1 = (bf16[128,2048]{1,0:T(8,128)(2,1)S(1)}, bf16[128,2048]{1,0:T(8,128)(2,1)S(1)}) custom-call(s32[2]{0:T(128)S(1)} %pad_add_fusion.place_ref, bf16[32,2176]{1,0:T(8,128)(2,1)S(1)} %prepare.1.refs_0_, bf16[32,2176]{1,0:T(8,128)(2,1)S(1)} %collective-permute-done.1.refs_1_, bf16[32,2176]{1,0:T(8,128)(2,1)S(1)} %collective-permute-done.2.refs_2_, ...), custom_call_target="tpu_custom_call" | custom-call | flops 8589934592 | bytes 2097152 | tf_op jit(solution)/shard_map/hidden/pallas_call | solution.py:129
  42.2 0.0 slice-done
  42.2 0.0 slice-done.1
  42.2 1.8 %other.3 = bf16[128,2048]{1,0:T(8,128)(2,1)S(1)} custom-call(s32[2]{0:T(128)S(1)} %pad_add_fusion.place_ref, bf16[128,2048]{1,0:T(8,128)(2,1)S(1)} %get-tuple-element.22.hidden_ref, bf16[4,512,4096]{2,1,0:T(8,128)(2,1)S(1)} %bitcast.5), custom_call_target="tpu_custom_call" | custom-call | flops 1073741824 | bytes 1048576 | tf_op jit(solution)/shard_map/other/pallas_call | solution.py:170
  44.0 0.2 collective-permute-start.17
  44.3 1.8 %other.2 = bf16[128,2048]{1,0:T(8,128)(2,1)S(1)} custom-call(s32[2]{0:T(128)S(1)} %pad_add_fusion.place_ref, bf16[128,2048]{1,0:T(8,128)(2,1)S(1)} %get-tuple-element.19.hidden_ref, bf16[4,512,4096]{2,1,0:T(8,128)(2,1)S(1)} %bitcast.5), custom_call_target="tpu_custom_call" | custom-call | flops 1073741824 | bytes 1048576 | tf_op jit(solution)/shard_map/other/pallas_call | solution.py:170
  46.1 0.0 copy-start.2
  46.1 0.4 collective-permute-start.15
  46.5 0.0 collective-permute-done.17.refs_0_
  46.5 1.8 %mine.3 = (f32[32,2048]{1,0:T(8,128)S(1)}, bf16[32,2048]{1,0:T(8,128)(2,1)S(1)}, bf16[32,2048]{1,0:T(8,128)(2,1)S(1)}, bf16[32,2048]{1,0:T(8,128)(2,1)S(1)}) custom-call(s32[2]{0:T(128)S(1)} %pad_add_fusion.place_ref, bf16[128,2048]{1,0:T(8,128)(2,1)S(1)} %get-tuple-element.22.hidden_ref, bf16[4,512,4096]{2,1,0:T(8,128)(2,1)S(1)} %bitcast.5, ...), custom_call_target="tpu_custom_call" | custom-call | flops 1073741824 | bytes 1048576 | tf_op jit(solution)/shard_map/mine/pallas_call | solution.py:170
  48.4 0.1 collective-permute-start.22
  48.5 0.6 collective-permute-start.18
  49.0 1.5 %collective-permute-start.20 = (bf16[32,2048]{1,0:T(8,128)(2,1)S(1)}, bf16[32,2048]{1,0:T(8,128)(2,1)S(1)}, u32[]{:S(2)}, u32[]{:S(2)}) collective-permute-start(bf16[32,2048]{1,0:T(8,128)(2,1)S(1)} %get-tuple-element.25), channel_id=1, source_target_pairs={{0,2},{2,0},{4,6},{6,4},{8,10},{10,8},{12,14},{14,12},{1,3},{3,1},... | collective-permute-start | bytes 393224 | tf_op jit(solution)/shard_map/ppermute | solution.py:246
  50.6 0.0 collective-permute-done.15.refs_0_
  50.6 1.8 %mine.2 = (f32[32,2048]{1,0:T(8,128)S(1)}, bf16[32,2048]{1,0:T(8,128)(2,1)S(1)}, f32[32,2048]{1,0:T(8,128)S(1)}, f32[32,2048]{1,0:T(8,128)S(1)}) custom-call(s32[2]{0:T(128)S(1)} %pad_add_fusion.place_ref, bf16[128,2048]{1,0:T(8,128)(2,1)S(1)} %get-tuple-element.19.hidden_ref, bf16[4,512,4096]{2,1,0:T(8,128)(2,1)S(1)} %bitcast.5, ...), custom_call_target="tpu_custom_call" | custom-call | flops 1073741824 | bytes 1048576 | tf_op jit(solution)/shard_map/mine/pallas_call | solution.py:170
  52.4 1.2 %collective-permute-start.16 = (bf16[32,2048]{1,0:T(8,128)(2,1)S(1)}, bf16[32,2048]{1,0:T(8,128)(2,1)S(1)}, u32[]{:S(2)}, u32[]{:S(2)}) collective-permute-start(bf16[32,2048]{1,0:T(8,128)(2,1)S(1)} %get-tuple-element.20), channel_id=1, source_target_pairs={{0,12},{2,14},{4,0},{6,2},{8,4},{10,6},{12,8},{14,10},{1,13},{3,15... | collective-permute-start | bytes 393224 | tf_op jit(solution)/shard_map/ppermute | solution.py:244
  53.6 0.4 collective-permute-done.22
  54.0 0.6 collective-permute-start.23
  54.6 0.3 collective-permute-done.18
  54.9 1.6 %collective-permute-start.19 = (bf16[32,2048]{1,0:T(8,128)(2,1)S(1)}, bf16[32,2048]{1,0:T(8,128)(2,1)S(1)}, u32[]{:S(2)}, u32[]{:S(2)}) collective-permute-start(bf16[32,2048]{1,0:T(8,128)(2,1)S(1)} %add_convert_fusion.3), channel_id=1, source_target_pairs={{0,8},{2,10},{4,12},{6,14},{8,0},{10,2},{12,4},{14,6},{1,9},{3,11}... | collective-permute-start | bytes 393224 | tf_op jit(solution)/shard_map/ppermute | solution.py:249
  56.6 1.1 %collective-permute-done.20 = bf16[32,2048]{1,0:T(8,128)(2,1)S(1)} collective-permute-done((bf16[32,2048]{1,0:T(8,128)(2,1)S(1)}, bf16[32,2048]{1,0:T(8,128)(2,1)S(1)}, u32[]{:S(2)}, u32[]{:S(2)}) %collective-permute-start.20) | collective-permute-done | bytes 131104 | tf_op jit(solution)/shard_map/ppermute | solution.py:246
  57.7 2.0 %collective-permute-start.21 = (bf16[32,2048]{1,0:T(8,128)(2,1)S(1)}, bf16[32,2048]{1,0:T(8,128)(2,1)S(1)}, u32[]{:S(2)}, u32[]{:S(2)}) collective-permute-start(bf16[32,2048]{1,0:T(8,128)(2,1)S(1)} %add_convert_fusion.2), channel_id=1, source_target_pairs={{0,4},{2,6},{4,8},{6,10},{8,12},{10,14},{12,0},{14,2},{1,5},{3,7},... | collective-permute-start | bytes 393224 | tf_op jit(solution)/shard_map/ppermute | solution.py:249
  59.7 0.0 collective-permute-done.16
  59.7 0.0 collective-permute-done.23
  59.8 7.3 %collective-permute-done.19 = bf16[32,2048]{1,0:T(8,128)(2,1)S(1)} collective-permute-done((bf16[32,2048]{1,0:T(8,128)(2,1)S(1)}, bf16[32,2048]{1,0:T(8,128)(2,1)S(1)}, u32[]{:S(2)}, u32[]{:S(2)}) %collective-permute-start.19) | collective-permute-done | bytes 131104 | tf_op jit(solution)/shard_map/ppermute | solution.py:249
  67.1 0.0 collective-permute-done.21
  67.1 0.0 copy-done.2
  67.1 0.8 %add_convert_fusion = bf16[32,2048]{1,0:T(8,128)(2,1)} fusion(f32[32,2048]{1,0:T(8,128)S(1)} %get-tuple-element.26, bf16[32,2048]{1,0:T(8,128)(2,1)S(1)} %collective-permute-done.23, bf16[32,2048]{1,0:T(8,128)(2,1)S(1)} %collective-permute-done.21, bf16[32,2048]{1,0:T(8,128)(2,1)S(1)} %collective-permute-done.19, ...), kind=kLoop, calls=%fused_computation | loop fusion | flops 720896 | bytes 1048580 | tf_op jit(solution)/shard_map/convert_element_type | solution.py:251
  (10 shorter events, 0.1 us)
Async XLA Ops:
  0.1 42.1 %slice-start = ((s8[16777216]{0:T(1024)(128)(4,1)}), s8[4194304]{0:T(1024)(128)(4,1)S(1)}, s32[]{:S(2)}) async-start(s8[16777216]{0:T(1024)(128)(4,1)} %bitcast.4), calls=%async_computation | async-start | bytes 8388608
  0.1 32.6 %copy-start = (bf16[4,4096,512]{2,1,0:T(8,128)(2,1)S(1)}, bf16[4,4096,512]{2,1,0:T(8,128)(2,1)}, u32[]{:S(2)}) copy-start(bf16[4,4096,512]{2,1,0:T(8,128)(2,1)} %refs_16_.1) | copy-start | bytes 50331652
  0.1 32.6 %copy-start.1 = (bf16[4,4096,512]{2,1,0:T(8,128)(2,1)S(1)}, bf16[4,4096,512]{2,1,0:T(8,128)(2,1)}, u32[]{:S(2)}) copy-start(bf16[4,4096,512]{2,1,0:T(8,128)(2,1)} %refs_17_.1) | copy-start | bytes 50331652
  0.1 42.1 %slice-start.1 = ((s8[16777216]{0:T(1024)(128)(4,1)}), s8[4194304]{0:T(1024)(128)(4,1)S(1)}, s32[]{:S(2)}) async-start(s8[16777216]{0:T(1024)(128)(4,1)} %bitcast.4), calls=%async_computation.1 | async-start | bytes 8388608
  0.1 42.1 %slice-start.2 = ((s8[16777216]{0:T(1024)(128)(4,1)}), s8[4194304]{0:T(1024)(128)(4,1)S(1)}, s32[]{:S(2)}) async-start(s8[16777216]{0:T(1024)(128)(4,1)} %bitcast.4), calls=%async_computation.2 | async-start | bytes 8388608
  0.1 42.1 %slice-start.3 = ((s8[16777216]{0:T(1024)(128)(4,1)}), s8[4194304]{0:T(1024)(128)(4,1)S(1)}, s32[]{:S(2)}) async-start(s8[16777216]{0:T(1024)(128)(4,1)} %bitcast.4), calls=%async_computation.3 | async-start | bytes 8388608
  2.2 6.7 %collective-permute-start = (bf16[32,2176]{1,0:T(8,128)(2,1)S(1)}, bf16[32,2176]{1,0:T(8,128)(2,1)S(1)}, u32[]{:S(2)}, u32[]{:S(2)}) collective-permute-start(bf16[32,2176]{1,0:T(8,128)(2,1)S(1)} %prepare.1.refs_0_), channel_id=1, source_target_pairs={{0,2},{2,0},{4,6},{6,4},{8,10},{10,8},{12,14},{14,12},{1,3},{3,1},... | collective-permute-start | bytes 417800 | tf_op jit(solution)/shard_map/ppermute | solution.py:214
  5.2 7.7 %collective-permute-start.3 = (bf16[32,2176]{1,0:T(8,128)(2,1)S(1)}, bf16[32,2176]{1,0:T(8,128)(2,1)S(1)}, u32[]{:S(2)}, u32[]{:S(2)}) collective-permute-start(bf16[32,2176]{1,0:T(8,128)(2,1)S(1)} %prepare.1.refs_0_), channel_id=1, source_target_pairs={{0,12},{2,14},{4,0},{6,2},{8,4},{10,6},{12,8},{14,10},{1,13},{3,15... | collective-permute-start | bytes 417800 | tf_op jit(solution)/shard_map/ppermute | solution.py:217
  8.8 14.5 %collective-permute-start.2 = (bf16[32,2176]{1,0:T(8,128)(2,1)S(1)}, bf16[32,2176]{1,0:T(8,128)(2,1)S(1)}, u32[]{:S(2)}, u32[]{:S(2)}) collective-permute-start(bf16[32,2176]{1,0:T(8,128)(2,1)S(1)} %prepare.1.refs_0_), channel_id=1, source_target_pairs={{0,8},{2,10},{4,12},{6,14},{8,0},{10,2},{12,4},{14,6},{1,9},{3,11}... | collective-permute-start | bytes 417800 | tf_op jit(solution)/shard_map/ppermute | solution.py:217
  8.9 14.9 %collective-permute-start.1 = (bf16[32,2176]{1,0:T(8,128)(2,1)S(1)}, bf16[32,2176]{1,0:T(8,128)(2,1)S(1)}, u32[]{:S(2)}, u32[]{:S(2)}) collective-permute-start(bf16[32,2176]{1,0:T(8,128)(2,1)S(1)} %prepare.1.refs_0_), channel_id=1, source_target_pairs={{0,4},{2,6},{4,8},{6,10},{8,12},{10,14},{12,0},{14,2},{1,5},{3,7},... | collective-permute-start | bytes 417800 | tf_op jit(solution)/shard_map/ppermute | solution.py:219
  10.7 13.1 %collective-permute-start.4 = (bf16[32,2176]{1,0:T(8,128)(2,1)S(1)}, bf16[32,2176]{1,0:T(8,128)(2,1)S(1)}, u32[]{:S(2)}, u32[]{:S(2)}) collective-permute-start(bf16[32,2176]{1,0:T(8,128)(2,1)S(1)} %collective-permute-done.refs_4_), channel_id=1, source_target_pairs={{0,4},{2,6},{4,8},{6,10},{8,12},{10,14},{12,0},{14,2},{1,5},{3,7},... | collective-permute-start | bytes 417800 | tf_op jit(solution)/shard_map/ppermute | solution.py:220
  12.3 13.1 %collective-permute-start.7 = (bf16[32,2176]{1,0:T(8,128)(2,1)S(1)}, bf16[32,2176]{1,0:T(8,128)(2,1)S(1)}, u32[]{:S(2)}, u32[]{:S(2)}) collective-permute-start(bf16[32,2176]{1,0:T(8,128)(2,1)S(1)} %prepare.1.refs_0_), channel_id=1, source_target_pairs={{0,1},{1,0},{2,3},{3,2},{4,5},{5,4},{6,7},{7,6},{8,9},{9,8},{10,11... | collective-permute-start | bytes 417800 | tf_op jit(solution)/shard_map/ppermute | solution.py:229
  12.9 12.6 %collective-permute-start.10 = (bf16[32,2176]{1,0:T(8,128)(2,1)S(1)}, bf16[32,2176]{1,0:T(8,128)(2,1)S(1)}, u32[]{:S(2)}, u32[]{:S(2)}) collective-permute-start(bf16[32,2176]{1,0:T(8,128)(2,1)S(1)} %collective-permute-done.3.refs_3_), channel_id=1, source_target_pairs={{0,1},{1,0},{2,3},{3,2},{4,5},{5,4},{6,7},{7,6},{8,9},{9,8},{10,11... | collective-permute-start | bytes 417800 | tf_op jit(solution)/shard_map/ppermute | solution.py:229
  23.3 6.5 %collective-permute-start.6 = (bf16[32,2176]{1,0:T(8,128)(2,1)S(1)}, bf16[32,2176]{1,0:T(8,128)(2,1)S(1)}, u32[]{:S(2)}, u32[]{:S(2)}) collective-permute-start(bf16[32,2176]{1,0:T(8,128)(2,1)S(1)} %collective-permute-done.3.refs_3_), channel_id=1, source_target_pairs={{0,2},{2,0},{4,6},{6,4},{8,10},{10,8},{12,14},{14,12},{1,3},{3,1},... | collective-permute-start | bytes 417800 | tf_op jit(solution)/shard_map/ppermute | solution.py:226
  23.8 6.0 %collective-permute-start.9 = (bf16[32,2176]{1,0:T(8,128)(2,1)S(1)}, bf16[32,2176]{1,0:T(8,128)(2,1)S(1)}, u32[]{:S(2)}, u32[]{:S(2)}) collective-permute-start(bf16[32,2176]{1,0:T(8,128)(2,1)S(1)} %collective-permute-done.2.refs_2_), channel_id=1, source_target_pairs={{0,1},{1,0},{2,3},{3,2},{4,5},{5,4},{6,7},{7,6},{8,9},{9,8},{10,11... | collective-permute-start | bytes 417800 | tf_op jit(solution)/shard_map/ppermute | solution.py:229
  23.8 7.5 %collective-permute-start.5 = (bf16[32,2176]{1,0:T(8,128)(2,1)S(1)}, bf16[32,2176]{1,0:T(8,128)(2,1)S(1)}, u32[]{:S(2)}, u32[]{:S(2)}) collective-permute-start(bf16[32,2176]{1,0:T(8,128)(2,1)S(1)} %collective-permute-done.2.refs_2_), channel_id=1, source_target_pairs={{0,2},{2,0},{4,6},{6,4},{8,10},{10,8},{12,14},{14,12},{1,3},{3,1},... | collective-permute-start | bytes 417800 | tf_op jit(solution)/shard_map/ppermute | solution.py:226
  25.4 5.9 %collective-permute-start.11 = (bf16[32,2176]{1,0:T(8,128)(2,1)S(1)}, bf16[32,2176]{1,0:T(8,128)(2,1)S(1)}, u32[]{:S(2)}, u32[]{:S(2)}) collective-permute-start(bf16[32,2176]{1,0:T(8,128)(2,1)S(1)} %collective-permute-done.refs_4_), channel_id=1, source_target_pairs={{0,1},{1,0},{2,3},{3,2},{4,5},{5,4},{6,7},{7,6},{8,9},{9,8},{10,11... | collective-permute-start | bytes 417800 | tf_op jit(solution)/shard_map/ppermute | solution.py:230
  25.5 5.8 %collective-permute-start.8 = (bf16[32,2176]{1,0:T(8,128)(2,1)S(1)}, bf16[32,2176]{1,0:T(8,128)(2,1)S(1)}, u32[]{:S(2)}, u32[]{:S(2)}) collective-permute-start(bf16[32,2176]{1,0:T(8,128)(2,1)S(1)} %collective-permute-done.1.refs_1_), channel_id=1, source_target_pairs={{0,1},{1,0},{2,3},{3,2},{4,5},{5,4},{6,7},{7,6},{8,9},{9,8},{10,11... | collective-permute-start | bytes 417800 | tf_op jit(solution)/shard_map/ppermute | solution.py:229
  29.8 1.6 %collective-permute-start.14 = (bf16[32,2176]{1,0:T(8,128)(2,1)S(1)}, bf16[32,2176]{1,0:T(8,128)(2,1)S(1)}, u32[]{:S(2)}, u32[]{:S(2)}) collective-permute-start(bf16[32,2176]{1,0:T(8,128)(2,1)S(1)} %collective-permute-done.6.refs_7_), channel_id=1, source_target_pairs={{0,1},{1,0},{2,3},{3,2},{4,5},{5,4},{6,7},{7,6},{8,9},{9,8},{10,11... | collective-permute-start | bytes 417800 | tf_op jit(solution)/shard_map/ppermute | solution.py:230
  29.8 1.6 %collective-permute-start.12 = (bf16[32,2176]{1,0:T(8,128)(2,1)S(1)}, bf16[32,2176]{1,0:T(8,128)(2,1)S(1)}, u32[]{:S(2)}, u32[]{:S(2)}) collective-permute-start(bf16[32,2176]{1,0:T(8,128)(2,1)S(1)} %collective-permute-done.4.refs_5_), channel_id=1, source_target_pairs={{0,1},{1,0},{2,3},{3,2},{4,5},{5,4},{6,7},{7,6},{8,9},{9,8},{10,11... | collective-permute-start | bytes 417800 | tf_op jit(solution)/shard_map/ppermute | solution.py:230
  31.3 1.4 %collective-permute-start.13 = (bf16[32,2176]{1,0:T(8,128)(2,1)S(1)}, bf16[32,2176]{1,0:T(8,128)(2,1)S(1)}, u32[]{:S(2)}, u32[]{:S(2)}) collective-permute-start(bf16[32,2176]{1,0:T(8,128)(2,1)S(1)} %collective-permute-done.5.refs_6_), channel_id=1, source_target_pairs={{0,1},{1,0},{2,3},{3,2},{4,5},{5,4},{6,7},{7,6},{8,9},{9,8},{10,11... | collective-permute-start | bytes 417800 | tf_op jit(solution)/shard_map/ppermute | solution.py:230
  44.0 2.5 %collective-permute-start.17 = (bf16[128,2048]{1,0:T(8,128)(2,1)S(1)}, bf16[128,2048]{1,0:T(8,128)(2,1)S(1)}, u32[]{:S(2)}, u32[]{:S(2)}) collective-permute-start(bf16[128,2048]{1,0:T(8,128)(2,1)S(1)} %other.3), channel_id=1, source_target_pairs={{0,1},{1,0},{2,3},{3,2},{4,5},{5,4},{6,7},{7,6},{8,9},{9,8},{10,11... | collective-permute-start | bytes 1572872 | tf_op jit(solution)/shard_map/ppermute | solution.py:234
  46.1 21.0 %copy-start.2 = (bf16[32,4096]{1,0:T(8,128)(2,1)S(1)}, bf16[32,4096]{1,0:T(8,128)(2,1)}, u32[]{:S(2)}) copy-start(bf16[32,4096]{1,0:T(8,128)(2,1)} %refs_1_.1) | copy-start | bytes 786436
  46.1 4.5 %collective-permute-start.15 = (bf16[128,2048]{1,0:T(8,128)(2,1)S(1)}, bf16[128,2048]{1,0:T(8,128)(2,1)S(1)}, u32[]{:S(2)}, u32[]{:S(2)}) collective-permute-start(bf16[128,2048]{1,0:T(8,128)(2,1)S(1)} %other.2), channel_id=1, source_target_pairs={{0,1},{1,0},{2,3},{3,2},{4,5},{5,4},{6,7},{7,6},{8,9},{9,8},{10,11... | collective-permute-start | bytes 1572872 | tf_op jit(solution)/shard_map/ppermute | solution.py:235
  48.4 5.6 %collective-permute-start.22 = (bf16[32,2048]{1,0:T(8,128)(2,1)S(1)}, bf16[32,2048]{1,0:T(8,128)(2,1)S(1)}, u32[]{:S(2)}, u32[]{:S(2)}) collective-permute-start(bf16[32,2048]{1,0:T(8,128)(2,1)S(1)} %get-tuple-element.28), channel_id=1, source_target_pairs={{0,12},{2,14},{4,0},{6,2},{8,4},{10,6},{12,8},{14,10},{1,13},{3,15... | collective-permute-start | bytes 393224 | tf_op jit(solution)/shard_map/ppermute | solution.py:242
  48.5 6.4 %collective-permute-start.18 = (bf16[32,2048]{1,0:T(8,128)(2,1)S(1)}, bf16[32,2048]{1,0:T(8,128)(2,1)S(1)}, u32[]{:S(2)}, u32[]{:S(2)}) collective-permute-start(bf16[32,2048]{1,0:T(8,128)(2,1)S(1)} %get-tuple-element.23), channel_id=1, source_target_pairs={{0,2},{2,0},{4,6},{6,4},{8,10},{10,8},{12,14},{14,12},{1,3},{3,1},... | collective-permute-start | bytes 393224 | tf_op jit(solution)/shard_map/ppermute | solution.py:246
  49.0 8.7 %collective-permute-start.20 = (bf16[32,2048]{1,0:T(8,128)(2,1)S(1)}, bf16[32,2048]{1,0:T(8,128)(2,1)S(1)}, u32[]{:S(2)}, u32[]{:S(2)}) collective-permute-start(bf16[32,2048]{1,0:T(8,128)(2,1)S(1)} %get-tuple-element.25), channel_id=1, source_target_pairs={{0,2},{2,0},{4,6},{6,4},{8,10},{10,8},{12,14},{14,12},{1,3},{3,1},... | collective-permute-start | bytes 393224 | tf_op jit(solution)/shard_map/ppermute | solution.py:246
  52.4 7.3 %collective-permute-start.16 = (bf16[32,2048]{1,0:T(8,128)(2,1)S(1)}, bf16[32,2048]{1,0:T(8,128)(2,1)S(1)}, u32[]{:S(2)}, u32[]{:S(2)}) collective-permute-start(bf16[32,2048]{1,0:T(8,128)(2,1)S(1)} %get-tuple-element.20), channel_id=1, source_target_pairs={{0,12},{2,14},{4,0},{6,2},{8,4},{10,6},{12,8},{14,10},{1,13},{3,15... | collective-permute-start | bytes 393224 | tf_op jit(solution)/shard_map/ppermute | solution.py:244
  54.0 5.7 %collective-permute-start.23 = (bf16[32,2048]{1,0:T(8,128)(2,1)S(1)}, bf16[32,2048]{1,0:T(8,128)(2,1)S(1)}, u32[]{:S(2)}, u32[]{:S(2)}) collective-permute-start(bf16[32,2048]{1,0:T(8,128)(2,1)S(1)} %add_convert_fusion.1), channel_id=1, source_target_pairs={{0,2},{2,0},{4,6},{6,4},{8,10},{10,8},{12,14},{14,12},{1,3},{3,1},... | collective-permute-start | bytes 393224 | tf_op jit(solution)/shard_map/ppermute | solution.py:246
  54.9 12.1 %collective-permute-start.19 = (bf16[32,2048]{1,0:T(8,128)(2,1)S(1)}, bf16[32,2048]{1,0:T(8,128)(2,1)S(1)}, u32[]{:S(2)}, u32[]{:S(2)}) collective-permute-start(bf16[32,2048]{1,0:T(8,128)(2,1)S(1)} %add_convert_fusion.3), channel_id=1, source_target_pairs={{0,8},{2,10},{4,12},{6,14},{8,0},{10,2},{12,4},{14,6},{1,9},{3,11}... | collective-permute-start | bytes 393224 | tf_op jit(solution)/shard_map/ppermute | solution.py:249
  57.7 9.3 %collective-permute-start.21 = (bf16[32,2048]{1,0:T(8,128)(2,1)S(1)}, bf16[32,2048]{1,0:T(8,128)(2,1)S(1)}, u32[]{:S(2)}, u32[]{:S(2)}) collective-permute-start(bf16[32,2048]{1,0:T(8,128)(2,1)S(1)} %add_convert_fusion.2), channel_id=1, source_target_pairs={{0,4},{2,6},{4,8},{6,10},{8,12},{10,14},{12,0},{14,2},{1,5},{3,7},... | collective-permute-start | bytes 393224 | tf_op jit(solution)/shard_map/ppermute | solution.py:249

commit v6 on v5

--- a/solution.py
+++ b/solution.py
@@ -109,9 +109,11 @@
             hidden = gate_act / (1.0 + jnp.exp(-gate_act)) * up_act
             hidden = jnp.where(weight > 0.0, hidden * weight, 0.0)
             columns = slice(e * units + at, e * units + at + block)
-            for i, out_ref in enumerate(out_refs):
-                rows = out_ref.shape[0]
-                out_ref[:, columns] = hidden[i * rows : (i + 1) * rows].astype(jnp.bfloat16)
+            row = 0
+            for out_ref in out_refs:
+                rows = slice(row, row + out_ref.shape[0])
+                out_ref[:, columns] = hidden[rows].astype(jnp.bfloat16)
+                row += out_ref.shape[0]
 
 
 def hidden_kernel(half, experts, blocks, place_ref, *refs):
@@ -121,14 +123,17 @@
     hidden_units(half, experts, place_ref, gate_ref, up_ref, own, other, coded, out_refs)
 
 
-def run_hidden(place, own, other, gate, up, experts):
+def run_hidden(place, own, other, gate, up, experts, first):
     blocks = len(own)
     local, features, width = gate.shape
     rows, half, units = blocks * own[0].shape[0], features // 2, local * width
     vmem = pl.BlockSpec(memory_space=pltpu.VMEM)
     return pl.pallas_call(
         functools.partial(hidden_kernel, half, experts, blocks),
-        out_shape=[jax.ShapeDtypeStruct((rows // 2, units), jnp.bfloat16)] * 2,
+        out_shape=[
+            jax.ShapeDtypeStruct((count * own[0].shape[0], units), jnp.bfloat16)
+            for count in (first, blocks - first)
+        ],
         in_specs=[pl.BlockSpec(memory_space=pltpu.SMEM)] + [vmem] * (2 * blocks + 2),
         out_specs=[vmem] * 2,
         scratch_shapes=[
@@ -174,7 +179,7 @@
         out_specs=[vmem] * len(kinds),
         compiler_params=pltpu.CompilerParams(vmem_limit_bytes=LIMIT),
         cost_estimate=pl.CostEstimate(
-            flops=2 * rows * half * hidden.shape[1], bytes_accessed=4 * rows * half, transcendentals=0
+            flops=2 * rows * half, bytes_accessed=4 * rows, transcendentals=0
         ),
         name="mine" if extra else "other",
     )(place, hidden, down, *extra)
@@ -212,31 +217,28 @@
     turned = 1
     order = sorted(range(1, outer), key=lambda k: -min(k, outer - k))
     same, opposite = {0: packed}, {0: lax.ppermute(packed, "sect", across)}
-    for k in order:
-        if k != turned:
-            same[k] = lax.ppermute(packed, "sect", along(k))
-    if turned < outer:
-        same[turned] = lax.ppermute(after(packed, opposite[0]), "sect", along(turned))
-        opposite[turned] = lax.ppermute(opposite[0], "sect", along(turned))
     for k in order[::-1]:
-        if k != turned:
-            block = same[k]
-            if k == order[0]:
-                block = after(block, same[turned], opposite[turned])
-            opposite[k] = lax.ppermute(block, "sect", across)
-    near = [same[k] for k in range(outer)]
-    far = [opposite[k] for k in range(outer)]
-    near_other = [lax.ppermute(block, "tp", cores) for block in near]
-    far_other = [lax.ppermute(block, "tp", cores) for block in far]
-    near, far = run_hidden(
-        place, near + far, near_other + far_other, gate_matrix, up_matrix, experts
-    )
-    far_send = lax.ppermute(run_down(place, far, down_matrix, None, [bf16])[0], "tp", cores)
-    near_send = lax.ppermute(run_down(place, near, down_matrix, None, [bf16])[0], "tp", cores)
-    kinds = [f32] + [bf16] * (outer - 1)
-    far_sum = list(run_down(place, far, down_matrix, far_send, kinds))
-    kinds = [bf16 if k == turned else f32 for k in range(outer)]
-    near_sum = run_down(place, near, down_matrix, near_send, kinds)
+        block = after(packed, opposite[0]) if k == order[0] and outer > 2 else packed
+        same[k] = lax.ppermute(block, "sect", along(k))
+    for k in order[::-1]:
+        opposite[k] = lax.ppermute(same[k], "sect", across)
+    early = [(opposite, k) for k in range(outer)] + [(same, k) for k in range(outer) if k == turned]
+    late = [(same, k) for k in range(outer) if k != turned]
+    blocks = [side[k] for side, k in early + late]
+    others = [lax.ppermute(block, "tp", cores) for block in blocks]
+    groups = run_hidden(place, blocks, others, gate_matrix, up_matrix, experts, len(early))
+    sent = [
+        lax.ppermute(run_down(place, hidden, down_matrix, None, [bf16])[0], "tp", cores)
+        for hidden in groups
+    ]
+    far_sum, near_sum = {}, {}
+    for group, hidden, received in zip((early, late), groups, sent):
+        kinds = [
+            bf16 if k == turned or (side is opposite and k) else f32 for side, k in group
+        ]
+        sums = run_down(place, hidden, down_matrix, received, kinds)
+        for (side, k), total in zip(group, sums):
+            (far_sum if side is opposite else near_sum)[k] = total
     result = lax.dynamic_slice_in_dim(hidden_in, core * half, half, 1).astype(f32)
     if turned < outer:
         gone = lax.ppermute(far_sum[turned], "sect", along(-turned)).astype(f32)

time: 68 us -> 65.7 us (0.966); the launches traced: 67.8 us -> 64.6 us
  starting transfers between devices: 21.4 us -> 19.1 us
  waiting for transfers between devices: 26.4 us -> 24.6 us
  Pallas kernels: 18.9 us -> 19.8 us
    ppermute x16, waiting for transfers between devices: 17.2 us -> 14.5 us  [the longest x3 9.06 us: on_device(): same[k] = lax.ppermute(block, 'sect', along(k))]
    ppermute x2, starting transfers between devices: 3.66 us -> 1.04 us  [on_device(): block = lax.ppermute(block.astype(bf16), 'sect', along(-k)).astype(f32)]
    ppermute x2, waiting for transfers between devices: 7.31 us -> 5.52 us  [on_device(): block = lax.ppermute(block.astype(bf16), 'sect', along(-k)).astype(f32)]
    ppermute x1, waiting for transfers between devices: 0.39 us -> 2.16 us  [on_device(): gone = lax.ppermute(far_sum[turned], 'sect', along(-turned)).astype(f32)]
    ppermute x16, starting transfers between devices: 10.8 us -> 9.21 us  [the longest x3 6.41 us: on_device(): same[k] = lax.ppermute(block, 'sect', along(k))]
    ppermute x1, starting transfers between devices: 1.19 us -> 2.71 us  [on_device(): lax.ppermute(near_sum[turned], 'sect', along(-turned)).astype(f32)]
    ppermute x3, waiting for transfers between devices: 1.43 us -> 2.38 us  [on_device(): crossed = lax.ppermute(far_sum[k].astype(bf16), 'sect', across).astype(f32)]
    pallas_call x4, Pallas kernels: 7.33 us -> 8.26 us  [run_down(): pl.pallas_call(functools.partial(down_kernel, len(extra)), out_shape=[jax...]
  transfers between devices with their start and end apart: 24 -> 24, of which waited for: 10 -> 10; matrix products, arithmetic and copies ran while one was open for 0% -> 0% of each run, Pallas kernels for 8% -> 10%
where the time goes in v6:
time: 65.7 us; the launch traced here: 64.6 us
  waiting for transfers between devices  24.6 us (37%)
  Pallas kernels  19.8 us (30%)
  starting transfers between devices  19.1 us (29%)
  other arithmetic  0.91 us (1%)
    pallas_call x1, Pallas kernels, run_hidden(): pl.pallas_call(functools.partial(hidden_kernel, half, experts, blocks), o...  9.49 us
    ppermute x3, waiting for transfers between devices, on_device(): same[k] = lax.ppermute(block, 'sect', along(k))  9.06 us
    pallas_call x4, Pallas kernels, run_down(): pl.pallas_call(functools.partial(down_kernel, len(extra)), out_shape=[jax...  8.26 us
    ppermute x3, starting transfers between devices, on_device(): same[k] = lax.ppermute(block, 'sect', along(k))  6.41 us
    ppermute x2, waiting for transfers between devices, on_device(): block = lax.ppermute(block.astype(bf16), 'sect', along(-k)).astype(f32)  5.52 us
    ppermute x3, waiting for transfers between devices, on_device(): opposite[k] = lax.ppermute(same[k], 'sect', across)  4.09 us
    ppermute x3, starting transfers between devices, on_device(): crossed = lax.ppermute(far_sum[k].astype(bf16), 'sect', across).astype(f32)  3.04 us
    ppermute x1, starting transfers between devices, on_device(): same, opposite = ({0: packed}, {0: lax.ppermute(packed, 'sect', across)})  3.03 us
  transfers between devices with their start and end apart: 24, of which 10 were waited for; matrix products, arithmetic and copies ran while one was open for 0% of the time, Pallas kernels for 10%

profile of v6, /device:TPU:0, one launch (start us, length us, event | category | flops | bytes accessed | tf_op | source)
XLA Modules:
  0.0 64.6 jit_solution(14475280642980252873)
XLA Ops:
  0.0 0.1 pad_add_fusion.place_ref
  0.1 0.0 slice-start.2
  0.1 0.0 slice-start.3
  0.1 2.0 %prepare.1.refs_5_ = bf16[32,2176]{1,0:T(8,128)(2,1)S(1)} custom-call(s32[2]{0:T(128)S(1)} %pad_add_fusion.place_ref, s32[32]{0:T(128)} %refs_0_.1, bf16[32,4096]{1,0:T(8,128)(2,1)} %refs_1_.1, s32[8,32]{1,0:T(8,128)} %bitcast.6, f32[8,32]{1,0:T(8,128)} %bitcast.7), custom_call_target="tpu_custom_call" | custom-call | flops 40000000000 | bytes 262144 | tf_op jit(solution)/shard_map/prepare/pallas_call | solution.py:61
  2.2 3.0 %collective-permute-start = (bf16[32,2176]{1,0:T(8,128)(2,1)S(1)}, bf16[32,2176]{1,0:T(8,128)(2,1)S(1)}, u32[]{:S(2)}, u32[]{:S(2)}) collective-permute-start(bf16[32,2176]{1,0:T(8,128)(2,1)S(1)} %prepare.1.refs_5_), channel_id=1, source_target_pairs={{0,2},{2,0},{4,6},{6,4},{8,10},{10,8},{12,14},{14,12},{1,3},{3,1},... | collective-permute-start | bytes 417800 | tf_op jit(solution)/shard_map/ppermute | solution.py:219
  5.2 3.6 %collective-permute-start.5 = (bf16[32,2176]{1,0:T(8,128)(2,1)S(1)}, bf16[32,2176]{1,0:T(8,128)(2,1)S(1)}, u32[]{:S(2)}, u32[]{:S(2)}) collective-permute-start(bf16[32,2176]{1,0:T(8,128)(2,1)S(1)} %prepare.1.refs_5_), channel_id=1, source_target_pairs={{0,12},{2,14},{4,0},{6,2},{8,4},{10,6},{12,8},{14,10},{1,13},{3,15... | collective-permute-start | bytes 417800 | tf_op jit(solution)/shard_map/ppermute | solution.py:222
  8.8 0.0 collective-permute-start.12
  8.8 0.0 collective-permute-start.1
  8.8 0.1 collective-permute-done.refs_0_
  8.9 2.8 %collective-permute-start.3 = (bf16[32,2176]{1,0:T(8,128)(2,1)S(1)}, bf16[32,2176]{1,0:T(8,128)(2,1)S(1)}, u32[]{:S(2)}, u32[]{:S(2)}) collective-permute-start(bf16[32,2176]{1,0:T(8,128)(2,1)S(1)} %prepare.1.refs_5_), channel_id=1, source_target_pairs={{0,8},{2,10},{4,12},{6,14},{8,0},{10,2},{12,4},{14,6},{1,9},{3,11}... | collective-permute-start | bytes 417800 | tf_op jit(solution)/shard_map/ppermute | solution.py:222
  11.7 1.2 %collective-permute-done.5.refs_7_ = bf16[32,2176]{1,0:T(8,128)(2,1)S(1)} collective-permute-done((bf16[32,2176]{1,0:T(8,128)(2,1)S(1)}, bf16[32,2176]{1,0:T(8,128)(2,1)S(1)}, u32[]{:S(2)}, u32[]{:S(2)}) %collective-permute-start.5) | collective-permute-done | bytes 139296 | tf_op jit(solution)/shard_map/ppermute | solution.py:222
  12.9 0.0 collective-permute-start.14
  12.9 0.5 collective-permute-start.6
  13.4 3.7 %collective-permute-done.1.refs_4_ = bf16[32,2176]{1,0:T(8,128)(2,1)S(1)} collective-permute-done((bf16[32,2176]{1,0:T(8,128)(2,1)S(1)}, bf16[32,2176]{1,0:T(8,128)(2,1)S(1)}, u32[]{:S(2)}, u32[]{:S(2)}) %collective-permute-start.1) | collective-permute-done | bytes 139296 | tf_op jit(solution)/shard_map/ppermute | solution.py:222
  17.2 0.0 collective-permute-start.11
  17.2 0.0 collective-permute-done.12.refs_13_
  17.2 0.5 collective-permute-start.2
  17.7 4.1 %collective-permute-done.3.refs_6_ = bf16[32,2176]{1,0:T(8,128)(2,1)S(1)} collective-permute-done((bf16[32,2176]{1,0:T(8,128)(2,1)S(1)}, bf16[32,2176]{1,0:T(8,128)(2,1)S(1)}, u32[]{:S(2)}, u32[]{:S(2)}) %collective-permute-start.3) | collective-permute-done | bytes 139296 | tf_op jit(solution)/shard_map/ppermute | solution.py:222
  21.8 0.5 collective-permute-start.4
  22.3 0.0 collective-permute-done.14.refs_15_
  22.3 0.0 collective-permute-start.7
  22.3 0.0 collective-permute-done.6.refs_3_
  22.3 0.5 collective-permute-start.13
  22.8 0.0 collective-permute-done.11.refs_12_
  22.8 0.1 collective-permute-start.10
  22.9 0.4 collective-permute-done.2.refs_1_
  23.3 0.0 collective-permute-start.8
  23.3 3.7 %collective-permute-done.4.refs_2_ = bf16[32,2176]{1,0:T(8,128)(2,1)S(1)} collective-permute-done((bf16[32,2176]{1,0:T(8,128)(2,1)S(1)}, bf16[32,2176]{1,0:T(8,128)(2,1)S(1)}, u32[]{:S(2)}, u32[]{:S(2)}) %collective-permute-start.4) | collective-permute-done | bytes 139296 | tf_op jit(solution)/shard_map/ppermute | solution.py:224
  27.0 0.0 collective-permute-start.9
  27.0 0.0 collective-permute-done.7.refs_8_
  27.0 0.0 collective-permute-done.10.refs_11_
  27.0 0.0 collective-permute-done.8.refs_9_
  27.0 0.0 collective-permute-done.13.refs_14_
  27.0 1.3 %collective-permute-done.9.refs_10_ = bf16[32,2176]{1,0:T(8,128)(2,1)S(1)} collective-permute-done((bf16[32,2176]{1,0:T(8,128)(2,1)S(1)}, bf16[32,2176]{1,0:T(8,128)(2,1)S(1)}, u32[]{:S(2)}, u32[]{:S(2)}) %collective-permute-start.9) | collective-permute-done | bytes 139296 | tf_op jit(solution)/shard_map/ppermute | solution.py:228
  28.3 0.0 copy-done
  28.3 0.0 copy-done.1
  28.3 9.5 %hidden.1 = (bf16[160,2048]{1,0:T(8,128)(2,1)S(1)}, bf16[96,2048]{1,0:T(8,128)(2,1)S(1)}) custom-call(s32[2]{0:T(128)S(1)} %pad_add_fusion.place_ref, bf16[32,2176]{1,0:T(8,128)(2,1)S(1)} %collective-permute-done.refs_0_, bf16[32,2176]{1,0:T(8,128)(2,1)S(1)} %collective-permute-done.2.refs_1_, bf16[32,2176]{1,0:T(8,128)(2,1)S(1)} %collective-permute-done.4.refs_2_, ...), custom_call_target="tpu_custom_call" | custom-call | flops 8589934592 | bytes 2097152 | tf_op jit(solution)/shard_map/hidden/pallas_call | solution.py:131
  37.8 0.0 slice-done
  37.9 0.0 slice-done.1
  37.9 0.0 slice-done.2
  37.9 2.1 %other.2 = bf16[160,2048]{1,0:T(8,128)(2,1)S(1)} custom-call(s32[2]{0:T(128)S(1)} %pad_add_fusion.place_ref, bf16[160,2048]{1,0:T(8,128)(2,1)S(1)} %get-tuple-element.17.hidden_ref, bf16[4,512,4096]{2,1,0:T(8,128)(2,1)S(1)} %bitcast.5), custom_call_target="tpu_custom_call" | custom-call | flops 655360 | bytes 640 | tf_op jit(solution)/shard_map/other/pallas_call | solution.py:175
  40.0 0.2 collective-permute-start.15
  40.2 2.0 %other.3 = bf16[96,2048]{1,0:T(8,128)(2,1)S(1)} custom-call(s32[2]{0:T(128)S(1)} %pad_add_fusion.place_ref, bf16[96,2048]{1,0:T(8,128)(2,1)S(1)} %get-tuple-element.19.hidden_ref, bf16[4,512,4096]{2,1,0:T(8,128)(2,1)S(1)} %bitcast.5), custom_call_target="tpu_custom_call" | custom-call | flops 393216 | bytes 384 | tf_op jit(solution)/shard_map/other/pallas_call | solution.py:175
  42.2 0.0 copy-start.2
  42.3 0.4 collective-permute-start.17
  42.7 0.0 collective-permute-done.15.refs_0_
  42.7 2.1 %mine.2 = (f32[32,2048]{1,0:T(8,128)S(1)}, bf16[32,2048]{1,0:T(8,128)(2,1)S(1)}, bf16[32,2048]{1,0:T(8,128)(2,1)S(1)}, bf16[32,2048]{1,0:T(8,128)(2,1)S(1)}, bf16[32,2048]{1,0:T(8,128)(2,1)S(1)}) custom-call(s32[2]{0:T(128)S(1)} %pad_add_fusion.place_ref, bf16[160,2048]{1,0:T(8,128)(2,1)S(1)} %get-tuple-element.17.hidden_ref, ...), custom_call_target="tpu_custom_call" | custom-call | flops 655360 | bytes 640 | tf_op jit(solution)/shard_map/mine/pallas_call | solution.py:175
  44.8 0.4 collective-permute-start.18
  45.2 0.0 collective-permute-done.17.refs_0_
  45.2 2.0 %mine.3 = (f32[32,2048]{1,0:T(8,128)S(1)}, f32[32,2048]{1,0:T(8,128)S(1)}, f32[32,2048]{1,0:T(8,128)S(1)}) custom-call(s32[2]{0:T(128)S(1)} %pad_add_fusion.place_ref, bf16[96,2048]{1,0:T(8,128)(2,1)S(1)} %get-tuple-element.19.hidden_ref, bf16[4,512,4096]{2,1,0:T(8,128)(2,1)S(1)} %bitcast.5, bf16[96,2048]{1,0:T(8,128)(2,1)S(1)} %collective-permute-done.17.refs_0_), custom_call_target="tpu_custom_call" | custom-call | flops 393216 | bytes 384 | tf_op jit(solution)/shard_map/mine/pallas_call | solution.py:175
  47.2 2.7 %collective-permute-start.16 = (bf16[32,2048]{1,0:T(8,128)(2,1)S(1)}, bf16[32,2048]{1,0:T(8,128)(2,1)S(1)}, u32[]{:S(2)}, u32[]{:S(2)}) collective-permute-start(bf16[32,2048]{1,0:T(8,128)(2,1)S(1)} %get-tuple-element.18), channel_id=1, source_target_pairs={{0,12},{2,14},{4,0},{6,2},{8,4},{10,6},{12,8},{14,10},{1,13},{3,15... | collective-permute-start | bytes 393224 | tf_op jit(solution)/shard_map/ppermute | solution.py:246
  50.0 1.5 %collective-permute-start.20 = (bf16[32,2048]{1,0:T(8,128)(2,1)S(1)}, bf16[32,2048]{1,0:T(8,128)(2,1)S(1)}, u32[]{:S(2)}, u32[]{:S(2)}) collective-permute-start(bf16[32,2048]{1,0:T(8,128)(2,1)S(1)} %get-tuple-element.23), channel_id=1, source_target_pairs={{0,2},{2,0},{4,6},{6,4},{8,10},{10,8},{12,14},{14,12},{1,3},{3,1},... | collective-permute-start | bytes 393224 | tf_op jit(solution)/shard_map/ppermute | solution.py:248
  51.5 0.1 collective-permute-start.22
  51.5 0.0 collective-permute-done.18
  51.6 1.0 %collective-permute-start.19 = (bf16[32,2048]{1,0:T(8,128)(2,1)S(1)}, bf16[32,2048]{1,0:T(8,128)(2,1)S(1)}, u32[]{:S(2)}, u32[]{:S(2)}) collective-permute-start(bf16[32,2048]{1,0:T(8,128)(2,1)S(1)} %add_convert_fusion.3), channel_id=1, source_target_pairs={{0,8},{2,10},{4,12},{6,14},{8,0},{10,2},{12,4},{14,6},{1,9},{3,11}... | collective-permute-start | bytes 393224 | tf_op jit(solution)/shard_map/ppermute | solution.py:251
  52.6 2.4 %collective-permute-done.20 = bf16[32,2048]{1,0:T(8,128)(2,1)S(1)} collective-permute-done((bf16[32,2048]{1,0:T(8,128)(2,1)S(1)}, bf16[32,2048]{1,0:T(8,128)(2,1)S(1)}, u32[]{:S(2)}, u32[]{:S(2)}) %collective-permute-start.20) | collective-permute-done | bytes 131104 | tf_op jit(solution)/shard_map/ppermute | solution.py:248
  55.0 0.1 collective-permute-start.21
  55.0 2.2 %collective-permute-done.22 = bf16[32,2048]{1,0:T(8,128)(2,1)S(1)} collective-permute-done((bf16[32,2048]{1,0:T(8,128)(2,1)S(1)}, bf16[32,2048]{1,0:T(8,128)(2,1)S(1)}, u32[]{:S(2)}, u32[]{:S(2)}) %collective-permute-start.22) | collective-permute-done | bytes 131104 | tf_op jit(solution)/shard_map/ppermute | solution.py:244
  57.2 1.1 %collective-permute-start.23 = (bf16[32,2048]{1,0:T(8,128)(2,1)S(1)}, bf16[32,2048]{1,0:T(8,128)(2,1)S(1)}, u32[]{:S(2)}, u32[]{:S(2)}) collective-permute-start(bf16[32,2048]{1,0:T(8,128)(2,1)S(1)} %add_convert_fusion.1), channel_id=1, source_target_pairs={{0,2},{2,0},{4,6},{6,4},{8,10},{10,8},{12,14},{14,12},{1,3},{3,1},... | collective-permute-start | bytes 393224 | tf_op jit(solution)/shard_map/ppermute | solution.py:248
  58.4 0.0 collective-permute-done.16
  58.4 5.5 %collective-permute-done.19 = bf16[32,2048]{1,0:T(8,128)(2,1)S(1)} collective-permute-done((bf16[32,2048]{1,0:T(8,128)(2,1)S(1)}, bf16[32,2048]{1,0:T(8,128)(2,1)S(1)}, u32[]{:S(2)}, u32[]{:S(2)}) %collective-permute-start.19) | collective-permute-done | bytes 131104 | tf_op jit(solution)/shard_map/ppermute | solution.py:251
  63.9 0.0 collective-permute-done.21
  63.9 0.0 collective-permute-done.23
  63.9 0.8 %add_convert_fusion = bf16[32,2048]{1,0:T(8,128)(2,1)} fusion(f32[32,2048]{1,0:T(8,128)S(1)} %get-tuple-element.24, bf16[32,2048]{1,0:T(8,128)(2,1)S(1)} %collective-permute-done.23, bf16[32,2048]{1,0:T(8,128)(2,1)S(1)} %collective-permute-done.21, bf16[32,2048]{1,0:T(8,128)(2,1)S(1)} %collective-permute-done.19, ...), kind=kLoop, calls=%fused_computation | loop fusion | flops 720896 | bytes 1048580 | tf_op jit(solution)/shard_map/convert_element_type | solution.py:253
  (10 shorter events, 0.1 us)
Async XLA Ops:
  0.1 37.8 %slice-start = ((s8[16777216]{0:T(1024)(128)(4,1)}), s8[4194304]{0:T(1024)(128)(4,1)S(1)}, s32[]{:S(2)}) async-start(s8[16777216]{0:T(1024)(128)(4,1)} %bitcast.4), calls=%async_computation | async-start | bytes 8388608
  0.1 28.3 %copy-start = (bf16[4,4096,512]{2,1,0:T(8,128)(2,1)S(1)}, bf16[4,4096,512]{2,1,0:T(8,128)(2,1)}, u32[]{:S(2)}) copy-start(bf16[4,4096,512]{2,1,0:T(8,128)(2,1)} %refs_16_.1) | copy-start | bytes 50331652
  0.1 28.3 %copy-start.1 = (bf16[4,4096,512]{2,1,0:T(8,128)(2,1)S(1)}, bf16[4,4096,512]{2,1,0:T(8,128)(2,1)}, u32[]{:S(2)}) copy-start(bf16[4,4096,512]{2,1,0:T(8,128)(2,1)} %refs_17_.1) | copy-start | bytes 50331652
  0.1 37.8 %slice-start.1 = ((s8[16777216]{0:T(1024)(128)(4,1)}), s8[4194304]{0:T(1024)(128)(4,1)S(1)}, s32[]{:S(2)}) async-start(s8[16777216]{0:T(1024)(128)(4,1)} %bitcast.4), calls=%async_computation.1 | async-start | bytes 8388608
  0.1 37.8 %slice-start.2 = ((s8[16777216]{0:T(1024)(128)(4,1)}), s8[4194304]{0:T(1024)(128)(4,1)S(1)}, s32[]{:S(2)}) async-start(s8[16777216]{0:T(1024)(128)(4,1)} %bitcast.4), calls=%async_computation.2 | async-start | bytes 8388608
  0.1 37.8 %slice-start.3 = ((s8[16777216]{0:T(1024)(128)(4,1)}), s8[4194304]{0:T(1024)(128)(4,1)S(1)}, s32[]{:S(2)}) async-start(s8[16777216]{0:T(1024)(128)(4,1)} %bitcast.4), calls=%async_computation.3 | async-start | bytes 8388608
  2.2 6.7 %collective-permute-start = (bf16[32,2176]{1,0:T(8,128)(2,1)S(1)}, bf16[32,2176]{1,0:T(8,128)(2,1)S(1)}, u32[]{:S(2)}, u32[]{:S(2)}) collective-permute-start(bf16[32,2176]{1,0:T(8,128)(2,1)S(1)} %prepare.1.refs_5_), channel_id=1, source_target_pairs={{0,2},{2,0},{4,6},{6,4},{8,10},{10,8},{12,14},{14,12},{1,3},{3,1},... | collective-permute-start | bytes 417800 | tf_op jit(solution)/shard_map/ppermute | solution.py:219
  5.2 7.7 %collective-permute-start.5 = (bf16[32,2176]{1,0:T(8,128)(2,1)S(1)}, bf16[32,2176]{1,0:T(8,128)(2,1)S(1)}, u32[]{:S(2)}, u32[]{:S(2)}) collective-permute-start(bf16[32,2176]{1,0:T(8,128)(2,1)S(1)} %prepare.1.refs_5_), channel_id=1, source_target_pairs={{0,12},{2,14},{4,0},{6,2},{8,4},{10,6},{12,8},{14,10},{1,13},{3,15... | collective-permute-start | bytes 417800 | tf_op jit(solution)/shard_map/ppermute | solution.py:222
  8.8 8.4 %collective-permute-start.12 = (bf16[32,2176]{1,0:T(8,128)(2,1)S(1)}, bf16[32,2176]{1,0:T(8,128)(2,1)S(1)}, u32[]{:S(2)}, u32[]{:S(2)}) collective-permute-start(bf16[32,2176]{1,0:T(8,128)(2,1)S(1)} %prepare.1.refs_5_), channel_id=1, source_target_pairs={{0,1},{1,0},{2,3},{3,2},{4,5},{5,4},{6,7},{7,6},{8,9},{9,8},{10,11... | collective-permute-start | bytes 417800 | tf_op jit(solution)/shard_map/ppermute | solution.py:228
  8.8 8.4 %collective-permute-start.1 = (bf16[32,2176]{1,0:T(8,128)(2,1)S(1)}, bf16[32,2176]{1,0:T(8,128)(2,1)S(1)}, u32[]{:S(2)}, u32[]{:S(2)}) collective-permute-start(bf16[32,2176]{1,0:T(8,128)(2,1)S(1)} %prepare.1.refs_5_), channel_id=1, source_target_pairs={{0,4},{2,6},{4,8},{6,10},{8,12},{10,14},{12,0},{14,2},{1,5},{3,7},... | collective-permute-start | bytes 417800 | tf_op jit(solution)/shard_map/ppermute | solution.py:222
  8.9 12.9 %collective-permute-start.3 = (bf16[32,2176]{1,0:T(8,128)(2,1)S(1)}, bf16[32,2176]{1,0:T(8,128)(2,1)S(1)}, u32[]{:S(2)}, u32[]{:S(2)}) collective-permute-start(bf16[32,2176]{1,0:T(8,128)(2,1)S(1)} %prepare.1.refs_5_), channel_id=1, source_target_pairs={{0,8},{2,10},{4,12},{6,14},{8,0},{10,2},{12,4},{14,6},{1,9},{3,11}... | collective-permute-start | bytes 417800 | tf_op jit(solution)/shard_map/ppermute | solution.py:222
  12.9 9.4 %collective-permute-start.14 = (bf16[32,2176]{1,0:T(8,128)(2,1)S(1)}, bf16[32,2176]{1,0:T(8,128)(2,1)S(1)}, u32[]{:S(2)}, u32[]{:S(2)}) collective-permute-start(bf16[32,2176]{1,0:T(8,128)(2,1)S(1)} %collective-permute-done.5.refs_7_), channel_id=1, source_target_pairs={{0,1},{1,0},{2,3},{3,2},{4,5},{5,4},{6,7},{7,6},{8,9},{9,8},{10,11... | collective-permute-start | bytes 417800 | tf_op jit(solution)/shard_map/ppermute | solution.py:228
  12.9 9.4 %collective-permute-start.6 = (bf16[32,2176]{1,0:T(8,128)(2,1)S(1)}, bf16[32,2176]{1,0:T(8,128)(2,1)S(1)}, u32[]{:S(2)}, u32[]{:S(2)}) collective-permute-start(bf16[32,2176]{1,0:T(8,128)(2,1)S(1)} %collective-permute-done.5.refs_7_), channel_id=1, source_target_pairs={{0,2},{2,0},{4,6},{6,4},{8,10},{10,8},{12,14},{14,12},{1,3},{3,1},... | collective-permute-start | bytes 417800 | tf_op jit(solution)/shard_map/ppermute | solution.py:224
  17.2 5.6 %collective-permute-start.11 = (bf16[32,2176]{1,0:T(8,128)(2,1)S(1)}, bf16[32,2176]{1,0:T(8,128)(2,1)S(1)}, u32[]{:S(2)}, u32[]{:S(2)}) collective-permute-start(bf16[32,2176]{1,0:T(8,128)(2,1)S(1)} %collective-permute-done.1.refs_4_), channel_id=1, source_target_pairs={{0,1},{1,0},{2,3},{3,2},{4,5},{5,4},{6,7},{7,6},{8,9},{9,8},{10,11... | collective-permute-start | bytes 417800 | tf_op jit(solution)/shard_map/ppermute | solution.py:228
  17.2 6.1 %collective-permute-start.2 = (bf16[32,2176]{1,0:T(8,128)(2,1)S(1)}, bf16[32,2176]{1,0:T(8,128)(2,1)S(1)}, u32[]{:S(2)}, u32[]{:S(2)}) collective-permute-start(bf16[32,2176]{1,0:T(8,128)(2,1)S(1)} %collective-permute-done.1.refs_4_), channel_id=1, source_target_pairs={{0,2},{2,0},{4,6},{6,4},{8,10},{10,8},{12,14},{14,12},{1,3},{3,1},... | collective-permute-start | bytes 417800 | tf_op jit(solution)/shard_map/ppermute | solution.py:224
  21.8 5.2 %collective-permute-start.4 = (bf16[32,2176]{1,0:T(8,128)(2,1)S(1)}, bf16[32,2176]{1,0:T(8,128)(2,1)S(1)}, u32[]{:S(2)}, u32[]{:S(2)}) collective-permute-start(bf16[32,2176]{1,0:T(8,128)(2,1)S(1)} %collective-permute-done.3.refs_6_), channel_id=1, source_target_pairs={{0,2},{2,0},{4,6},{6,4},{8,10},{10,8},{12,14},{14,12},{1,3},{3,1},... | collective-permute-start | bytes 417800 | tf_op jit(solution)/shard_map/ppermute | solution.py:224
  22.3 4.7 %collective-permute-start.7 = (bf16[32,2176]{1,0:T(8,128)(2,1)S(1)}, bf16[32,2176]{1,0:T(8,128)(2,1)S(1)}, u32[]{:S(2)}, u32[]{:S(2)}) collective-permute-start(bf16[32,2176]{1,0:T(8,128)(2,1)S(1)} %collective-permute-done.refs_0_), channel_id=1, source_target_pairs={{0,1},{1,0},{2,3},{3,2},{4,5},{5,4},{6,7},{7,6},{8,9},{9,8},{10,11... | collective-permute-start | bytes 417800 | tf_op jit(solution)/shard_map/ppermute | solution.py:228
  22.3 4.7 %collective-permute-start.13 = (bf16[32,2176]{1,0:T(8,128)(2,1)S(1)}, bf16[32,2176]{1,0:T(8,128)(2,1)S(1)}, u32[]{:S(2)}, u32[]{:S(2)}) collective-permute-start(bf16[32,2176]{1,0:T(8,128)(2,1)S(1)} %collective-permute-done.3.refs_6_), channel_id=1, source_target_pairs={{0,1},{1,0},{2,3},{3,2},{4,5},{5,4},{6,7},{7,6},{8,9},{9,8},{10,11... | collective-permute-start | bytes 417800 | tf_op jit(solution)/shard_map/ppermute | solution.py:228
  22.8 4.2 %collective-permute-start.10 = (bf16[32,2176]{1,0:T(8,128)(2,1)S(1)}, bf16[32,2176]{1,0:T(8,128)(2,1)S(1)}, u32[]{:S(2)}, u32[]{:S(2)}) collective-permute-start(bf16[32,2176]{1,0:T(8,128)(2,1)S(1)} %collective-permute-done.6.refs_3_), channel_id=1, source_target_pairs={{0,1},{1,0},{2,3},{3,2},{4,5},{5,4},{6,7},{7,6},{8,9},{9,8},{10,11... | collective-permute-start | bytes 417800 | tf_op jit(solution)/shard_map/ppermute | solution.py:228
  23.3 3.7 %collective-permute-start.8 = (bf16[32,2176]{1,0:T(8,128)(2,1)S(1)}, bf16[32,2176]{1,0:T(8,128)(2,1)S(1)}, u32[]{:S(2)}, u32[]{:S(2)}) collective-permute-start(bf16[32,2176]{1,0:T(8,128)(2,1)S(1)} %collective-permute-done.2.refs_1_), channel_id=1, source_target_pairs={{0,1},{1,0},{2,3},{3,2},{4,5},{5,4},{6,7},{7,6},{8,9},{9,8},{10,11... | collective-permute-start | bytes 417800 | tf_op jit(solution)/shard_map/ppermute | solution.py:228
  27.0 1.4 %collective-permute-start.9 = (bf16[32,2176]{1,0:T(8,128)(2,1)S(1)}, bf16[32,2176]{1,0:T(8,128)(2,1)S(1)}, u32[]{:S(2)}, u32[]{:S(2)}) collective-permute-start(bf16[32,2176]{1,0:T(8,128)(2,1)S(1)} %collective-permute-done.4.refs_2_), channel_id=1, source_target_pairs={{0,1},{1,0},{2,3},{3,2},{4,5},{5,4},{6,7},{7,6},{8,9},{9,8},{10,11... | collective-permute-start | bytes 417800 | tf_op jit(solution)/shard_map/ppermute | solution.py:228
  40.0 2.7 %collective-permute-start.15 = (bf16[160,2048]{1,0:T(8,128)(2,1)S(1)}, bf16[160,2048]{1,0:T(8,128)(2,1)S(1)}, u32[]{:S(2)}, u32[]{:S(2)}) collective-permute-start(bf16[160,2048]{1,0:T(8,128)(2,1)S(1)} %other.2), channel_id=1, source_target_pairs={{0,1},{1,0},{2,3},{3,2},{4,5},{5,4},{6,7},{7,6},{8,9},{9,8},{10,11... | collective-permute-start | bytes 1966088 | tf_op jit(solution)/shard_map/ppermute | solution.py:231
  42.2 21.6 %copy-start.2 = (bf16[32,4096]{1,0:T(8,128)(2,1)S(1)}, bf16[32,4096]{1,0:T(8,128)(2,1)}, u32[]{:S(2)}) copy-start(bf16[32,4096]{1,0:T(8,128)(2,1)} %refs_1_.1) | copy-start | bytes 786436
  42.3 3.0 %collective-permute-start.17 = (bf16[96,2048]{1,0:T(8,128)(2,1)S(1)}, bf16[96,2048]{1,0:T(8,128)(2,1)S(1)}, u32[]{:S(2)}, u32[]{:S(2)}) collective-permute-start(bf16[96,2048]{1,0:T(8,128)(2,1)S(1)} %other.3), channel_id=1, source_target_pairs={{0,1},{1,0},{2,3},{3,2},{4,5},{5,4},{6,7},{7,6},{8,9},{9,8},{10,11... | collective-permute-start | bytes 1179656 | tf_op jit(solution)/shard_map/ppermute | solution.py:231
  44.8 6.7 %collective-permute-start.18 = (bf16[32,2048]{1,0:T(8,128)(2,1)S(1)}, bf16[32,2048]{1,0:T(8,128)(2,1)S(1)}, u32[]{:S(2)}, u32[]{:S(2)}) collective-permute-start(bf16[32,2048]{1,0:T(8,128)(2,1)S(1)} %get-tuple-element.21), channel_id=1, source_target_pairs={{0,2},{2,0},{4,6},{6,4},{8,10},{10,8},{12,14},{14,12},{1,3},{3,1},... | collective-permute-start | bytes 393224 | tf_op jit(solution)/shard_map/ppermute | solution.py:248
  47.2 11.1 %collective-permute-start.16 = (bf16[32,2048]{1,0:T(8,128)(2,1)S(1)}, bf16[32,2048]{1,0:T(8,128)(2,1)S(1)}, u32[]{:S(2)}, u32[]{:S(2)}) collective-permute-start(bf16[32,2048]{1,0:T(8,128)(2,1)S(1)} %get-tuple-element.18), channel_id=1, source_target_pairs={{0,12},{2,14},{4,0},{6,2},{8,4},{10,6},{12,8},{14,10},{1,13},{3,15... | collective-permute-start | bytes 393224 | tf_op jit(solution)/shard_map/ppermute | solution.py:246
  50.0 5.0 %collective-permute-start.20 = (bf16[32,2048]{1,0:T(8,128)(2,1)S(1)}, bf16[32,2048]{1,0:T(8,128)(2,1)S(1)}, u32[]{:S(2)}, u32[]{:S(2)}) collective-permute-start(bf16[32,2048]{1,0:T(8,128)(2,1)S(1)} %get-tuple-element.23), channel_id=1, source_target_pairs={{0,2},{2,0},{4,6},{6,4},{8,10},{10,8},{12,14},{14,12},{1,3},{3,1},... | collective-permute-start | bytes 393224 | tf_op jit(solution)/shard_map/ppermute | solution.py:248
  51.5 5.7 %collective-permute-start.22 = (bf16[32,2048]{1,0:T(8,128)(2,1)S(1)}, bf16[32,2048]{1,0:T(8,128)(2,1)S(1)}, u32[]{:S(2)}, u32[]{:S(2)}) collective-permute-start(bf16[32,2048]{1,0:T(8,128)(2,1)S(1)} %get-tuple-element.26), channel_id=1, source_target_pairs={{0,12},{2,14},{4,0},{6,2},{8,4},{10,6},{12,8},{14,10},{1,13},{3,15... | collective-permute-start | bytes 393224 | tf_op jit(solution)/shard_map/ppermute | solution.py:244
  51.6 12.3 %collective-permute-start.19 = (bf16[32,2048]{1,0:T(8,128)(2,1)S(1)}, bf16[32,2048]{1,0:T(8,128)(2,1)S(1)}, u32[]{:S(2)}, u32[]{:S(2)}) collective-permute-start(bf16[32,2048]{1,0:T(8,128)(2,1)S(1)} %add_convert_fusion.3), channel_id=1, source_target_pairs={{0,8},{2,10},{4,12},{6,14},{8,0},{10,2},{12,4},{14,6},{1,9},{3,11}... | collective-permute-start | bytes 393224 | tf_op jit(solution)/shard_map/ppermute | solution.py:251
  55.0 8.9 %collective-permute-start.21 = (bf16[32,2048]{1,0:T(8,128)(2,1)S(1)}, bf16[32,2048]{1,0:T(8,128)(2,1)S(1)}, u32[]{:S(2)}, u32[]{:S(2)}) collective-permute-start(bf16[32,2048]{1,0:T(8,128)(2,1)S(1)} %add_convert_fusion.2), channel_id=1, source_target_pairs={{0,4},{2,6},{4,8},{6,10},{8,12},{10,14},{12,0},{14,2},{1,5},{3,7},... | collective-permute-start | bytes 393224 | tf_op jit(solution)/shard_map/ppermute | solution.py:251
  57.2 6.7 %collective-permute-start.23 = (bf16[32,2048]{1,0:T(8,128)(2,1)S(1)}, bf16[32,2048]{1,0:T(8,128)(2,1)S(1)}, u32[]{:S(2)}, u32[]{:S(2)}) collective-permute-start(bf16[32,2048]{1,0:T(8,128)(2,1)S(1)} %add_convert_fusion.1), channel_id=1, source_target_pairs={{0,2},{2,0},{4,6},{6,4},{8,10},{10,8},{12,14},{14,12},{1,3},{3,1},... | collective-permute-start | bytes 393224 | tf_op jit(solution)/shard_map/ppermute | solution.py:248

commit v7 on v6

--- a/solution.py
+++ b/solution.py
@@ -214,7 +214,6 @@
     bf16, f32 = jnp.bfloat16, jnp.float32
 
     packed = prepare(place, hidden_in, expert_ids, route_scores, expert_slot)
-    turned = 1
     order = sorted(range(1, outer), key=lambda k: -min(k, outer - k))
     same, opposite = {0: packed}, {0: lax.ppermute(packed, "sect", across)}
     for k in order[::-1]:
@@ -222,31 +221,18 @@
         same[k] = lax.ppermute(block, "sect", along(k))
     for k in order[::-1]:
         opposite[k] = lax.ppermute(same[k], "sect", across)
-    early = [(opposite, k) for k in range(outer)] + [(same, k) for k in range(outer) if k == turned]
-    late = [(same, k) for k in range(outer) if k != turned]
-    blocks = [side[k] for side, k in early + late]
+    blocks = [side[k] for side in (opposite, same) for k in range(outer)]
     others = [lax.ppermute(block, "tp", cores) for block in blocks]
-    groups = run_hidden(place, blocks, others, gate_matrix, up_matrix, experts, len(early))
+    groups = run_hidden(place, blocks, others, gate_matrix, up_matrix, experts, outer)
     sent = [
         lax.ppermute(run_down(place, hidden, down_matrix, None, [bf16])[0], "tp", cores)
         for hidden in groups
     ]
-    far_sum, near_sum = {}, {}
-    for group, hidden, received in zip((early, late), groups, sent):
-        kinds = [
-            bf16 if k == turned or (side is opposite and k) else f32 for side, k in group
-        ]
-        sums = run_down(place, hidden, down_matrix, received, kinds)
-        for (side, k), total in zip(group, sums):
-            (far_sum if side is opposite else near_sum)[k] = total
+    far_sum = run_down(place, groups[0], down_matrix, sent[0], [bf16] * outer)
+    near_sum = run_down(place, groups[1], down_matrix, sent[1], [f32] * outer)
     result = lax.dynamic_slice_in_dim(hidden_in, core * half, half, 1).astype(f32)
-    if turned < outer:
-        gone = lax.ppermute(far_sum[turned], "sect", along(-turned)).astype(f32)
-        far_sum[0] = (far_sum[0] + gone).astype(bf16)
-        result = result + lax.ppermute(near_sum[turned], "sect", along(-turned)).astype(f32)
-    for k in [k for k in order if k != turned] + [0]:
-        crossed = lax.ppermute(far_sum[k].astype(bf16), "sect", across).astype(f32)
-        block = near_sum[k] + crossed
+    for k in order + [0]:
+        block = near_sum[k] + lax.ppermute(far_sum[k], "sect", across).astype(f32)
         if k:
             block = lax.ppermute(block.astype(bf16), "sect", along(-k)).astype(f32)
         result = result + block

time: 65.7 us -> 64.8 us (0.986); the launches traced: 64.6 us -> 64.6 us
  starting transfers between devices: 19.1 us -> 20.6 us
  Pallas kernels: 19.8 us -> 18.8 us
    ppermute x2 -> x3, starting transfers between devices: 1.04 us -> 4.21 us  [on_device(): block = lax.ppermute(block.astype(bf16), 'sect', along(-k)).astype(f32)]
    ppermute x5 -> x4, starting transfers between devices: 5.84 us -> 4.12 us  [on_device(): block = near_sum[k] + lax.ppermute(far_sum[k], 'sect', across).astype(f32)]
    pallas_call x4, Pallas kernels: 8.26 us -> 7.32 us  [run_down(): pl.pallas_call(functools.partial(down_kernel, len(extra)), out_shape=[jax...]
    ppermute x5 -> x4, waiting for transfers between devices: 4.54 us -> 3.75 us  [on_device(): block = near_sum[k] + lax.ppermute(far_sum[k], 'sect', across).astype(f32)]
    ppermute x2 -> x3, waiting for transfers between devices: 5.52 us -> 5.78 us  [on_device(): block = lax.ppermute(block.astype(bf16), 'sect', along(-k)).astype(f32)]
  transfers between devices with their start and end apart: 24 -> 24, of which waited for: 10 -> 12; matrix products, arithmetic and copies ran while one was open for 0% -> 0% of each run, Pallas kernels for 10% -> 9%
where the time goes in v7:
time: 64.8 us; the launch traced here: 64.6 us
  waiting for transfers between devices  24.1 us (37%)
  starting transfers between devices  20.6 us (32%)
  Pallas kernels  18.8 us (29%)
  other arithmetic  0.93 us (1%)
    pallas_call x1, Pallas kernels, run_hidden(): pl.pallas_call(functools.partial(hidden_kernel, half, experts, blocks), o...  9.48 us
    ppermute x3, waiting for transfers between devices, on_device(): same[k] = lax.ppermute(block, 'sect', along(k))  9.06 us
    pallas_call x4, Pallas kernels, run_down(): pl.pallas_call(functools.partial(down_kernel, len(extra)), out_shape=[jax...  7.32 us
    ppermute x3, starting transfers between devices, on_device(): same[k] = lax.ppermute(block, 'sect', along(k))  6.41 us
    ppermute x3, waiting for transfers between devices, on_device(): block = lax.ppermute(block.astype(bf16), 'sect', along(-k)).astype(f32)  5.78 us
    ppermute x3, starting transfers between devices, on_device(): block = lax.ppermute(block.astype(bf16), 'sect', along(-k)).astype(f32)  4.21 us
    ppermute x4, starting transfers between devices, on_device(): block = near_sum[k] + lax.ppermute(far_sum[k], 'sect', across).astype(f32)  4.12 us
    ppermute x3, waiting for transfers between devices, on_device(): opposite[k] = lax.ppermute(same[k], 'sect', across)  4.09 us
  transfers between devices with their start and end apart: 24, of which 12 were waited for; matrix products, arithmetic and copies ran while one was open for 0% of the time, Pallas kernels for 9%

profile of v7, /device:TPU:0, one launch (start us, length us, event | category | flops | bytes accessed | tf_op | source)
XLA Modules:
  0.0 64.6 jit_solution(9202998868539460779)
XLA Ops:
  0.0 0.1 pad_add_fusion.place_ref
  0.1 0.0 slice-start.2
  0.1 0.0 slice-start.3
  0.1 2.0 %prepare.1.refs_4_ = bf16[32,2176]{1,0:T(8,128)(2,1)S(1)} custom-call(s32[2]{0:T(128)S(1)} %pad_add_fusion.place_ref, s32[32]{0:T(128)} %refs_0_.1, bf16[32,4096]{1,0:T(8,128)(2,1)} %refs_1_.1, s32[8,32]{1,0:T(8,128)} %bitcast.6, f32[8,32]{1,0:T(8,128)} %bitcast.7), custom_call_target="tpu_custom_call" | custom-call | flops 40000000000 | bytes 262144 | tf_op jit(solution)/shard_map/prepare/pallas_call | solution.py:61
  2.2 3.0 %collective-permute-start = (bf16[32,2176]{1,0:T(8,128)(2,1)S(1)}, bf16[32,2176]{1,0:T(8,128)(2,1)S(1)}, u32[]{:S(2)}, u32[]{:S(2)}) collective-permute-start(bf16[32,2176]{1,0:T(8,128)(2,1)S(1)} %prepare.1.refs_4_), channel_id=1, source_target_pairs={{0,2},{2,0},{4,6},{6,4},{8,10},{10,8},{12,14},{14,12},{1,3},{3,1},... | collective-permute-start | bytes 417800 | tf_op jit(solution)/shard_map/ppermute | solution.py:218
  5.2 3.6 %collective-permute-start.5 = (bf16[32,2176]{1,0:T(8,128)(2,1)S(1)}, bf16[32,2176]{1,0:T(8,128)(2,1)S(1)}, u32[]{:S(2)}, u32[]{:S(2)}) collective-permute-start(bf16[32,2176]{1,0:T(8,128)(2,1)S(1)} %prepare.1.refs_4_), channel_id=1, source_target_pairs={{0,12},{2,14},{4,0},{6,2},{8,4},{10,6},{12,8},{14,10},{1,13},{3,15... | collective-permute-start | bytes 417800 | tf_op jit(solution)/shard_map/ppermute | solution.py:221
  8.8 0.0 collective-permute-start.11
  8.8 0.0 collective-permute-start.1
  8.8 0.1 collective-permute-done.refs_0_
  8.9 2.8 %collective-permute-start.3 = (bf16[32,2176]{1,0:T(8,128)(2,1)S(1)}, bf16[32,2176]{1,0:T(8,128)(2,1)S(1)}, u32[]{:S(2)}, u32[]{:S(2)}) collective-permute-start(bf16[32,2176]{1,0:T(8,128)(2,1)S(1)} %prepare.1.refs_4_), channel_id=1, source_target_pairs={{0,8},{2,10},{4,12},{6,14},{8,0},{10,2},{12,4},{14,6},{1,9},{3,11}... | collective-permute-start | bytes 417800 | tf_op jit(solution)/shard_map/ppermute | solution.py:221
  11.7 1.2 %collective-permute-done.5.refs_7_ = bf16[32,2176]{1,0:T(8,128)(2,1)S(1)} collective-permute-done((bf16[32,2176]{1,0:T(8,128)(2,1)S(1)}, bf16[32,2176]{1,0:T(8,128)(2,1)S(1)}, u32[]{:S(2)}, u32[]{:S(2)}) %collective-permute-start.5) | collective-permute-done | bytes 139296 | tf_op jit(solution)/shard_map/ppermute | solution.py:221
  12.9 0.0 collective-permute-start.14
  12.9 0.5 collective-permute-start.6
  13.4 3.7 %collective-permute-done.1.refs_5_ = bf16[32,2176]{1,0:T(8,128)(2,1)S(1)} collective-permute-done((bf16[32,2176]{1,0:T(8,128)(2,1)S(1)}, bf16[32,2176]{1,0:T(8,128)(2,1)S(1)}, u32[]{:S(2)}, u32[]{:S(2)}) %collective-permute-start.1) | collective-permute-done | bytes 139296 | tf_op jit(solution)/shard_map/ppermute | solution.py:221
  17.2 0.0 collective-permute-start.12
  17.2 0.0 collective-permute-done.11.refs_12_
  17.2 0.5 collective-permute-start.2
  17.7 4.1 %collective-permute-done.3.refs_6_ = bf16[32,2176]{1,0:T(8,128)(2,1)S(1)} collective-permute-done((bf16[32,2176]{1,0:T(8,128)(2,1)S(1)}, bf16[32,2176]{1,0:T(8,128)(2,1)S(1)}, u32[]{:S(2)}, u32[]{:S(2)}) %collective-permute-start.3) | collective-permute-done | bytes 139296 | tf_op jit(solution)/shard_map/ppermute | solution.py:221
  21.8 0.5 collective-permute-start.4
  22.3 0.0 collective-permute-done.14.refs_15_
  22.3 0.0 collective-permute-start.7
  22.3 0.0 collective-permute-done.6.refs_3_
  22.3 0.5 collective-permute-start.13
  22.8 0.0 collective-permute-done.12.refs_13_
  22.8 0.1 collective-permute-start.10
  22.9 0.4 collective-permute-done.2.refs_1_
  23.3 0.0 collective-permute-start.8
  23.3 3.7 %collective-permute-done.4.refs_2_ = bf16[32,2176]{1,0:T(8,128)(2,1)S(1)} collective-permute-done((bf16[32,2176]{1,0:T(8,128)(2,1)S(1)}, bf16[32,2176]{1,0:T(8,128)(2,1)S(1)}, u32[]{:S(2)}, u32[]{:S(2)}) %collective-permute-start.4) | collective-permute-done | bytes 139296 | tf_op jit(solution)/shard_map/ppermute | solution.py:223
  27.0 0.0 collective-permute-start.9
  27.0 0.0 collective-permute-done.7.refs_8_
  27.0 0.0 collective-permute-done.10.refs_11_
  27.0 0.0 collective-permute-done.8.refs_9_
  27.0 0.0 collective-permute-done.13.refs_14_
  27.0 1.3 %collective-permute-done.9.refs_10_ = bf16[32,2176]{1,0:T(8,128)(2,1)S(1)} collective-permute-done((bf16[32,2176]{1,0:T(8,128)(2,1)S(1)}, bf16[32,2176]{1,0:T(8,128)(2,1)S(1)}, u32[]{:S(2)}, u32[]{:S(2)}) %collective-permute-start.9) | collective-permute-done | bytes 139296 | tf_op jit(solution)/shard_map/ppermute | solution.py:225
  28.3 0.0 copy-done
  28.3 0.0 copy-done.1
  28.3 9.5 %hidden.1 = (bf16[128,2048]{1,0:T(8,128)(2,1)S(1)}, bf16[128,2048]{1,0:T(8,128)(2,1)S(1)}) custom-call(s32[2]{0:T(128)S(1)} %pad_add_fusion.place_ref, bf16[32,2176]{1,0:T(8,128)(2,1)S(1)} %collective-permute-done.refs_0_, bf16[32,2176]{1,0:T(8,128)(2,1)S(1)} %collective-permute-done.2.refs_1_, bf16[32,2176]{1,0:T(8,128)(2,1)S(1)} %collective-permute-done.4.refs_2_, ...), custom_call_target="tpu_custom_call" | custom-call | flops 8589934592 | bytes 2097152 | tf_op jit(solution)/shard_map/hidden/pallas_call | solution.py:131
  37.8 0.0 slice-done
  37.8 0.0 slice-done.1
  37.9 0.0 slice-done.2
  37.9 1.8 %other.3 = bf16[128,2048]{1,0:T(8,128)(2,1)S(1)} custom-call(s32[2]{0:T(128)S(1)} %pad_add_fusion.place_ref, bf16[128,2048]{1,0:T(8,128)(2,1)S(1)} %get-tuple-element.19.hidden_ref, bf16[4,512,4096]{2,1,0:T(8,128)(2,1)S(1)} %bitcast.5), custom_call_target="tpu_custom_call" | custom-call | flops 524288 | bytes 512 | tf_op jit(solution)/shard_map/other/pallas_call | solution.py:175
  39.7 0.2 collective-permute-start.16
  39.9 1.8 %other.2 = bf16[128,2048]{1,0:T(8,128)(2,1)S(1)} custom-call(s32[2]{0:T(128)S(1)} %pad_add_fusion.place_ref, bf16[128,2048]{1,0:T(8,128)(2,1)S(1)} %get-tuple-element.17.hidden_ref, bf16[4,512,4096]{2,1,0:T(8,128)(2,1)S(1)} %bitcast.5), custom_call_target="tpu_custom_call" | custom-call | flops 524288 | bytes 512 | tf_op jit(solution)/shard_map/other/pallas_call | solution.py:175
  41.8 0.0 copy-start.2
  41.8 0.4 collective-permute-start.15
  42.2 0.0 collective-permute-done.16.refs_0_
  42.2 1.8 %mine.3 = (bf16[32,2048]{1,0:T(8,128)(2,1)S(1)}, bf16[32,2048]{1,0:T(8,128)(2,1)S(1)}, bf16[32,2048]{1,0:T(8,128)(2,1)S(1)}, bf16[32,2048]{1,0:T(8,128)(2,1)S(1)}) custom-call(s32[2]{0:T(128)S(1)} %pad_add_fusion.place_ref, bf16[128,2048]{1,0:T(8,128)(2,1)S(1)} %get-tuple-element.19.hidden_ref, bf16[4,512,4096]{2,1,0:T(8,128)(2,1)S(1)} %bitcast.5, ...), custom_call_target="tpu_custom_call" | custom-call | flops 524288 | bytes 512 | tf_op jit(solution)/shard_map/mine/pallas_call | solution.py:175
  44.1 0.4 collective-permute-start.19
  44.5 1.7 %collective-permute-start.17 = (bf16[32,2048]{1,0:T(8,128)(2,1)S(1)}, bf16[32,2048]{1,0:T(8,128)(2,1)S(1)}, u32[]{:S(2)}, u32[]{:S(2)}) collective-permute-start(bf16[32,2048]{1,0:T(8,128)(2,1)S(1)} %get-tuple-element.20), channel_id=1, source_target_pairs={{0,2},{2,0},{4,6},{6,4},{8,10},{10,8},{12,14},{14,12},{1,3},{3,1},... | collective-permute-start | bytes 393224 | tf_op jit(solution)/shard_map/ppermute | solution.py:235
  46.2 0.3 collective-permute-start.21
  46.5 1.7 %collective-permute-start.23 = (bf16[32,2048]{1,0:T(8,128)(2,1)S(1)}, bf16[32,2048]{1,0:T(8,128)(2,1)S(1)}, u32[]{:S(2)}, u32[]{:S(2)}) collective-permute-start(bf16[32,2048]{1,0:T(8,128)(2,1)S(1)} %get-tuple-element.26), channel_id=1, source_target_pairs={{0,2},{2,0},{4,6},{6,4},{8,10},{10,8},{12,14},{14,12},{1,3},{3,1},... | collective-permute-start | bytes 393224 | tf_op jit(solution)/shard_map/ppermute | solution.py:235
  48.2 0.0 collective-permute-done.15.refs_0_
  48.2 1.8 %mine.2 = (f32[32,2048]{1,0:T(8,128)S(1)}, f32[32,2048]{1,0:T(8,128)S(1)}, f32[32,2048]{1,0:T(8,128)S(1)}, f32[32,2048]{1,0:T(8,128)S(1)}) custom-call(s32[2]{0:T(128)S(1)} %pad_add_fusion.place_ref, bf16[128,2048]{1,0:T(8,128)(2,1)S(1)} %get-tuple-element.17.hidden_ref, bf16[4,512,4096]{2,1,0:T(8,128)(2,1)S(1)} %bitcast.5, ...), custom_call_target="tpu_custom_call" | custom-call | flops 524288 | bytes 512 | tf_op jit(solution)/shard_map/mine/pallas_call | solution.py:175
  50.0 0.4 collective-permute-done.19
  50.5 2.5 %collective-permute-start.20 = (bf16[32,2048]{1,0:T(8,128)(2,1)S(1)}, bf16[32,2048]{1,0:T(8,128)(2,1)S(1)}, u32[]{:S(2)}, u32[]{:S(2)}) collective-permute-start(bf16[32,2048]{1,0:T(8,128)(2,1)S(1)} %add_convert_fusion.2), channel_id=1, source_target_pairs={{0,12},{2,14},{4,0},{6,2},{8,4},{10,6},{12,8},{14,10},{1,13},{3,15... | collective-permute-start | bytes 393224 | tf_op jit(solution)/shard_map/ppermute | solution.py:237
  53.1 0.2 collective-permute-done.17
  53.3 1.1 %collective-permute-start.18 = (bf16[32,2048]{1,0:T(8,128)(2,1)S(1)}, bf16[32,2048]{1,0:T(8,128)(2,1)S(1)}, u32[]{:S(2)}, u32[]{:S(2)}) collective-permute-start(bf16[32,2048]{1,0:T(8,128)(2,1)S(1)} %add_convert_fusion.3), channel_id=1, source_target_pairs={{0,8},{2,10},{4,12},{6,14},{8,0},{10,2},{12,4},{14,6},{1,9},{3,11}... | collective-permute-start | bytes 393224 | tf_op jit(solution)/shard_map/ppermute | solution.py:237
  54.4 1.7 %collective-permute-done.21 = bf16[32,2048]{1,0:T(8,128)(2,1)S(1)} collective-permute-done((bf16[32,2048]{1,0:T(8,128)(2,1)S(1)}, bf16[32,2048]{1,0:T(8,128)(2,1)S(1)}, u32[]{:S(2)}, u32[]{:S(2)}) %collective-permute-start.21) | collective-permute-done | bytes 131104 | tf_op jit(solution)/shard_map/ppermute | solution.py:235
  56.1 0.5 collective-permute-start.22
  56.7 1.4 %collective-permute-done.23 = bf16[32,2048]{1,0:T(8,128)(2,1)S(1)} collective-permute-done((bf16[32,2048]{1,0:T(8,128)(2,1)S(1)}, bf16[32,2048]{1,0:T(8,128)(2,1)S(1)}, u32[]{:S(2)}, u32[]{:S(2)}) %collective-permute-start.23) | collective-permute-done | bytes 131104 | tf_op jit(solution)/shard_map/ppermute | solution.py:235
  58.1 0.0 collective-permute-done.20
  58.1 5.8 %collective-permute-done.18 = bf16[32,2048]{1,0:T(8,128)(2,1)S(1)} collective-permute-done((bf16[32,2048]{1,0:T(8,128)(2,1)S(1)}, bf16[32,2048]{1,0:T(8,128)(2,1)S(1)}, u32[]{:S(2)}, u32[]{:S(2)}) %collective-permute-start.18) | collective-permute-done | bytes 131104 | tf_op jit(solution)/shard_map/ppermute | solution.py:237
  63.9 0.0 collective-permute-done.22
  63.9 0.8 %add_convert_fusion = bf16[32,2048]{1,0:T(8,128)(2,1)} fusion(f32[32,2048]{1,0:T(8,128)S(1)} %get-tuple-element.25, bf16[32,2048]{1,0:T(8,128)(2,1)S(1)} %collective-permute-done.23, bf16[32,2048]{1,0:T(8,128)(2,1)S(1)} %collective-permute-done.22, bf16[32,2048]{1,0:T(8,128)(2,1)S(1)} %collective-permute-done.20, ...), kind=kLoop, calls=%fused_computation | loop fusion | flops 720896 | bytes 1048580 | tf_op jit(solution)/shard_map/convert_element_type | solution.py:239
  (10 shorter events, 0.1 us)
Async XLA Ops:
  0.1 37.8 %slice-start = ((s8[16777216]{0:T(1024)(128)(4,1)}), s8[4194304]{0:T(1024)(128)(4,1)S(1)}, s32[]{:S(2)}) async-start(s8[16777216]{0:T(1024)(128)(4,1)} %bitcast.4), calls=%async_computation | async-start | bytes 8388608
  0.1 28.3 %copy-start = (bf16[4,4096,512]{2,1,0:T(8,128)(2,1)S(1)}, bf16[4,4096,512]{2,1,0:T(8,128)(2,1)}, u32[]{:S(2)}) copy-start(bf16[4,4096,512]{2,1,0:T(8,128)(2,1)} %refs_16_.1) | copy-start | bytes 50331652
  0.1 28.3 %copy-start.1 = (bf16[4,4096,512]{2,1,0:T(8,128)(2,1)S(1)}, bf16[4,4096,512]{2,1,0:T(8,128)(2,1)}, u32[]{:S(2)}) copy-start(bf16[4,4096,512]{2,1,0:T(8,128)(2,1)} %refs_17_.1) | copy-start | bytes 50331652
  0.1 37.8 %slice-start.1 = ((s8[16777216]{0:T(1024)(128)(4,1)}), s8[4194304]{0:T(1024)(128)(4,1)S(1)}, s32[]{:S(2)}) async-start(s8[16777216]{0:T(1024)(128)(4,1)} %bitcast.4), calls=%async_computation.1 | async-start | bytes 8388608
  0.1 37.8 %slice-start.2 = ((s8[16777216]{0:T(1024)(128)(4,1)}), s8[4194304]{0:T(1024)(128)(4,1)S(1)}, s32[]{:S(2)}) async-start(s8[16777216]{0:T(1024)(128)(4,1)} %bitcast.4), calls=%async_computation.2 | async-start | bytes 8388608
  0.1 37.8 %slice-start.3 = ((s8[16777216]{0:T(1024)(128)(4,1)}), s8[4194304]{0:T(1024)(128)(4,1)S(1)}, s32[]{:S(2)}) async-start(s8[16777216]{0:T(1024)(128)(4,1)} %bitcast.4), calls=%async_computation.3 | async-start | bytes 8388608
  2.2 6.7 %collective-permute-start = (bf16[32,2176]{1,0:T(8,128)(2,1)S(1)}, bf16[32,2176]{1,0:T(8,128)(2,1)S(1)}, u32[]{:S(2)}, u32[]{:S(2)}) collective-permute-start(bf16[32,2176]{1,0:T(8,128)(2,1)S(1)} %prepare.1.refs_4_), channel_id=1, source_target_pairs={{0,2},{2,0},{4,6},{6,4},{8,10},{10,8},{12,14},{14,12},{1,3},{3,1},... | collective-permute-start | bytes 417800 | tf_op jit(solution)/shard_map/ppermute | solution.py:218
  5.2 7.7 %collective-permute-start.5 = (bf16[32,2176]{1,0:T(8,128)(2,1)S(1)}, bf16[32,2176]{1,0:T(8,128)(2,1)S(1)}, u32[]{:S(2)}, u32[]{:S(2)}) collective-permute-start(bf16[32,2176]{1,0:T(8,128)(2,1)S(1)} %prepare.1.refs_4_), channel_id=1, source_target_pairs={{0,12},{2,14},{4,0},{6,2},{8,4},{10,6},{12,8},{14,10},{1,13},{3,15... | collective-permute-start | bytes 417800 | tf_op jit(solution)/shard_map/ppermute | solution.py:221
  8.8 8.4 %collective-permute-start.11 = (bf16[32,2176]{1,0:T(8,128)(2,1)S(1)}, bf16[32,2176]{1,0:T(8,128)(2,1)S(1)}, u32[]{:S(2)}, u32[]{:S(2)}) collective-permute-start(bf16[32,2176]{1,0:T(8,128)(2,1)S(1)} %prepare.1.refs_4_), channel_id=1, source_target_pairs={{0,1},{1,0},{2,3},{3,2},{4,5},{5,4},{6,7},{7,6},{8,9},{9,8},{10,11... | collective-permute-start | bytes 417800 | tf_op jit(solution)/shard_map/ppermute | solution.py:225
  8.8 8.4 %collective-permute-start.1 = (bf16[32,2176]{1,0:T(8,128)(2,1)S(1)}, bf16[32,2176]{1,0:T(8,128)(2,1)S(1)}, u32[]{:S(2)}, u32[]{:S(2)}) collective-permute-start(bf16[32,2176]{1,0:T(8,128)(2,1)S(1)} %prepare.1.refs_4_), channel_id=1, source_target_pairs={{0,4},{2,6},{4,8},{6,10},{8,12},{10,14},{12,0},{14,2},{1,5},{3,7},... | collective-permute-start | bytes 417800 | tf_op jit(solution)/shard_map/ppermute | solution.py:221
  8.9 12.9 %collective-permute-start.3 = (bf16[32,2176]{1,0:T(8,128)(2,1)S(1)}, bf16[32,2176]{1,0:T(8,128)(2,1)S(1)}, u32[]{:S(2)}, u32[]{:S(2)}) collective-permute-start(bf16[32,2176]{1,0:T(8,128)(2,1)S(1)} %prepare.1.refs_4_), channel_id=1, source_target_pairs={{0,8},{2,10},{4,12},{6,14},{8,0},{10,2},{12,4},{14,6},{1,9},{3,11}... | collective-permute-start | bytes 417800 | tf_op jit(solution)/shard_map/ppermute | solution.py:221
  12.9 9.4 %collective-permute-start.14 = (bf16[32,2176]{1,0:T(8,128)(2,1)S(1)}, bf16[32,2176]{1,0:T(8,128)(2,1)S(1)}, u32[]{:S(2)}, u32[]{:S(2)}) collective-permute-start(bf16[32,2176]{1,0:T(8,128)(2,1)S(1)} %collective-permute-done.5.refs_7_), channel_id=1, source_target_pairs={{0,1},{1,0},{2,3},{3,2},{4,5},{5,4},{6,7},{7,6},{8,9},{9,8},{10,11... | collective-permute-start | bytes 417800 | tf_op jit(solution)/shard_map/ppermute | solution.py:225
  12.9 9.4 %collective-permute-start.6 = (bf16[32,2176]{1,0:T(8,128)(2,1)S(1)}, bf16[32,2176]{1,0:T(8,128)(2,1)S(1)}, u32[]{:S(2)}, u32[]{:S(2)}) collective-permute-start(bf16[32,2176]{1,0:T(8,128)(2,1)S(1)} %collective-permute-done.5.refs_7_), channel_id=1, source_target_pairs={{0,2},{2,0},{4,6},{6,4},{8,10},{10,8},{12,14},{14,12},{1,3},{3,1},... | collective-permute-start | bytes 417800 | tf_op jit(solution)/shard_map/ppermute | solution.py:223
  17.2 5.6 %collective-permute-start.12 = (bf16[32,2176]{1,0:T(8,128)(2,1)S(1)}, bf16[32,2176]{1,0:T(8,128)(2,1)S(1)}, u32[]{:S(2)}, u32[]{:S(2)}) collective-permute-start(bf16[32,2176]{1,0:T(8,128)(2,1)S(1)} %collective-permute-done.1.refs_5_), channel_id=1, source_target_pairs={{0,1},{1,0},{2,3},{3,2},{4,5},{5,4},{6,7},{7,6},{8,9},{9,8},{10,11... | collective-permute-start | bytes 417800 | tf_op jit(solution)/shard_map/ppermute | solution.py:225
  17.2 6.1 %collective-permute-start.2 = (bf16[32,2176]{1,0:T(8,128)(2,1)S(1)}, bf16[32,2176]{1,0:T(8,128)(2,1)S(1)}, u32[]{:S(2)}, u32[]{:S(2)}) collective-permute-start(bf16[32,2176]{1,0:T(8,128)(2,1)S(1)} %collective-permute-done.1.refs_5_), channel_id=1, source_target_pairs={{0,2},{2,0},{4,6},{6,4},{8,10},{10,8},{12,14},{14,12},{1,3},{3,1},... | collective-permute-start | bytes 417800 | tf_op jit(solution)/shard_map/ppermute | solution.py:223
  21.8 5.2 %collective-permute-start.4 = (bf16[32,2176]{1,0:T(8,128)(2,1)S(1)}, bf16[32,2176]{1,0:T(8,128)(2,1)S(1)}, u32[]{:S(2)}, u32[]{:S(2)}) collective-permute-start(bf16[32,2176]{1,0:T(8,128)(2,1)S(1)} %collective-permute-done.3.refs_6_), channel_id=1, source_target_pairs={{0,2},{2,0},{4,6},{6,4},{8,10},{10,8},{12,14},{14,12},{1,3},{3,1},... | collective-permute-start | bytes 417800 | tf_op jit(solution)/shard_map/ppermute | solution.py:223
  22.3 4.7 %collective-permute-start.7 = (bf16[32,2176]{1,0:T(8,128)(2,1)S(1)}, bf16[32,2176]{1,0:T(8,128)(2,1)S(1)}, u32[]{:S(2)}, u32[]{:S(2)}) collective-permute-start(bf16[32,2176]{1,0:T(8,128)(2,1)S(1)} %collective-permute-done.refs_0_), channel_id=1, source_target_pairs={{0,1},{1,0},{2,3},{3,2},{4,5},{5,4},{6,7},{7,6},{8,9},{9,8},{10,11... | collective-permute-start | bytes 417800 | tf_op jit(solution)/shard_map/ppermute | solution.py:225
  22.3 4.7 %collective-permute-start.13 = (bf16[32,2176]{1,0:T(8,128)(2,1)S(1)}, bf16[32,2176]{1,0:T(8,128)(2,1)S(1)}, u32[]{:S(2)}, u32[]{:S(2)}) collective-permute-start(bf16[32,2176]{1,0:T(8,128)(2,1)S(1)} %collective-permute-done.3.refs_6_), channel_id=1, source_target_pairs={{0,1},{1,0},{2,3},{3,2},{4,5},{5,4},{6,7},{7,6},{8,9},{9,8},{10,11... | collective-permute-start | bytes 417800 | tf_op jit(solution)/shard_map/ppermute | solution.py:225
  22.8 4.2 %collective-permute-start.10 = (bf16[32,2176]{1,0:T(8,128)(2,1)S(1)}, bf16[32,2176]{1,0:T(8,128)(2,1)S(1)}, u32[]{:S(2)}, u32[]{:S(2)}) collective-permute-start(bf16[32,2176]{1,0:T(8,128)(2,1)S(1)} %collective-permute-done.6.refs_3_), channel_id=1, source_target_pairs={{0,1},{1,0},{2,3},{3,2},{4,5},{5,4},{6,7},{7,6},{8,9},{9,8},{10,11... | collective-permute-start | bytes 417800 | tf_op jit(solution)/shard_map/ppermute | solution.py:225
  23.3 3.7 %collective-permute-start.8 = (bf16[32,2176]{1,0:T(8,128)(2,1)S(1)}, bf16[32,2176]{1,0:T(8,128)(2,1)S(1)}, u32[]{:S(2)}, u32[]{:S(2)}) collective-permute-start(bf16[32,2176]{1,0:T(8,128)(2,1)S(1)} %collective-permute-done.2.refs_1_), channel_id=1, source_target_pairs={{0,1},{1,0},{2,3},{3,2},{4,5},{5,4},{6,7},{7,6},{8,9},{9,8},{10,11... | collective-permute-start | bytes 417800 | tf_op jit(solution)/shard_map/ppermute | solution.py:225
  27.0 1.4 %collective-permute-start.9 = (bf16[32,2176]{1,0:T(8,128)(2,1)S(1)}, bf16[32,2176]{1,0:T(8,128)(2,1)S(1)}, u32[]{:S(2)}, u32[]{:S(2)}) collective-permute-start(bf16[32,2176]{1,0:T(8,128)(2,1)S(1)} %collective-permute-done.4.refs_2_), channel_id=1, source_target_pairs={{0,1},{1,0},{2,3},{3,2},{4,5},{5,4},{6,7},{7,6},{8,9},{9,8},{10,11... | collective-permute-start | bytes 417800 | tf_op jit(solution)/shard_map/ppermute | solution.py:225
  39.7 2.5 %collective-permute-start.16 = (bf16[128,2048]{1,0:T(8,128)(2,1)S(1)}, bf16[128,2048]{1,0:T(8,128)(2,1)S(1)}, u32[]{:S(2)}, u32[]{:S(2)}) collective-permute-start(bf16[128,2048]{1,0:T(8,128)(2,1)S(1)} %other.3), channel_id=1, source_target_pairs={{0,1},{1,0},{2,3},{3,2},{4,5},{5,4},{6,7},{7,6},{8,9},{9,8},{10,11... | collective-permute-start | bytes 1572872 | tf_op jit(solution)/shard_map/ppermute | solution.py:228
  41.8 22.1 %copy-start.2 = (bf16[32,4096]{1,0:T(8,128)(2,1)S(1)}, bf16[32,4096]{1,0:T(8,128)(2,1)}, u32[]{:S(2)}) copy-start(bf16[32,4096]{1,0:T(8,128)(2,1)} %refs_1_.1) | copy-start | bytes 786436
  41.8 6.4 %collective-permute-start.15 = (bf16[128,2048]{1,0:T(8,128)(2,1)S(1)}, bf16[128,2048]{1,0:T(8,128)(2,1)S(1)}, u32[]{:S(2)}, u32[]{:S(2)}) collective-permute-start(bf16[128,2048]{1,0:T(8,128)(2,1)S(1)} %other.2), channel_id=1, source_target_pairs={{0,1},{1,0},{2,3},{3,2},{4,5},{5,4},{6,7},{7,6},{8,9},{9,8},{10,11... | collective-permute-start | bytes 1572872 | tf_op jit(solution)/shard_map/ppermute | solution.py:228
  44.1 6.4 %collective-permute-start.19 = (bf16[32,2048]{1,0:T(8,128)(2,1)S(1)}, bf16[32,2048]{1,0:T(8,128)(2,1)S(1)}, u32[]{:S(2)}, u32[]{:S(2)}) collective-permute-start(bf16[32,2048]{1,0:T(8,128)(2,1)S(1)} %get-tuple-element.22), channel_id=1, source_target_pairs={{0,2},{2,0},{4,6},{6,4},{8,10},{10,8},{12,14},{14,12},{1,3},{3,1},... | collective-permute-start | bytes 393224 | tf_op jit(solution)/shard_map/ppermute | solution.py:235
  44.5 8.8 %collective-permute-start.17 = (bf16[32,2048]{1,0:T(8,128)(2,1)S(1)}, bf16[32,2048]{1,0:T(8,128)(2,1)S(1)}, u32[]{:S(2)}, u32[]{:S(2)}) collective-permute-start(bf16[32,2048]{1,0:T(8,128)(2,1)S(1)} %get-tuple-element.20), channel_id=1, source_target_pairs={{0,2},{2,0},{4,6},{6,4},{8,10},{10,8},{12,14},{14,12},{1,3},{3,1},... | collective-permute-start | bytes 393224 | tf_op jit(solution)/shard_map/ppermute | solution.py:235
  46.2 9.9 %collective-permute-start.21 = (bf16[32,2048]{1,0:T(8,128)(2,1)S(1)}, bf16[32,2048]{1,0:T(8,128)(2,1)S(1)}, u32[]{:S(2)}, u32[]{:S(2)}) collective-permute-start(bf16[32,2048]{1,0:T(8,128)(2,1)S(1)} %get-tuple-element.24), channel_id=1, source_target_pairs={{0,2},{2,0},{4,6},{6,4},{8,10},{10,8},{12,14},{14,12},{1,3},{3,1},... | collective-permute-start | bytes 393224 | tf_op jit(solution)/shard_map/ppermute | solution.py:235
  46.5 11.6 %collective-permute-start.23 = (bf16[32,2048]{1,0:T(8,128)(2,1)S(1)}, bf16[32,2048]{1,0:T(8,128)(2,1)S(1)}, u32[]{:S(2)}, u32[]{:S(2)}) collective-permute-start(bf16[32,2048]{1,0:T(8,128)(2,1)S(1)} %get-tuple-element.26), channel_id=1, source_target_pairs={{0,2},{2,0},{4,6},{6,4},{8,10},{10,8},{12,14},{14,12},{1,3},{3,1},... | collective-permute-start | bytes 393224 | tf_op jit(solution)/shard_map/ppermute | solution.py:235
  50.5 7.6 %collective-permute-start.20 = (bf16[32,2048]{1,0:T(8,128)(2,1)S(1)}, bf16[32,2048]{1,0:T(8,128)(2,1)S(1)}, u32[]{:S(2)}, u32[]{:S(2)}) collective-permute-start(bf16[32,2048]{1,0:T(8,128)(2,1)S(1)} %add_convert_fusion.2), channel_id=1, source_target_pairs={{0,12},{2,14},{4,0},{6,2},{8,4},{10,6},{12,8},{14,10},{1,13},{3,15... | collective-permute-start | bytes 393224 | tf_op jit(solution)/shard_map/ppermute | solution.py:237
  53.3 10.6 %collective-permute-start.18 = (bf16[32,2048]{1,0:T(8,128)(2,1)S(1)}, bf16[32,2048]{1,0:T(8,128)(2,1)S(1)}, u32[]{:S(2)}, u32[]{:S(2)}) collective-permute-start(bf16[32,2048]{1,0:T(8,128)(2,1)S(1)} %add_convert_fusion.3), channel_id=1, source_target_pairs={{0,8},{2,10},{4,12},{6,14},{8,0},{10,2},{12,4},{14,6},{1,9},{3,11}... | collective-permute-start | bytes 393224 | tf_op jit(solution)/shard_map/ppermute | solution.py:237
  56.1 7.8 %collective-permute-start.22 = (bf16[32,2048]{1,0:T(8,128)(2,1)S(1)}, bf16[32,2048]{1,0:T(8,128)(2,1)S(1)}, u32[]{:S(2)}, u32[]{:S(2)}) collective-permute-start(bf16[32,2048]{1,0:T(8,128)(2,1)S(1)} %add_convert_fusion.1), channel_id=1, source_target_pairs={{0,4},{2,6},{4,8},{6,10},{8,12},{10,14},{12,0},{14,2},{1,5},{3,7},... | collective-permute-start | bytes 393224 | tf_op jit(solution)/shard_map/ppermute | solution.py:237

commit v8 on v7

--- a/solution.py
+++ b/solution.py
@@ -13,7 +13,7 @@
 LEAD_FLOPS = 40_000_000_000
 
 
-def prepare_kernel(half, experts, place_ref, *refs):
+def prepare_kernel(half, experts, *refs):
     out_ref, slot_ref, hidden_ref, ids_ref, scores_ref, sem = refs[4:]
     copies = [
         pltpu.make_async_copy(refs[i], refs[5 + i], sem.at[i]) for i in range(4)
@@ -24,7 +24,7 @@
         copy.wait()
     resid = hidden_ref[...].astype(jnp.float32)
     scale = lax.rsqrt(jnp.mean(resid * resid, axis=-1, keepdims=True) + 1e-06)
-    own = hidden_ref[:, pl.ds(pl.multiple_of(place_ref[1] * half, half), half)]
+    own = hidden_ref[:, pl.ds(pl.multiple_of(lax.axis_index("tp") * half, half), half)]
     out_ref[:, :half] = (own.astype(jnp.float32) * scale).astype(jnp.bfloat16)
     scores = scores_ref[...]
     mixing = scores / jnp.sum(scores, axis=0, keepdims=True)
@@ -49,19 +49,19 @@
     out_ref[:, half:] = coded.T.astype(jnp.bfloat16)
 
 
-def prepare(place, hidden_in, expert_ids, route_scores, expert_slot):
+def prepare(hidden_in, expert_ids, route_scores, expert_slot):
     rows, features = hidden_in.shape
     half = features // 2
     experts = expert_slot.shape[0]
     width = -(-3 * experts // LANES) * LANES
     vmem = pl.BlockSpec(memory_space=pltpu.VMEM)
-    smem, hbm = pl.BlockSpec(memory_space=pltpu.SMEM), pl.BlockSpec(memory_space=pltpu.HBM)
+    hbm = pl.BlockSpec(memory_space=pltpu.HBM)
     far = [expert_slot, hidden_in, expert_ids.T, route_scores.T]
     far = [pltpu.with_memory_space_constraint(a, pltpu.HBM) for a in far]
     return pl.pallas_call(
         functools.partial(prepare_kernel, half, experts),
         out_shape=jax.ShapeDtypeStruct((rows, half + width), jnp.bfloat16),
-        in_specs=[smem, hbm, hbm, hbm, hbm],
+        in_specs=[hbm] * 4,
         out_specs=vmem,
         scratch_shapes=[
             pltpu.SMEM(expert_slot.shape, jnp.int32),
@@ -75,7 +75,7 @@
             flops=LEAD_FLOPS, bytes_accessed=2 * rows * features, transcendentals=0
         ),
         name="prepare",
-    )(place, *far)
+    )(*far)
 
 
 def fill_rows(half, blocks, refs, own, other, coded):
@@ -87,11 +87,11 @@
         coded[rows, :] = refs[i][:, half:].astype(jnp.float32)
 
 
-def hidden_units(half, experts, place_ref, gate_ref, up_ref, own, other, coded, out_refs):
+def hidden_units(half, experts, gate_ref, up_ref, own, other, coded, out_refs):
     local, _, units = gate_ref.shape
-    first_slot = place_ref[0] * local
-    own_at = pl.ds(pl.multiple_of(place_ref[1] * half, half), half)
-    other_at = pl.ds(pl.multiple_of((1 - place_ref[1]) * half, half), half)
+    first_slot = lax.axis_index("sect") * local
+    own_at = pl.ds(pl.multiple_of(lax.axis_index("tp") * half, half), half)
+    other_at = pl.ds(pl.multiple_of((1 - lax.axis_index("tp")) * half, half), half)
     slot = lax.rem(lax.broadcasted_iota(jnp.int32, coded.shape, 1), experts)
     block = min(units, 256)
     for e in range(local):
@@ -116,14 +116,14 @@
                 row += out_ref.shape[0]
 
 
-def hidden_kernel(half, experts, blocks, place_ref, *refs):
+def hidden_kernel(half, experts, blocks, *refs):
     gate_ref, up_ref, *out_refs = refs[2 * blocks : 2 * blocks + 4]
     own, other, coded = refs[2 * blocks + 4 :]
     fill_rows(half, blocks, refs, own, other, coded)
-    hidden_units(half, experts, place_ref, gate_ref, up_ref, own, other, coded, out_refs)
-
-
-def run_hidden(place, own, other, gate, up, experts, first):
+    hidden_units(half, experts, gate_ref, up_ref, own, other, coded, out_refs)
+
+
+def run_hidden(own, other, gate, up, experts, first):
     blocks = len(own)
     local, features, width = gate.shape
     rows, half, units = blocks * own[0].shape[0], features // 2, local * width
@@ -134,7 +134,7 @@
             jax.ShapeDtypeStruct((count * own[0].shape[0], units), jnp.bfloat16)
             for count in (first, blocks - first)
         ],
-        in_specs=[pl.BlockSpec(memory_space=pltpu.SMEM)] + [vmem] * (2 * blocks + 2),
+        in_specs=[vmem] * (2 * blocks + 2),
         out_specs=[vmem] * 2,
         scratch_shapes=[
             pltpu.VMEM((rows, half), jnp.bfloat16),
@@ -146,14 +146,14 @@
             flops=4 * rows * units * features, bytes_accessed=4 * rows * half, transcendentals=rows * units
         ),
         name="hidden",
-    )(place, *own, *other, gate, up)
-
-
-def down_kernel(mine, place_ref, hidden_ref, down_ref, *refs):
+    )(*own, *other, gate, up)
+
+
+def down_kernel(mine, hidden_ref, down_ref, *refs):
     out_refs = refs[mine:]
     local, units, features = down_ref.shape
     half = features // 2
-    core = place_ref[1] if mine else 1 - place_ref[1]
+    core = lax.axis_index("tp") if mine else 1 - lax.axis_index("tp")
     tokens = out_refs[0].shape[0]
     for at in range(0, half, WIDTH):
         cut = pl.ds(pl.multiple_of(core * half + at, WIDTH), WIDTH)
@@ -168,21 +168,21 @@
             out_ref[:, at : at + WIDTH] = total[i * tokens : (i + 1) * tokens].astype(out_ref.dtype)
 
 
-def run_down(place, hidden, down, received, kinds):
+def run_down(hidden, down, received, kinds):
     rows, half = hidden.shape[0], down.shape[2] // 2
     vmem = pl.BlockSpec(memory_space=pltpu.VMEM)
     extra = [] if received is None else [received]
     return pl.pallas_call(
         functools.partial(down_kernel, len(extra)),
         out_shape=[jax.ShapeDtypeStruct((rows // len(kinds), half), kind) for kind in kinds],
-        in_specs=[pl.BlockSpec(memory_space=pltpu.SMEM)] + [vmem] * (2 + len(extra)),
+        in_specs=[vmem] * (2 + len(extra)),
         out_specs=[vmem] * len(kinds),
         compiler_params=pltpu.CompilerParams(vmem_limit_bytes=LIMIT),
         cost_estimate=pl.CostEstimate(
             flops=2 * rows * half, bytes_accessed=4 * rows, transcendentals=0
         ),
         name="mine" if extra else "other",
-    )(place, hidden, down, *extra)
+    )(hidden, down, *extra)
 
 
 def after(value, *others):
@@ -197,7 +197,6 @@
     devices = lax.axis_size("sect")
     half = feature_count // 2
     core = lax.axis_index("tp")
-    sect = lax.axis_index("sect")
     inner = 2
     outer = devices // inner
 
@@ -210,10 +209,9 @@
 
     across = [(d, d ^ 1) for d in range(devices)]
     cores = [(0, 1), (1, 0)]
-    place = jnp.stack([sect, core]).astype(jnp.int32)
     bf16, f32 = jnp.bfloat16, jnp.float32
 
-    packed = prepare(place, hidden_in, expert_ids, route_scores, expert_slot)
+    packed = prepare(hidden_in, expert_ids, route_scores, expert_slot)
     order = sorted(range(1, outer), key=lambda k: -min(k, outer - k))
     same, opposite = {0: packed}, {0: lax.ppermute(packed, "sect", across)}
     for k in order[::-1]:
@@ -223,13 +221,13 @@
         opposite[k] = lax.ppermute(same[k], "sect", across)
     blocks = [side[k] for side in (opposite, same) for k in range(outer)]
     others = [lax.ppermute(block, "tp", cores) for block in blocks]
-    groups = run_hidden(place, blocks, others, gate_matrix, up_matrix, experts, outer)
+    groups = run_hidden(blocks, others, gate_matrix, up_matrix, experts, outer)
     sent = [
-        lax.ppermute(run_down(place, hidden, down_matrix, None, [bf16])[0], "tp", cores)
+        lax.ppermute(run_down(hidden, down_matrix, None, [bf16])[0], "tp", cores)
         for hidden in groups
     ]
-    far_sum = run_down(place, groups[0], down_matrix, sent[0], [bf16] * outer)
-    near_sum = run_down(place, groups[1], down_matrix, sent[1], [f32] * outer)
+    far_sum = run_down(groups[0], down_matrix, sent[0], [bf16] * outer)
+    near_sum = run_down(groups[1], down_matrix, sent[1], [f32] * outer)
     result = lax.dynamic_slice_in_dim(hidden_in, core * half, half, 1).astype(f32)
     for k in order + [0]:
         block = near_sum[k] + lax.ppermute(far_sum[k], "sect", across).astype(f32)

time: 64.8 us -> 61 us (0.941)
  Pallas kernels: 18.8 us -> 15.5 us
  starting transfers between devices: 20.6 us -> 18.9 us
  waiting for transfers between devices: 24.1 us -> 25.5 us
    ppermute x4, waiting for transfers between devices: 3.75 us -> 6.75 us  [on_device(): block = near_sum[k] + lax.ppermute(far_sum[k], 'sect', across).astype(f32)]
    ppermute x3, starting transfers between devices: 4.21 us -> 1.75 us  [on_device(): block = lax.ppermute(block.astype(bf16), 'sect', along(-k)).astype(f32)]
    pallas_call x4, Pallas kernels: 7.32 us -> 5.16 us  [run_down(): pl.pallas_call(functools.partial(down_kernel, len(extra)), out_shape=[jax...]
    ppermute x3, waiting for transfers between devices: 5.78 us -> 4.84 us  [on_device(): block = lax.ppermute(block.astype(bf16), 'sect', along(-k)).astype(f32)]
    ppermute x3, waiting for transfers between devices: 9.06 us -> 8.21 us  [on_device(): same[k] = lax.ppermute(block, 'sect', along(k))]
    ppermute x8, starting transfers between devices: 0.63 us -> 1.38 us  [on_device(): others = [lax.ppermute(block, 'tp', cores) for block in blocks]]
  transfers between devices with their start and end apart: 24 -> 24, of which waited for: 12 -> 14; matrix products, arithmetic and copies ran while one was open for 0% -> 0% of each run, Pallas kernels for 9% -> 6%
where the time goes in v8:
time: 61 us; the launch traced here: 60.9 us
  waiting for transfers between devices  25.5 us (42%)
  starting transfers between devices  18.9 us (31%)
  Pallas kernels  15.5 us (25%)
  other arithmetic  0.83 us (1%)
    pallas_call x1, Pallas kernels, run_hidden(): pl.pallas_call(functools.partial(hidden_kernel, half, experts, blocks), o...  8.91 us
    ppermute x3, waiting for transfers between devices, on_device(): same[k] = lax.ppermute(block, 'sect', along(k))  8.21 us
    ppermute x4, waiting for transfers between devices, on_device(): block = near_sum[k] + lax.ppermute(far_sum[k], 'sect', across).astype(f32)  6.75 us
    ppermute x3, starting transfers between devices, on_device(): same[k] = lax.ppermute(block, 'sect', along(k))  6.41 us
    pallas_call x4, Pallas kernels, run_down(): pl.pallas_call(functools.partial(down_kernel, len(extra)), out_shape=[jax...  5.16 us
    ppermute x3, waiting for transfers between devices, on_device(): block = lax.ppermute(block.astype(bf16), 'sect', along(-k)).astype(f32)  4.84 us
    ppermute x3, waiting for transfers between devices, on_device(): opposite[k] = lax.ppermute(same[k], 'sect', across)  4.27 us
    ppermute x4, starting transfers between devices, on_device(): block = near_sum[k] + lax.ppermute(far_sum[k], 'sect', across).astype(f32)  4.12 us
  transfers between devices with their start and end apart: 24, of which 14 were waited for; matrix products, arithmetic and copies ran while one was open for 0% of the time, Pallas kernels for 6%

profile of v8, /device:TPU:0, one launch (start us, length us, event | category | flops | bytes accessed | tf_op | source)
XLA Modules:
  0.0 60.9 jit_solution(2738695986809620727)
XLA Ops:
  0.0 0.0 slice-start.3
  0.0 1.4 %prepare.1.refs_4_ = bf16[32,2176]{1,0:T(8,128)(2,1)S(1)} custom-call(s32[32]{0:T(128)} %refs_0_.1, bf16[32,4096]{1,0:T(8,128)(2,1)} %refs_1_.1, s32[8,32]{1,0:T(8,128)} %bitcast.4, f32[8,32]{1,0:T(8,128)} %bitcast.5), custom_call_target="tpu_custom_call" | custom-call | flops 40000000000 | bytes 262144 | tf_op jit(solution)/shard_map/prepare/pallas_call | solution.py:61
  1.4 3.0 %collective-permute-start = (bf16[32,2176]{1,0:T(8,128)(2,1)S(1)}, bf16[32,2176]{1,0:T(8,128)(2,1)S(1)}, u32[]{:S(2)}, u32[]{:S(2)}) collective-permute-start(bf16[32,2176]{1,0:T(8,128)(2,1)S(1)} %prepare.1.refs_4_), channel_id=1, source_target_pairs={{0,2},{2,0},{4,6},{6,4},{8,10},{10,8},{12,14},{14,12},{1,3},{3,1},... | collective-permute-start | bytes 417800 | tf_op jit(solution)/shard_map/ppermute | solution.py:216
  4.5 3.6 %collective-permute-start.5 = (bf16[32,2176]{1,0:T(8,128)(2,1)S(1)}, bf16[32,2176]{1,0:T(8,128)(2,1)S(1)}, u32[]{:S(2)}, u32[]{:S(2)}) collective-permute-start(bf16[32,2176]{1,0:T(8,128)(2,1)S(1)} %prepare.1.refs_4_), channel_id=1, source_target_pairs={{0,12},{2,14},{4,0},{6,2},{8,4},{10,6},{12,8},{14,10},{1,13},{3,15... | collective-permute-start | bytes 417800 | tf_op jit(solution)/shard_map/ppermute | solution.py:219
  8.1 0.0 collective-permute-start.1
  8.1 0.0 collective-permute-start.11
  8.1 0.1 collective-permute-done.refs_0_
  8.2 2.8 %collective-permute-start.3 = (bf16[32,2176]{1,0:T(8,128)(2,1)S(1)}, bf16[32,2176]{1,0:T(8,128)(2,1)S(1)}, u32[]{:S(2)}, u32[]{:S(2)}) collective-permute-start(bf16[32,2176]{1,0:T(8,128)(2,1)S(1)} %prepare.1.refs_4_), channel_id=1, source_target_pairs={{0,8},{2,10},{4,12},{6,14},{8,0},{10,2},{12,4},{14,6},{1,9},{3,11}... | collective-permute-start | bytes 417800 | tf_op jit(solution)/shard_map/ppermute | solution.py:219
  11.0 1.2 %collective-permute-done.5.refs_7_ = bf16[32,2176]{1,0:T(8,128)(2,1)S(1)} collective-permute-done((bf16[32,2176]{1,0:T(8,128)(2,1)S(1)}, bf16[32,2176]{1,0:T(8,128)(2,1)S(1)}, u32[]{:S(2)}, u32[]{:S(2)}) %collective-permute-start.5) | collective-permute-done | bytes 139296 | tf_op jit(solution)/shard_map/ppermute | solution.py:219
  12.2 0.5 collective-permute-start.6
  12.7 3.6 %collective-permute-done.1.refs_5_ = bf16[32,2176]{1,0:T(8,128)(2,1)S(1)} collective-permute-done((bf16[32,2176]{1,0:T(8,128)(2,1)S(1)}, bf16[32,2176]{1,0:T(8,128)(2,1)S(1)}, u32[]{:S(2)}, u32[]{:S(2)}) %collective-permute-start.1) | collective-permute-done | bytes 139296 | tf_op jit(solution)/shard_map/ppermute | solution.py:219
  16.3 0.5 collective-permute-start.2
  16.8 0.0 collective-permute-start.12
  16.8 0.0 collective-permute-done.11.refs_12_
  16.8 0.5 collective-permute-start.14
  17.4 3.4 %collective-permute-done.3.refs_6_ = bf16[32,2176]{1,0:T(8,128)(2,1)S(1)} collective-permute-done((bf16[32,2176]{1,0:T(8,128)(2,1)S(1)}, bf16[32,2176]{1,0:T(8,128)(2,1)S(1)}, u32[]{:S(2)}, u32[]{:S(2)}) %collective-permute-start.3) | collective-permute-done | bytes 139296 | tf_op jit(solution)/shard_map/ppermute | solution.py:219
  20.7 0.5 collective-permute-start.4
  21.2 0.0 collective-permute-done.6.refs_3_
  21.2 0.0 collective-permute-start.7
  21.2 0.2 collective-permute-done.2.refs_1_
  21.4 0.3 collective-permute-start.13
  21.7 0.0 collective-permute-done.12.refs_13_
  21.7 0.2 collective-permute-start.10
  21.9 0.0 collective-permute-done.14.refs_15_
  21.9 0.3 collective-permute-start.8
  22.3 4.1 %collective-permute-done.4.refs_2_ = bf16[32,2176]{1,0:T(8,128)(2,1)S(1)} collective-permute-done((bf16[32,2176]{1,0:T(8,128)(2,1)S(1)}, bf16[32,2176]{1,0:T(8,128)(2,1)S(1)}, u32[]{:S(2)}, u32[]{:S(2)}) %collective-permute-start.4) | collective-permute-done | bytes 139296 | tf_op jit(solution)/shard_map/ppermute | solution.py:221
  26.4 0.0 collective-permute-start.9
  26.4 0.0 collective-permute-done.7.refs_8_
  26.4 0.0 collective-permute-done.13.refs_14_
  26.4 0.0 collective-permute-done.10.refs_11_
  26.4 0.0 collective-permute-done.8.refs_9_
  26.4 1.3 %collective-permute-done.9.refs_10_ = bf16[32,2176]{1,0:T(8,128)(2,1)S(1)} collective-permute-done((bf16[32,2176]{1,0:T(8,128)(2,1)S(1)}, bf16[32,2176]{1,0:T(8,128)(2,1)S(1)}, u32[]{:S(2)}, u32[]{:S(2)}) %collective-permute-start.9) | collective-permute-done | bytes 139296 | tf_op jit(solution)/shard_map/ppermute | solution.py:223
  27.7 0.0 copy-done
  27.7 0.0 copy-done.1
  27.7 8.9 %hidden.1 = (bf16[128,2048]{1,0:T(8,128)(2,1)S(1)}, bf16[128,2048]{1,0:T(8,128)(2,1)S(1)}) custom-call(bf16[32,2176]{1,0:T(8,128)(2,1)S(1)} %collective-permute-done.refs_0_, bf16[32,2176]{1,0:T(8,128)(2,1)S(1)} %collective-permute-done.2.refs_1_, bf16[32,2176]{1,0:T(8,128)(2,1)S(1)} %collective-permute-done.4.refs_2_, ...), custom_call_target="tpu_custom_call" | custom-call | flops 8589934592 | bytes 2097152 | tf_op jit(solution)/shard_map/hidden/pallas_call | solution.py:131
  36.6 0.0 slice-done
  36.6 0.0 slice-done.1
  36.7 0.0 slice-done.2
  36.7 0.0 slice-done.3
  36.7 1.3 %other.3 = bf16[128,2048]{1,0:T(8,128)(2,1)S(1)} custom-call(bf16[128,2048]{1,0:T(8,128)(2,1)S(1)} %get-tuple-element.19.hidden_ref, bf16[4,512,4096]{2,1,0:T(8,128)(2,1)S(1)} %bitcast.3), custom_call_target="tpu_custom_call" | custom-call | flops 524288 | bytes 512 | tf_op jit(solution)/shard_map/other/pallas_call | solution.py:175
  38.0 0.2 collective-permute-start.16
  38.2 1.3 %other.2 = bf16[128,2048]{1,0:T(8,128)(2,1)S(1)} custom-call(bf16[128,2048]{1,0:T(8,128)(2,1)S(1)} %get-tuple-element.17.hidden_ref, bf16[4,512,4096]{2,1,0:T(8,128)(2,1)S(1)} %bitcast.3), custom_call_target="tpu_custom_call" | custom-call | flops 524288 | bytes 512 | tf_op jit(solution)/shard_map/other/pallas_call | solution.py:175
  39.5 0.0 copy-start.2
  39.5 0.4 collective-permute-start.15
  39.9 0.0 collective-permute-done.16.refs_0_
  40.0 1.3 %mine.3 = (bf16[32,2048]{1,0:T(8,128)(2,1)S(1)}, bf16[32,2048]{1,0:T(8,128)(2,1)S(1)}, bf16[32,2048]{1,0:T(8,128)(2,1)S(1)}, bf16[32,2048]{1,0:T(8,128)(2,1)S(1)}) custom-call(bf16[128,2048]{1,0:T(8,128)(2,1)S(1)} %get-tuple-element.19.hidden_ref, bf16[4,512,4096]{2,1,0:T(8,128)(2,1)S(1)} %bitcast.3, bf16[128,2048]{1,0:T(8,128)(2,1)S(1)} %collective-permute-done.16.refs_0_), custom_call_target="tpu_custom_call" | custom-call | flops 524288 | bytes 512 | tf_op jit(solution)/shard_map/mine/pallas_call | solution.py:175
  41.3 0.5 collective-permute-start.17
  41.8 1.6 %collective-permute-start.19 = (bf16[32,2048]{1,0:T(8,128)(2,1)S(1)}, bf16[32,2048]{1,0:T(8,128)(2,1)S(1)}, u32[]{:S(2)}, u32[]{:S(2)}) collective-permute-start(bf16[32,2048]{1,0:T(8,128)(2,1)S(1)} %get-tuple-element.22), channel_id=1, source_target_pairs={{0,2},{2,0},{4,6},{6,4},{8,10},{10,8},{12,14},{14,12},{1,3},{3,1},... | collective-permute-start | bytes 393224 | tf_op jit(solution)/shard_map/ppermute | solution.py:233
  43.4 0.5 collective-permute-start.21
  43.8 1.6 %collective-permute-start.23 = (bf16[32,2048]{1,0:T(8,128)(2,1)S(1)}, bf16[32,2048]{1,0:T(8,128)(2,1)S(1)}, u32[]{:S(2)}, u32[]{:S(2)}) collective-permute-start(bf16[32,2048]{1,0:T(8,128)(2,1)S(1)} %get-tuple-element.26), channel_id=1, source_target_pairs={{0,2},{2,0},{4,6},{6,4},{8,10},{10,8},{12,14},{14,12},{1,3},{3,1},... | collective-permute-start | bytes 393224 | tf_op jit(solution)/shard_map/ppermute | solution.py:233
  45.4 0.0 collective-permute-done.15.refs_0_
  45.4 1.3 %mine.2 = (f32[32,2048]{1,0:T(8,128)S(1)}, f32[32,2048]{1,0:T(8,128)S(1)}, f32[32,2048]{1,0:T(8,128)S(1)}, f32[32,2048]{1,0:T(8,128)S(1)}) custom-call(bf16[128,2048]{1,0:T(8,128)(2,1)S(1)} %get-tuple-element.17.hidden_ref, bf16[4,512,4096]{2,1,0:T(8,128)(2,1)S(1)} %bitcast.3, bf16[128,2048]{1,0:T(8,128)(2,1)S(1)} %collective-permute-done.15.refs_0_), custom_call_target="tpu_custom_call" | custom-call | flops 524288 | bytes 512 | tf_op jit(solution)/shard_map/mine/pallas_call | solution.py:175
  46.7 1.0 %collective-permute-done.17 = bf16[32,2048]{1,0:T(8,128)(2,1)S(1)} collective-permute-done((bf16[32,2048]{1,0:T(8,128)(2,1)S(1)}, bf16[32,2048]{1,0:T(8,128)(2,1)S(1)}, u32[]{:S(2)}, u32[]{:S(2)}) %collective-permute-start.17) | collective-permute-done | bytes 131104 | tf_op jit(solution)/shard_map/ppermute | solution.py:233
  47.7 0.1 collective-permute-start.18
  47.8 2.7 %collective-permute-done.19 = bf16[32,2048]{1,0:T(8,128)(2,1)S(1)} collective-permute-done((bf16[32,2048]{1,0:T(8,128)(2,1)S(1)}, bf16[32,2048]{1,0:T(8,128)(2,1)S(1)}, u32[]{:S(2)}, u32[]{:S(2)}) %collective-permute-start.19) | collective-permute-done | bytes 131104 | tf_op jit(solution)/shard_map/ppermute | solution.py:233
  50.5 1.6 %collective-permute-start.20 = (bf16[32,2048]{1,0:T(8,128)(2,1)S(1)}, bf16[32,2048]{1,0:T(8,128)(2,1)S(1)}, u32[]{:S(2)}, u32[]{:S(2)}) collective-permute-start(bf16[32,2048]{1,0:T(8,128)(2,1)S(1)} %add_convert_fusion.2), channel_id=1, source_target_pairs={{0,12},{2,14},{4,0},{6,2},{8,4},{10,6},{12,8},{14,10},{1,13},{3,15... | collective-permute-start | bytes 393224 | tf_op jit(solution)/shard_map/ppermute | solution.py:235
  52.1 1.2 %collective-permute-done.21 = bf16[32,2048]{1,0:T(8,128)(2,1)S(1)} collective-permute-done((bf16[32,2048]{1,0:T(8,128)(2,1)S(1)}, bf16[32,2048]{1,0:T(8,128)(2,1)S(1)}, u32[]{:S(2)}, u32[]{:S(2)}) %collective-permute-start.21) | collective-permute-done | bytes 131104 | tf_op jit(solution)/shard_map/ppermute | solution.py:233
  53.3 0.1 collective-permute-start.22
  53.4 1.9 %collective-permute-done.23 = bf16[32,2048]{1,0:T(8,128)(2,1)S(1)} collective-permute-done((bf16[32,2048]{1,0:T(8,128)(2,1)S(1)}, bf16[32,2048]{1,0:T(8,128)(2,1)S(1)}, u32[]{:S(2)}, u32[]{:S(2)}) %collective-permute-start.23) | collective-permute-done | bytes 131104 | tf_op jit(solution)/shard_map/ppermute | solution.py:233
  55.3 0.4 collective-permute-done.18
  55.7 0.6 %collective-permute-done.20 = bf16[32,2048]{1,0:T(8,128)(2,1)S(1)} collective-permute-done((bf16[32,2048]{1,0:T(8,128)(2,1)S(1)}, bf16[32,2048]{1,0:T(8,128)(2,1)S(1)}, u32[]{:S(2)}, u32[]{:S(2)}) %collective-permute-start.20) | collective-permute-done | bytes 131104 | tf_op jit(solution)/shard_map/ppermute | solution.py:235
  56.3 3.8 %collective-permute-done.22 = bf16[32,2048]{1,0:T(8,128)(2,1)S(1)} collective-permute-done((bf16[32,2048]{1,0:T(8,128)(2,1)S(1)}, bf16[32,2048]{1,0:T(8,128)(2,1)S(1)}, u32[]{:S(2)}, u32[]{:S(2)}) %collective-permute-start.22) | collective-permute-done | bytes 131104 | tf_op jit(solution)/shard_map/ppermute | solution.py:235
  60.1 0.0 copy-done.2
  60.1 0.8 %add_convert_fusion = bf16[32,2048]{1,0:T(8,128)(2,1)} fusion(f32[32,2048]{1,0:T(8,128)S(1)} %get-tuple-element.25, bf16[32,2048]{1,0:T(8,128)(2,1)S(1)} %collective-permute-done.23, bf16[32,2048]{1,0:T(8,128)(2,1)S(1)} %collective-permute-done.22, bf16[32,2048]{1,0:T(8,128)(2,1)S(1)} %collective-permute-done.20, ...), kind=kLoop, calls=%fused_computation | loop fusion | flops 720896 | bytes 1048580 | tf_op jit(solution)/shard_map/convert_element_type | solution.py:237
  (9 shorter events, 0.1 us)
Async XLA Ops:
  0.0 36.6 %slice-start = ((s8[16777216]{0:T(1024)(128)(4,1)}), s8[4194304]{0:T(1024)(128)(4,1)S(1)}, s32[]{:S(2)}) async-start(s8[16777216]{0:T(1024)(128)(4,1)} %bitcast.2), calls=%async_computation | async-start | bytes 8388608
  0.0 27.7 %copy-start = (bf16[4,4096,512]{2,1,0:T(8,128)(2,1)S(1)}, bf16[4,4096,512]{2,1,0:T(8,128)(2,1)}, u32[]{:S(2)}) copy-start(bf16[4,4096,512]{2,1,0:T(8,128)(2,1)} %refs_16_.1) | copy-start | bytes 50331652
  0.0 27.7 %copy-start.1 = (bf16[4,4096,512]{2,1,0:T(8,128)(2,1)S(1)}, bf16[4,4096,512]{2,1,0:T(8,128)(2,1)}, u32[]{:S(2)}) copy-start(bf16[4,4096,512]{2,1,0:T(8,128)(2,1)} %refs_17_.1) | copy-start | bytes 50331652
  0.0 36.6 %slice-start.1 = ((s8[16777216]{0:T(1024)(128)(4,1)}), s8[4194304]{0:T(1024)(128)(4,1)S(1)}, s32[]{:S(2)}) async-start(s8[16777216]{0:T(1024)(128)(4,1)} %bitcast.2), calls=%async_computation.1 | async-start | bytes 8388608
  0.0 36.6 %slice-start.2 = ((s8[16777216]{0:T(1024)(128)(4,1)}), s8[4194304]{0:T(1024)(128)(4,1)S(1)}, s32[]{:S(2)}) async-start(s8[16777216]{0:T(1024)(128)(4,1)} %bitcast.2), calls=%async_computation.2 | async-start | bytes 8388608
  0.0 36.7 %slice-start.3 = ((s8[16777216]{0:T(1024)(128)(4,1)}), s8[4194304]{0:T(1024)(128)(4,1)S(1)}, s32[]{:S(2)}) async-start(s8[16777216]{0:T(1024)(128)(4,1)} %bitcast.2), calls=%async_computation.3 | async-start | bytes 8388608
  1.4 6.7 %collective-permute-start = (bf16[32,2176]{1,0:T(8,128)(2,1)S(1)}, bf16[32,2176]{1,0:T(8,128)(2,1)S(1)}, u32[]{:S(2)}, u32[]{:S(2)}) collective-permute-start(bf16[32,2176]{1,0:T(8,128)(2,1)S(1)} %prepare.1.refs_4_), channel_id=1, source_target_pairs={{0,2},{2,0},{4,6},{6,4},{8,10},{10,8},{12,14},{14,12},{1,3},{3,1},... | collective-permute-start | bytes 417800 | tf_op jit(solution)/shard_map/ppermute | solution.py:216
  4.5 7.7 %collective-permute-start.5 = (bf16[32,2176]{1,0:T(8,128)(2,1)S(1)}, bf16[32,2176]{1,0:T(8,128)(2,1)S(1)}, u32[]{:S(2)}, u32[]{:S(2)}) collective-permute-start(bf16[32,2176]{1,0:T(8,128)(2,1)S(1)} %prepare.1.refs_4_), channel_id=1, source_target_pairs={{0,12},{2,14},{4,0},{6,2},{8,4},{10,6},{12,8},{14,10},{1,13},{3,15... | collective-permute-start | bytes 417800 | tf_op jit(solution)/shard_map/ppermute | solution.py:219
  8.1 8.2 %collective-permute-start.1 = (bf16[32,2176]{1,0:T(8,128)(2,1)S(1)}, bf16[32,2176]{1,0:T(8,128)(2,1)S(1)}, u32[]{:S(2)}, u32[]{:S(2)}) collective-permute-start(bf16[32,2176]{1,0:T(8,128)(2,1)S(1)} %prepare.1.refs_4_), channel_id=1, source_target_pairs={{0,4},{2,6},{4,8},{6,10},{8,12},{10,14},{12,0},{14,2},{1,5},{3,7},... | collective-permute-start | bytes 417800 | tf_op jit(solution)/shard_map/ppermute | solution.py:219
  8.1 8.8 %collective-permute-start.11 = (bf16[32,2176]{1,0:T(8,128)(2,1)S(1)}, bf16[32,2176]{1,0:T(8,128)(2,1)S(1)}, u32[]{:S(2)}, u32[]{:S(2)}) collective-permute-start(bf16[32,2176]{1,0:T(8,128)(2,1)S(1)} %prepare.1.refs_4_), channel_id=1, source_target_pairs={{0,1},{1,0},{2,3},{3,2},{4,5},{5,4},{6,7},{7,6},{8,9},{9,8},{10,11... | collective-permute-start | bytes 417800 | tf_op jit(solution)/shard_map/ppermute | solution.py:223
  8.2 12.5 %collective-permute-start.3 = (bf16[32,2176]{1,0:T(8,128)(2,1)S(1)}, bf16[32,2176]{1,0:T(8,128)(2,1)S(1)}, u32[]{:S(2)}, u32[]{:S(2)}) collective-permute-start(bf16[32,2176]{1,0:T(8,128)(2,1)S(1)} %prepare.1.refs_4_), channel_id=1, source_target_pairs={{0,8},{2,10},{4,12},{6,14},{8,0},{10,2},{12,4},{14,6},{1,9},{3,11}... | collective-permute-start | bytes 417800 | tf_op jit(solution)/shard_map/ppermute | solution.py:219
  12.2 9.0 %collective-permute-start.6 = (bf16[32,2176]{1,0:T(8,128)(2,1)S(1)}, bf16[32,2176]{1,0:T(8,128)(2,1)S(1)}, u32[]{:S(2)}, u32[]{:S(2)}) collective-permute-start(bf16[32,2176]{1,0:T(8,128)(2,1)S(1)} %collective-permute-done.5.refs_7_), channel_id=1, source_target_pairs={{0,2},{2,0},{4,6},{6,4},{8,10},{10,8},{12,14},{14,12},{1,3},{3,1},... | collective-permute-start | bytes 417800 | tf_op jit(solution)/shard_map/ppermute | solution.py:221
  16.3 5.1 %collective-permute-start.2 = (bf16[32,2176]{1,0:T(8,128)(2,1)S(1)}, bf16[32,2176]{1,0:T(8,128)(2,1)S(1)}, u32[]{:S(2)}, u32[]{:S(2)}) collective-permute-start(bf16[32,2176]{1,0:T(8,128)(2,1)S(1)} %collective-permute-done.1.refs_5_), channel_id=1, source_target_pairs={{0,2},{2,0},{4,6},{6,4},{8,10},{10,8},{12,14},{14,12},{1,3},{3,1},... | collective-permute-start | bytes 417800 | tf_op jit(solution)/shard_map/ppermute | solution.py:221
  16.8 4.9 %collective-permute-start.12 = (bf16[32,2176]{1,0:T(8,128)(2,1)S(1)}, bf16[32,2176]{1,0:T(8,128)(2,1)S(1)}, u32[]{:S(2)}, u32[]{:S(2)}) collective-permute-start(bf16[32,2176]{1,0:T(8,128)(2,1)S(1)} %collective-permute-done.1.refs_5_), channel_id=1, source_target_pairs={{0,1},{1,0},{2,3},{3,2},{4,5},{5,4},{6,7},{7,6},{8,9},{9,8},{10,11... | collective-permute-start | bytes 417800 | tf_op jit(solution)/shard_map/ppermute | solution.py:223
  16.8 5.1 %collective-permute-start.14 = (bf16[32,2176]{1,0:T(8,128)(2,1)S(1)}, bf16[32,2176]{1,0:T(8,128)(2,1)S(1)}, u32[]{:S(2)}, u32[]{:S(2)}) collective-permute-start(bf16[32,2176]{1,0:T(8,128)(2,1)S(1)} %collective-permute-done.5.refs_7_), channel_id=1, source_target_pairs={{0,1},{1,0},{2,3},{3,2},{4,5},{5,4},{6,7},{7,6},{8,9},{9,8},{10,11... | collective-permute-start | bytes 417800 | tf_op jit(solution)/shard_map/ppermute | solution.py:223
  20.7 5.6 %collective-permute-start.4 = (bf16[32,2176]{1,0:T(8,128)(2,1)S(1)}, bf16[32,2176]{1,0:T(8,128)(2,1)S(1)}, u32[]{:S(2)}, u32[]{:S(2)}) collective-permute-start(bf16[32,2176]{1,0:T(8,128)(2,1)S(1)} %collective-permute-done.3.refs_6_), channel_id=1, source_target_pairs={{0,2},{2,0},{4,6},{6,4},{8,10},{10,8},{12,14},{14,12},{1,3},{3,1},... | collective-permute-start | bytes 417800 | tf_op jit(solution)/shard_map/ppermute | solution.py:221
  21.2 5.1 %collective-permute-start.7 = (bf16[32,2176]{1,0:T(8,128)(2,1)S(1)}, bf16[32,2176]{1,0:T(8,128)(2,1)S(1)}, u32[]{:S(2)}, u32[]{:S(2)}) collective-permute-start(bf16[32,2176]{1,0:T(8,128)(2,1)S(1)} %collective-permute-done.refs_0_), channel_id=1, source_target_pairs={{0,1},{1,0},{2,3},{3,2},{4,5},{5,4},{6,7},{7,6},{8,9},{9,8},{10,11... | collective-permute-start | bytes 417800 | tf_op jit(solution)/shard_map/ppermute | solution.py:223
  21.4 5.0 %collective-permute-start.13 = (bf16[32,2176]{1,0:T(8,128)(2,1)S(1)}, bf16[32,2176]{1,0:T(8,128)(2,1)S(1)}, u32[]{:S(2)}, u32[]{:S(2)}) collective-permute-start(bf16[32,2176]{1,0:T(8,128)(2,1)S(1)} %collective-permute-done.3.refs_6_), channel_id=1, source_target_pairs={{0,1},{1,0},{2,3},{3,2},{4,5},{5,4},{6,7},{7,6},{8,9},{9,8},{10,11... | collective-permute-start | bytes 417800 | tf_op jit(solution)/shard_map/ppermute | solution.py:223
  21.7 4.6 %collective-permute-start.10 = (bf16[32,2176]{1,0:T(8,128)(2,1)S(1)}, bf16[32,2176]{1,0:T(8,128)(2,1)S(1)}, u32[]{:S(2)}, u32[]{:S(2)}) collective-permute-start(bf16[32,2176]{1,0:T(8,128)(2,1)S(1)} %collective-permute-done.6.refs_3_), channel_id=1, source_target_pairs={{0,1},{1,0},{2,3},{3,2},{4,5},{5,4},{6,7},{7,6},{8,9},{9,8},{10,11... | collective-permute-start | bytes 417800 | tf_op jit(solution)/shard_map/ppermute | solution.py:223
  21.9 4.5 %collective-permute-start.8 = (bf16[32,2176]{1,0:T(8,128)(2,1)S(1)}, bf16[32,2176]{1,0:T(8,128)(2,1)S(1)}, u32[]{:S(2)}, u32[]{:S(2)}) collective-permute-start(bf16[32,2176]{1,0:T(8,128)(2,1)S(1)} %collective-permute-done.2.refs_1_), channel_id=1, source_target_pairs={{0,1},{1,0},{2,3},{3,2},{4,5},{5,4},{6,7},{7,6},{8,9},{9,8},{10,11... | collective-permute-start | bytes 417800 | tf_op jit(solution)/shard_map/ppermute | solution.py:223
  26.4 1.4 %collective-permute-start.9 = (bf16[32,2176]{1,0:T(8,128)(2,1)S(1)}, bf16[32,2176]{1,0:T(8,128)(2,1)S(1)}, u32[]{:S(2)}, u32[]{:S(2)}) collective-permute-start(bf16[32,2176]{1,0:T(8,128)(2,1)S(1)} %collective-permute-done.4.refs_2_), channel_id=1, source_target_pairs={{0,1},{1,0},{2,3},{3,2},{4,5},{5,4},{6,7},{7,6},{8,9},{9,8},{10,11... | collective-permute-start | bytes 417800 | tf_op jit(solution)/shard_map/ppermute | solution.py:223
  38.0 2.0 %collective-permute-start.16 = (bf16[128,2048]{1,0:T(8,128)(2,1)S(1)}, bf16[128,2048]{1,0:T(8,128)(2,1)S(1)}, u32[]{:S(2)}, u32[]{:S(2)}) collective-permute-start(bf16[128,2048]{1,0:T(8,128)(2,1)S(1)} %other.3), channel_id=1, source_target_pairs={{0,1},{1,0},{2,3},{3,2},{4,5},{5,4},{6,7},{7,6},{8,9},{9,8},{10,11... | collective-permute-start | bytes 1572872 | tf_op jit(solution)/shard_map/ppermute | solution.py:226
  39.5 20.7 %copy-start.2 = (bf16[32,4096]{1,0:T(8,128)(2,1)S(1)}, bf16[32,4096]{1,0:T(8,128)(2,1)}, u32[]{:S(2)}) copy-start(bf16[32,4096]{1,0:T(8,128)(2,1)} %refs_1_.1) | copy-start | bytes 786436
  39.5 5.9 %collective-permute-start.15 = (bf16[128,2048]{1,0:T(8,128)(2,1)S(1)}, bf16[128,2048]{1,0:T(8,128)(2,1)S(1)}, u32[]{:S(2)}, u32[]{:S(2)}) collective-permute-start(bf16[128,2048]{1,0:T(8,128)(2,1)S(1)} %other.2), channel_id=1, source_target_pairs={{0,1},{1,0},{2,3},{3,2},{4,5},{5,4},{6,7},{7,6},{8,9},{9,8},{10,11... | collective-permute-start | bytes 1572872 | tf_op jit(solution)/shard_map/ppermute | solution.py:226
  41.3 6.4 %collective-permute-start.17 = (bf16[32,2048]{1,0:T(8,128)(2,1)S(1)}, bf16[32,2048]{1,0:T(8,128)(2,1)S(1)}, u32[]{:S(2)}, u32[]{:S(2)}) collective-permute-start(bf16[32,2048]{1,0:T(8,128)(2,1)S(1)} %get-tuple-element.20), channel_id=1, source_target_pairs={{0,2},{2,0},{4,6},{6,4},{8,10},{10,8},{12,14},{14,12},{1,3},{3,1},... | collective-permute-start | bytes 393224 | tf_op jit(solution)/shard_map/ppermute | solution.py:233
  41.8 8.7 %collective-permute-start.19 = (bf16[32,2048]{1,0:T(8,128)(2,1)S(1)}, bf16[32,2048]{1,0:T(8,128)(2,1)S(1)}, u32[]{:S(2)}, u32[]{:S(2)}) collective-permute-start(bf16[32,2048]{1,0:T(8,128)(2,1)S(1)} %get-tuple-element.22), channel_id=1, source_target_pairs={{0,2},{2,0},{4,6},{6,4},{8,10},{10,8},{12,14},{14,12},{1,3},{3,1},... | collective-permute-start | bytes 393224 | tf_op jit(solution)/shard_map/ppermute | solution.py:233
  43.4 9.9 %collective-permute-start.21 = (bf16[32,2048]{1,0:T(8,128)(2,1)S(1)}, bf16[32,2048]{1,0:T(8,128)(2,1)S(1)}, u32[]{:S(2)}, u32[]{:S(2)}) collective-permute-start(bf16[32,2048]{1,0:T(8,128)(2,1)S(1)} %get-tuple-element.24), channel_id=1, source_target_pairs={{0,2},{2,0},{4,6},{6,4},{8,10},{10,8},{12,14},{14,12},{1,3},{3,1},... | collective-permute-start | bytes 393224 | tf_op jit(solution)/shard_map/ppermute | solution.py:233
  43.8 11.5 %collective-permute-start.23 = (bf16[32,2048]{1,0:T(8,128)(2,1)S(1)}, bf16[32,2048]{1,0:T(8,128)(2,1)S(1)}, u32[]{:S(2)}, u32[]{:S(2)}) collective-permute-start(bf16[32,2048]{1,0:T(8,128)(2,1)S(1)} %get-tuple-element.26), channel_id=1, source_target_pairs={{0,2},{2,0},{4,6},{6,4},{8,10},{10,8},{12,14},{14,12},{1,3},{3,1},... | collective-permute-start | bytes 393224 | tf_op jit(solution)/shard_map/ppermute | solution.py:233
  47.7 8.0 %collective-permute-start.18 = (bf16[32,2048]{1,0:T(8,128)(2,1)S(1)}, bf16[32,2048]{1,0:T(8,128)(2,1)S(1)}, u32[]{:S(2)}, u32[]{:S(2)}) collective-permute-start(bf16[32,2048]{1,0:T(8,128)(2,1)S(1)} %add_convert_fusion.3), channel_id=1, source_target_pairs={{0,8},{2,10},{4,12},{6,14},{8,0},{10,2},{12,4},{14,6},{1,9},{3,11}... | collective-permute-start | bytes 393224 | tf_op jit(solution)/shard_map/ppermute | solution.py:235
  50.5 5.8 %collective-permute-start.20 = (bf16[32,2048]{1,0:T(8,128)(2,1)S(1)}, bf16[32,2048]{1,0:T(8,128)(2,1)S(1)}, u32[]{:S(2)}, u32[]{:S(2)}) collective-permute-start(bf16[32,2048]{1,0:T(8,128)(2,1)S(1)} %add_convert_fusion.2), channel_id=1, source_target_pairs={{0,12},{2,14},{4,0},{6,2},{8,4},{10,6},{12,8},{14,10},{1,13},{3,15... | collective-permute-start | bytes 393224 | tf_op jit(solution)/shard_map/ppermute | solution.py:235
  53.3 6.8 %collective-permute-start.22 = (bf16[32,2048]{1,0:T(8,128)(2,1)S(1)}, bf16[32,2048]{1,0:T(8,128)(2,1)S(1)}, u32[]{:S(2)}, u32[]{:S(2)}) collective-permute-start(bf16[32,2048]{1,0:T(8,128)(2,1)S(1)} %add_convert_fusion.1), channel_id=1, source_target_pairs={{0,4},{2,6},{4,8},{6,10},{8,12},{10,14},{12,0},{14,2},{1,5},{3,7},... | collective-permute-start | bytes 393224 | tf_op jit(solution)/shard_map/ppermute | solution.py:235

commit v9 on v8

--- a/solution.py
+++ b/solution.py
@@ -14,9 +14,9 @@
 
 
 def prepare_kernel(half, experts, *refs):
-    out_ref, slot_ref, hidden_ref, ids_ref, scores_ref, sem = refs[4:]
+    out_ref, left_ref, right_ref, slot_ref, hidden_ref, ids_ref, scores_ref, sem = refs[4:]
     copies = [
-        pltpu.make_async_copy(refs[i], refs[5 + i], sem.at[i]) for i in range(4)
+        pltpu.make_async_copy(refs[i], refs[7 + i], sem.at[i]) for i in range(4)
     ]
     for copy in copies:
         copy.start()
@@ -47,6 +47,9 @@
         jnp.where(row < 2 * experts, middle, jnp.where(row < 3 * experts, low, 0.0)),
     )
     out_ref[:, half:] = coded.T.astype(jnp.bfloat16)
+    left = left_ref.shape[1]
+    left_ref[...] = out_ref[:, :left]
+    right_ref[...] = out_ref[:, left:]
 
 
 def prepare(hidden_in, expert_ids, route_scores, expert_slot):
@@ -60,9 +63,12 @@
     far = [pltpu.with_memory_space_constraint(a, pltpu.HBM) for a in far]
     return pl.pallas_call(
         functools.partial(prepare_kernel, half, experts),
-        out_shape=jax.ShapeDtypeStruct((rows, half + width), jnp.bfloat16),
+        out_shape=[
+            jax.ShapeDtypeStruct((rows, columns), jnp.bfloat16)
+            for columns in (half + width, half // 2, half // 2 + width)
+        ],
         in_specs=[hbm] * 4,
-        out_specs=vmem,
+        out_specs=[vmem] * 3,
         scratch_shapes=[
             pltpu.SMEM(expert_slot.shape, jnp.int32),
             pltpu.VMEM(hidden_in.shape, hidden_in.dtype),
@@ -78,13 +84,20 @@
     )(*far)
 
 
-def fill_rows(half, blocks, refs, own, other, coded):
-    tokens = refs[0].shape[0]
-    for i in range(blocks):
+def fill_rows(half, pieces, own_refs, other_refs, own, other, coded):
+    tokens = own_refs[0].shape[0]
+    at = 0
+    for i, count in enumerate(pieces):
         rows = slice(i * tokens, (i + 1) * tokens)
-        own[rows, :] = refs[i][:, :half]
-        other[rows, :] = refs[blocks + i][:, :half]
-        coded[rows, :] = refs[i][:, half:].astype(jnp.float32)
+        column = 0
+        for j in range(at, at + count):
+            width = min(own_refs[j].shape[1], half - column)
+            columns = slice(column, column + width)
+            own[rows, columns] = own_refs[j][:, :width]
+            other[rows, columns] = other_refs[j][:, :width]
+            column += width
+        coded[rows, :] = own_refs[at + count - 1][:, width:].astype(jnp.float32)
+        at += count
 
 
 def hidden_units(half, experts, gate_ref, up_ref, own, other, coded, out_refs):
@@ -116,30 +129,35 @@
                 row += out_ref.shape[0]
 
 
-def hidden_kernel(half, experts, blocks, *refs):
-    gate_ref, up_ref, *out_refs = refs[2 * blocks : 2 * blocks + 4]
-    own, other, coded = refs[2 * blocks + 4 :]
-    fill_rows(half, blocks, refs, own, other, coded)
+def hidden_kernel(half, experts, pieces, *refs):
+    count = sum(pieces)
+    gate_ref, up_ref, *out_refs = refs[2 * count : 2 * count + 4]
+    own, other, coded = refs[2 * count + 4 :]
+    fill_rows(half, pieces, refs[:count], refs[count : 2 * count], own, other, coded)
     hidden_units(half, experts, gate_ref, up_ref, own, other, coded, out_refs)
 
 
 def run_hidden(own, other, gate, up, experts, first):
-    blocks = len(own)
+    pieces = [len(block) for block in own]
+    own = [piece for block in own for piece in block]
+    other = [piece for block in other for piece in block]
+    blocks, tokens = len(pieces), own[0].shape[0]
     local, features, width = gate.shape
-    rows, half, units = blocks * own[0].shape[0], features // 2, local * width
+    rows, half, units = blocks * tokens, features // 2, local * width
+    coded = -(-3 * experts // LANES) * LANES
     vmem = pl.BlockSpec(memory_space=pltpu.VMEM)
     return pl.pallas_call(
-        functools.partial(hidden_kernel, half, experts, blocks),
+        functools.partial(hidden_kernel, half, experts, pieces),
         out_shape=[
-            jax.ShapeDtypeStruct((count * own[0].shape[0], units), jnp.bfloat16)
+            jax.ShapeDtypeStruct((count * tokens, units), jnp.bfloat16)
             for count in (first, blocks - first)
         ],
-        in_specs=[vmem] * (2 * blocks + 2),
+        in_specs=[vmem] * (2 * len(own) + 2),
         out_specs=[vmem] * 2,
         scratch_shapes=[
             pltpu.VMEM((rows, half), jnp.bfloat16),
             pltpu.VMEM((rows, half), jnp.bfloat16),
-            pltpu.VMEM((rows, own[0].shape[1] - half), jnp.float32),
+            pltpu.VMEM((rows, coded), jnp.float32),
         ],
         compiler_params=pltpu.CompilerParams(vmem_limit_bytes=LIMIT),
         cost_estimate=pl.CostEstimate(
@@ -211,16 +229,19 @@
     cores = [(0, 1), (1, 0)]
     bf16, f32 = jnp.bfloat16, jnp.float32
 
-    packed = prepare(hidden_in, expert_ids, route_scores, expert_slot)
+    packed, *halves = prepare(hidden_in, expert_ids, route_scores, expert_slot)
     order = sorted(range(1, outer), key=lambda k: -min(k, outer - k))
-    same, opposite = {0: packed}, {0: lax.ppermute(packed, "sect", across)}
+    crossed = lax.ppermute(packed, "sect", across)
+    same, opposite = {0: [packed]}, {0: [crossed]}
     for k in order[::-1]:
-        block = after(packed, opposite[0]) if k == order[0] and outer > 2 else packed
-        same[k] = lax.ppermute(block, "sect", along(k))
+        pieces = [packed]
+        if k == order[0] and outer > 2:
+            pieces = [after(piece, crossed) for piece in halves]
+        same[k] = [lax.ppermute(piece, "sect", along(k)) for piece in pieces]
     for k in order[::-1]:
-        opposite[k] = lax.ppermute(same[k], "sect", across)
+        opposite[k] = [lax.ppermute(piece, "sect", across) for piece in same[k]]
     blocks = [side[k] for side in (opposite, same) for k in range(outer)]
-    others = [lax.ppermute(block, "tp", cores) for block in blocks]
+    others = [[lax.ppermute(piece, "tp", cores) for piece in block] for block in blocks]
     groups = run_hidden(blocks, others, gate_matrix, up_matrix, experts, outer)
     sent = [
         lax.ppermute(run_down(hidden, down_matrix, None, [bf16])[0], "tp", cores)

time: 61 us -> 63.8 us (1.046)
  starting transfers between devices: 18.9 us -> 21.8 us
    ppermute x15 -> x19, starting transfers between devices: 12.4 us -> 14.6 us  [the longest x4 6.81 us: on_device(): same[k] = [lax.ppermute(piece, 'sect', along(k)) for piece in pieces]]
    ppermute x3, starting transfers between devices: 1.75 us -> 2.5 us  [on_device(): block = lax.ppermute(block.astype(bf16), 'sect', along(-k)).astype(f32)]
    ppermute x15 -> x19, waiting for transfers between devices: 13.9 us -> 14.4 us  [the longest x4 7.54 us: on_device(): same[k] = [lax.ppermute(piece, 'sect', along(k)) for piece in pieces]]
  transfers between devices with their start and end apart: 24 -> 28, of which waited for: 14 -> 12; matrix products, arithmetic and copies ran while one was open for 0% -> 0% of each run, Pallas kernels for 6% -> 6%
where the time goes in v9:
time: 63.8 us; the launch traced here: 63.6 us
  waiting for transfers between devices  25.2 us (39%)
  starting transfers between devices  21.8 us (34%)
  Pallas kernels  15.5 us (24%)
  other arithmetic  0.83 us (1%)
    pallas_call x1, Pallas kernels, run_hidden(): pl.pallas_call(functools.partial(hidden_kernel, half, experts, pieces), o...  8.94 us
    ppermute x4, waiting for transfers between devices, on_device(): same[k] = [lax.ppermute(piece, 'sect', along(k)) for piece in pieces]  7.54 us
    ppermute x4, starting transfers between devices, on_device(): same[k] = [lax.ppermute(piece, 'sect', along(k)) for piece in pieces]  6.81 us
    ppermute x4, waiting for transfers between devices, on_device(): block = near_sum[k] + lax.ppermute(far_sum[k], 'sect', across).astype(f32)  6.22 us
    ppermute x4, waiting for transfers between devices, on_device(): opposite[k] = [lax.ppermute(piece, 'sect', across) for piece in same[k]]  5.91 us
    pallas_call x4, Pallas kernels, run_down(): pl.pallas_call(functools.partial(down_kernel, len(extra)), out_shape=[jax...  5.16 us
    ppermute x3, waiting for transfers between devices, on_device(): block = lax.ppermute(block.astype(bf16), 'sect', along(-k)).astype(f32)  4.6 us
    ppermute x4, starting transfers between devices, on_device(): block = near_sum[k] + lax.ppermute(far_sum[k], 'sect', across).astype(f32)  4.13 us
  transfers between devices with their start and end apart: 28, of which 12 were waited for; matrix products, arithmetic and copies ran while one was open for 0% of the time, Pallas kernels for 6%

profile of v9, /device:TPU:0, one launch (start us, length us, event | category | flops | bytes accessed | tf_op | source)
XLA Modules:
  0.0 63.6 jit_solution(9386587153905598831)
XLA Ops:
  0.0 1.4 %prepare.1 = (bf16[32,2176]{1,0:T(8,128)(2,1)S(1)}, bf16[32,1024]{1,0:T(8,128)(2,1)S(1)}, bf16[32,1152]{1,0:T(8,128)(2,1)S(1)}) custom-call(s32[32]{0:T(128)} %refs_0_.1, bf16[32,4096]{1,0:T(8,128)(2,1)} %refs_1_.1, s32[8,32]{1,0:T(8,128)} %bitcast.4, f32[8,32]{1,0:T(8,128)} %bitcast.5), custom_call_target="tpu_custom_call" | custom-call | flops 40000000000 | bytes 262144 | tf_op jit(solution)/shard_map/prepare/pallas_call | solution.py:64
  1.4 3.0 %collective-permute-start = (bf16[32,2176]{1,0:T(8,128)(2,1)S(1)}, bf16[32,2176]{1,0:T(8,128)(2,1)S(1)}, u32[]{:S(2)}, u32[]{:S(2)}) collective-permute-start(bf16[32,2176]{1,0:T(8,128)(2,1)S(1)} %get-tuple-element.20.refs_5_), channel_id=1, source_target_pairs={{0,2},{2,0},{4,6},{6,4},{8,10},{10,8},{12,14},{14,12},{1,3},{3,1},... | collective-permute-start | bytes 417800 | tf_op jit(solution)/shard_map/ppermute | solution.py:234
  4.5 1.6 %collective-permute-start.1 = (bf16[32,2176]{1,0:T(8,128)(2,1)S(1)}, bf16[32,2176]{1,0:T(8,128)(2,1)S(1)}, u32[]{:S(2)}, u32[]{:S(2)}) collective-permute-start(bf16[32,2176]{1,0:T(8,128)(2,1)S(1)} %get-tuple-element.20.refs_5_), channel_id=1, source_target_pairs={{0,4},{2,6},{4,8},{6,10},{8,12},{10,14},{12,0},{14,2},{1,5},{3,7},... | collective-permute-start | bytes 417800 | tf_op jit(solution)/shard_map/ppermute | solution.py:240
  6.0 2.2 %collective-permute-start.7 = (bf16[32,2176]{1,0:T(8,128)(2,1)S(1)}, bf16[32,2176]{1,0:T(8,128)(2,1)S(1)}, u32[]{:S(2)}, u32[]{:S(2)}) collective-permute-start(bf16[32,2176]{1,0:T(8,128)(2,1)S(1)} %get-tuple-element.20.refs_5_), channel_id=1, source_target_pairs={{0,12},{2,14},{4,0},{6,2},{8,4},{10,6},{12,8},{14,10},{1,13},{3,15... | collective-permute-start | bytes 417800 | tf_op jit(solution)/shard_map/ppermute | solution.py:240
  8.3 0.0 collective-permute-start.14
  8.3 0.0 collective-permute-done.refs_0_
  8.3 0.0 slice-start.1
  8.3 0.0 slice-start.2
  8.3 0.0 slice-start.3
  8.3 2.7 %collective-permute-start.3 = (bf16[32,1024]{1,0:T(8,128)(2,1)S(1)}, bf16[32,1024]{1,0:T(8,128)(2,1)S(1)}, u32[]{:S(2)}, u32[]{:S(2)}) collective-permute-start(bf16[32,1024]{1,0:T(8,128)(2,1)S(1)} %get-tuple-element.22), channel_id=1, source_target_pairs={{0,8},{2,10},{4,12},{6,14},{8,0},{10,2},{12,4},{14,6},{1,9},{3,11}... | collective-permute-start | bytes 196616 | tf_op jit(solution)/shard_map/ppermute | solution.py:240
  11.0 0.3 collective-permute-start.5
  11.3 1.5 %collective-permute-done.1.refs_6_ = bf16[32,2176]{1,0:T(8,128)(2,1)S(1)} collective-permute-done((bf16[32,2176]{1,0:T(8,128)(2,1)S(1)}, bf16[32,2176]{1,0:T(8,128)(2,1)S(1)}, u32[]{:S(2)}, u32[]{:S(2)}) %collective-permute-start.1) | collective-permute-done | bytes 139296 | tf_op jit(solution)/shard_map/ppermute | solution.py:240
  12.8 0.3 collective-permute-start.2
  13.1 6.0 %collective-permute-done.3.refs_7_ = bf16[32,1024]{1,0:T(8,128)(2,1)S(1)} collective-permute-done((bf16[32,1024]{1,0:T(8,128)(2,1)S(1)}, bf16[32,1024]{1,0:T(8,128)(2,1)S(1)}, u32[]{:S(2)}, u32[]{:S(2)}) %collective-permute-start.3) | collective-permute-done | bytes 65568 | tf_op jit(solution)/shard_map/ppermute | solution.py:240
  19.1 0.4 collective-permute-start.4
  19.5 0.0 collective-permute-done.7.refs_9_
  19.5 1.6 %collective-permute-start.8 = (bf16[32,2176]{1,0:T(8,128)(2,1)S(1)}, bf16[32,2176]{1,0:T(8,128)(2,1)S(1)}, u32[]{:S(2)}, u32[]{:S(2)}) collective-permute-start(bf16[32,2176]{1,0:T(8,128)(2,1)S(1)} %collective-permute-done.7.refs_9_), channel_id=1, source_target_pairs={{0,2},{2,0},{4,6},{6,4},{8,10},{10,8},{12,14},{14,12},{1,3},{3,1},... | collective-permute-start | bytes 417800 | tf_op jit(solution)/shard_map/ppermute | solution.py:242
  21.1 0.0 collective-permute-done.14.refs_15_
  21.1 0.0 collective-permute-start.9
  21.1 0.0 collective-permute-done.5.refs_8_
  21.1 0.5 collective-permute-start.16
  21.6 2.5 %collective-permute-done.4.refs_2_ = bf16[32,1024]{1,0:T(8,128)(2,1)S(1)} collective-permute-done((bf16[32,1024]{1,0:T(8,128)(2,1)S(1)}, bf16[32,1024]{1,0:T(8,128)(2,1)S(1)}, u32[]{:S(2)}, u32[]{:S(2)}) %collective-permute-start.4) | collective-permute-done | bytes 65568 | tf_op jit(solution)/shard_map/ppermute | solution.py:242
  24.1 0.0 collective-permute-start.15
  24.1 0.0 collective-permute-done.16.refs_17_
  24.1 0.5 collective-permute-start.18
  24.6 0.0 collective-permute-done.2.refs_1_
  24.6 0.3 collective-permute-start.6
  25.0 0.7 %collective-permute-done.8.refs_4_ = bf16[32,2176]{1,0:T(8,128)(2,1)S(1)} collective-permute-done((bf16[32,2176]{1,0:T(8,128)(2,1)S(1)}, bf16[32,2176]{1,0:T(8,128)(2,1)S(1)}, u32[]{:S(2)}, u32[]{:S(2)}) %collective-permute-start.8) | collective-permute-done | bytes 139296 | tf_op jit(solution)/shard_map/ppermute | solution.py:242
  25.6 0.0 collective-permute-start.10
  25.6 0.5 collective-permute-start.13
  26.1 0.1 collective-permute-start.17
  26.2 2.8 %collective-permute-done.6.refs_3_ = bf16[32,1152]{1,0:T(8,128)(2,1)S(1)} collective-permute-done((bf16[32,1152]{1,0:T(8,128)(2,1)S(1)}, bf16[32,1152]{1,0:T(8,128)(2,1)S(1)}, u32[]{:S(2)}, u32[]{:S(2)}) %collective-permute-start.6) | collective-permute-done | bytes 73760 | tf_op jit(solution)/shard_map/ppermute | solution.py:242
  29.0 0.0 collective-permute-start.12
  29.0 0.0 collective-permute-done.18.refs_19_
  29.0 0.5 collective-permute-start.11
  29.5 0.0 collective-permute-done.17.refs_18_
  29.5 0.9 %collective-permute-done.11.refs_12_ = bf16[32,1024]{1,0:T(8,128)(2,1)S(1)} collective-permute-done((bf16[32,1024]{1,0:T(8,128)(2,1)S(1)}, bf16[32,1024]{1,0:T(8,128)(2,1)S(1)}, u32[]{:S(2)}, u32[]{:S(2)}) %collective-permute-start.11) | collective-permute-done | bytes 65568 | tf_op jit(solution)/shard_map/ppermute | solution.py:244
  30.4 0.0 copy-done
  30.4 0.0 copy-done.1
  30.4 8.9 %hidden.1 = (bf16[128,2048]{1,0:T(8,128)(2,1)S(1)}, bf16[128,2048]{1,0:T(8,128)(2,1)S(1)}) custom-call(bf16[32,2176]{1,0:T(8,128)(2,1)S(1)} %collective-permute-done.refs_0_, bf16[32,2176]{1,0:T(8,128)(2,1)S(1)} %collective-permute-done.2.refs_1_, bf16[32,1024]{1,0:T(8,128)(2,1)S(1)} %collective-permute-done.4.refs_2_, ...), custom_call_target="tpu_custom_call" | custom-call | flops 8589934592 | bytes 2097152 | tf_op jit(solution)/shard_map/hidden/pallas_call | solution.py:149
  39.4 1.3 %other.3 = bf16[128,2048]{1,0:T(8,128)(2,1)S(1)} custom-call(bf16[128,2048]{1,0:T(8,128)(2,1)S(1)} %get-tuple-element.27.hidden_ref, bf16[4,512,4096]{2,1,0:T(8,128)(2,1)S(1)} %bitcast.3), custom_call_target="tpu_custom_call" | custom-call | flops 524288 | bytes 512 | tf_op jit(solution)/shard_map/other/pallas_call | solution.py:193
  40.7 0.4 collective-permute-start.20
  41.2 1.3 %other.2 = bf16[128,2048]{1,0:T(8,128)(2,1)S(1)} custom-call(bf16[128,2048]{1,0:T(8,128)(2,1)S(1)} %get-tuple-element.25.hidden_ref, bf16[4,512,4096]{2,1,0:T(8,128)(2,1)S(1)} %bitcast.3), custom_call_target="tpu_custom_call" | custom-call | flops 524288 | bytes 512 | tf_op jit(solution)/shard_map/other/pallas_call | solution.py:193
  42.4 0.0 copy-start.2
  42.5 0.2 collective-permute-start.19
  42.7 0.0 collective-permute-done.20.refs_0_
  42.7 1.3 %mine.3 = (bf16[32,2048]{1,0:T(8,128)(2,1)S(1)}, bf16[32,2048]{1,0:T(8,128)(2,1)S(1)}, bf16[32,2048]{1,0:T(8,128)(2,1)S(1)}, bf16[32,2048]{1,0:T(8,128)(2,1)S(1)}) custom-call(bf16[128,2048]{1,0:T(8,128)(2,1)S(1)} %get-tuple-element.27.hidden_ref, bf16[4,512,4096]{2,1,0:T(8,128)(2,1)S(1)} %bitcast.3, bf16[128,2048]{1,0:T(8,128)(2,1)S(1)} %collective-permute-done.20.refs_0_), custom_call_target="tpu_custom_call" | custom-call | flops 524288 | bytes 512 | tf_op jit(solution)/shard_map/mine/pallas_call | solution.py:193
  44.0 0.4 collective-permute-start.21
  44.4 1.7 %collective-permute-start.23 = (bf16[32,2048]{1,0:T(8,128)(2,1)S(1)}, bf16[32,2048]{1,0:T(8,128)(2,1)S(1)}, u32[]{:S(2)}, u32[]{:S(2)}) collective-permute-start(bf16[32,2048]{1,0:T(8,128)(2,1)S(1)} %get-tuple-element.30), channel_id=1, source_target_pairs={{0,2},{2,0},{4,6},{6,4},{8,10},{10,8},{12,14},{14,12},{1,3},{3,1},... | collective-permute-start | bytes 393224 | tf_op jit(solution)/shard_map/ppermute | solution.py:254
  46.1 0.3 collective-permute-start.25
  46.5 1.7 %collective-permute-start.27 = (bf16[32,2048]{1,0:T(8,128)(2,1)S(1)}, bf16[32,2048]{1,0:T(8,128)(2,1)S(1)}, u32[]{:S(2)}, u32[]{:S(2)}) collective-permute-start(bf16[32,2048]{1,0:T(8,128)(2,1)S(1)} %get-tuple-element.34), channel_id=1, source_target_pairs={{0,2},{2,0},{4,6},{6,4},{8,10},{10,8},{12,14},{14,12},{1,3},{3,1},... | collective-permute-start | bytes 393224 | tf_op jit(solution)/shard_map/ppermute | solution.py:254
  48.1 0.0 collective-permute-done.19.refs_0_
  48.2 1.3 %mine.2 = (f32[32,2048]{1,0:T(8,128)S(1)}, f32[32,2048]{1,0:T(8,128)S(1)}, f32[32,2048]{1,0:T(8,128)S(1)}, f32[32,2048]{1,0:T(8,128)S(1)}) custom-call(bf16[128,2048]{1,0:T(8,128)(2,1)S(1)} %get-tuple-element.25.hidden_ref, bf16[4,512,4096]{2,1,0:T(8,128)(2,1)S(1)} %bitcast.3, bf16[128,2048]{1,0:T(8,128)(2,1)S(1)} %collective-permute-done.19.refs_0_), custom_call_target="tpu_custom_call" | custom-call | flops 524288 | bytes 512 | tf_op jit(solution)/shard_map/mine/pallas_call | solution.py:193
  49.4 1.0 %collective-permute-done.21 = bf16[32,2048]{1,0:T(8,128)(2,1)S(1)} collective-permute-done((bf16[32,2048]{1,0:T(8,128)(2,1)S(1)}, bf16[32,2048]{1,0:T(8,128)(2,1)S(1)}, u32[]{:S(2)}, u32[]{:S(2)}) %collective-permute-start.21) | collective-permute-done | bytes 131104 | tf_op jit(solution)/shard_map/ppermute | solution.py:254
  50.4 1.1 %collective-permute-start.22 = (bf16[32,2048]{1,0:T(8,128)(2,1)S(1)}, bf16[32,2048]{1,0:T(8,128)(2,1)S(1)}, u32[]{:S(2)}, u32[]{:S(2)}) collective-permute-start(bf16[32,2048]{1,0:T(8,128)(2,1)S(1)} %add_convert_fusion.3), channel_id=1, source_target_pairs={{0,8},{2,10},{4,12},{6,14},{8,0},{10,2},{12,4},{14,6},{1,9},{3,11}... | collective-permute-start | bytes 393224 | tf_op jit(solution)/shard_map/ppermute | solution.py:256
  51.6 1.7 %collective-permute-done.23 = bf16[32,2048]{1,0:T(8,128)(2,1)S(1)} collective-permute-done((bf16[32,2048]{1,0:T(8,128)(2,1)S(1)}, bf16[32,2048]{1,0:T(8,128)(2,1)S(1)}, u32[]{:S(2)}, u32[]{:S(2)}) %collective-permute-start.23) | collective-permute-done | bytes 131104 | tf_op jit(solution)/shard_map/ppermute | solution.py:254
  53.2 1.3 %collective-permute-start.24 = (bf16[32,2048]{1,0:T(8,128)(2,1)S(1)}, bf16[32,2048]{1,0:T(8,128)(2,1)S(1)}, u32[]{:S(2)}, u32[]{:S(2)}) collective-permute-start(bf16[32,2048]{1,0:T(8,128)(2,1)S(1)} %add_convert_fusion.2), channel_id=1, source_target_pairs={{0,12},{2,14},{4,0},{6,2},{8,4},{10,6},{12,8},{14,10},{1,13},{3,15... | collective-permute-start | bytes 393224 | tf_op jit(solution)/shard_map/ppermute | solution.py:256
  54.6 1.5 %collective-permute-done.25 = bf16[32,2048]{1,0:T(8,128)(2,1)S(1)} collective-permute-done((bf16[32,2048]{1,0:T(8,128)(2,1)S(1)}, bf16[32,2048]{1,0:T(8,128)(2,1)S(1)}, u32[]{:S(2)}, u32[]{:S(2)}) %collective-permute-start.25) | collective-permute-done | bytes 131104 | tf_op jit(solution)/shard_map/ppermute | solution.py:254
  56.1 0.1 collective-permute-start.26
  56.1 2.1 %collective-permute-done.27 = bf16[32,2048]{1,0:T(8,128)(2,1)S(1)} collective-permute-done((bf16[32,2048]{1,0:T(8,128)(2,1)S(1)}, bf16[32,2048]{1,0:T(8,128)(2,1)S(1)}, u32[]{:S(2)}, u32[]{:S(2)}) %collective-permute-start.27) | collective-permute-done | bytes 131104 | tf_op jit(solution)/shard_map/ppermute | solution.py:254
  58.3 0.0 collective-permute-done.22
  58.3 3.2 %collective-permute-done.24 = bf16[32,2048]{1,0:T(8,128)(2,1)S(1)} collective-permute-done((bf16[32,2048]{1,0:T(8,128)(2,1)S(1)}, bf16[32,2048]{1,0:T(8,128)(2,1)S(1)}, u32[]{:S(2)}, u32[]{:S(2)}) %collective-permute-start.24) | collective-permute-done | bytes 131104 | tf_op jit(solution)/shard_map/ppermute | solution.py:256
  61.4 1.4 %collective-permute-done.26 = bf16[32,2048]{1,0:T(8,128)(2,1)S(1)} collective-permute-done((bf16[32,2048]{1,0:T(8,128)(2,1)S(1)}, bf16[32,2048]{1,0:T(8,128)(2,1)S(1)}, u32[]{:S(2)}, u32[]{:S(2)}) %collective-permute-start.26) | collective-permute-done | bytes 131104 | tf_op jit(solution)/shard_map/ppermute | solution.py:256
  62.9 0.8 %add_convert_fusion = bf16[32,2048]{1,0:T(8,128)(2,1)} fusion(f32[32,2048]{1,0:T(8,128)S(1)} %get-tuple-element.33, bf16[32,2048]{1,0:T(8,128)(2,1)S(1)} %collective-permute-done.27, bf16[32,2048]{1,0:T(8,128)(2,1)S(1)} %collective-permute-done.26, bf16[32,2048]{1,0:T(8,128)(2,1)S(1)} %collective-permute-done.24, ...), kind=kLoop, calls=%fused_computation | loop fusion | flops 720896 | bytes 1048580 | tf_op jit(solution)/shard_map/convert_element_type | solution.py:258
  (17 shorter events, 0.1 us)
Async XLA Ops:
  0.0 30.4 %copy-start = (bf16[4,4096,512]{2,1,0:T(8,128)(2,1)S(1)}, bf16[4,4096,512]{2,1,0:T(8,128)(2,1)}, u32[]{:S(2)}) copy-start(bf16[4,4096,512]{2,1,0:T(8,128)(2,1)} %refs_20_.1) | copy-start | bytes 50331652
  0.0 30.4 %copy-start.1 = (bf16[4,4096,512]{2,1,0:T(8,128)(2,1)S(1)}, bf16[4,4096,512]{2,1,0:T(8,128)(2,1)}, u32[]{:S(2)}) copy-start(bf16[4,4096,512]{2,1,0:T(8,128)(2,1)} %refs_21_.1) | copy-start | bytes 50331652
  1.4 6.9 %collective-permute-start = (bf16[32,2176]{1,0:T(8,128)(2,1)S(1)}, bf16[32,2176]{1,0:T(8,128)(2,1)S(1)}, u32[]{:S(2)}, u32[]{:S(2)}) collective-permute-start(bf16[32,2176]{1,0:T(8,128)(2,1)S(1)} %get-tuple-element.20.refs_5_), channel_id=1, source_target_pairs={{0,2},{2,0},{4,6},{6,4},{8,10},{10,8},{12,14},{14,12},{1,3},{3,1},... | collective-permute-start | bytes 417800 | tf_op jit(solution)/shard_map/ppermute | solution.py:234
  4.5 8.4 %collective-permute-start.1 = (bf16[32,2176]{1,0:T(8,128)(2,1)S(1)}, bf16[32,2176]{1,0:T(8,128)(2,1)S(1)}, u32[]{:S(2)}, u32[]{:S(2)}) collective-permute-start(bf16[32,2176]{1,0:T(8,128)(2,1)S(1)} %get-tuple-element.20.refs_5_), channel_id=1, source_target_pairs={{0,4},{2,6},{4,8},{6,10},{8,12},{10,14},{12,0},{14,2},{1,5},{3,7},... | collective-permute-start | bytes 417800 | tf_op jit(solution)/shard_map/ppermute | solution.py:240
  6.0 13.5 %collective-permute-start.7 = (bf16[32,2176]{1,0:T(8,128)(2,1)S(1)}, bf16[32,2176]{1,0:T(8,128)(2,1)S(1)}, u32[]{:S(2)}, u32[]{:S(2)}) collective-permute-start(bf16[32,2176]{1,0:T(8,128)(2,1)S(1)} %get-tuple-element.20.refs_5_), channel_id=1, source_target_pairs={{0,12},{2,14},{4,0},{6,2},{8,4},{10,6},{12,8},{14,10},{1,13},{3,15... | collective-permute-start | bytes 417800 | tf_op jit(solution)/shard_map/ppermute | solution.py:240
  8.3 12.9 %collective-permute-start.14 = (bf16[32,2176]{1,0:T(8,128)(2,1)S(1)}, bf16[32,2176]{1,0:T(8,128)(2,1)S(1)}, u32[]{:S(2)}, u32[]{:S(2)}) collective-permute-start(bf16[32,2176]{1,0:T(8,128)(2,1)S(1)} %get-tuple-element.20.refs_5_), channel_id=1, source_target_pairs={{0,1},{1,0},{2,3},{3,2},{4,5},{5,4},{6,7},{7,6},{8,9},{9,8},{10,11... | collective-permute-start | bytes 417800 | tf_op jit(solution)/shard_map/ppermute | solution.py:244
  8.3 31.1 %slice-start = ((s8[16777216]{0:T(1024)(128)(4,1)}), s8[4194304]{0:T(1024)(128)(4,1)S(1)}, s32[]{:S(2)}) async-start(s8[16777216]{0:T(1024)(128)(4,1)} %bitcast.2), calls=%async_computation | async-start | bytes 8388608
  8.3 31.1 %slice-start.1 = ((s8[16777216]{0:T(1024)(128)(4,1)}), s8[4194304]{0:T(1024)(128)(4,1)S(1)}, s32[]{:S(2)}) async-start(s8[16777216]{0:T(1024)(128)(4,1)} %bitcast.2), calls=%async_computation.1 | async-start | bytes 8388608
  8.3 31.1 %slice-start.2 = ((s8[16777216]{0:T(1024)(128)(4,1)}), s8[4194304]{0:T(1024)(128)(4,1)S(1)}, s32[]{:S(2)}) async-start(s8[16777216]{0:T(1024)(128)(4,1)} %bitcast.2), calls=%async_computation.2 | async-start | bytes 8388608
  8.3 31.1 %slice-start.3 = ((s8[16777216]{0:T(1024)(128)(4,1)}), s8[4194304]{0:T(1024)(128)(4,1)S(1)}, s32[]{:S(2)}) async-start(s8[16777216]{0:T(1024)(128)(4,1)} %bitcast.2), calls=%async_computation.3 | async-start | bytes 8388608
  8.3 10.8 %collective-permute-start.3 = (bf16[32,1024]{1,0:T(8,128)(2,1)S(1)}, bf16[32,1024]{1,0:T(8,128)(2,1)S(1)}, u32[]{:S(2)}, u32[]{:S(2)}) collective-permute-start(bf16[32,1024]{1,0:T(8,128)(2,1)S(1)} %get-tuple-element.22), channel_id=1, source_target_pairs={{0,8},{2,10},{4,12},{6,14},{8,0},{10,2},{12,4},{14,6},{1,9},{3,11}... | collective-permute-start | bytes 196616 | tf_op jit(solution)/shard_map/ppermute | solution.py:240
  11.0 10.1 %collective-permute-start.5 = (bf16[32,1152]{1,0:T(8,128)(2,1)S(1)}, bf16[32,1152]{1,0:T(8,128)(2,1)S(1)}, u32[]{:S(2)}, u32[]{:S(2)}) collective-permute-start(bf16[32,1152]{1,0:T(8,128)(2,1)S(1)} %get-tuple-element.24), channel_id=1, source_target_pairs={{0,8},{2,10},{4,12},{6,14},{8,0},{10,2},{12,4},{14,6},{1,9},{3,11}... | collective-permute-start | bytes 221192 | tf_op jit(solution)/shard_map/ppermute | solution.py:240
  12.8 11.8 %collective-permute-start.2 = (bf16[32,2176]{1,0:T(8,128)(2,1)S(1)}, bf16[32,2176]{1,0:T(8,128)(2,1)S(1)}, u32[]{:S(2)}, u32[]{:S(2)}) collective-permute-start(bf16[32,2176]{1,0:T(8,128)(2,1)S(1)} %collective-permute-done.1.refs_6_), channel_id=1, source_target_pairs={{0,2},{2,0},{4,6},{6,4},{8,10},{10,8},{12,14},{14,12},{1,3},{3,1},... | collective-permute-start | bytes 417800 | tf_op jit(solution)/shard_map/ppermute | solution.py:242
  19.1 5.0 %collective-permute-start.4 = (bf16[32,1024]{1,0:T(8,128)(2,1)S(1)}, bf16[32,1024]{1,0:T(8,128)(2,1)S(1)}, u32[]{:S(2)}, u32[]{:S(2)}) collective-permute-start(bf16[32,1024]{1,0:T(8,128)(2,1)S(1)} %collective-permute-done.3.refs_7_), channel_id=1, source_target_pairs={{0,2},{2,0},{4,6},{6,4},{8,10},{10,8},{12,14},{14,12},{1,3},{3,1},... | collective-permute-start | bytes 196616 | tf_op jit(solution)/shard_map/ppermute | solution.py:242
  19.5 6.1 %collective-permute-start.8 = (bf16[32,2176]{1,0:T(8,128)(2,1)S(1)}, bf16[32,2176]{1,0:T(8,128)(2,1)S(1)}, u32[]{:S(2)}, u32[]{:S(2)}) collective-permute-start(bf16[32,2176]{1,0:T(8,128)(2,1)S(1)} %collective-permute-done.7.refs_9_), channel_id=1, source_target_pairs={{0,2},{2,0},{4,6},{6,4},{8,10},{10,8},{12,14},{14,12},{1,3},{3,1},... | collective-permute-start | bytes 417800 | tf_op jit(solution)/shard_map/ppermute | solution.py:242
  21.1 4.5 %collective-permute-start.9 = (bf16[32,2176]{1,0:T(8,128)(2,1)S(1)}, bf16[32,2176]{1,0:T(8,128)(2,1)S(1)}, u32[]{:S(2)}, u32[]{:S(2)}) collective-permute-start(bf16[32,2176]{1,0:T(8,128)(2,1)S(1)} %collective-permute-done.refs_0_), channel_id=1, source_target_pairs={{0,1},{1,0},{2,3},{3,2},{4,5},{5,4},{6,7},{7,6},{8,9},{9,8},{10,11... | collective-permute-start | bytes 417800 | tf_op jit(solution)/shard_map/ppermute | solution.py:244
  21.1 3.0 %collective-permute-start.16 = (bf16[32,1024]{1,0:T(8,128)(2,1)S(1)}, bf16[32,1024]{1,0:T(8,128)(2,1)S(1)}, u32[]{:S(2)}, u32[]{:S(2)}) collective-permute-start(bf16[32,1024]{1,0:T(8,128)(2,1)S(1)} %collective-permute-done.3.refs_7_), channel_id=1, source_target_pairs={{0,1},{1,0},{2,3},{3,2},{4,5},{5,4},{6,7},{7,6},{8,9},{9,8},{10,11... | collective-permute-start | bytes 196616 | tf_op jit(solution)/shard_map/ppermute | solution.py:244
  24.1 2.0 %collective-permute-start.15 = (bf16[32,2176]{1,0:T(8,128)(2,1)S(1)}, bf16[32,2176]{1,0:T(8,128)(2,1)S(1)}, u32[]{:S(2)}, u32[]{:S(2)}) collective-permute-start(bf16[32,2176]{1,0:T(8,128)(2,1)S(1)} %collective-permute-done.1.refs_6_), channel_id=1, source_target_pairs={{0,1},{1,0},{2,3},{3,2},{4,5},{5,4},{6,7},{7,6},{8,9},{9,8},{10,11... | collective-permute-start | bytes 417800 | tf_op jit(solution)/shard_map/ppermute | solution.py:244
  24.1 4.9 %collective-permute-start.18 = (bf16[32,2176]{1,0:T(8,128)(2,1)S(1)}, bf16[32,2176]{1,0:T(8,128)(2,1)S(1)}, u32[]{:S(2)}, u32[]{:S(2)}) collective-permute-start(bf16[32,2176]{1,0:T(8,128)(2,1)S(1)} %collective-permute-done.7.refs_9_), channel_id=1, source_target_pairs={{0,1},{1,0},{2,3},{3,2},{4,5},{5,4},{6,7},{7,6},{8,9},{9,8},{10,11... | collective-permute-start | bytes 417800 | tf_op jit(solution)/shard_map/ppermute | solution.py:244
  24.6 4.4 %collective-permute-start.6 = (bf16[32,1152]{1,0:T(8,128)(2,1)S(1)}, bf16[32,1152]{1,0:T(8,128)(2,1)S(1)}, u32[]{:S(2)}, u32[]{:S(2)}) collective-permute-start(bf16[32,1152]{1,0:T(8,128)(2,1)S(1)} %collective-permute-done.5.refs_8_), channel_id=1, source_target_pairs={{0,2},{2,0},{4,6},{6,4},{8,10},{10,8},{12,14},{14,12},{1,3},{3,1},... | collective-permute-start | bytes 221192 | tf_op jit(solution)/shard_map/ppermute | solution.py:242
  25.6 4.8 %collective-permute-start.10 = (bf16[32,2176]{1,0:T(8,128)(2,1)S(1)}, bf16[32,2176]{1,0:T(8,128)(2,1)S(1)}, u32[]{:S(2)}, u32[]{:S(2)}) collective-permute-start(bf16[32,2176]{1,0:T(8,128)(2,1)S(1)} %collective-permute-done.2.refs_1_), channel_id=1, source_target_pairs={{0,1},{1,0},{2,3},{3,2},{4,5},{5,4},{6,7},{7,6},{8,9},{9,8},{10,11... | collective-permute-start | bytes 417800 | tf_op jit(solution)/shard_map/ppermute | solution.py:244
  25.6 4.8 %collective-permute-start.13 = (bf16[32,2176]{1,0:T(8,128)(2,1)S(1)}, bf16[32,2176]{1,0:T(8,128)(2,1)S(1)}, u32[]{:S(2)}, u32[]{:S(2)}) collective-permute-start(bf16[32,2176]{1,0:T(8,128)(2,1)S(1)} %collective-permute-done.8.refs_4_), channel_id=1, source_target_pairs={{0,1},{1,0},{2,3},{3,2},{4,5},{5,4},{6,7},{7,6},{8,9},{9,8},{10,11... | collective-permute-start | bytes 417800 | tf_op jit(solution)/shard_map/ppermute | solution.py:244
  26.1 3.4 %collective-permute-start.17 = (bf16[32,1152]{1,0:T(8,128)(2,1)S(1)}, bf16[32,1152]{1,0:T(8,128)(2,1)S(1)}, u32[]{:S(2)}, u32[]{:S(2)}) collective-permute-start(bf16[32,1152]{1,0:T(8,128)(2,1)S(1)} %collective-permute-done.5.refs_8_), channel_id=1, source_target_pairs={{0,1},{1,0},{2,3},{3,2},{4,5},{5,4},{6,7},{7,6},{8,9},{9,8},{10,11... | collective-permute-start | bytes 221192 | tf_op jit(solution)/shard_map/ppermute | solution.py:244
  29.0 1.4 %collective-permute-start.12 = (bf16[32,1152]{1,0:T(8,128)(2,1)S(1)}, bf16[32,1152]{1,0:T(8,128)(2,1)S(1)}, u32[]{:S(2)}, u32[]{:S(2)}) collective-permute-start(bf16[32,1152]{1,0:T(8,128)(2,1)S(1)} %collective-permute-done.6.refs_3_), channel_id=1, source_target_pairs={{0,1},{1,0},{2,3},{3,2},{4,5},{5,4},{6,7},{7,6},{8,9},{9,8},{10,11... | collective-permute-start | bytes 221192 | tf_op jit(solution)/shard_map/ppermute | solution.py:244
  29.0 1.4 %collective-permute-start.11 = (bf16[32,1024]{1,0:T(8,128)(2,1)S(1)}, bf16[32,1024]{1,0:T(8,128)(2,1)S(1)}, u32[]{:S(2)}, u32[]{:S(2)}) collective-permute-start(bf16[32,1024]{1,0:T(8,128)(2,1)S(1)} %collective-permute-done.4.refs_2_), channel_id=1, source_target_pairs={{0,1},{1,0},{2,3},{3,2},{4,5},{5,4},{6,7},{7,6},{8,9},{9,8},{10,11... | collective-permute-start | bytes 196616 | tf_op jit(solution)/shard_map/ppermute | solution.py:244
  40.7 2.0 %collective-permute-start.20 = (bf16[128,2048]{1,0:T(8,128)(2,1)S(1)}, bf16[128,2048]{1,0:T(8,128)(2,1)S(1)}, u32[]{:S(2)}, u32[]{:S(2)}) collective-permute-start(bf16[128,2048]{1,0:T(8,128)(2,1)S(1)} %other.3), channel_id=1, source_target_pairs={{0,1},{1,0},{2,3},{3,2},{4,5},{5,4},{6,7},{7,6},{8,9},{9,8},{10,11... | collective-permute-start | bytes 1572872 | tf_op jit(solution)/shard_map/ppermute | solution.py:247
  42.4 20.4 %copy-start.2 = (bf16[32,4096]{1,0:T(8,128)(2,1)S(1)}, bf16[32,4096]{1,0:T(8,128)(2,1)}, u32[]{:S(2)}) copy-start(bf16[32,4096]{1,0:T(8,128)(2,1)} %refs_1_.1) | copy-start | bytes 786436
  42.5 5.7 %collective-permute-start.19 = (bf16[128,2048]{1,0:T(8,128)(2,1)S(1)}, bf16[128,2048]{1,0:T(8,128)(2,1)S(1)}, u32[]{:S(2)}, u32[]{:S(2)}) collective-permute-start(bf16[128,2048]{1,0:T(8,128)(2,1)S(1)} %other.2), channel_id=1, source_target_pairs={{0,1},{1,0},{2,3},{3,2},{4,5},{5,4},{6,7},{7,6},{8,9},{9,8},{10,11... | collective-permute-start | bytes 1572872 | tf_op jit(solution)/shard_map/ppermute | solution.py:247
  44.0 6.4 %collective-permute-start.21 = (bf16[32,2048]{1,0:T(8,128)(2,1)S(1)}, bf16[32,2048]{1,0:T(8,128)(2,1)S(1)}, u32[]{:S(2)}, u32[]{:S(2)}) collective-permute-start(bf16[32,2048]{1,0:T(8,128)(2,1)S(1)} %get-tuple-element.28), channel_id=1, source_target_pairs={{0,2},{2,0},{4,6},{6,4},{8,10},{10,8},{12,14},{14,12},{1,3},{3,1},... | collective-permute-start | bytes 393224 | tf_op jit(solution)/shard_map/ppermute | solution.py:254
  44.4 8.8 %collective-permute-start.23 = (bf16[32,2048]{1,0:T(8,128)(2,1)S(1)}, bf16[32,2048]{1,0:T(8,128)(2,1)S(1)}, u32[]{:S(2)}, u32[]{:S(2)}) collective-permute-start(bf16[32,2048]{1,0:T(8,128)(2,1)S(1)} %get-tuple-element.30), channel_id=1, source_target_pairs={{0,2},{2,0},{4,6},{6,4},{8,10},{10,8},{12,14},{14,12},{1,3},{3,1},... | collective-permute-start | bytes 393224 | tf_op jit(solution)/shard_map/ppermute | solution.py:254
  46.1 9.9 %collective-permute-start.25 = (bf16[32,2048]{1,0:T(8,128)(2,1)S(1)}, bf16[32,2048]{1,0:T(8,128)(2,1)S(1)}, u32[]{:S(2)}, u32[]{:S(2)}) collective-permute-start(bf16[32,2048]{1,0:T(8,128)(2,1)S(1)} %get-tuple-element.32), channel_id=1, source_target_pairs={{0,2},{2,0},{4,6},{6,4},{8,10},{10,8},{12,14},{14,12},{1,3},{3,1},... | collective-permute-start | bytes 393224 | tf_op jit(solution)/shard_map/ppermute | solution.py:254
  46.5 11.8 %collective-permute-start.27 = (bf16[32,2048]{1,0:T(8,128)(2,1)S(1)}, bf16[32,2048]{1,0:T(8,128)(2,1)S(1)}, u32[]{:S(2)}, u32[]{:S(2)}) collective-permute-start(bf16[32,2048]{1,0:T(8,128)(2,1)S(1)} %get-tuple-element.34), channel_id=1, source_target_pairs={{0,2},{2,0},{4,6},{6,4},{8,10},{10,8},{12,14},{14,12},{1,3},{3,1},... | collective-permute-start | bytes 393224 | tf_op jit(solution)/shard_map/ppermute | solution.py:254
  50.4 7.8 %collective-permute-start.22 = (bf16[32,2048]{1,0:T(8,128)(2,1)S(1)}, bf16[32,2048]{1,0:T(8,128)(2,1)S(1)}, u32[]{:S(2)}, u32[]{:S(2)}) collective-permute-start(bf16[32,2048]{1,0:T(8,128)(2,1)S(1)} %add_convert_fusion.3), channel_id=1, source_target_pairs={{0,8},{2,10},{4,12},{6,14},{8,0},{10,2},{12,4},{14,6},{1,9},{3,11}... | collective-permute-start | bytes 393224 | tf_op jit(solution)/shard_map/ppermute | solution.py:256
  53.2 8.2 %collective-permute-start.24 = (bf16[32,2048]{1,0:T(8,128)(2,1)S(1)}, bf16[32,2048]{1,0:T(8,128)(2,1)S(1)}, u32[]{:S(2)}, u32[]{:S(2)}) collective-permute-start(bf16[32,2048]{1,0:T(8,128)(2,1)S(1)} %add_convert_fusion.2), channel_id=1, source_target_pairs={{0,12},{2,14},{4,0},{6,2},{8,4},{10,6},{12,8},{14,10},{1,13},{3,15... | collective-permute-start | bytes 393224 | tf_op jit(solution)/shard_map/ppermute | solution.py:256
  56.1 6.8 %collective-permute-start.26 = (bf16[32,2048]{1,0:T(8,128)(2,1)S(1)}, bf16[32,2048]{1,0:T(8,128)(2,1)S(1)}, u32[]{:S(2)}, u32[]{:S(2)}) collective-permute-start(bf16[32,2048]{1,0:T(8,128)(2,1)S(1)} %add_convert_fusion.1), channel_id=1, source_target_pairs={{0,4},{2,6},{4,8},{6,10},{8,12},{10,14},{12,0},{14,2},{1,5},{3,7},... | collective-permute-start | bytes 393224 | tf_op jit(solution)/shard_map/ppermute | solution.py:256

commit v10 on v8

--- a/solution.py
+++ b/solution.py
@@ -213,10 +213,13 @@
 
     packed = prepare(hidden_in, expert_ids, route_scores, expert_slot)
     order = sorted(range(1, outer), key=lambda k: -min(k, outer - k))
-    same, opposite = {0: packed}, {0: lax.ppermute(packed, "sect", across)}
+    same, opposite = {0: packed}, {}
+    held = packed
     for k in order[::-1]:
-        block = after(packed, opposite[0]) if k == order[0] and outer > 2 else packed
-        same[k] = lax.ppermute(block, "sect", along(k))
+        same[k] = lax.ppermute(held if k == order[0] else packed, "sect", along(k))
+        if held is packed:
+            held = after(packed, same[k])
+    opposite[0] = lax.ppermute(held, "sect", across)
     for k in order[::-1]:
         opposite[k] = lax.ppermute(same[k], "sect", across)
     blocks = [side[k] for side in (opposite, same) for k in range(outer)]

time: 61 us -> 60.3 us (0.989)
  waiting for transfers between devices: 25.5 us -> 22.4 us
  starting transfers between devices: 18.9 us -> 21.2 us
    ppermute x3, starting transfers between devices: 1.75 us -> 4.93 us  [on_device(): block = lax.ppermute(block.astype(bf16), 'sect', along(-k)).astype(f32)]
    ppermute x4, waiting for transfers between devices: 6.75 us -> 3.74 us  [on_device(): block = near_sum[k] + lax.ppermute(far_sum[k], 'sect', across).astype(f32)]
    ppermute x4, starting transfers between devices: 9.46 us -> 6.96 us  [the longest x3 5.44 us: on_device(): same[k] = lax.ppermute(held if k == order[0] else packed, 'sect', along(k))]
    ppermute x3, starting transfers between devices: 1.52 us -> 3.55 us  [on_device(): opposite[k] = lax.ppermute(same[k], 'sect', across)]
    ppermute x4, waiting for transfers between devices: 8.27 us -> 9.02 us  [the longest x3 9.02 us: on_device(): same[k] = lax.ppermute(held if k == order[0] else packed, 'sect', along(k))]
    ppermute x3, waiting for transfers between devices: 4.27 us -> 3.53 us  [on_device(): opposite[k] = lax.ppermute(same[k], 'sect', across)]
  transfers between devices with their start and end apart: 24 -> 24, of which waited for: 14 -> 11; matrix products, arithmetic and copies ran while one was open for 0% -> 0% of each run, Pallas kernels for 6% -> 6%
where the time goes in v10:
time: 60.3 us; the launch traced here: 60.1 us
  waiting for transfers between devices  22.4 us (37%)
  starting transfers between devices  21.2 us (35%)
  Pallas kernels  15.5 us (26%)
  other arithmetic  0.83 us (1%)
    ppermute x3, waiting for transfers between devices, on_device(): same[k] = lax.ppermute(held if k == order[0] else packed, 'sect', along(k))  9.02 us
    pallas_call x1, Pallas kernels, run_hidden(): pl.pallas_call(functools.partial(hidden_kernel, half, experts, blocks), o...  8.9 us
    ppermute x3, starting transfers between devices, on_device(): same[k] = lax.ppermute(held if k == order[0] else packed, 'sect', along(k))  5.44 us
    pallas_call x4, Pallas kernels, run_down(): pl.pallas_call(functools.partial(down_kernel, len(extra)), out_shape=[jax...  5.17 us
    ppermute x3, starting transfers between devices, on_device(): block = lax.ppermute(block.astype(bf16), 'sect', along(-k)).astype(f32)  4.93 us
    ppermute x3, waiting for transfers between devices, on_device(): block = lax.ppermute(block.astype(bf16), 'sect', along(-k)).astype(f32)  4.74 us
    ppermute x4, starting transfers between devices, on_device(): block = near_sum[k] + lax.ppermute(far_sum[k], 'sect', across).astype(f32)  4.12 us
    ppermute x4, waiting for transfers between devices, on_device(): block = near_sum[k] + lax.ppermute(far_sum[k], 'sect', across).astype(f32)  3.74 us
  transfers between devices with their start and end apart: 24, of which 11 were waited for; matrix products, arithmetic and copies ran while one was open for 0% of the time, Pallas kernels for 6%

profile of v10, /device:TPU:0, one launch (start us, length us, event | category | flops | bytes accessed | tf_op | source)
XLA Modules:
  0.0 60.1 jit_solution(6990909239799465661)
XLA Ops:
  0.0 0.0 slice-start.3
  0.0 1.4 %prepare.1.refs_4_ = bf16[32,2176]{1,0:T(8,128)(2,1)S(1)} custom-call(s32[32]{0:T(128)} %refs_0_.1, bf16[32,4096]{1,0:T(8,128)(2,1)} %refs_1_.1, s32[8,32]{1,0:T(8,128)} %bitcast.4, f32[8,32]{1,0:T(8,128)} %bitcast.5), custom_call_target="tpu_custom_call" | custom-call | flops 40000000000 | bytes 262144 | tf_op jit(solution)/shard_map/prepare/pallas_call | solution.py:61
  1.4 5.1 %collective-permute-start = (bf16[32,2176]{1,0:T(8,128)(2,1)S(1)}, bf16[32,2176]{1,0:T(8,128)(2,1)S(1)}, u32[]{:S(2)}, u32[]{:S(2)}) collective-permute-start(bf16[32,2176]{1,0:T(8,128)(2,1)S(1)} %prepare.1.refs_4_), channel_id=1, source_target_pairs={{0,12},{2,14},{4,0},{6,2},{8,4},{10,6},{12,8},{14,10},{1,13},{3,15... | collective-permute-start | bytes 417800 | tf_op jit(solution)/shard_map/ppermute | solution.py:219
  6.6 0.0 collective-permute-start.2
  6.6 0.0 collective-permute-start.11
  6.6 4.1 %collective-permute-done.refs_7_ = bf16[32,2176]{1,0:T(8,128)(2,1)S(1)} collective-permute-done((bf16[32,2176]{1,0:T(8,128)(2,1)S(1)}, bf16[32,2176]{1,0:T(8,128)(2,1)S(1)}, u32[]{:S(2)}, u32[]{:S(2)}) %collective-permute-start) | collective-permute-done | bytes 139296 | tf_op jit(solution)/shard_map/ppermute | solution.py:219
  10.6 0.3 collective-permute-start.4
  11.0 1.5 %collective-permute-start.1 = (bf16[32,2176]{1,0:T(8,128)(2,1)S(1)}, bf16[32,2176]{1,0:T(8,128)(2,1)S(1)}, u32[]{:S(2)}, u32[]{:S(2)}) collective-permute-start(bf16[32,2176]{1,0:T(8,128)(2,1)S(1)} %prepare.1.refs_4_), channel_id=1, source_target_pairs={{0,2},{2,0},{4,6},{6,4},{8,10},{10,8},{12,14},{14,12},{1,3},{3,1},... | collective-permute-start | bytes 417800 | tf_op jit(solution)/shard_map/ppermute | solution.py:222
  12.5 0.5 collective-permute-start.6
  13.0 0.6 %collective-permute-done.2.refs_5_ = bf16[32,2176]{1,0:T(8,128)(2,1)S(1)} collective-permute-done((bf16[32,2176]{1,0:T(8,128)(2,1)S(1)}, bf16[32,2176]{1,0:T(8,128)(2,1)S(1)}, u32[]{:S(2)}, u32[]{:S(2)}) %collective-permute-start.2) | collective-permute-done | bytes 139296 | tf_op jit(solution)/shard_map/ppermute | solution.py:219
  13.6 1.5 %collective-permute-start.3 = (bf16[32,2176]{1,0:T(8,128)(2,1)S(1)}, bf16[32,2176]{1,0:T(8,128)(2,1)S(1)}, u32[]{:S(2)}, u32[]{:S(2)}) collective-permute-start(bf16[32,2176]{1,0:T(8,128)(2,1)S(1)} %collective-permute-done.2.refs_5_), channel_id=1, source_target_pairs={{0,2},{2,0},{4,6},{6,4},{8,10},{10,8},{12,14},{14,12},{1,3},{3,1},... | collective-permute-start | bytes 417800 | tf_op jit(solution)/shard_map/ppermute | solution.py:224
  15.1 0.0 collective-permute-done.11.refs_12_
  15.1 0.0 collective-permute-start.14
  15.1 4.3 %collective-permute-done.4.refs_6_ = bf16[32,2176]{1,0:T(8,128)(2,1)S(1)} collective-permute-done((bf16[32,2176]{1,0:T(8,128)(2,1)S(1)}, bf16[32,2176]{1,0:T(8,128)(2,1)S(1)}, u32[]{:S(2)}, u32[]{:S(2)}) %collective-permute-start.4) | collective-permute-done | bytes 139296 | tf_op jit(solution)/shard_map/ppermute | solution.py:219
  19.5 0.0 collective-permute-start.12
  19.5 0.0 collective-permute-done.1.refs_0_
  19.5 1.5 %collective-permute-start.5 = (bf16[32,2176]{1,0:T(8,128)(2,1)S(1)}, bf16[32,2176]{1,0:T(8,128)(2,1)S(1)}, u32[]{:S(2)}, u32[]{:S(2)}) collective-permute-start(bf16[32,2176]{1,0:T(8,128)(2,1)S(1)} %collective-permute-done.4.refs_6_), channel_id=1, source_target_pairs={{0,2},{2,0},{4,6},{6,4},{8,10},{10,8},{12,14},{14,12},{1,3},{3,1},... | collective-permute-start | bytes 417800 | tf_op jit(solution)/shard_map/ppermute | solution.py:224
  21.0 0.0 collective-permute-done.6.refs_3_
  21.0 0.2 collective-permute-start.13
  21.2 0.0 collective-permute-done.3.refs_1_
  21.2 0.3 collective-permute-start.7
  21.5 0.0 collective-permute-done.14.refs_15_
  21.5 0.2 collective-permute-start.10
  21.7 0.0 collective-permute-done.12.refs_13_
  21.7 0.3 collective-permute-start.8
  22.0 3.5 %collective-permute-done.5.refs_2_ = bf16[32,2176]{1,0:T(8,128)(2,1)S(1)} collective-permute-done((bf16[32,2176]{1,0:T(8,128)(2,1)S(1)}, bf16[32,2176]{1,0:T(8,128)(2,1)S(1)}, u32[]{:S(2)}, u32[]{:S(2)}) %collective-permute-start.5) | collective-permute-done | bytes 139296 | tf_op jit(solution)/shard_map/ppermute | solution.py:224
  25.5 0.0 collective-permute-start.9
  25.6 0.0 collective-permute-done.13.refs_14_
  25.6 0.0 collective-permute-done.7.refs_8_
  25.6 0.0 collective-permute-done.10.refs_11_
  25.6 0.0 collective-permute-done.8.refs_9_
  25.6 1.3 %collective-permute-done.9.refs_10_ = bf16[32,2176]{1,0:T(8,128)(2,1)S(1)} collective-permute-done((bf16[32,2176]{1,0:T(8,128)(2,1)S(1)}, bf16[32,2176]{1,0:T(8,128)(2,1)S(1)}, u32[]{:S(2)}, u32[]{:S(2)}) %collective-permute-start.9) | collective-permute-done | bytes 139296 | tf_op jit(solution)/shard_map/ppermute | solution.py:226
  26.9 0.0 copy-done
  26.9 0.0 copy-done.1
  26.9 8.9 %hidden.1 = (bf16[128,2048]{1,0:T(8,128)(2,1)S(1)}, bf16[128,2048]{1,0:T(8,128)(2,1)S(1)}) custom-call(bf16[32,2176]{1,0:T(8,128)(2,1)S(1)} %collective-permute-done.1.refs_0_, bf16[32,2176]{1,0:T(8,128)(2,1)S(1)} %collective-permute-done.3.refs_1_, bf16[32,2176]{1,0:T(8,128)(2,1)S(1)} %collective-permute-done.5.refs_2_, ...), custom_call_target="tpu_custom_call" | custom-call | flops 8589934592 | bytes 2097152 | tf_op jit(solution)/shard_map/hidden/pallas_call | solution.py:131
  35.8 0.0 slice-done
  35.8 0.0 slice-done.1
  35.8 0.0 slice-done.2
  35.9 0.0 slice-done.3
  35.9 1.3 %other.3 = bf16[128,2048]{1,0:T(8,128)(2,1)S(1)} custom-call(bf16[128,2048]{1,0:T(8,128)(2,1)S(1)} %get-tuple-element.19.hidden_ref, bf16[4,512,4096]{2,1,0:T(8,128)(2,1)S(1)} %bitcast.3), custom_call_target="tpu_custom_call" | custom-call | flops 524288 | bytes 512 | tf_op jit(solution)/shard_map/other/pallas_call | solution.py:175
  37.2 0.2 collective-permute-start.16
  37.4 1.3 %other.2 = bf16[128,2048]{1,0:T(8,128)(2,1)S(1)} custom-call(bf16[128,2048]{1,0:T(8,128)(2,1)S(1)} %get-tuple-element.17.hidden_ref, bf16[4,512,4096]{2,1,0:T(8,128)(2,1)S(1)} %bitcast.3), custom_call_target="tpu_custom_call" | custom-call | flops 524288 | bytes 512 | tf_op jit(solution)/shard_map/other/pallas_call | solution.py:175
  38.7 0.0 copy-start.2
  38.7 0.4 collective-permute-start.15
  39.1 0.0 collective-permute-done.16.refs_0_
  39.1 1.3 %mine.3 = (bf16[32,2048]{1,0:T(8,128)(2,1)S(1)}, bf16[32,2048]{1,0:T(8,128)(2,1)S(1)}, bf16[32,2048]{1,0:T(8,128)(2,1)S(1)}, bf16[32,2048]{1,0:T(8,128)(2,1)S(1)}) custom-call(bf16[128,2048]{1,0:T(8,128)(2,1)S(1)} %get-tuple-element.19.hidden_ref, bf16[4,512,4096]{2,1,0:T(8,128)(2,1)S(1)} %bitcast.3, bf16[128,2048]{1,0:T(8,128)(2,1)S(1)} %collective-permute-done.16.refs_0_), custom_call_target="tpu_custom_call" | custom-call | flops 524288 | bytes 512 | tf_op jit(solution)/shard_map/mine/pallas_call | solution.py:175
  40.5 1.6 %collective-permute-start.17 = (bf16[32,2048]{1,0:T(8,128)(2,1)S(1)}, bf16[32,2048]{1,0:T(8,128)(2,1)S(1)}, u32[]{:S(2)}, u32[]{:S(2)}) collective-permute-start(bf16[32,2048]{1,0:T(8,128)(2,1)S(1)} %get-tuple-element.20), channel_id=1, source_target_pairs={{0,2},{2,0},{4,6},{6,4},{8,10},{10,8},{12,14},{14,12},{1,3},{3,1},... | collective-permute-start | bytes 393224 | tf_op jit(solution)/shard_map/ppermute | solution.py:236
  42.1 0.5 collective-permute-start.19
  42.5 1.5 %collective-permute-start.21 = (bf16[32,2048]{1,0:T(8,128)(2,1)S(1)}, bf16[32,2048]{1,0:T(8,128)(2,1)S(1)}, u32[]{:S(2)}, u32[]{:S(2)}) collective-permute-start(bf16[32,2048]{1,0:T(8,128)(2,1)S(1)} %get-tuple-element.24), channel_id=1, source_target_pairs={{0,2},{2,0},{4,6},{6,4},{8,10},{10,8},{12,14},{14,12},{1,3},{3,1},... | collective-permute-start | bytes 393224 | tf_op jit(solution)/shard_map/ppermute | solution.py:236
  44.1 0.5 collective-permute-start.23
  44.6 0.0 collective-permute-done.15.refs_0_
  44.6 1.3 %mine.2 = (f32[32,2048]{1,0:T(8,128)S(1)}, f32[32,2048]{1,0:T(8,128)S(1)}, f32[32,2048]{1,0:T(8,128)S(1)}, f32[32,2048]{1,0:T(8,128)S(1)}) custom-call(bf16[128,2048]{1,0:T(8,128)(2,1)S(1)} %get-tuple-element.17.hidden_ref, bf16[4,512,4096]{2,1,0:T(8,128)(2,1)S(1)} %bitcast.3, bf16[128,2048]{1,0:T(8,128)(2,1)S(1)} %collective-permute-done.15.refs_0_), custom_call_target="tpu_custom_call" | custom-call | flops 524288 | bytes 512 | tf_op jit(solution)/shard_map/mine/pallas_call | solution.py:175
  45.9 1.0 %collective-permute-done.17 = bf16[32,2048]{1,0:T(8,128)(2,1)S(1)} collective-permute-done((bf16[32,2048]{1,0:T(8,128)(2,1)S(1)}, bf16[32,2048]{1,0:T(8,128)(2,1)S(1)}, u32[]{:S(2)}, u32[]{:S(2)}) %collective-permute-start.17) | collective-permute-done | bytes 131104 | tf_op jit(solution)/shard_map/ppermute | solution.py:236
  46.9 0.2 collective-permute-start.18
  47.1 2.5 %collective-permute-done.19 = bf16[32,2048]{1,0:T(8,128)(2,1)S(1)} collective-permute-done((bf16[32,2048]{1,0:T(8,128)(2,1)S(1)}, bf16[32,2048]{1,0:T(8,128)(2,1)S(1)}, u32[]{:S(2)}, u32[]{:S(2)}) %collective-permute-start.19) | collective-permute-done | bytes 131104 | tf_op jit(solution)/shard_map/ppermute | solution.py:236
  49.7 2.6 %collective-permute-start.20 = (bf16[32,2048]{1,0:T(8,128)(2,1)S(1)}, bf16[32,2048]{1,0:T(8,128)(2,1)S(1)}, u32[]{:S(2)}, u32[]{:S(2)}) collective-permute-start(bf16[32,2048]{1,0:T(8,128)(2,1)S(1)} %add_convert_fusion.2), channel_id=1, source_target_pairs={{0,12},{2,14},{4,0},{6,2},{8,4},{10,6},{12,8},{14,10},{1,13},{3,15... | collective-permute-start | bytes 393224 | tf_op jit(solution)/shard_map/ppermute | solution.py:238
  52.3 0.2 collective-permute-done.21
  52.5 2.1 %collective-permute-start.22 = (bf16[32,2048]{1,0:T(8,128)(2,1)S(1)}, bf16[32,2048]{1,0:T(8,128)(2,1)S(1)}, u32[]{:S(2)}, u32[]{:S(2)}) collective-permute-start(bf16[32,2048]{1,0:T(8,128)(2,1)S(1)} %add_convert_fusion.1), channel_id=1, source_target_pairs={{0,4},{2,6},{4,8},{6,10},{8,12},{10,14},{12,0},{14,2},{1,5},{3,7},... | collective-permute-start | bytes 393224 | tf_op jit(solution)/shard_map/ppermute | solution.py:238
  54.6 0.0 collective-permute-done.23
  54.7 1.0 %collective-permute-done.18 = bf16[32,2048]{1,0:T(8,128)(2,1)S(1)} collective-permute-done((bf16[32,2048]{1,0:T(8,128)(2,1)S(1)}, bf16[32,2048]{1,0:T(8,128)(2,1)S(1)}, u32[]{:S(2)}, u32[]{:S(2)}) %collective-permute-start.18) | collective-permute-done | bytes 131104 | tf_op jit(solution)/shard_map/ppermute | solution.py:238
  55.7 0.4 collective-permute-done.20
  56.1 3.3 %collective-permute-done.22 = bf16[32,2048]{1,0:T(8,128)(2,1)S(1)} collective-permute-done((bf16[32,2048]{1,0:T(8,128)(2,1)S(1)}, bf16[32,2048]{1,0:T(8,128)(2,1)S(1)}, u32[]{:S(2)}, u32[]{:S(2)}) %collective-permute-start.22) | collective-permute-done | bytes 131104 | tf_op jit(solution)/shard_map/ppermute | solution.py:238
  59.4 0.0 copy-done.2
  59.4 0.8 %add_convert_fusion = bf16[32,2048]{1,0:T(8,128)(2,1)} fusion(f32[32,2048]{1,0:T(8,128)S(1)} %get-tuple-element.25, bf16[32,2048]{1,0:T(8,128)(2,1)S(1)} %collective-permute-done.23, bf16[32,2048]{1,0:T(8,128)(2,1)S(1)} %collective-permute-done.22, bf16[32,2048]{1,0:T(8,128)(2,1)S(1)} %collective-permute-done.20, ...), kind=kLoop, calls=%fused_computation | loop fusion | flops 720896 | bytes 1048580 | tf_op jit(solution)/shard_map/convert_element_type | solution.py:240
  (9 shorter events, 0.1 us)
Async XLA Ops:
  0.0 35.8 %slice-start = ((s8[16777216]{0:T(1024)(128)(4,1)}), s8[4194304]{0:T(1024)(128)(4,1)S(1)}, s32[]{:S(2)}) async-start(s8[16777216]{0:T(1024)(128)(4,1)} %bitcast.2), calls=%async_computation | async-start | bytes 8388608
  0.0 26.9 %copy-start = (bf16[4,4096,512]{2,1,0:T(8,128)(2,1)S(1)}, bf16[4,4096,512]{2,1,0:T(8,128)(2,1)}, u32[]{:S(2)}) copy-start(bf16[4,4096,512]{2,1,0:T(8,128)(2,1)} %refs_16_.1) | copy-start | bytes 50331652
  0.0 26.9 %copy-start.1 = (bf16[4,4096,512]{2,1,0:T(8,128)(2,1)S(1)}, bf16[4,4096,512]{2,1,0:T(8,128)(2,1)}, u32[]{:S(2)}) copy-start(bf16[4,4096,512]{2,1,0:T(8,128)(2,1)} %refs_17_.1) | copy-start | bytes 50331652
  0.0 35.8 %slice-start.1 = ((s8[16777216]{0:T(1024)(128)(4,1)}), s8[4194304]{0:T(1024)(128)(4,1)S(1)}, s32[]{:S(2)}) async-start(s8[16777216]{0:T(1024)(128)(4,1)} %bitcast.2), calls=%async_computation.1 | async-start | bytes 8388608
  0.0 35.8 %slice-start.2 = ((s8[16777216]{0:T(1024)(128)(4,1)}), s8[4194304]{0:T(1024)(128)(4,1)S(1)}, s32[]{:S(2)}) async-start(s8[16777216]{0:T(1024)(128)(4,1)} %bitcast.2), calls=%async_computation.2 | async-start | bytes 8388608
  0.0 35.8 %slice-start.3 = ((s8[16777216]{0:T(1024)(128)(4,1)}), s8[4194304]{0:T(1024)(128)(4,1)S(1)}, s32[]{:S(2)}) async-start(s8[16777216]{0:T(1024)(128)(4,1)} %bitcast.2), calls=%async_computation.3 | async-start | bytes 8388608
  1.4 9.2 %collective-permute-start = (bf16[32,2176]{1,0:T(8,128)(2,1)S(1)}, bf16[32,2176]{1,0:T(8,128)(2,1)S(1)}, u32[]{:S(2)}, u32[]{:S(2)}) collective-permute-start(bf16[32,2176]{1,0:T(8,128)(2,1)S(1)} %prepare.1.refs_4_), channel_id=1, source_target_pairs={{0,12},{2,14},{4,0},{6,2},{8,4},{10,6},{12,8},{14,10},{1,13},{3,15... | collective-permute-start | bytes 417800 | tf_op jit(solution)/shard_map/ppermute | solution.py:219
  6.6 7.1 %collective-permute-start.2 = (bf16[32,2176]{1,0:T(8,128)(2,1)S(1)}, bf16[32,2176]{1,0:T(8,128)(2,1)S(1)}, u32[]{:S(2)}, u32[]{:S(2)}) collective-permute-start(bf16[32,2176]{1,0:T(8,128)(2,1)S(1)} %prepare.1.refs_4_), channel_id=1, source_target_pairs={{0,4},{2,6},{4,8},{6,10},{8,12},{10,14},{12,0},{14,2},{1,5},{3,7},... | collective-permute-start | bytes 417800 | tf_op jit(solution)/shard_map/ppermute | solution.py:219
  6.6 8.6 %collective-permute-start.11 = (bf16[32,2176]{1,0:T(8,128)(2,1)S(1)}, bf16[32,2176]{1,0:T(8,128)(2,1)S(1)}, u32[]{:S(2)}, u32[]{:S(2)}) collective-permute-start(bf16[32,2176]{1,0:T(8,128)(2,1)S(1)} %prepare.1.refs_4_), channel_id=1, source_target_pairs={{0,1},{1,0},{2,3},{3,2},{4,5},{5,4},{6,7},{7,6},{8,9},{9,8},{10,11... | collective-permute-start | bytes 417800 | tf_op jit(solution)/shard_map/ppermute | solution.py:226
  10.6 8.8 %collective-permute-start.4 = (bf16[32,2176]{1,0:T(8,128)(2,1)S(1)}, bf16[32,2176]{1,0:T(8,128)(2,1)S(1)}, u32[]{:S(2)}, u32[]{:S(2)}) collective-permute-start(bf16[32,2176]{1,0:T(8,128)(2,1)S(1)} %prepare.1.refs_4_), channel_id=1, source_target_pairs={{0,8},{2,10},{4,12},{6,14},{8,0},{10,2},{12,4},{14,6},{1,9},{3,11}... | collective-permute-start | bytes 417800 | tf_op jit(solution)/shard_map/ppermute | solution.py:219
  11.0 8.5 %collective-permute-start.1 = (bf16[32,2176]{1,0:T(8,128)(2,1)S(1)}, bf16[32,2176]{1,0:T(8,128)(2,1)S(1)}, u32[]{:S(2)}, u32[]{:S(2)}) collective-permute-start(bf16[32,2176]{1,0:T(8,128)(2,1)S(1)} %prepare.1.refs_4_), channel_id=1, source_target_pairs={{0,2},{2,0},{4,6},{6,4},{8,10},{10,8},{12,14},{14,12},{1,3},{3,1},... | collective-permute-start | bytes 417800 | tf_op jit(solution)/shard_map/ppermute | solution.py:222
  12.5 8.5 %collective-permute-start.6 = (bf16[32,2176]{1,0:T(8,128)(2,1)S(1)}, bf16[32,2176]{1,0:T(8,128)(2,1)S(1)}, u32[]{:S(2)}, u32[]{:S(2)}) collective-permute-start(bf16[32,2176]{1,0:T(8,128)(2,1)S(1)} %collective-permute-done.refs_7_), channel_id=1, source_target_pairs={{0,2},{2,0},{4,6},{6,4},{8,10},{10,8},{12,14},{14,12},{1,3},{3,1},... | collective-permute-start | bytes 417800 | tf_op jit(solution)/shard_map/ppermute | solution.py:224
  13.6 7.6 %collective-permute-start.3 = (bf16[32,2176]{1,0:T(8,128)(2,1)S(1)}, bf16[32,2176]{1,0:T(8,128)(2,1)S(1)}, u32[]{:S(2)}, u32[]{:S(2)}) collective-permute-start(bf16[32,2176]{1,0:T(8,128)(2,1)S(1)} %collective-permute-done.2.refs_5_), channel_id=1, source_target_pairs={{0,2},{2,0},{4,6},{6,4},{8,10},{10,8},{12,14},{14,12},{1,3},{3,1},... | collective-permute-start | bytes 417800 | tf_op jit(solution)/shard_map/ppermute | solution.py:224
  15.1 6.4 %collective-permute-start.14 = (bf16[32,2176]{1,0:T(8,128)(2,1)S(1)}, bf16[32,2176]{1,0:T(8,128)(2,1)S(1)}, u32[]{:S(2)}, u32[]{:S(2)}) collective-permute-start(bf16[32,2176]{1,0:T(8,128)(2,1)S(1)} %collective-permute-done.refs_7_), channel_id=1, source_target_pairs={{0,1},{1,0},{2,3},{3,2},{4,5},{5,4},{6,7},{7,6},{8,9},{9,8},{10,11... | collective-permute-start | bytes 417800 | tf_op jit(solution)/shard_map/ppermute | solution.py:226
  19.5 2.3 %collective-permute-start.12 = (bf16[32,2176]{1,0:T(8,128)(2,1)S(1)}, bf16[32,2176]{1,0:T(8,128)(2,1)S(1)}, u32[]{:S(2)}, u32[]{:S(2)}) collective-permute-start(bf16[32,2176]{1,0:T(8,128)(2,1)S(1)} %collective-permute-done.2.refs_5_), channel_id=1, source_target_pairs={{0,1},{1,0},{2,3},{3,2},{4,5},{5,4},{6,7},{7,6},{8,9},{9,8},{10,11... | collective-permute-start | bytes 417800 | tf_op jit(solution)/shard_map/ppermute | solution.py:226
  19.5 6.1 %collective-permute-start.5 = (bf16[32,2176]{1,0:T(8,128)(2,1)S(1)}, bf16[32,2176]{1,0:T(8,128)(2,1)S(1)}, u32[]{:S(2)}, u32[]{:S(2)}) collective-permute-start(bf16[32,2176]{1,0:T(8,128)(2,1)S(1)} %collective-permute-done.4.refs_6_), channel_id=1, source_target_pairs={{0,2},{2,0},{4,6},{6,4},{8,10},{10,8},{12,14},{14,12},{1,3},{3,1},... | collective-permute-start | bytes 417800 | tf_op jit(solution)/shard_map/ppermute | solution.py:224
  21.0 4.6 %collective-permute-start.13 = (bf16[32,2176]{1,0:T(8,128)(2,1)S(1)}, bf16[32,2176]{1,0:T(8,128)(2,1)S(1)}, u32[]{:S(2)}, u32[]{:S(2)}) collective-permute-start(bf16[32,2176]{1,0:T(8,128)(2,1)S(1)} %collective-permute-done.4.refs_6_), channel_id=1, source_target_pairs={{0,1},{1,0},{2,3},{3,2},{4,5},{5,4},{6,7},{7,6},{8,9},{9,8},{10,11... | collective-permute-start | bytes 417800 | tf_op jit(solution)/shard_map/ppermute | solution.py:226
  21.2 4.3 %collective-permute-start.7 = (bf16[32,2176]{1,0:T(8,128)(2,1)S(1)}, bf16[32,2176]{1,0:T(8,128)(2,1)S(1)}, u32[]{:S(2)}, u32[]{:S(2)}) collective-permute-start(bf16[32,2176]{1,0:T(8,128)(2,1)S(1)} %collective-permute-done.1.refs_0_), channel_id=1, source_target_pairs={{0,1},{1,0},{2,3},{3,2},{4,5},{5,4},{6,7},{7,6},{8,9},{9,8},{10,11... | collective-permute-start | bytes 417800 | tf_op jit(solution)/shard_map/ppermute | solution.py:226
  21.5 4.1 %collective-permute-start.10 = (bf16[32,2176]{1,0:T(8,128)(2,1)S(1)}, bf16[32,2176]{1,0:T(8,128)(2,1)S(1)}, u32[]{:S(2)}, u32[]{:S(2)}) collective-permute-start(bf16[32,2176]{1,0:T(8,128)(2,1)S(1)} %collective-permute-done.6.refs_3_), channel_id=1, source_target_pairs={{0,1},{1,0},{2,3},{3,2},{4,5},{5,4},{6,7},{7,6},{8,9},{9,8},{10,11... | collective-permute-start | bytes 417800 | tf_op jit(solution)/shard_map/ppermute | solution.py:226
  21.7 3.8 %collective-permute-start.8 = (bf16[32,2176]{1,0:T(8,128)(2,1)S(1)}, bf16[32,2176]{1,0:T(8,128)(2,1)S(1)}, u32[]{:S(2)}, u32[]{:S(2)}) collective-permute-start(bf16[32,2176]{1,0:T(8,128)(2,1)S(1)} %collective-permute-done.3.refs_1_), channel_id=1, source_target_pairs={{0,1},{1,0},{2,3},{3,2},{4,5},{5,4},{6,7},{7,6},{8,9},{9,8},{10,11... | collective-permute-start | bytes 417800 | tf_op jit(solution)/shard_map/ppermute | solution.py:226
  25.5 1.4 %collective-permute-start.9 = (bf16[32,2176]{1,0:T(8,128)(2,1)S(1)}, bf16[32,2176]{1,0:T(8,128)(2,1)S(1)}, u32[]{:S(2)}, u32[]{:S(2)}) collective-permute-start(bf16[32,2176]{1,0:T(8,128)(2,1)S(1)} %collective-permute-done.5.refs_2_), channel_id=1, source_target_pairs={{0,1},{1,0},{2,3},{3,2},{4,5},{5,4},{6,7},{7,6},{8,9},{9,8},{10,11... | collective-permute-start | bytes 417800 | tf_op jit(solution)/shard_map/ppermute | solution.py:226
  37.2 2.0 %collective-permute-start.16 = (bf16[128,2048]{1,0:T(8,128)(2,1)S(1)}, bf16[128,2048]{1,0:T(8,128)(2,1)S(1)}, u32[]{:S(2)}, u32[]{:S(2)}) collective-permute-start(bf16[128,2048]{1,0:T(8,128)(2,1)S(1)} %other.3), channel_id=1, source_target_pairs={{0,1},{1,0},{2,3},{3,2},{4,5},{5,4},{6,7},{7,6},{8,9},{9,8},{10,11... | collective-permute-start | bytes 1572872 | tf_op jit(solution)/shard_map/ppermute | solution.py:229
  38.7 20.7 %copy-start.2 = (bf16[32,4096]{1,0:T(8,128)(2,1)S(1)}, bf16[32,4096]{1,0:T(8,128)(2,1)}, u32[]{:S(2)}) copy-start(bf16[32,4096]{1,0:T(8,128)(2,1)} %refs_1_.1) | copy-start | bytes 786436
  38.7 5.9 %collective-permute-start.15 = (bf16[128,2048]{1,0:T(8,128)(2,1)S(1)}, bf16[128,2048]{1,0:T(8,128)(2,1)S(1)}, u32[]{:S(2)}, u32[]{:S(2)}) collective-permute-start(bf16[128,2048]{1,0:T(8,128)(2,1)S(1)} %other.2), channel_id=1, source_target_pairs={{0,1},{1,0},{2,3},{3,2},{4,5},{5,4},{6,7},{7,6},{8,9},{9,8},{10,11... | collective-permute-start | bytes 1572872 | tf_op jit(solution)/shard_map/ppermute | solution.py:229
  40.5 6.4 %collective-permute-start.17 = (bf16[32,2048]{1,0:T(8,128)(2,1)S(1)}, bf16[32,2048]{1,0:T(8,128)(2,1)S(1)}, u32[]{:S(2)}, u32[]{:S(2)}) collective-permute-start(bf16[32,2048]{1,0:T(8,128)(2,1)S(1)} %get-tuple-element.20), channel_id=1, source_target_pairs={{0,2},{2,0},{4,6},{6,4},{8,10},{10,8},{12,14},{14,12},{1,3},{3,1},... | collective-permute-start | bytes 393224 | tf_op jit(solution)/shard_map/ppermute | solution.py:236
  42.1 7.6 %collective-permute-start.19 = (bf16[32,2048]{1,0:T(8,128)(2,1)S(1)}, bf16[32,2048]{1,0:T(8,128)(2,1)S(1)}, u32[]{:S(2)}, u32[]{:S(2)}) collective-permute-start(bf16[32,2048]{1,0:T(8,128)(2,1)S(1)} %get-tuple-element.22), channel_id=1, source_target_pairs={{0,2},{2,0},{4,6},{6,4},{8,10},{10,8},{12,14},{14,12},{1,3},{3,1},... | collective-permute-start | bytes 393224 | tf_op jit(solution)/shard_map/ppermute | solution.py:236
  42.5 9.9 %collective-permute-start.21 = (bf16[32,2048]{1,0:T(8,128)(2,1)S(1)}, bf16[32,2048]{1,0:T(8,128)(2,1)S(1)}, u32[]{:S(2)}, u32[]{:S(2)}) collective-permute-start(bf16[32,2048]{1,0:T(8,128)(2,1)S(1)} %get-tuple-element.24), channel_id=1, source_target_pairs={{0,2},{2,0},{4,6},{6,4},{8,10},{10,8},{12,14},{14,12},{1,3},{3,1},... | collective-permute-start | bytes 393224 | tf_op jit(solution)/shard_map/ppermute | solution.py:236
  44.1 10.6 %collective-permute-start.23 = (bf16[32,2048]{1,0:T(8,128)(2,1)S(1)}, bf16[32,2048]{1,0:T(8,128)(2,1)S(1)}, u32[]{:S(2)}, u32[]{:S(2)}) collective-permute-start(bf16[32,2048]{1,0:T(8,128)(2,1)S(1)} %get-tuple-element.26), channel_id=1, source_target_pairs={{0,2},{2,0},{4,6},{6,4},{8,10},{10,8},{12,14},{14,12},{1,3},{3,1},... | collective-permute-start | bytes 393224 | tf_op jit(solution)/shard_map/ppermute | solution.py:236
  46.9 8.8 %collective-permute-start.18 = (bf16[32,2048]{1,0:T(8,128)(2,1)S(1)}, bf16[32,2048]{1,0:T(8,128)(2,1)S(1)}, u32[]{:S(2)}, u32[]{:S(2)}) collective-permute-start(bf16[32,2048]{1,0:T(8,128)(2,1)S(1)} %add_convert_fusion.3), channel_id=1, source_target_pairs={{0,8},{2,10},{4,12},{6,14},{8,0},{10,2},{12,4},{14,6},{1,9},{3,11}... | collective-permute-start | bytes 393224 | tf_op jit(solution)/shard_map/ppermute | solution.py:238
  49.7 6.4 %collective-permute-start.20 = (bf16[32,2048]{1,0:T(8,128)(2,1)S(1)}, bf16[32,2048]{1,0:T(8,128)(2,1)S(1)}, u32[]{:S(2)}, u32[]{:S(2)}) collective-permute-start(bf16[32,2048]{1,0:T(8,128)(2,1)S(1)} %add_convert_fusion.2), channel_id=1, source_target_pairs={{0,12},{2,14},{4,0},{6,2},{8,4},{10,6},{12,8},{14,10},{1,13},{3,15... | collective-permute-start | bytes 393224 | tf_op jit(solution)/shard_map/ppermute | solution.py:238
  52.5 6.9 %collective-permute-start.22 = (bf16[32,2048]{1,0:T(8,128)(2,1)S(1)}, bf16[32,2048]{1,0:T(8,128)(2,1)S(1)}, u32[]{:S(2)}, u32[]{:S(2)}) collective-permute-start(bf16[32,2048]{1,0:T(8,128)(2,1)S(1)} %add_convert_fusion.1), channel_id=1, source_target_pairs={{0,4},{2,6},{4,8},{6,10},{8,12},{10,14},{12,0},{14,2},{1,5},{3,7},... | collective-permute-start | bytes 393224 | tf_op jit(solution)/shard_map/ppermute | solution.py:238

commit v11 on v10

--- a/solution.py
+++ b/solution.py
@@ -216,7 +216,7 @@
     same, opposite = {0: packed}, {}
     held = packed
     for k in order[::-1]:
-        same[k] = lax.ppermute(held if k == order[0] else packed, "sect", along(k))
+        same[k] = lax.ppermute(packed, "sect", along(k))
         if held is packed:
             held = after(packed, same[k])
     opposite[0] = lax.ppermute(held, "sect", across)

time: 60.3 us -> 59.9 us (level)
  waiting for transfers between devices: 22.4 us -> 19.5 us
  starting transfers between devices: 21.2 us -> 23.7 us
    ppermute x3, waiting for transfers between devices: 9.02 us -> 7.44 us  [on_device(): same[k] = lax.ppermute(packed, 'sect', along(k))]
    ppermute x3, starting transfers between devices: 4.93 us -> 6.19 us  [on_device(): block = lax.ppermute(block.astype(bf16), 'sect', along(-k)).astype(f32)]
    ppermute x3, waiting for transfers between devices: 3.53 us -> 2.5 us  [on_device(): opposite[k] = lax.ppermute(same[k], 'sect', across)]
    ppermute x4, waiting for transfers between devices: 3.74 us -> 2.78 us  [on_device(): block = near_sum[k] + lax.ppermute(far_sum[k], 'sect', across).astype(f32)]
    ppermute x3, waiting for transfers between devices: 4.74 us -> 5.45 us  [on_device(): block = lax.ppermute(block.astype(bf16), 'sect', along(-k)).astype(f32)]
    ppermute x3, starting transfers between devices: 5.44 us -> 6.13 us  [on_device(): same[k] = lax.ppermute(packed, 'sect', along(k))]
  transfers between devices with their start and end apart: 24 -> 24, of which waited for: 11 -> 12; matrix products, arithmetic and copies ran while one was open for 0% -> 0% of each run, Pallas kernels for 6% -> 7%
where the time goes in v11:
time: 59.9 us; the launch traced here: 59.7 us
  starting transfers between devices  23.7 us (40%)
  waiting for transfers between devices  19.5 us (33%)
  Pallas kernels  15.5 us (26%)
  other arithmetic  0.83 us (1%)
    pallas_call x1, Pallas kernels, run_hidden(): pl.pallas_call(functools.partial(hidden_kernel, half, experts, blocks), o...  8.9 us
    ppermute x3, waiting for transfers between devices, on_device(): same[k] = lax.ppermute(packed, 'sect', along(k))  7.44 us
    ppermute x3, starting transfers between devices, on_device(): block = lax.ppermute(block.astype(bf16), 'sect', along(-k)).astype(f32)  6.19 us
    ppermute x3, starting transfers between devices, on_device(): same[k] = lax.ppermute(packed, 'sect', along(k))  6.13 us
    ppermute x3, waiting for transfers between devices, on_device(): block = lax.ppermute(block.astype(bf16), 'sect', along(-k)).astype(f32)  5.45 us
    pallas_call x4, Pallas kernels, run_down(): pl.pallas_call(functools.partial(down_kernel, len(extra)), out_shape=[jax...  5.18 us
    ppermute x4, starting transfers between devices, on_device(): block = near_sum[k] + lax.ppermute(far_sum[k], 'sect', across).astype(f32)  4.12 us
    ppermute x3, starting transfers between devices, on_device(): opposite[k] = lax.ppermute(same[k], 'sect', across)  3.55 us
  transfers between devices with their start and end apart: 24, of which 12 were waited for; matrix products, arithmetic and copies ran while one was open for 0% of the time, Pallas kernels for 7%

profile of v11, /device:TPU:0, one launch (start us, length us, event | category | flops | bytes accessed | tf_op | source)
XLA Modules:
  0.0 59.7 jit_solution(5210538985900108738)
XLA Ops:
  0.0 0.0 slice-start.3
  0.0 1.4 %prepare.1.refs_4_ = bf16[32,2176]{1,0:T(8,128)(2,1)S(1)} custom-call(s32[32]{0:T(128)} %refs_0_.1, bf16[32,4096]{1,0:T(8,128)(2,1)} %refs_1_.1, s32[8,32]{1,0:T(8,128)} %bitcast.4, f32[8,32]{1,0:T(8,128)} %bitcast.5), custom_call_target="tpu_custom_call" | custom-call | flops 40000000000 | bytes 262144 | tf_op jit(solution)/shard_map/prepare/pallas_call | solution.py:61
  1.4 5.1 %collective-permute-start = (bf16[32,2176]{1,0:T(8,128)(2,1)S(1)}, bf16[32,2176]{1,0:T(8,128)(2,1)S(1)}, u32[]{:S(2)}, u32[]{:S(2)}) collective-permute-start(bf16[32,2176]{1,0:T(8,128)(2,1)S(1)} %prepare.1.refs_4_), channel_id=1, source_target_pairs={{0,12},{2,14},{4,0},{6,2},{8,4},{10,6},{12,8},{14,10},{1,13},{3,15... | collective-permute-start | bytes 417800 | tf_op jit(solution)/shard_map/ppermute | solution.py:219
  6.6 0.0 collective-permute-start.2
  6.6 1.0 %collective-permute-start.4 = (bf16[32,2176]{1,0:T(8,128)(2,1)S(1)}, bf16[32,2176]{1,0:T(8,128)(2,1)S(1)}, u32[]{:S(2)}, u32[]{:S(2)}) collective-permute-start(bf16[32,2176]{1,0:T(8,128)(2,1)S(1)} %prepare.1.refs_4_), channel_id=1, source_target_pairs={{0,8},{2,10},{4,12},{6,14},{8,0},{10,2},{12,4},{14,6},{1,9},{3,11}... | collective-permute-start | bytes 417800 | tf_op jit(solution)/shard_map/ppermute | solution.py:219
  7.6 0.0 collective-permute-start.11
  7.6 3.1 %collective-permute-done.refs_7_ = bf16[32,2176]{1,0:T(8,128)(2,1)S(1)} collective-permute-done((bf16[32,2176]{1,0:T(8,128)(2,1)S(1)}, bf16[32,2176]{1,0:T(8,128)(2,1)S(1)}, u32[]{:S(2)}, u32[]{:S(2)}) %collective-permute-start) | collective-permute-done | bytes 139296 | tf_op jit(solution)/shard_map/ppermute | solution.py:219
  10.6 1.5 %collective-permute-start.1 = (bf16[32,2176]{1,0:T(8,128)(2,1)S(1)}, bf16[32,2176]{1,0:T(8,128)(2,1)S(1)}, u32[]{:S(2)}, u32[]{:S(2)}) collective-permute-start(bf16[32,2176]{1,0:T(8,128)(2,1)S(1)} %prepare.1.refs_4_), channel_id=1, source_target_pairs={{0,2},{2,0},{4,6},{6,4},{8,10},{10,8},{12,14},{14,12},{1,3},{3,1},... | collective-permute-start | bytes 417800 | tf_op jit(solution)/shard_map/ppermute | solution.py:222
  12.2 0.5 collective-permute-start.6
  12.7 2.3 %collective-permute-done.2.refs_5_ = bf16[32,2176]{1,0:T(8,128)(2,1)S(1)} collective-permute-done((bf16[32,2176]{1,0:T(8,128)(2,1)S(1)}, bf16[32,2176]{1,0:T(8,128)(2,1)S(1)}, u32[]{:S(2)}, u32[]{:S(2)}) %collective-permute-start.2) | collective-permute-done | bytes 139296 | tf_op jit(solution)/shard_map/ppermute | solution.py:219
  15.0 1.5 %collective-permute-start.3 = (bf16[32,2176]{1,0:T(8,128)(2,1)S(1)}, bf16[32,2176]{1,0:T(8,128)(2,1)S(1)}, u32[]{:S(2)}, u32[]{:S(2)}) collective-permute-start(bf16[32,2176]{1,0:T(8,128)(2,1)S(1)} %collective-permute-done.2.refs_5_), channel_id=1, source_target_pairs={{0,2},{2,0},{4,6},{6,4},{8,10},{10,8},{12,14},{14,12},{1,3},{3,1},... | collective-permute-start | bytes 417800 | tf_op jit(solution)/shard_map/ppermute | solution.py:224
  16.5 2.0 %collective-permute-done.4.refs_6_ = bf16[32,2176]{1,0:T(8,128)(2,1)S(1)} collective-permute-done((bf16[32,2176]{1,0:T(8,128)(2,1)S(1)}, bf16[32,2176]{1,0:T(8,128)(2,1)S(1)}, u32[]{:S(2)}, u32[]{:S(2)}) %collective-permute-start.4) | collective-permute-done | bytes 139296 | tf_op jit(solution)/shard_map/ppermute | solution.py:219
  18.6 1.5 %collective-permute-start.5 = (bf16[32,2176]{1,0:T(8,128)(2,1)S(1)}, bf16[32,2176]{1,0:T(8,128)(2,1)S(1)}, u32[]{:S(2)}, u32[]{:S(2)}) collective-permute-start(bf16[32,2176]{1,0:T(8,128)(2,1)S(1)} %collective-permute-done.4.refs_6_), channel_id=1, source_target_pairs={{0,2},{2,0},{4,6},{6,4},{8,10},{10,8},{12,14},{14,12},{1,3},{3,1},... | collective-permute-start | bytes 417800 | tf_op jit(solution)/shard_map/ppermute | solution.py:224
  20.1 0.0 collective-permute-done.11.refs_12_
  20.1 0.0 collective-permute-start.14
  20.1 0.0 collective-permute-done.1.refs_0_
  20.1 0.5 collective-permute-start.12
  20.6 0.0 collective-permute-done.6.refs_3_
  20.6 0.1 collective-permute-start.13
  20.7 0.0 collective-permute-done.3.refs_1_
  20.7 0.4 collective-permute-start.7
  21.1 2.5 %collective-permute-done.5.refs_2_ = bf16[32,2176]{1,0:T(8,128)(2,1)S(1)} collective-permute-done((bf16[32,2176]{1,0:T(8,128)(2,1)S(1)}, bf16[32,2176]{1,0:T(8,128)(2,1)S(1)}, u32[]{:S(2)}, u32[]{:S(2)}) %collective-permute-start.5) | collective-permute-done | bytes 139296 | tf_op jit(solution)/shard_map/ppermute | solution.py:224
  23.6 0.0 collective-permute-start.10
  23.6 0.0 collective-permute-done.14.refs_15_
  23.6 0.5 collective-permute-start.8
  24.1 0.0 collective-permute-done.12.refs_13_
  24.1 0.1 collective-permute-start.9
  24.2 0.0 collective-permute-done.13.refs_14_
  24.2 0.0 collective-permute-done.7.refs_8_
  24.2 0.8 %collective-permute-done.10.refs_11_ = bf16[32,2176]{1,0:T(8,128)(2,1)S(1)} collective-permute-done((bf16[32,2176]{1,0:T(8,128)(2,1)S(1)}, bf16[32,2176]{1,0:T(8,128)(2,1)S(1)}, u32[]{:S(2)}, u32[]{:S(2)}) %collective-permute-start.10) | collective-permute-done | bytes 139296 | tf_op jit(solution)/shard_map/ppermute | solution.py:226
  25.0 0.2 collective-permute-done.8.refs_9_
  25.2 0.3 collective-permute-done.9.refs_10_
  25.5 0.0 copy-done
  25.5 0.0 copy-done.1
  25.5 8.9 %hidden.1 = (bf16[128,2048]{1,0:T(8,128)(2,1)S(1)}, bf16[128,2048]{1,0:T(8,128)(2,1)S(1)}) custom-call(bf16[32,2176]{1,0:T(8,128)(2,1)S(1)} %collective-permute-done.1.refs_0_, bf16[32,2176]{1,0:T(8,128)(2,1)S(1)} %collective-permute-done.3.refs_1_, bf16[32,2176]{1,0:T(8,128)(2,1)S(1)} %collective-permute-done.5.refs_2_, ...), custom_call_target="tpu_custom_call" | custom-call | flops 8589934592 | bytes 2097152 | tf_op jit(solution)/shard_map/hidden/pallas_call | solution.py:131
  34.4 0.0 slice-done
  34.4 0.0 slice-done.1
  34.4 0.0 slice-done.2
  34.4 0.0 slice-done.3
  34.5 1.3 %other.3 = bf16[128,2048]{1,0:T(8,128)(2,1)S(1)} custom-call(bf16[128,2048]{1,0:T(8,128)(2,1)S(1)} %get-tuple-element.19.hidden_ref, bf16[4,512,4096]{2,1,0:T(8,128)(2,1)S(1)} %bitcast.3), custom_call_target="tpu_custom_call" | custom-call | flops 524288 | bytes 512 | tf_op jit(solution)/shard_map/other/pallas_call | solution.py:175
  35.8 0.3 collective-permute-start.16
  36.0 1.3 %other.2 = bf16[128,2048]{1,0:T(8,128)(2,1)S(1)} custom-call(bf16[128,2048]{1,0:T(8,128)(2,1)S(1)} %get-tuple-element.17.hidden_ref, bf16[4,512,4096]{2,1,0:T(8,128)(2,1)S(1)} %bitcast.3), custom_call_target="tpu_custom_call" | custom-call | flops 524288 | bytes 512 | tf_op jit(solution)/shard_map/other/pallas_call | solution.py:175
  37.3 0.0 copy-start.2
  37.3 0.4 collective-permute-start.15
  37.7 0.0 collective-permute-done.16.refs_0_
  37.7 1.3 %mine.3 = (bf16[32,2048]{1,0:T(8,128)(2,1)S(1)}, bf16[32,2048]{1,0:T(8,128)(2,1)S(1)}, bf16[32,2048]{1,0:T(8,128)(2,1)S(1)}, bf16[32,2048]{1,0:T(8,128)(2,1)S(1)}) custom-call(bf16[128,2048]{1,0:T(8,128)(2,1)S(1)} %get-tuple-element.19.hidden_ref, bf16[4,512,4096]{2,1,0:T(8,128)(2,1)S(1)} %bitcast.3, bf16[128,2048]{1,0:T(8,128)(2,1)S(1)} %collective-permute-done.16.refs_0_), custom_call_target="tpu_custom_call" | custom-call | flops 524288 | bytes 512 | tf_op jit(solution)/shard_map/mine/pallas_call | solution.py:175
  39.0 1.6 %collective-permute-start.17 = (bf16[32,2048]{1,0:T(8,128)(2,1)S(1)}, bf16[32,2048]{1,0:T(8,128)(2,1)S(1)}, u32[]{:S(2)}, u32[]{:S(2)}) collective-permute-start(bf16[32,2048]{1,0:T(8,128)(2,1)S(1)} %get-tuple-element.20), channel_id=1, source_target_pairs={{0,2},{2,0},{4,6},{6,4},{8,10},{10,8},{12,14},{14,12},{1,3},{3,1},... | collective-permute-start | bytes 393224 | tf_op jit(solution)/shard_map/ppermute | solution.py:236
  40.6 0.5 collective-permute-start.19
  41.1 1.5 %collective-permute-start.21 = (bf16[32,2048]{1,0:T(8,128)(2,1)S(1)}, bf16[32,2048]{1,0:T(8,128)(2,1)S(1)}, u32[]{:S(2)}, u32[]{:S(2)}) collective-permute-start(bf16[32,2048]{1,0:T(8,128)(2,1)S(1)} %get-tuple-element.24), channel_id=1, source_target_pairs={{0,2},{2,0},{4,6},{6,4},{8,10},{10,8},{12,14},{14,12},{1,3},{3,1},... | collective-permute-start | bytes 393224 | tf_op jit(solution)/shard_map/ppermute | solution.py:236
  42.7 0.5 collective-permute-start.23
  43.2 0.0 collective-permute-done.15.refs_0_
  43.2 1.3 %mine.2 = (f32[32,2048]{1,0:T(8,128)S(1)}, f32[32,2048]{1,0:T(8,128)S(1)}, f32[32,2048]{1,0:T(8,128)S(1)}, f32[32,2048]{1,0:T(8,128)S(1)}) custom-call(bf16[128,2048]{1,0:T(8,128)(2,1)S(1)} %get-tuple-element.17.hidden_ref, bf16[4,512,4096]{2,1,0:T(8,128)(2,1)S(1)} %bitcast.3, bf16[128,2048]{1,0:T(8,128)(2,1)S(1)} %collective-permute-done.15.refs_0_), custom_call_target="tpu_custom_call" | custom-call | flops 524288 | bytes 512 | tf_op jit(solution)/shard_map/mine/pallas_call | solution.py:175
  44.5 1.0 %collective-permute-done.17 = bf16[32,2048]{1,0:T(8,128)(2,1)S(1)} collective-permute-done((bf16[32,2048]{1,0:T(8,128)(2,1)S(1)}, bf16[32,2048]{1,0:T(8,128)(2,1)S(1)}, u32[]{:S(2)}, u32[]{:S(2)}) %collective-permute-start.17) | collective-permute-done | bytes 131104 | tf_op jit(solution)/shard_map/ppermute | solution.py:236
  45.5 1.0 %collective-permute-start.18 = (bf16[32,2048]{1,0:T(8,128)(2,1)S(1)}, bf16[32,2048]{1,0:T(8,128)(2,1)S(1)}, u32[]{:S(2)}, u32[]{:S(2)}) collective-permute-start(bf16[32,2048]{1,0:T(8,128)(2,1)S(1)} %add_convert_fusion.3), channel_id=1, source_target_pairs={{0,8},{2,10},{4,12},{6,14},{8,0},{10,2},{12,4},{14,6},{1,9},{3,11}... | collective-permute-start | bytes 393224 | tf_op jit(solution)/shard_map/ppermute | solution.py:238
  46.5 1.8 %collective-permute-done.19 = bf16[32,2048]{1,0:T(8,128)(2,1)S(1)} collective-permute-done((bf16[32,2048]{1,0:T(8,128)(2,1)S(1)}, bf16[32,2048]{1,0:T(8,128)(2,1)S(1)}, u32[]{:S(2)}, u32[]{:S(2)}) %collective-permute-start.19) | collective-permute-done | bytes 131104 | tf_op jit(solution)/shard_map/ppermute | solution.py:236
  48.3 3.8 %collective-permute-start.20 = (bf16[32,2048]{1,0:T(8,128)(2,1)S(1)}, bf16[32,2048]{1,0:T(8,128)(2,1)S(1)}, u32[]{:S(2)}, u32[]{:S(2)}) collective-permute-start(bf16[32,2048]{1,0:T(8,128)(2,1)S(1)} %add_convert_fusion.2), channel_id=1, source_target_pairs={{0,12},{2,14},{4,0},{6,2},{8,4},{10,6},{12,8},{14,10},{1,13},{3,15... | collective-permute-start | bytes 393224 | tf_op jit(solution)/shard_map/ppermute | solution.py:238
  52.1 0.0 collective-permute-done.21
  52.1 1.4 %collective-permute-start.22 = (bf16[32,2048]{1,0:T(8,128)(2,1)S(1)}, bf16[32,2048]{1,0:T(8,128)(2,1)S(1)}, u32[]{:S(2)}, u32[]{:S(2)}) collective-permute-start(bf16[32,2048]{1,0:T(8,128)(2,1)S(1)} %add_convert_fusion.1), channel_id=1, source_target_pairs={{0,4},{2,6},{4,8},{6,10},{8,12},{10,14},{12,0},{14,2},{1,5},{3,7},... | collective-permute-start | bytes 393224 | tf_op jit(solution)/shard_map/ppermute | solution.py:238
  53.5 0.0 collective-permute-done.23
  53.5 1.0 %collective-permute-done.18 = bf16[32,2048]{1,0:T(8,128)(2,1)S(1)} collective-permute-done((bf16[32,2048]{1,0:T(8,128)(2,1)S(1)}, bf16[32,2048]{1,0:T(8,128)(2,1)S(1)}, u32[]{:S(2)}, u32[]{:S(2)}) %collective-permute-start.18) | collective-permute-done | bytes 131104 | tf_op jit(solution)/shard_map/ppermute | solution.py:238
  54.5 0.5 collective-permute-done.20
  55.1 3.9 %collective-permute-done.22 = bf16[32,2048]{1,0:T(8,128)(2,1)S(1)} collective-permute-done((bf16[32,2048]{1,0:T(8,128)(2,1)S(1)}, bf16[32,2048]{1,0:T(8,128)(2,1)S(1)}, u32[]{:S(2)}, u32[]{:S(2)}) %collective-permute-start.22) | collective-permute-done | bytes 131104 | tf_op jit(solution)/shard_map/ppermute | solution.py:238
  59.0 0.0 copy-done.2
  59.0 0.8 %add_convert_fusion = bf16[32,2048]{1,0:T(8,128)(2,1)} fusion(f32[32,2048]{1,0:T(8,128)S(1)} %get-tuple-element.25, bf16[32,2048]{1,0:T(8,128)(2,1)S(1)} %collective-permute-done.23, bf16[32,2048]{1,0:T(8,128)(2,1)S(1)} %collective-permute-done.22, bf16[32,2048]{1,0:T(8,128)(2,1)S(1)} %collective-permute-done.20, ...), kind=kLoop, calls=%fused_computation | loop fusion | flops 720896 | bytes 1048580 | tf_op jit(solution)/shard_map/convert_element_type | solution.py:240
  (9 shorter events, 0.1 us)
Async XLA Ops:
  0.0 34.4 %slice-start = ((s8[16777216]{0:T(1024)(128)(4,1)}), s8[4194304]{0:T(1024)(128)(4,1)S(1)}, s32[]{:S(2)}) async-start(s8[16777216]{0:T(1024)(128)(4,1)} %bitcast.2), calls=%async_computation | async-start | bytes 8388608
  0.0 25.5 %copy-start = (bf16[4,4096,512]{2,1,0:T(8,128)(2,1)S(1)}, bf16[4,4096,512]{2,1,0:T(8,128)(2,1)}, u32[]{:S(2)}) copy-start(bf16[4,4096,512]{2,1,0:T(8,128)(2,1)} %refs_16_.1) | copy-start | bytes 50331652
  0.0 25.5 %copy-start.1 = (bf16[4,4096,512]{2,1,0:T(8,128)(2,1)S(1)}, bf16[4,4096,512]{2,1,0:T(8,128)(2,1)}, u32[]{:S(2)}) copy-start(bf16[4,4096,512]{2,1,0:T(8,128)(2,1)} %refs_17_.1) | copy-start | bytes 50331652
  0.0 34.4 %slice-start.1 = ((s8[16777216]{0:T(1024)(128)(4,1)}), s8[4194304]{0:T(1024)(128)(4,1)S(1)}, s32[]{:S(2)}) async-start(s8[16777216]{0:T(1024)(128)(4,1)} %bitcast.2), calls=%async_computation.1 | async-start | bytes 8388608
  0.0 34.4 %slice-start.2 = ((s8[16777216]{0:T(1024)(128)(4,1)}), s8[4194304]{0:T(1024)(128)(4,1)S(1)}, s32[]{:S(2)}) async-start(s8[16777216]{0:T(1024)(128)(4,1)} %bitcast.2), calls=%async_computation.2 | async-start | bytes 8388608
  0.0 34.4 %slice-start.3 = ((s8[16777216]{0:T(1024)(128)(4,1)}), s8[4194304]{0:T(1024)(128)(4,1)S(1)}, s32[]{:S(2)}) async-start(s8[16777216]{0:T(1024)(128)(4,1)} %bitcast.2), calls=%async_computation.3 | async-start | bytes 8388608
  1.4 9.2 %collective-permute-start = (bf16[32,2176]{1,0:T(8,128)(2,1)S(1)}, bf16[32,2176]{1,0:T(8,128)(2,1)S(1)}, u32[]{:S(2)}, u32[]{:S(2)}) collective-permute-start(bf16[32,2176]{1,0:T(8,128)(2,1)S(1)} %prepare.1.refs_4_), channel_id=1, source_target_pairs={{0,12},{2,14},{4,0},{6,2},{8,4},{10,6},{12,8},{14,10},{1,13},{3,15... | collective-permute-start | bytes 417800 | tf_op jit(solution)/shard_map/ppermute | solution.py:219
  6.6 8.5 %collective-permute-start.2 = (bf16[32,2176]{1,0:T(8,128)(2,1)S(1)}, bf16[32,2176]{1,0:T(8,128)(2,1)S(1)}, u32[]{:S(2)}, u32[]{:S(2)}) collective-permute-start(bf16[32,2176]{1,0:T(8,128)(2,1)S(1)} %prepare.1.refs_4_), channel_id=1, source_target_pairs={{0,4},{2,6},{4,8},{6,10},{8,12},{10,14},{12,0},{14,2},{1,5},{3,7},... | collective-permute-start | bytes 417800 | tf_op jit(solution)/shard_map/ppermute | solution.py:219
  6.6 12.0 %collective-permute-start.4 = (bf16[32,2176]{1,0:T(8,128)(2,1)S(1)}, bf16[32,2176]{1,0:T(8,128)(2,1)S(1)}, u32[]{:S(2)}, u32[]{:S(2)}) collective-permute-start(bf16[32,2176]{1,0:T(8,128)(2,1)S(1)} %prepare.1.refs_4_), channel_id=1, source_target_pairs={{0,8},{2,10},{4,12},{6,14},{8,0},{10,2},{12,4},{14,6},{1,9},{3,11}... | collective-permute-start | bytes 417800 | tf_op jit(solution)/shard_map/ppermute | solution.py:219
  7.6 12.5 %collective-permute-start.11 = (bf16[32,2176]{1,0:T(8,128)(2,1)S(1)}, bf16[32,2176]{1,0:T(8,128)(2,1)S(1)}, u32[]{:S(2)}, u32[]{:S(2)}) collective-permute-start(bf16[32,2176]{1,0:T(8,128)(2,1)S(1)} %prepare.1.refs_4_), channel_id=1, source_target_pairs={{0,1},{1,0},{2,3},{3,2},{4,5},{5,4},{6,7},{7,6},{8,9},{9,8},{10,11... | collective-permute-start | bytes 417800 | tf_op jit(solution)/shard_map/ppermute | solution.py:226
  10.6 9.5 %collective-permute-start.1 = (bf16[32,2176]{1,0:T(8,128)(2,1)S(1)}, bf16[32,2176]{1,0:T(8,128)(2,1)S(1)}, u32[]{:S(2)}, u32[]{:S(2)}) collective-permute-start(bf16[32,2176]{1,0:T(8,128)(2,1)S(1)} %prepare.1.refs_4_), channel_id=1, source_target_pairs={{0,2},{2,0},{4,6},{6,4},{8,10},{10,8},{12,14},{14,12},{1,3},{3,1},... | collective-permute-start | bytes 417800 | tf_op jit(solution)/shard_map/ppermute | solution.py:222
  12.2 8.4 %collective-permute-start.6 = (bf16[32,2176]{1,0:T(8,128)(2,1)S(1)}, bf16[32,2176]{1,0:T(8,128)(2,1)S(1)}, u32[]{:S(2)}, u32[]{:S(2)}) collective-permute-start(bf16[32,2176]{1,0:T(8,128)(2,1)S(1)} %collective-permute-done.refs_7_), channel_id=1, source_target_pairs={{0,2},{2,0},{4,6},{6,4},{8,10},{10,8},{12,14},{14,12},{1,3},{3,1},... | collective-permute-start | bytes 417800 | tf_op jit(solution)/shard_map/ppermute | solution.py:224
  15.0 5.7 %collective-permute-start.3 = (bf16[32,2176]{1,0:T(8,128)(2,1)S(1)}, bf16[32,2176]{1,0:T(8,128)(2,1)S(1)}, u32[]{:S(2)}, u32[]{:S(2)}) collective-permute-start(bf16[32,2176]{1,0:T(8,128)(2,1)S(1)} %collective-permute-done.2.refs_5_), channel_id=1, source_target_pairs={{0,2},{2,0},{4,6},{6,4},{8,10},{10,8},{12,14},{14,12},{1,3},{3,1},... | collective-permute-start | bytes 417800 | tf_op jit(solution)/shard_map/ppermute | solution.py:224
  18.6 5.1 %collective-permute-start.5 = (bf16[32,2176]{1,0:T(8,128)(2,1)S(1)}, bf16[32,2176]{1,0:T(8,128)(2,1)S(1)}, u32[]{:S(2)}, u32[]{:S(2)}) collective-permute-start(bf16[32,2176]{1,0:T(8,128)(2,1)S(1)} %collective-permute-done.4.refs_6_), channel_id=1, source_target_pairs={{0,2},{2,0},{4,6},{6,4},{8,10},{10,8},{12,14},{14,12},{1,3},{3,1},... | collective-permute-start | bytes 417800 | tf_op jit(solution)/shard_map/ppermute | solution.py:224
  20.1 3.5 %collective-permute-start.14 = (bf16[32,2176]{1,0:T(8,128)(2,1)S(1)}, bf16[32,2176]{1,0:T(8,128)(2,1)S(1)}, u32[]{:S(2)}, u32[]{:S(2)}) collective-permute-start(bf16[32,2176]{1,0:T(8,128)(2,1)S(1)} %collective-permute-done.refs_7_), channel_id=1, source_target_pairs={{0,1},{1,0},{2,3},{3,2},{4,5},{5,4},{6,7},{7,6},{8,9},{9,8},{10,11... | collective-permute-start | bytes 417800 | tf_op jit(solution)/shard_map/ppermute | solution.py:226
  20.1 4.0 %collective-permute-start.12 = (bf16[32,2176]{1,0:T(8,128)(2,1)S(1)}, bf16[32,2176]{1,0:T(8,128)(2,1)S(1)}, u32[]{:S(2)}, u32[]{:S(2)}) collective-permute-start(bf16[32,2176]{1,0:T(8,128)(2,1)S(1)} %collective-permute-done.2.refs_5_), channel_id=1, source_target_pairs={{0,1},{1,0},{2,3},{3,2},{4,5},{5,4},{6,7},{7,6},{8,9},{9,8},{10,11... | collective-permute-start | bytes 417800 | tf_op jit(solution)/shard_map/ppermute | solution.py:226
  20.6 3.6 %collective-permute-start.13 = (bf16[32,2176]{1,0:T(8,128)(2,1)S(1)}, bf16[32,2176]{1,0:T(8,128)(2,1)S(1)}, u32[]{:S(2)}, u32[]{:S(2)}) collective-permute-start(bf16[32,2176]{1,0:T(8,128)(2,1)S(1)} %collective-permute-done.4.refs_6_), channel_id=1, source_target_pairs={{0,1},{1,0},{2,3},{3,2},{4,5},{5,4},{6,7},{7,6},{8,9},{9,8},{10,11... | collective-permute-start | bytes 417800 | tf_op jit(solution)/shard_map/ppermute | solution.py:226
  20.7 3.5 %collective-permute-start.7 = (bf16[32,2176]{1,0:T(8,128)(2,1)S(1)}, bf16[32,2176]{1,0:T(8,128)(2,1)S(1)}, u32[]{:S(2)}, u32[]{:S(2)}) collective-permute-start(bf16[32,2176]{1,0:T(8,128)(2,1)S(1)} %collective-permute-done.1.refs_0_), channel_id=1, source_target_pairs={{0,1},{1,0},{2,3},{3,2},{4,5},{5,4},{6,7},{7,6},{8,9},{9,8},{10,11... | collective-permute-start | bytes 417800 | tf_op jit(solution)/shard_map/ppermute | solution.py:226
  23.6 1.4 %collective-permute-start.10 = (bf16[32,2176]{1,0:T(8,128)(2,1)S(1)}, bf16[32,2176]{1,0:T(8,128)(2,1)S(1)}, u32[]{:S(2)}, u32[]{:S(2)}) collective-permute-start(bf16[32,2176]{1,0:T(8,128)(2,1)S(1)} %collective-permute-done.6.refs_3_), channel_id=1, source_target_pairs={{0,1},{1,0},{2,3},{3,2},{4,5},{5,4},{6,7},{7,6},{8,9},{9,8},{10,11... | collective-permute-start | bytes 417800 | tf_op jit(solution)/shard_map/ppermute | solution.py:226
  23.6 1.6 %collective-permute-start.8 = (bf16[32,2176]{1,0:T(8,128)(2,1)S(1)}, bf16[32,2176]{1,0:T(8,128)(2,1)S(1)}, u32[]{:S(2)}, u32[]{:S(2)}) collective-permute-start(bf16[32,2176]{1,0:T(8,128)(2,1)S(1)} %collective-permute-done.3.refs_1_), channel_id=1, source_target_pairs={{0,1},{1,0},{2,3},{3,2},{4,5},{5,4},{6,7},{7,6},{8,9},{9,8},{10,11... | collective-permute-start | bytes 417800 | tf_op jit(solution)/shard_map/ppermute | solution.py:226
  24.1 1.4 %collective-permute-start.9 = (bf16[32,2176]{1,0:T(8,128)(2,1)S(1)}, bf16[32,2176]{1,0:T(8,128)(2,1)S(1)}, u32[]{:S(2)}, u32[]{:S(2)}) collective-permute-start(bf16[32,2176]{1,0:T(8,128)(2,1)S(1)} %collective-permute-done.5.refs_2_), channel_id=1, source_target_pairs={{0,1},{1,0},{2,3},{3,2},{4,5},{5,4},{6,7},{7,6},{8,9},{9,8},{10,11... | collective-permute-start | bytes 417800 | tf_op jit(solution)/shard_map/ppermute | solution.py:226
  35.8 2.0 %collective-permute-start.16 = (bf16[128,2048]{1,0:T(8,128)(2,1)S(1)}, bf16[128,2048]{1,0:T(8,128)(2,1)S(1)}, u32[]{:S(2)}, u32[]{:S(2)}) collective-permute-start(bf16[128,2048]{1,0:T(8,128)(2,1)S(1)} %other.3), channel_id=1, source_target_pairs={{0,1},{1,0},{2,3},{3,2},{4,5},{5,4},{6,7},{7,6},{8,9},{9,8},{10,11... | collective-permute-start | bytes 1572872 | tf_op jit(solution)/shard_map/ppermute | solution.py:229
  37.3 21.7 %copy-start.2 = (bf16[32,4096]{1,0:T(8,128)(2,1)S(1)}, bf16[32,4096]{1,0:T(8,128)(2,1)}, u32[]{:S(2)}) copy-start(bf16[32,4096]{1,0:T(8,128)(2,1)} %refs_1_.1) | copy-start | bytes 786436
  37.3 5.8 %collective-permute-start.15 = (bf16[128,2048]{1,0:T(8,128)(2,1)S(1)}, bf16[128,2048]{1,0:T(8,128)(2,1)S(1)}, u32[]{:S(2)}, u32[]{:S(2)}) collective-permute-start(bf16[128,2048]{1,0:T(8,128)(2,1)S(1)} %other.2), channel_id=1, source_target_pairs={{0,1},{1,0},{2,3},{3,2},{4,5},{5,4},{6,7},{7,6},{8,9},{9,8},{10,11... | collective-permute-start | bytes 1572872 | tf_op jit(solution)/shard_map/ppermute | solution.py:229
  39.0 6.4 %collective-permute-start.17 = (bf16[32,2048]{1,0:T(8,128)(2,1)S(1)}, bf16[32,2048]{1,0:T(8,128)(2,1)S(1)}, u32[]{:S(2)}, u32[]{:S(2)}) collective-permute-start(bf16[32,2048]{1,0:T(8,128)(2,1)S(1)} %get-tuple-element.20), channel_id=1, source_target_pairs={{0,2},{2,0},{4,6},{6,4},{8,10},{10,8},{12,14},{14,12},{1,3},{3,1},... | collective-permute-start | bytes 393224 | tf_op jit(solution)/shard_map/ppermute | solution.py:236
  40.6 7.6 %collective-permute-start.19 = (bf16[32,2048]{1,0:T(8,128)(2,1)S(1)}, bf16[32,2048]{1,0:T(8,128)(2,1)S(1)}, u32[]{:S(2)}, u32[]{:S(2)}) collective-permute-start(bf16[32,2048]{1,0:T(8,128)(2,1)S(1)} %get-tuple-element.22), channel_id=1, source_target_pairs={{0,2},{2,0},{4,6},{6,4},{8,10},{10,8},{12,14},{14,12},{1,3},{3,1},... | collective-permute-start | bytes 393224 | tf_op jit(solution)/shard_map/ppermute | solution.py:236
  41.1 10.9 %collective-permute-start.21 = (bf16[32,2048]{1,0:T(8,128)(2,1)S(1)}, bf16[32,2048]{1,0:T(8,128)(2,1)S(1)}, u32[]{:S(2)}, u32[]{:S(2)}) collective-permute-start(bf16[32,2048]{1,0:T(8,128)(2,1)S(1)} %get-tuple-element.24), channel_id=1, source_target_pairs={{0,2},{2,0},{4,6},{6,4},{8,10},{10,8},{12,14},{14,12},{1,3},{3,1},... | collective-permute-start | bytes 393224 | tf_op jit(solution)/shard_map/ppermute | solution.py:236
  42.7 10.9 %collective-permute-start.23 = (bf16[32,2048]{1,0:T(8,128)(2,1)S(1)}, bf16[32,2048]{1,0:T(8,128)(2,1)S(1)}, u32[]{:S(2)}, u32[]{:S(2)}) collective-permute-start(bf16[32,2048]{1,0:T(8,128)(2,1)S(1)} %get-tuple-element.26), channel_id=1, source_target_pairs={{0,2},{2,0},{4,6},{6,4},{8,10},{10,8},{12,14},{14,12},{1,3},{3,1},... | collective-permute-start | bytes 393224 | tf_op jit(solution)/shard_map/ppermute | solution.py:236
  45.5 9.1 %collective-permute-start.18 = (bf16[32,2048]{1,0:T(8,128)(2,1)S(1)}, bf16[32,2048]{1,0:T(8,128)(2,1)S(1)}, u32[]{:S(2)}, u32[]{:S(2)}) collective-permute-start(bf16[32,2048]{1,0:T(8,128)(2,1)S(1)} %add_convert_fusion.3), channel_id=1, source_target_pairs={{0,8},{2,10},{4,12},{6,14},{8,0},{10,2},{12,4},{14,6},{1,9},{3,11}... | collective-permute-start | bytes 393224 | tf_op jit(solution)/shard_map/ppermute | solution.py:238
  48.3 6.8 %collective-permute-start.20 = (bf16[32,2048]{1,0:T(8,128)(2,1)S(1)}, bf16[32,2048]{1,0:T(8,128)(2,1)S(1)}, u32[]{:S(2)}, u32[]{:S(2)}) collective-permute-start(bf16[32,2048]{1,0:T(8,128)(2,1)S(1)} %add_convert_fusion.2), channel_id=1, source_target_pairs={{0,12},{2,14},{4,0},{6,2},{8,4},{10,6},{12,8},{14,10},{1,13},{3,15... | collective-permute-start | bytes 393224 | tf_op jit(solution)/shard_map/ppermute | solution.py:238
  52.1 6.9 %collective-permute-start.22 = (bf16[32,2048]{1,0:T(8,128)(2,1)S(1)}, bf16[32,2048]{1,0:T(8,128)(2,1)S(1)}, u32[]{:S(2)}, u32[]{:S(2)}) collective-permute-start(bf16[32,2048]{1,0:T(8,128)(2,1)S(1)} %add_convert_fusion.1), channel_id=1, source_target_pairs={{0,4},{2,6},{4,8},{6,10},{8,12},{10,14},{12,0},{14,2},{1,5},{3,7},... | collective-permute-start | bytes 393224 | tf_op jit(solution)/shard_map/ppermute | solution.py:238

commit v12 on v11

--- a/solution.py
+++ b/solution.py
@@ -214,16 +214,16 @@
     packed = prepare(hidden_in, expert_ids, route_scores, expert_slot)
     order = sorted(range(1, outer), key=lambda k: -min(k, outer - k))
     same, opposite = {0: packed}, {}
-    held = packed
     for k in order[::-1]:
         same[k] = lax.ppermute(packed, "sect", along(k))
-        if held is packed:
-            held = after(packed, same[k])
-    opposite[0] = lax.ppermute(held, "sect", across)
+    own_other = lax.ppermute(packed, "tp", cores)
+    opposite[0] = lax.ppermute(after(packed, own_other), "sect", across)
     for k in order[::-1]:
         opposite[k] = lax.ppermute(same[k], "sect", across)
     blocks = [side[k] for side in (opposite, same) for k in range(outer)]
-    others = [lax.ppermute(block, "tp", cores) for block in blocks]
+    others = [
+        own_other if block is packed else lax.ppermute(block, "tp", cores) for block in blocks
+    ]
     groups = run_hidden(blocks, others, gate_matrix, up_matrix, experts, outer)
     sent = [
         lax.ppermute(run_down(hidden, down_matrix, None, [bf16])[0], "tp", cores)

time: 59.9 us -> 63.6 us (1.062)
  starting transfers between devices: 23.7 us -> 26.8 us
    ppermute x3, starting transfers between devices: 6.19 us -> 9.64 us  [on_device(): block = lax.ppermute(block.astype(bf16), 'sect', along(-k)).astype(f32)]
    ppermute x3, waiting for transfers between devices: 2.5 us -> 5.19 us  [on_device(): opposite[k] = lax.ppermute(same[k], 'sect', across)]
    ppermute x4, waiting for transfers between devices: 2.78 us -> 0.97 us  [on_device(): block = near_sum[k] + lax.ppermute(far_sum[k], 'sect', across).astype(f32)]
    ppermute x3, waiting for transfers between devices: 7.44 us -> 5.89 us  [on_device(): same[k] = lax.ppermute(packed, 'sect', along(k))]
    ppermute x3, waiting for transfers between devices: 5.45 us -> 6.73 us  [on_device(): block = lax.ppermute(block.astype(bf16), 'sect', along(-k)).astype(f32)]
  transfers between devices with their start and end apart: 24 -> 24, of which waited for: 12 -> 11; matrix products, arithmetic and copies ran while one was open for 0% -> 0% of each run, Pallas kernels for 7% -> 6%
where the time goes in v12:
time: 63.6 us; the launch traced here: 63.4 us
  starting transfers between devices  26.8 us (42%)
  waiting for transfers between devices  20.1 us (32%)
  Pallas kernels  15.5 us (24%)
  other arithmetic  0.83 us (1%)
    ppermute x3, starting transfers between devices, on_device(): block = lax.ppermute(block.astype(bf16), 'sect', along(-k)).astype(f32)  9.64 us
    pallas_call x1, Pallas kernels, run_hidden(): pl.pallas_call(functools.partial(hidden_kernel, half, experts, blocks), o...  8.92 us
    ppermute x3, waiting for transfers between devices, on_device(): block = lax.ppermute(block.astype(bf16), 'sect', along(-k)).astype(f32)  6.73 us
    ppermute x3, waiting for transfers between devices, on_device(): same[k] = lax.ppermute(packed, 'sect', along(k))  5.89 us
    ppermute x3, starting transfers between devices, on_device(): same[k] = lax.ppermute(packed, 'sect', along(k))  5.69 us
    ppermute x3, waiting for transfers between devices, on_device(): opposite[k] = lax.ppermute(same[k], 'sect', across)  5.19 us
    pallas_call x4, Pallas kernels, run_down(): pl.pallas_call(functools.partial(down_kernel, len(extra)), out_shape=[jax...  5.19 us
    ppermute x4, starting transfers between devices, on_device(): block = near_sum[k] + lax.ppermute(far_sum[k], 'sect', across).astype(f32)  4.12 us
  transfers between devices with their start and end apart: 24, of which 11 were waited for; matrix products, arithmetic and copies ran while one was open for 0% of the time, Pallas kernels for 6%

profile of v12, /device:TPU:0, one launch (start us, length us, event | category | flops | bytes accessed | tf_op | source)
XLA Modules:
  0.0 63.4 jit_solution(14856434369474955840)
XLA Ops:
  0.0 0.0 slice-start.3
  0.0 1.4 %prepare.1.refs_4_ = bf16[32,2176]{1,0:T(8,128)(2,1)S(1)} custom-call(s32[32]{0:T(128)} %refs_0_.1, bf16[32,4096]{1,0:T(8,128)(2,1)} %refs_1_.1, s32[8,32]{1,0:T(8,128)} %bitcast.4, f32[8,32]{1,0:T(8,128)} %bitcast.5), custom_call_target="tpu_custom_call" | custom-call | flops 40000000000 | bytes 262144 | tf_op jit(solution)/shard_map/prepare/pallas_call | solution.py:61
  1.4 0.5 collective-permute-start
  2.0 3.7 %collective-permute-start.4 = (bf16[32,2176]{1,0:T(8,128)(2,1)S(1)}, bf16[32,2176]{1,0:T(8,128)(2,1)S(1)}, u32[]{:S(2)}, u32[]{:S(2)}) collective-permute-start(bf16[32,2176]{1,0:T(8,128)(2,1)S(1)} %prepare.1.refs_4_), channel_id=1, source_target_pairs={{0,8},{2,10},{4,12},{6,14},{8,0},{10,2},{12,4},{14,6},{1,9},{3,11}... | collective-permute-start | bytes 417800 | tf_op jit(solution)/shard_map/ppermute | solution.py:218
  5.6 1.3 %collective-permute-start.6 = (bf16[32,2176]{1,0:T(8,128)(2,1)S(1)}, bf16[32,2176]{1,0:T(8,128)(2,1)S(1)}, u32[]{:S(2)}, u32[]{:S(2)}) collective-permute-start(bf16[32,2176]{1,0:T(8,128)(2,1)S(1)} %prepare.1.refs_4_), channel_id=1, source_target_pairs={{0,12},{2,14},{4,0},{6,2},{8,4},{10,6},{12,8},{14,10},{1,13},{3,15... | collective-permute-start | bytes 417800 | tf_op jit(solution)/shard_map/ppermute | solution.py:218
  7.0 0.7 %collective-permute-start.2 = (bf16[32,2176]{1,0:T(8,128)(2,1)S(1)}, bf16[32,2176]{1,0:T(8,128)(2,1)S(1)}, u32[]{:S(2)}, u32[]{:S(2)}) collective-permute-start(bf16[32,2176]{1,0:T(8,128)(2,1)S(1)} %prepare.1.refs_4_), channel_id=1, source_target_pairs={{0,4},{2,6},{4,8},{6,10},{8,12},{10,14},{12,0},{14,2},{1,5},{3,7},... | collective-permute-start | bytes 417800 | tf_op jit(solution)/shard_map/ppermute | solution.py:218
  7.7 0.0 collective-permute-done.refs_12_
  7.7 1.5 %collective-permute-start.1 = (bf16[32,2176]{1,0:T(8,128)(2,1)S(1)}, bf16[32,2176]{1,0:T(8,128)(2,1)S(1)}, u32[]{:S(2)}, u32[]{:S(2)}) collective-permute-start(bf16[32,2176]{1,0:T(8,128)(2,1)S(1)} %prepare.1.refs_4_), channel_id=1, source_target_pairs={{0,2},{2,0},{4,6},{6,4},{8,10},{10,8},{12,14},{14,12},{1,3},{3,1},... | collective-permute-start | bytes 417800 | tf_op jit(solution)/shard_map/ppermute | solution.py:220
  9.2 4.0 %collective-permute-done.4.refs_6_ = bf16[32,2176]{1,0:T(8,128)(2,1)S(1)} collective-permute-done((bf16[32,2176]{1,0:T(8,128)(2,1)S(1)}, bf16[32,2176]{1,0:T(8,128)(2,1)S(1)}, u32[]{:S(2)}, u32[]{:S(2)}) %collective-permute-start.4) | collective-permute-done | bytes 139296 | tf_op jit(solution)/shard_map/ppermute | solution.py:218
  13.2 1.8 %collective-permute-start.5 = (bf16[32,2176]{1,0:T(8,128)(2,1)S(1)}, bf16[32,2176]{1,0:T(8,128)(2,1)S(1)}, u32[]{:S(2)}, u32[]{:S(2)}) collective-permute-start(bf16[32,2176]{1,0:T(8,128)(2,1)S(1)} %collective-permute-done.4.refs_6_), channel_id=1, source_target_pairs={{0,2},{2,0},{4,6},{6,4},{8,10},{10,8},{12,14},{14,12},{1,3},{3,1},... | collective-permute-start | bytes 417800 | tf_op jit(solution)/shard_map/ppermute | solution.py:222
  15.0 0.0 collective-permute-done.6.refs_7_
  15.0 0.2 collective-permute-start.7
  15.2 1.9 %collective-permute-done.2.refs_5_ = bf16[32,2176]{1,0:T(8,128)(2,1)S(1)} collective-permute-done((bf16[32,2176]{1,0:T(8,128)(2,1)S(1)}, bf16[32,2176]{1,0:T(8,128)(2,1)S(1)}, u32[]{:S(2)}, u32[]{:S(2)}) %collective-permute-start.2) | collective-permute-done | bytes 139296 | tf_op jit(solution)/shard_map/ppermute | solution.py:218
  17.1 1.5 %collective-permute-start.3 = (bf16[32,2176]{1,0:T(8,128)(2,1)S(1)}, bf16[32,2176]{1,0:T(8,128)(2,1)S(1)}, u32[]{:S(2)}, u32[]{:S(2)}) collective-permute-start(bf16[32,2176]{1,0:T(8,128)(2,1)S(1)} %collective-permute-done.2.refs_5_), channel_id=1, source_target_pairs={{0,2},{2,0},{4,6},{6,4},{8,10},{10,8},{12,14},{14,12},{1,3},{3,1},... | collective-permute-start | bytes 417800 | tf_op jit(solution)/shard_map/ppermute | solution.py:222
  18.6 0.0 collective-permute-start.12
  18.6 0.0 collective-permute-done.1.refs_0_
  18.6 0.5 collective-permute-start.13
  19.1 0.6 %collective-permute-done.5.refs_2_ = bf16[32,2176]{1,0:T(8,128)(2,1)S(1)} collective-permute-done((bf16[32,2176]{1,0:T(8,128)(2,1)S(1)}, bf16[32,2176]{1,0:T(8,128)(2,1)S(1)}, u32[]{:S(2)}, u32[]{:S(2)}) %collective-permute-start.5) | collective-permute-done | bytes 139296 | tf_op jit(solution)/shard_map/ppermute | solution.py:222
  19.8 0.0 collective-permute-start.14
  19.8 3.0 %collective-permute-done.7.refs_3_ = bf16[32,2176]{1,0:T(8,128)(2,1)S(1)} collective-permute-done((bf16[32,2176]{1,0:T(8,128)(2,1)S(1)}, bf16[32,2176]{1,0:T(8,128)(2,1)S(1)}, u32[]{:S(2)}, u32[]{:S(2)}) %collective-permute-start.7) | collective-permute-done | bytes 139296 | tf_op jit(solution)/shard_map/ppermute | solution.py:222
  22.8 0.0 collective-permute-start.8
  22.8 1.6 %collective-permute-done.3.refs_1_ = bf16[32,2176]{1,0:T(8,128)(2,1)S(1)} collective-permute-done((bf16[32,2176]{1,0:T(8,128)(2,1)S(1)}, bf16[32,2176]{1,0:T(8,128)(2,1)S(1)}, u32[]{:S(2)}, u32[]{:S(2)}) %collective-permute-start.3) | collective-permute-done | bytes 139296 | tf_op jit(solution)/shard_map/ppermute | solution.py:222
  24.3 0.0 collective-permute-start.10
  24.3 0.0 collective-permute-done.12.refs_13_
  24.3 0.5 collective-permute-start.11
  24.8 0.0 collective-permute-done.13.refs_14_
  24.8 0.1 collective-permute-start.9
  24.9 0.0 collective-permute-done.14.refs_15_
  24.9 0.0 collective-permute-done.8.refs_8_
  24.9 0.8 %collective-permute-done.10.refs_10_ = bf16[32,2176]{1,0:T(8,128)(2,1)S(1)} collective-permute-done((bf16[32,2176]{1,0:T(8,128)(2,1)S(1)}, bf16[32,2176]{1,0:T(8,128)(2,1)S(1)}, u32[]{:S(2)}, u32[]{:S(2)}) %collective-permute-start.10) | collective-permute-done | bytes 139296 | tf_op jit(solution)/shard_map/ppermute | solution.py:225
  25.7 0.2 collective-permute-done.11.refs_11_
  25.9 0.3 collective-permute-done.9.refs_9_
  26.2 0.0 copy-done
  26.2 0.0 copy-done.1
  26.2 8.9 %hidden.1 = (bf16[128,2048]{1,0:T(8,128)(2,1)S(1)}, bf16[128,2048]{1,0:T(8,128)(2,1)S(1)}) custom-call(bf16[32,2176]{1,0:T(8,128)(2,1)S(1)} %collective-permute-done.1.refs_0_, bf16[32,2176]{1,0:T(8,128)(2,1)S(1)} %collective-permute-done.3.refs_1_, bf16[32,2176]{1,0:T(8,128)(2,1)S(1)} %collective-permute-done.5.refs_2_, ...), custom_call_target="tpu_custom_call" | custom-call | flops 8589934592 | bytes 2097152 | tf_op jit(solution)/shard_map/hidden/pallas_call | solution.py:131
  35.1 0.0 slice-done
  35.2 0.0 slice-done.1
  35.2 0.0 slice-done.2
  35.2 0.0 slice-done.3
  35.2 1.3 %other.3 = bf16[128,2048]{1,0:T(8,128)(2,1)S(1)} custom-call(bf16[128,2048]{1,0:T(8,128)(2,1)S(1)} %get-tuple-element.19.hidden_ref, bf16[4,512,4096]{2,1,0:T(8,128)(2,1)S(1)} %bitcast.3), custom_call_target="tpu_custom_call" | custom-call | flops 524288 | bytes 512 | tf_op jit(solution)/shard_map/other/pallas_call | solution.py:175
  36.5 0.3 collective-permute-start.16
  36.8 1.3 %other.2 = bf16[128,2048]{1,0:T(8,128)(2,1)S(1)} custom-call(bf16[128,2048]{1,0:T(8,128)(2,1)S(1)} %get-tuple-element.17.hidden_ref, bf16[4,512,4096]{2,1,0:T(8,128)(2,1)S(1)} %bitcast.3), custom_call_target="tpu_custom_call" | custom-call | flops 524288 | bytes 512 | tf_op jit(solution)/shard_map/other/pallas_call | solution.py:175
  38.0 0.0 copy-start.2
  38.1 0.4 collective-permute-start.15
  38.4 0.0 collective-permute-done.16.refs_0_
  38.5 1.3 %mine.3 = (bf16[32,2048]{1,0:T(8,128)(2,1)S(1)}, bf16[32,2048]{1,0:T(8,128)(2,1)S(1)}, bf16[32,2048]{1,0:T(8,128)(2,1)S(1)}, bf16[32,2048]{1,0:T(8,128)(2,1)S(1)}) custom-call(bf16[128,2048]{1,0:T(8,128)(2,1)S(1)} %get-tuple-element.19.hidden_ref, bf16[4,512,4096]{2,1,0:T(8,128)(2,1)S(1)} %bitcast.3, bf16[128,2048]{1,0:T(8,128)(2,1)S(1)} %collective-permute-done.16.refs_0_), custom_call_target="tpu_custom_call" | custom-call | flops 524288 | bytes 512 | tf_op jit(solution)/shard_map/mine/pallas_call | solution.py:175
  39.8 1.5 %collective-permute-start.17 = (bf16[32,2048]{1,0:T(8,128)(2,1)S(1)}, bf16[32,2048]{1,0:T(8,128)(2,1)S(1)}, u32[]{:S(2)}, u32[]{:S(2)}) collective-permute-start(bf16[32,2048]{1,0:T(8,128)(2,1)S(1)} %get-tuple-element.20), channel_id=1, source_target_pairs={{0,2},{2,0},{4,6},{6,4},{8,10},{10,8},{12,14},{14,12},{1,3},{3,1},... | collective-permute-start | bytes 393224 | tf_op jit(solution)/shard_map/ppermute | solution.py:236
  41.2 0.6 collective-permute-start.19
  41.9 1.4 %collective-permute-start.21 = (bf16[32,2048]{1,0:T(8,128)(2,1)S(1)}, bf16[32,2048]{1,0:T(8,128)(2,1)S(1)}, u32[]{:S(2)}, u32[]{:S(2)}) collective-permute-start(bf16[32,2048]{1,0:T(8,128)(2,1)S(1)} %get-tuple-element.24), channel_id=1, source_target_pairs={{0,2},{2,0},{4,6},{6,4},{8,10},{10,8},{12,14},{14,12},{1,3},{3,1},... | collective-permute-start | bytes 393224 | tf_op jit(solution)/shard_map/ppermute | solution.py:236
  43.3 0.6 collective-permute-start.23
  43.9 0.0 collective-permute-done.15.refs_0_
  43.9 1.3 %mine.2 = (f32[32,2048]{1,0:T(8,128)S(1)}, f32[32,2048]{1,0:T(8,128)S(1)}, f32[32,2048]{1,0:T(8,128)S(1)}, f32[32,2048]{1,0:T(8,128)S(1)}) custom-call(bf16[128,2048]{1,0:T(8,128)(2,1)S(1)} %get-tuple-element.17.hidden_ref, bf16[4,512,4096]{2,1,0:T(8,128)(2,1)S(1)} %bitcast.3, bf16[128,2048]{1,0:T(8,128)(2,1)S(1)} %collective-permute-done.15.refs_0_), custom_call_target="tpu_custom_call" | custom-call | flops 524288 | bytes 512 | tf_op jit(solution)/shard_map/mine/pallas_call | solution.py:175
  45.2 1.0 %collective-permute-done.17 = bf16[32,2048]{1,0:T(8,128)(2,1)S(1)} collective-permute-done((bf16[32,2048]{1,0:T(8,128)(2,1)S(1)}, bf16[32,2048]{1,0:T(8,128)(2,1)S(1)}, u32[]{:S(2)}, u32[]{:S(2)}) %collective-permute-start.17) | collective-permute-done | bytes 131104 | tf_op jit(solution)/shard_map/ppermute | solution.py:236
  46.2 2.9 %collective-permute-start.18 = (bf16[32,2048]{1,0:T(8,128)(2,1)S(1)}, bf16[32,2048]{1,0:T(8,128)(2,1)S(1)}, u32[]{:S(2)}, u32[]{:S(2)}) collective-permute-start(bf16[32,2048]{1,0:T(8,128)(2,1)S(1)} %add_convert_fusion.3), channel_id=1, source_target_pairs={{0,8},{2,10},{4,12},{6,14},{8,0},{10,2},{12,4},{14,6},{1,9},{3,11}... | collective-permute-start | bytes 393224 | tf_op jit(solution)/shard_map/ppermute | solution.py:238
  49.1 0.0 collective-permute-done.19
  49.2 6.6 %collective-permute-start.20 = (bf16[32,2048]{1,0:T(8,128)(2,1)S(1)}, bf16[32,2048]{1,0:T(8,128)(2,1)S(1)}, u32[]{:S(2)}, u32[]{:S(2)}) collective-permute-start(bf16[32,2048]{1,0:T(8,128)(2,1)S(1)} %add_convert_fusion.2), channel_id=1, source_target_pairs={{0,12},{2,14},{4,0},{6,2},{8,4},{10,6},{12,8},{14,10},{1,13},{3,15... | collective-permute-start | bytes 393224 | tf_op jit(solution)/shard_map/ppermute | solution.py:238
  55.8 0.0 collective-permute-done.21
  55.9 0.1 collective-permute-start.22
  55.9 0.0 collective-permute-done.23
  55.9 0.0 collective-permute-done.18
  56.0 2.9 %collective-permute-done.20 = bf16[32,2048]{1,0:T(8,128)(2,1)S(1)} collective-permute-done((bf16[32,2048]{1,0:T(8,128)(2,1)S(1)}, bf16[32,2048]{1,0:T(8,128)(2,1)S(1)}, u32[]{:S(2)}, u32[]{:S(2)}) %collective-permute-start.20) | collective-permute-done | bytes 131104 | tf_op jit(solution)/shard_map/ppermute | solution.py:238
  58.8 3.9 %collective-permute-done.22 = bf16[32,2048]{1,0:T(8,128)(2,1)S(1)} collective-permute-done((bf16[32,2048]{1,0:T(8,128)(2,1)S(1)}, bf16[32,2048]{1,0:T(8,128)(2,1)S(1)}, u32[]{:S(2)}, u32[]{:S(2)}) %collective-permute-start.22) | collective-permute-done | bytes 131104 | tf_op jit(solution)/shard_map/ppermute | solution.py:238
  62.7 0.0 copy-done.2
  62.7 0.8 %add_convert_fusion = bf16[32,2048]{1,0:T(8,128)(2,1)} fusion(f32[32,2048]{1,0:T(8,128)S(1)} %get-tuple-element.25, bf16[32,2048]{1,0:T(8,128)(2,1)S(1)} %collective-permute-done.23, bf16[32,2048]{1,0:T(8,128)(2,1)S(1)} %collective-permute-done.22, bf16[32,2048]{1,0:T(8,128)(2,1)S(1)} %collective-permute-done.20, ...), kind=kLoop, calls=%fused_computation | loop fusion | flops 720896 | bytes 1048580 | tf_op jit(solution)/shard_map/convert_element_type | solution.py:240
  (9 shorter events, 0.1 us)
Async XLA Ops:
  0.0 35.1 %slice-start = ((s8[16777216]{0:T(1024)(128)(4,1)}), s8[4194304]{0:T(1024)(128)(4,1)S(1)}, s32[]{:S(2)}) async-start(s8[16777216]{0:T(1024)(128)(4,1)} %bitcast.2), calls=%async_computation | async-start | bytes 8388608
  0.0 26.2 %copy-start = (bf16[4,4096,512]{2,1,0:T(8,128)(2,1)S(1)}, bf16[4,4096,512]{2,1,0:T(8,128)(2,1)}, u32[]{:S(2)}) copy-start(bf16[4,4096,512]{2,1,0:T(8,128)(2,1)} %refs_16_.1) | copy-start | bytes 50331652
  0.0 26.2 %copy-start.1 = (bf16[4,4096,512]{2,1,0:T(8,128)(2,1)S(1)}, bf16[4,4096,512]{2,1,0:T(8,128)(2,1)}, u32[]{:S(2)}) copy-start(bf16[4,4096,512]{2,1,0:T(8,128)(2,1)} %refs_17_.1) | copy-start | bytes 50331652
  0.0 35.2 %slice-start.1 = ((s8[16777216]{0:T(1024)(128)(4,1)}), s8[4194304]{0:T(1024)(128)(4,1)S(1)}, s32[]{:S(2)}) async-start(s8[16777216]{0:T(1024)(128)(4,1)} %bitcast.2), calls=%async_computation.1 | async-start | bytes 8388608
  0.0 35.2 %slice-start.2 = ((s8[16777216]{0:T(1024)(128)(4,1)}), s8[4194304]{0:T(1024)(128)(4,1)S(1)}, s32[]{:S(2)}) async-start(s8[16777216]{0:T(1024)(128)(4,1)} %bitcast.2), calls=%async_computation.2 | async-start | bytes 8388608
  0.0 35.2 %slice-start.3 = ((s8[16777216]{0:T(1024)(128)(4,1)}), s8[4194304]{0:T(1024)(128)(4,1)S(1)}, s32[]{:S(2)}) async-start(s8[16777216]{0:T(1024)(128)(4,1)} %bitcast.2), calls=%async_computation.3 | async-start | bytes 8388608
  1.4 6.2 %collective-permute-start = (bf16[32,2176]{1,0:T(8,128)(2,1)S(1)}, bf16[32,2176]{1,0:T(8,128)(2,1)S(1)}, u32[]{:S(2)}, u32[]{:S(2)}) collective-permute-start(bf16[32,2176]{1,0:T(8,128)(2,1)S(1)} %prepare.1.refs_4_), channel_id=1, source_target_pairs={{0,1},{1,0},{2,3},{3,2},{4,5},{5,4},{6,7},{7,6},{8,9},{9,8},{10,11... | collective-permute-start | bytes 417800 | tf_op jit(solution)/shard_map/ppermute | solution.py:219
  2.0 11.2 %collective-permute-start.4 = (bf16[32,2176]{1,0:T(8,128)(2,1)S(1)}, bf16[32,2176]{1,0:T(8,128)(2,1)S(1)}, u32[]{:S(2)}, u32[]{:S(2)}) collective-permute-start(bf16[32,2176]{1,0:T(8,128)(2,1)S(1)} %prepare.1.refs_4_), channel_id=1, source_target_pairs={{0,8},{2,10},{4,12},{6,14},{8,0},{10,2},{12,4},{14,6},{1,9},{3,11}... | collective-permute-start | bytes 417800 | tf_op jit(solution)/shard_map/ppermute | solution.py:218
  5.6 9.3 %collective-permute-start.6 = (bf16[32,2176]{1,0:T(8,128)(2,1)S(1)}, bf16[32,2176]{1,0:T(8,128)(2,1)S(1)}, u32[]{:S(2)}, u32[]{:S(2)}) collective-permute-start(bf16[32,2176]{1,0:T(8,128)(2,1)S(1)} %prepare.1.refs_4_), channel_id=1, source_target_pairs={{0,12},{2,14},{4,0},{6,2},{8,4},{10,6},{12,8},{14,10},{1,13},{3,15... | collective-permute-start | bytes 417800 | tf_op jit(solution)/shard_map/ppermute | solution.py:218
  7.0 10.1 %collective-permute-start.2 = (bf16[32,2176]{1,0:T(8,128)(2,1)S(1)}, bf16[32,2176]{1,0:T(8,128)(2,1)S(1)}, u32[]{:S(2)}, u32[]{:S(2)}) collective-permute-start(bf16[32,2176]{1,0:T(8,128)(2,1)S(1)} %prepare.1.refs_4_), channel_id=1, source_target_pairs={{0,4},{2,6},{4,8},{6,10},{8,12},{10,14},{12,0},{14,2},{1,5},{3,7},... | collective-permute-start | bytes 417800 | tf_op jit(solution)/shard_map/ppermute | solution.py:218
  7.7 11.0 %collective-permute-start.1 = (bf16[32,2176]{1,0:T(8,128)(2,1)S(1)}, bf16[32,2176]{1,0:T(8,128)(2,1)S(1)}, u32[]{:S(2)}, u32[]{:S(2)}) collective-permute-start(bf16[32,2176]{1,0:T(8,128)(2,1)S(1)} %prepare.1.refs_4_), channel_id=1, source_target_pairs={{0,2},{2,0},{4,6},{6,4},{8,10},{10,8},{12,14},{14,12},{1,3},{3,1},... | collective-permute-start | bytes 417800 | tf_op jit(solution)/shard_map/ppermute | solution.py:220
  13.2 6.6 %collective-permute-start.5 = (bf16[32,2176]{1,0:T(8,128)(2,1)S(1)}, bf16[32,2176]{1,0:T(8,128)(2,1)S(1)}, u32[]{:S(2)}, u32[]{:S(2)}) collective-permute-start(bf16[32,2176]{1,0:T(8,128)(2,1)S(1)} %collective-permute-done.4.refs_6_), channel_id=1, source_target_pairs={{0,2},{2,0},{4,6},{6,4},{8,10},{10,8},{12,14},{14,12},{1,3},{3,1},... | collective-permute-start | bytes 417800 | tf_op jit(solution)/shard_map/ppermute | solution.py:222
  15.0 7.8 %collective-permute-start.7 = (bf16[32,2176]{1,0:T(8,128)(2,1)S(1)}, bf16[32,2176]{1,0:T(8,128)(2,1)S(1)}, u32[]{:S(2)}, u32[]{:S(2)}) collective-permute-start(bf16[32,2176]{1,0:T(8,128)(2,1)S(1)} %collective-permute-done.6.refs_7_), channel_id=1, source_target_pairs={{0,2},{2,0},{4,6},{6,4},{8,10},{10,8},{12,14},{14,12},{1,3},{3,1},... | collective-permute-start | bytes 417800 | tf_op jit(solution)/shard_map/ppermute | solution.py:222
  17.1 7.2 %collective-permute-start.3 = (bf16[32,2176]{1,0:T(8,128)(2,1)S(1)}, bf16[32,2176]{1,0:T(8,128)(2,1)S(1)}, u32[]{:S(2)}, u32[]{:S(2)}) collective-permute-start(bf16[32,2176]{1,0:T(8,128)(2,1)S(1)} %collective-permute-done.2.refs_5_), channel_id=1, source_target_pairs={{0,2},{2,0},{4,6},{6,4},{8,10},{10,8},{12,14},{14,12},{1,3},{3,1},... | collective-permute-start | bytes 417800 | tf_op jit(solution)/shard_map/ppermute | solution.py:222
  18.6 5.7 %collective-permute-start.12 = (bf16[32,2176]{1,0:T(8,128)(2,1)S(1)}, bf16[32,2176]{1,0:T(8,128)(2,1)S(1)}, u32[]{:S(2)}, u32[]{:S(2)}) collective-permute-start(bf16[32,2176]{1,0:T(8,128)(2,1)S(1)} %collective-permute-done.2.refs_5_), channel_id=1, source_target_pairs={{0,1},{1,0},{2,3},{3,2},{4,5},{5,4},{6,7},{7,6},{8,9},{9,8},{10,11... | collective-permute-start | bytes 417800 | tf_op jit(solution)/shard_map/ppermute | solution.py:225
  18.6 6.2 %collective-permute-start.13 = (bf16[32,2176]{1,0:T(8,128)(2,1)S(1)}, bf16[32,2176]{1,0:T(8,128)(2,1)S(1)}, u32[]{:S(2)}, u32[]{:S(2)}) collective-permute-start(bf16[32,2176]{1,0:T(8,128)(2,1)S(1)} %collective-permute-done.4.refs_6_), channel_id=1, source_target_pairs={{0,1},{1,0},{2,3},{3,2},{4,5},{5,4},{6,7},{7,6},{8,9},{9,8},{10,11... | collective-permute-start | bytes 417800 | tf_op jit(solution)/shard_map/ppermute | solution.py:225
  19.8 5.1 %collective-permute-start.14 = (bf16[32,2176]{1,0:T(8,128)(2,1)S(1)}, bf16[32,2176]{1,0:T(8,128)(2,1)S(1)}, u32[]{:S(2)}, u32[]{:S(2)}) collective-permute-start(bf16[32,2176]{1,0:T(8,128)(2,1)S(1)} %collective-permute-done.6.refs_7_), channel_id=1, source_target_pairs={{0,1},{1,0},{2,3},{3,2},{4,5},{5,4},{6,7},{7,6},{8,9},{9,8},{10,11... | collective-permute-start | bytes 417800 | tf_op jit(solution)/shard_map/ppermute | solution.py:225
  22.8 2.2 %collective-permute-start.8 = (bf16[32,2176]{1,0:T(8,128)(2,1)S(1)}, bf16[32,2176]{1,0:T(8,128)(2,1)S(1)}, u32[]{:S(2)}, u32[]{:S(2)}) collective-permute-start(bf16[32,2176]{1,0:T(8,128)(2,1)S(1)} %collective-permute-done.1.refs_0_), channel_id=1, source_target_pairs={{0,1},{1,0},{2,3},{3,2},{4,5},{5,4},{6,7},{7,6},{8,9},{9,8},{10,11... | collective-permute-start | bytes 417800 | tf_op jit(solution)/shard_map/ppermute | solution.py:225
  24.3 1.4 %collective-permute-start.10 = (bf16[32,2176]{1,0:T(8,128)(2,1)S(1)}, bf16[32,2176]{1,0:T(8,128)(2,1)S(1)}, u32[]{:S(2)}, u32[]{:S(2)}) collective-permute-start(bf16[32,2176]{1,0:T(8,128)(2,1)S(1)} %collective-permute-done.5.refs_2_), channel_id=1, source_target_pairs={{0,1},{1,0},{2,3},{3,2},{4,5},{5,4},{6,7},{7,6},{8,9},{9,8},{10,11... | collective-permute-start | bytes 417800 | tf_op jit(solution)/shard_map/ppermute | solution.py:225
  24.3 1.6 %collective-permute-start.11 = (bf16[32,2176]{1,0:T(8,128)(2,1)S(1)}, bf16[32,2176]{1,0:T(8,128)(2,1)S(1)}, u32[]{:S(2)}, u32[]{:S(2)}) collective-permute-start(bf16[32,2176]{1,0:T(8,128)(2,1)S(1)} %collective-permute-done.7.refs_3_), channel_id=1, source_target_pairs={{0,1},{1,0},{2,3},{3,2},{4,5},{5,4},{6,7},{7,6},{8,9},{9,8},{10,11... | collective-permute-start | bytes 417800 | tf_op jit(solution)/shard_map/ppermute | solution.py:225
  24.8 1.4 %collective-permute-start.9 = (bf16[32,2176]{1,0:T(8,128)(2,1)S(1)}, bf16[32,2176]{1,0:T(8,128)(2,1)S(1)}, u32[]{:S(2)}, u32[]{:S(2)}) collective-permute-start(bf16[32,2176]{1,0:T(8,128)(2,1)S(1)} %collective-permute-done.3.refs_1_), channel_id=1, source_target_pairs={{0,1},{1,0},{2,3},{3,2},{4,5},{5,4},{6,7},{7,6},{8,9},{9,8},{10,11... | collective-permute-start | bytes 417800 | tf_op jit(solution)/shard_map/ppermute | solution.py:225
  36.5 2.0 %collective-permute-start.16 = (bf16[128,2048]{1,0:T(8,128)(2,1)S(1)}, bf16[128,2048]{1,0:T(8,128)(2,1)S(1)}, u32[]{:S(2)}, u32[]{:S(2)}) collective-permute-start(bf16[128,2048]{1,0:T(8,128)(2,1)S(1)} %other.3), channel_id=1, source_target_pairs={{0,1},{1,0},{2,3},{3,2},{4,5},{5,4},{6,7},{7,6},{8,9},{9,8},{10,11... | collective-permute-start | bytes 1572872 | tf_op jit(solution)/shard_map/ppermute | solution.py:229
  38.0 24.6 %copy-start.2 = (bf16[32,4096]{1,0:T(8,128)(2,1)S(1)}, bf16[32,4096]{1,0:T(8,128)(2,1)}, u32[]{:S(2)}) copy-start(bf16[32,4096]{1,0:T(8,128)(2,1)} %refs_1_.1) | copy-start | bytes 786436
  38.1 5.9 %collective-permute-start.15 = (bf16[128,2048]{1,0:T(8,128)(2,1)S(1)}, bf16[128,2048]{1,0:T(8,128)(2,1)S(1)}, u32[]{:S(2)}, u32[]{:S(2)}) collective-permute-start(bf16[128,2048]{1,0:T(8,128)(2,1)S(1)} %other.2), channel_id=1, source_target_pairs={{0,1},{1,0},{2,3},{3,2},{4,5},{5,4},{6,7},{7,6},{8,9},{9,8},{10,11... | collective-permute-start | bytes 1572872 | tf_op jit(solution)/shard_map/ppermute | solution.py:229
  39.8 6.4 %collective-permute-start.17 = (bf16[32,2048]{1,0:T(8,128)(2,1)S(1)}, bf16[32,2048]{1,0:T(8,128)(2,1)S(1)}, u32[]{:S(2)}, u32[]{:S(2)}) collective-permute-start(bf16[32,2048]{1,0:T(8,128)(2,1)S(1)} %get-tuple-element.20), channel_id=1, source_target_pairs={{0,2},{2,0},{4,6},{6,4},{8,10},{10,8},{12,14},{14,12},{1,3},{3,1},... | collective-permute-start | bytes 393224 | tf_op jit(solution)/shard_map/ppermute | solution.py:236
  41.2 7.9 %collective-permute-start.19 = (bf16[32,2048]{1,0:T(8,128)(2,1)S(1)}, bf16[32,2048]{1,0:T(8,128)(2,1)S(1)}, u32[]{:S(2)}, u32[]{:S(2)}) collective-permute-start(bf16[32,2048]{1,0:T(8,128)(2,1)S(1)} %get-tuple-element.22), channel_id=1, source_target_pairs={{0,2},{2,0},{4,6},{6,4},{8,10},{10,8},{12,14},{14,12},{1,3},{3,1},... | collective-permute-start | bytes 393224 | tf_op jit(solution)/shard_map/ppermute | solution.py:236
  41.9 14.0 %collective-permute-start.21 = (bf16[32,2048]{1,0:T(8,128)(2,1)S(1)}, bf16[32,2048]{1,0:T(8,128)(2,1)S(1)}, u32[]{:S(2)}, u32[]{:S(2)}) collective-permute-start(bf16[32,2048]{1,0:T(8,128)(2,1)S(1)} %get-tuple-element.24), channel_id=1, source_target_pairs={{0,2},{2,0},{4,6},{6,4},{8,10},{10,8},{12,14},{14,12},{1,3},{3,1},... | collective-permute-start | bytes 393224 | tf_op jit(solution)/shard_map/ppermute | solution.py:236
  43.3 12.7 %collective-permute-start.23 = (bf16[32,2048]{1,0:T(8,128)(2,1)S(1)}, bf16[32,2048]{1,0:T(8,128)(2,1)S(1)}, u32[]{:S(2)}, u32[]{:S(2)}) collective-permute-start(bf16[32,2048]{1,0:T(8,128)(2,1)S(1)} %get-tuple-element.26), channel_id=1, source_target_pairs={{0,2},{2,0},{4,6},{6,4},{8,10},{10,8},{12,14},{14,12},{1,3},{3,1},... | collective-permute-start | bytes 393224 | tf_op jit(solution)/shard_map/ppermute | solution.py:236
  46.2 9.7 %collective-permute-start.18 = (bf16[32,2048]{1,0:T(8,128)(2,1)S(1)}, bf16[32,2048]{1,0:T(8,128)(2,1)S(1)}, u32[]{:S(2)}, u32[]{:S(2)}) collective-permute-start(bf16[32,2048]{1,0:T(8,128)(2,1)S(1)} %add_convert_fusion.3), channel_id=1, source_target_pairs={{0,8},{2,10},{4,12},{6,14},{8,0},{10,2},{12,4},{14,6},{1,9},{3,11}... | collective-permute-start | bytes 393224 | tf_op jit(solution)/shard_map/ppermute | solution.py:238
  49.2 9.6 %collective-permute-start.20 = (bf16[32,2048]{1,0:T(8,128)(2,1)S(1)}, bf16[32,2048]{1,0:T(8,128)(2,1)S(1)}, u32[]{:S(2)}, u32[]{:S(2)}) collective-permute-start(bf16[32,2048]{1,0:T(8,128)(2,1)S(1)} %add_convert_fusion.2), channel_id=1, source_target_pairs={{0,12},{2,14},{4,0},{6,2},{8,4},{10,6},{12,8},{14,10},{1,13},{3,15... | collective-permute-start | bytes 393224 | tf_op jit(solution)/shard_map/ppermute | solution.py:238
  55.9 6.8 %collective-permute-start.22 = (bf16[32,2048]{1,0:T(8,128)(2,1)S(1)}, bf16[32,2048]{1,0:T(8,128)(2,1)S(1)}, u32[]{:S(2)}, u32[]{:S(2)}) collective-permute-start(bf16[32,2048]{1,0:T(8,128)(2,1)S(1)} %add_convert_fusion.1), channel_id=1, source_target_pairs={{0,4},{2,6},{4,8},{6,10},{8,12},{10,14},{12,0},{14,2},{1,5},{3,7},... | collective-permute-start | bytes 393224 | tf_op jit(solution)/shard_map/ppermute | solution.py:238
